TPU v7x, 32 devices: a whole 2x2x4 slice. The times are simulated.
32 devices in a mesh: ta: 4 (over y, core), ha: 8 (over z, x).
Axes of the slice: x: 2, y: 2, z: 4, core: 2. Of those that a mesh axis runs over, the one named last changes fastest.
Arguments:
- query_states: bfloat16 [8, 16, 56, 768], P('ta', 'ha'), may hold values from -51 to 51
- key_states: bfloat16 [8, 16, 56, 768], P('ta', 'ha'), may hold values from -6 to 6
- value_states: bfloat16 [8, 16, 56, 768], P('ta', 'ha'), may hold values from -6 to 6
- conv_weight: bfloat16 [27, 768], replicated, may hold values from -1.1953125 to 1.1953125
- out_grad: bfloat16 [8, 16, 56, 768], P('ta', 'ha'), may hold values from -6 to 6
- tile_mask: int32 [4, 8, 9], replicated, may hold values from 0 to 1, as said below
- clip_lengths: int32 [8], replicated, may hold values from 2 to 56
Outputs:
- layer_out: bfloat16 [8, 16, 56, 768], P('ta', 'ha')
- query_grad: bfloat16 [8, 16, 56, 768], P('ta', 'ha')
- key_grad: bfloat16 [8, 16, 56, 768], P('ta', 'ha')
- value_grad: bfloat16 [8, 16, 56, 768], P('ta', 'ha')
Inputs may be any that keep to these rules, and one draw needn't show every extreme that they name: `tile_mask`: entries are 0 or 1; entry 4, a tile's own keys, is always 1.
All inputs are finite; a program needn't handle non-finite values.
Results may differ from a plain program's by a relative error of at most 0.0095.
Values may be sent and summed in bfloat16 or wider, within the bound.
No kernel may reach another device: no remote copies, remote signals or barrier semaphores. Data moves between devices by JAX's collectives and lax.ppermute only.
A program may use at most 128 MiB of HBM per device.

v0:
```python
import jax
import jax.numpy as jnp
from jax import lax
from jax.sharding import PartitionSpec as P

HEAD_DIM = 128


CONTRACT_LAST = (((1,), (1,)), ((), ()))
CONTRACT_FIRST = (((0,), (0,)), ((), ()))


def from_behind(x, axis, by):
    devices = lax.axis_size(axis)
    pairs = [(i, i + by) for i in range(devices) if 0 <= i + by < devices]
    return lax.ppermute(x, axis, pairs)


def padded(cells, sides, width):
    for axis, dim in sides:
        count = lax.axis_size(axis)
        ends = count - 1
        head = lax.slice_in_dim(cells, 0, width, axis=dim)
        tail = lax.slice_in_dim(cells, cells.shape[dim] - width, cells.shape[dim], axis=dim)
        cells = jnp.concatenate(
            [
                lax.ppermute(tail, axis, [(i, (i + 1) % count) for i in range(ends)]),
                cells,
                lax.ppermute(head, axis, [((i + 1) % count, i) for i in range(ends)]),
            ],
            axis=dim,
        )
    return cells


def depthwise(source, weight, size_t, size_h, width_len):
    result = jnp.zeros((size_t, size_h, width_len, source.shape[3]), jnp.float32)
    for offset_id in range(27):
        step_t, step_h, step_w = (offset_id // 9, offset_id // 3 % 3, offset_id % 3)
        piece = source[
            step_t : step_t + size_t, step_h : step_h + size_h, step_w : step_w + width_len
        ].astype(jnp.float32)
        result = result + weight[offset_id].astype(jnp.float32) * piece
    return result


def window_valid(tile_mask, clip_lengths, index_t, index_h, count_t, count_h, tile_side, width_len):
    tile_offset = jnp.arange(3 * tile_side) // tile_side
    frame_ids = index_t * tile_side - tile_side + jnp.arange(3 * tile_side)
    in_time = (frame_ids >= 0) & (frame_ids < count_t * tile_side)
    frame_lens = jnp.where(
        in_time, clip_lengths[jnp.clip(frame_ids, 0, count_t * tile_side - 1)], 0
    )
    height_ids = index_h + tile_offset - 1
    in_height = (height_ids >= 0) & (height_ids < count_h)
    entries = tile_mask[index_t, index_h].reshape(3, 3)
    kept_tiles = entries[tile_offset][:, tile_offset] == 1
    columns = jnp.arange(width_len)
    key_valid = (
        kept_tiles[:, :, None]
        & in_height[None, :, None]
        & (columns[None, None, :] < frame_lens[:, None, None])
    )
    return key_valid.reshape(-1)


def return_partials(partials, tile_side):
    upper_part = partials[:, :tile_side]
    middle = partials[:, tile_side : 2 * tile_side]
    lower_part = partials[:, 2 * tile_side :]
    for direction, piece_grad in ((-1, upper_part), (1, lower_part)):
        middle = middle + from_behind(piece_grad.astype(jnp.bfloat16), "ta", direction).astype(
            jnp.float32
        )
    left_part = middle[:, :, :tile_side]
    centre = middle[:, :, tile_side : 2 * tile_side]
    right_part = middle[:, :, 2 * tile_side :]
    for direction, piece_grad in ((-1, left_part), (1, right_part)):
        centre = centre + from_behind(piece_grad.astype(jnp.bfloat16), "ha", direction).astype(
            jnp.float32
        )
    return centre


def head_cols(matrix, head_id):
    return lax.dynamic_slice_in_dim(matrix, head_id * HEAD_DIM, HEAD_DIM, 1)


def heads_to_rows(stacked):
    return stacked.transpose(1, 0, 2).reshape(stacked.shape[1], -1)


def shards(query_states, key_states, value_states, conv_weight, out_grad, tile_mask, clip_lengths):
    tile_side, tile_other, width_len, channels = query_states.shape
    head_count = channels // HEAD_DIM
    score_scale = HEAD_DIM ** (-0.5)
    index_t = lax.axis_index("ta")
    index_h = lax.axis_index("ha")
    count_t = lax.axis_size("ta")
    count_h = lax.axis_size("ha")
    queries = tile_side * tile_side * width_len
    window_len = 3 * tile_side
    tile_shape = (tile_side, tile_side, width_len, channels)
    window_shape = (window_len, window_len, width_len, channels)
    window = padded(jnp.stack([key_states, value_states]), (("ta", 1), ("ha", 2)), tile_side)
    key_window = window[0]
    value_window = window[1]
    key_valid = window_valid(
        tile_mask, clip_lengths, index_t, index_h, count_t, count_h, tile_side, width_len
    )
    query_flat = query_states.reshape(queries, channels)
    grad_flat = out_grad.reshape(queries, channels)
    key_flat = key_window.reshape(-1, channels)
    value_flat = value_window.reshape(-1, channels)

    def forward_head(head_id):
        query_head = head_cols(query_flat, head_id)
        grad_head = head_cols(grad_flat, head_id)
        key_head = head_cols(key_flat, head_id)
        value_head = head_cols(value_flat, head_id)
        scores = (
            lax.dot_general(query_head, key_head, CONTRACT_LAST, preferred_element_type=jnp.float32)
            * score_scale
        )
        scores = jnp.where(key_valid[None, :], scores, -jnp.inf)
        row_max = jnp.max(scores, axis=-1, keepdims=True)
        exponent = jnp.exp(scores - row_max)
        row_total = jnp.sum(exponent, axis=-1, keepdims=True)
        softmax_p = exponent / row_total
        probs_bf = softmax_p.astype(jnp.bfloat16)
        attention = jnp.dot(probs_bf, value_head, preferred_element_type=jnp.float32)
        row_delta = jnp.sum(grad_head.astype(jnp.float32) * attention, axis=-1)
        dprobs = lax.dot_general(
            grad_head, value_head, CONTRACT_LAST, preferred_element_type=jnp.float32
        )
        dscores = (softmax_p * (dprobs - row_delta[:, None])).astype(jnp.bfloat16)
        query_part = jnp.dot(dscores, key_head, preferred_element_type=jnp.float32) * score_scale
        log_total = row_max[:, 0] + jnp.log(row_total[:, 0])
        key_part = (
            lax.dot_general(dscores, query_head, CONTRACT_FIRST, preferred_element_type=jnp.float32)
            * score_scale
        )
        value_part = lax.dot_general(
            probs_bf, grad_head, CONTRACT_FIRST, preferred_element_type=jnp.float32
        )
        return (attention, query_part, log_total, row_delta, key_part, value_part)

    attention_h, query_h, total_h, delta_h, key_h, value_h = lax.map(
        forward_head, jnp.arange(head_count, dtype=jnp.int32)
    )
    attention = heads_to_rows(attention_h)
    value_slab = value_window[tile_side - 1 : 2 * tile_side + 1, tile_side - 1 : 2 * tile_side + 1]
    value_slab = jnp.pad(value_slab, ((0, 0), (0, 0), (1, 1), (0, 0)))
    conv_out = depthwise(value_slab, conv_weight, tile_side, tile_side, width_len)
    layer_out = (attention.reshape(tile_shape) + conv_out).astype(jnp.bfloat16)
    query_grad = heads_to_rows(query_h).reshape(tile_shape).astype(jnp.bfloat16)
    key_part = heads_to_rows(key_h)
    value_part = heads_to_rows(value_h)
    value_padded = jnp.pad(value_part.reshape(window_shape), ((0, 0), (0, 0), (1, 1), (0, 0)))
    grad_full = out_grad.astype(jnp.float32)
    for offset_id in range(27):
        step_t, step_h, step_w = (offset_id // 9, offset_id // 3 % 3, offset_id % 3)
        first_t = tile_side - 1 + step_t
        first_h = tile_side - 1 + step_h
        value_padded = value_padded.at[
            first_t : first_t + tile_side,
            first_h : first_h + tile_side,
            step_w : step_w + width_len,
        ].add(conv_weight[offset_id].astype(jnp.float32) * grad_full)
    value_part = value_padded[:, :, 1 : width_len + 1]
    partials = jnp.stack([key_part.reshape(window_shape), value_part])
    owned_grads = return_partials(partials, tile_side)
    key_grad = owned_grads[0].astype(jnp.bfloat16)
    value_grad = owned_grads[1].astype(jnp.bfloat16)
    return (layer_out, query_grad, key_grad, value_grad)


def solution(mesh):
    placed = (
        P("ta", "ha", None, None),
        P("ta", "ha", None, None),
        P("ta", "ha", None, None),
        P(),
        P("ta", "ha", None, None),
        P(),
        P(),
    )
    return jax.shard_map(
        shards,
        mesh=mesh,
        in_specs=placed,
        out_specs=(
            P("ta", "ha", None, None),
            P("ta", "ha", None, None),
            P("ta", "ha", None, None),
            P("ta", "ha", None, None),
        ),
        check_vma=False,
    )
```

profile of v0, /device:TPU:9, one launch (start us, length us, event | category | flops | bytes accessed | tf_op | source)
XLA Modules:
  0.0 413.3 jit_solution(4228054760920114539)
XLA Ops:
  1.9 3.7 collective-permute-start
  7.6 5.9 %collective-permute-done = bf16[2,2,2,56,768]{4,3,2,1,0:T(8,128)(2,1)S(1)} collective-permute-done((bf16[2,2,2,56,768]{4,3,2,1,0:T(8,128)(2,1)S(1)}, bf16[2,2,2,56,768]{4,3,2,1,0:T(8,128)(2,1)S(1)}, u32[]{:S(2)}, u32[]{:S(2)}) %collective-permute-start) | collective-permute-done | bytes 688160 | tf_op jit(solution)/shard_map/ppermute | solution.py:27
  13.5 4.4 %collective-permute-done.1 = bf16[2,2,2,56,768]{4,3,2,1,0:T(8,128)(2,1)S(1)} collective-permute-done((bf16[2,2,2,56,768]{4,3,2,1,0:T(8,128)(2,1)S(1)}, bf16[2,2,2,56,768]{4,3,2,1,0:T(8,128)(2,1)S(1)}, u32[]{:S(2)}, u32[]{:S(2)}) %collective-permute-start.1) | collective-permute-done | bytes 688160 | tf_op jit(solution)/shard_map/ppermute | solution.py:29
  17.9 2.6 pad_maximum_fusion.2
  20.5 3.5 collective-permute-start.2
  24.0 2.7 collective-permute-start.3
  31.1 74.1 %collective-permute-done.2 = bf16[2,6,2,56,768]{4,3,2,1,0:T(8,128)(2,1)} collective-permute-done((bf16[2,6,2,56,768]{4,3,2,1,0:T(8,128)(2,1)}, bf16[2,6,2,56,768]{4,3,2,1,0:T(8,128)(2,1)}, u32[]{:S(2)}, u32[]{:S(2)}) %collective-permute-start.2) | collective-permute-done | bytes 2064416 | tf_op jit(solution)/shard_map/ppermute | solution.py:27
  107.0 3.2 pad_maximum_fusion.1
  110.2 3.3 slice_bitcast_fusion.3
  114.1 81.5 %while.44 = (s32[]{:T(128)}, f32[6,224,128]{2,1,0:T(8,128)}, bf16[6,224,128]{2,1,0:T(8,128)(2,1)}, f32[6,2016,128]{2,1,0:T(8,128)}, f32[6,2016,128]{2,1,0:T(8,12...) while((s32[]{:T(128)}, f32[6,224,128]{2,1,0:T(8,128)}, ...), condition=%wide.region_4.5_spmd.clone, body=%wide.region_0.4_spmd.clone.sunk | while | flops 701232448 | bytes 16710735 | solution.py:148
  120.4 2.2 bitcast_dynamic-update-slice_fusion.2
  124.3 2.4 fusion.111
  134.0 2.2 bitcast_dynamic-update-slice_fusion.2
  137.9 2.3 fusion.111
  147.5 2.2 bitcast_dynamic-update-slice_fusion.2
  151.5 2.3 fusion.111
  161.1 2.2 bitcast_dynamic-update-slice_fusion.2
  165.1 2.3 fusion.111
  174.7 2.2 bitcast_dynamic-update-slice_fusion.2
  178.6 2.4 fusion.111
  188.3 2.2 bitcast_dynamic-update-slice_fusion.2
  192.3 2.3 fusion.111
  195.6 10.7 %copy.22 = f32[2016,6,128]{2,1,0:T(8,128)} copy(f32[2016,6,128]{2,0,1:T(8,128)} %bitcast.91) | data formatting | bytes 12386304 | tf_op jit(solution)/shard_map/transpose | solution.py:90
  206.4 8.9 %reshape_reshape.8 = f32[6,6,56,768]{3,2,1,0:T(8,128)} reshape(f32[2016,6,128]{2,1,0:T(8,128)} %copy.22) | data formatting | bytes 12386304 | tf_op jit(solution)/shard_map/reshape;reshape | solution.py:159
  215.2 3.5 pad.117
  218.9 2.9 copy-done.3
  222.0 3.3 scatter-add.91
  226.5 3.3 scatter-add.94
  229.9 2.1 fusion.42
  233.2 3.3 scatter-add.96
  237.7 3.3 scatter-add.99
  241.1 2.0 fusion.46
  244.4 3.3 scatter-add.101
  248.9 3.3 scatter-add.104
  252.3 2.0 fusion.50
  255.5 3.3 scatter-add.106
  260.1 3.3 scatter-add.109
  266.7 3.3 scatter-add.111
  271.3 3.3 scatter-add.114
  274.6 2.0 fusion.58
  277.9 3.3 scatter-add.116
  282.5 3.3 scatter-add.119
  285.8 2.0 fusion.62
  289.1 3.4 scatter-add.121
  293.7 3.4 scatter-add.124
  300.3 3.3 scatter-add.126
  304.9 3.3 scatter-add.129
  308.2 2.0 fusion.70
  311.5 3.3 scatter-add.131
  316.1 3.5 scatter-add.134
  319.5 6.4 %slice_bitcast_fusion = f32[1,6,6,56,768]{4,3,2,1,0:T(8,128)} fusion(f32[6,6,58,768]{3,2,1,0:T(8,128)} %scatter-add.134), kind=kLoop, calls=%fused_computation.44 | loop fusion | bytes 12386304 | tf_op jit(solution)/shard_map/stack | solution.py:171
  326.0 12.6 %copy.21 = f32[2016,6,128]{2,1,0:T(8,128)} copy(f32[2016,6,128]{2,0,1:T(8,128)S(1)} %bitcast.90) | data formatting | bytes 12386304 | tf_op jit(solution)/shard_map/transpose | solution.py:90
  338.5 9.0 %stack_reshape_reshape.3 = f32[1,6,6,56,768]{4,3,2,1,0:T(8,128)} reshape(f32[2016,6,128]{2,1,0:T(8,128)} %copy.21) | data formatting | bytes 12386304 | tf_op jit(solution)/shard_map/stack;reshape;reshape | solution.py:171
  347.6 8.2 %fusion.31 = bf16[2,6,6,56,768]{4,3,2,1,0:T(8,128)(2,1)} fusion(f32[1,6,6,56,768]{4,3,2,1,0:T(8,128)} %slice_bitcast_fusion, f32[1,6,6,56,768]{4,3,2,1,0:T(8,128)} %stack_reshape_reshape.3), kind=kLoop, calls=%fused_computation.43 | loop fusion | flops 3096576 | bytes 18579456 | tf_op jit(solution)/shard_map/convert.32
  355.8 2.6 fusion.81
  358.4 2.5 collective-permute-start.4
  360.9 3.6 collective-permute-start.5
  364.5 21.5 %collective-permute-done.4 = bf16[2,2,6,56,768]{4,3,2,1,0:T(8,128)(2,1)S(1)} collective-permute-done((bf16[2,2,6,56,768]{4,3,2,1,0:T(8,128)(2,1)S(1)}, bf16[2,2,6,56,768]{4,3,2,1,0:T(8,128)(2,1)S(1)}, u32[]{:S(2)}, u32[]{:S(2)}) %collective-permute-start.4) | collective-permute-done | bytes 2064416 | tf_op jit(solution)/shard_map/ppermute | solution.py:16
  386.9 2.6 fusion.78
  390.7 2.0 collective-permute-start.6
  392.7 3.4 collective-permute-start.7
  397.4 2.3 reshape_reshape.7
  401.8 2.2 convert_element_type.514
  404.0 6.5 %add_convert_fusion = bf16[2,2,56,768]{3,2,1,0:T(8,128)(2,1)} fusion(f32[2,2,56,768]{3,2,1,0:T(8,128)} %reshape_reshape.7, bf16[6,6,56,768]{3,2,1,0:T(8,128)(2,1)S(1)} %copy-done.5, f32[768]{0:T(1024)S(1)} %get-tuple-element.469, f32[768]{0:T(1024)S(1)} %get-tuple-element.470, f32[768]{0:T(1024)S(1)} %get-tuple-element.445, f32[768]{0:T(1024)S(1)} %get-tuple-element.446, ...), kind=kLoop, calls=%fused_computation.117 | loop fusion | flops 14106624 | bytes 5587968 | tf_op jit(solution)/shard_map/convert_element_type | solution.py:155
  (169 shorter events, 93.8 us)
Async XLA Ops:
  0.6 26.1 %copy-start = (s32[4,8,9]{2,1,0:T(8,128)S(1)}, s32[4,8,9]{2,1,0:T(8,128)}, u32[]{:S(2)}) copy-start(s32[4,8,9]{2,1,0:T(8,128)} %param.68) | copy-start | bytes 3460
  0.6 106.3 %copy-start.7 = (bf16[2,2,56,768]{3,2,1,0:T(8,128)(2,1)S(1)}, bf16[2,2,56,768]{3,2,1,0:T(8,128)(2,1)}, u32[]{:S(2)}) copy-start(bf16[2,2,56,768]{3,2,1,0:T(8,128)(2,1)} %param.64) | copy-start | bytes 1032196
  0.7 106.3 %copy-start.6 = (bf16[2,2,56,768]{3,2,1,0:T(8,128)(2,1)S(1)}, bf16[2,2,56,768]{3,2,1,0:T(8,128)(2,1)}, u32[]{:S(2)}) copy-start(bf16[2,2,56,768]{3,2,1,0:T(8,128)(2,1)} %param.65) | copy-start | bytes 1032196
  0.7 29.0 %copy-start.10 = (bf16[27,768]{1,0:T(8,128)(2,1)S(1)}, bf16[27,768]{1,0:T(8,128)(2,1)}, u32[]{:S(2)}) copy-start(bf16[27,768]{1,0:T(8,128)(2,1)} %param.66) | copy-start | bytes 124420
  1.9 11.6 %collective-permute-start = (bf16[2,2,2,56,768]{4,3,2,1,0:T(8,128)(2,1)S(1)}, bf16[2,2,2,56,768]{4,3,2,1,0:T(8,128)(2,1)S(1)}, u32[]{:S(2)}, u32[]{:S(2)}) collective-permute-start(bf16[2,2,2,56,768]{4,3,2,1,0:T(8,128)(2,1)S(1)} %pad_maximum_fusion.3), channel_id=1, source_target_pairs={{0,8},{8,16},{16,24},{1,9},{9,17},{17,25},{2,10},{10,18},{18,26},{... | collective-permute-start | bytes 2064392 | tf_op jit(solution)/shard_map/ppermute | solution.py:27
  5.6 12.3 %collective-permute-start.1 = (bf16[2,2,2,56,768]{4,3,2,1,0:T(8,128)(2,1)S(1)}, bf16[2,2,2,56,768]{4,3,2,1,0:T(8,128)(2,1)S(1)}, u32[]{:S(2)}, u32[]{:S(2)}) collective-permute-start(bf16[2,2,2,56,768]{4,3,2,1,0:T(8,128)(2,1)S(1)} %pad_maximum_fusion.3), channel_id=1, source_target_pairs={{8,0},{16,8},{24,16},{9,1},{17,9},{25,17},{10,2},{18,10},{26,18},{... | collective-permute-start | bytes 2064392 | tf_op jit(solution)/shard_map/ppermute | solution.py:29
  20.5 84.7 %collective-permute-start.2 = (bf16[2,6,2,56,768]{4,3,2,1,0:T(8,128)(2,1)}, bf16[2,6,2,56,768]{4,3,2,1,0:T(8,128)(2,1)}, u32[]{:S(2)}, u32[]{:S(2)}) collective-permute-start(bf16[2,6,2,56,768]{4,3,2,1,0:T(8,128)(2,1)} %pad_maximum_fusion.2), channel_id=1, source_target_pairs={{0,1},{1,2},{2,3},{3,4},{4,5},{5,6},{6,7},{8,9},{9,10},{10,11},{11... | collective-permute-start | bytes 6193160 | tf_op jit(solution)/shard_map/ppermute | solution.py:27
  24.0 82.9 %collective-permute-start.3 = (bf16[2,6,2,56,768]{4,3,2,1,0:T(8,128)(2,1)}, bf16[2,6,2,56,768]{4,3,2,1,0:T(8,128)(2,1)}, u32[]{:S(2)}, u32[]{:S(2)}) collective-permute-start(bf16[2,6,2,56,768]{4,3,2,1,0:T(8,128)(2,1)} %pad_maximum_fusion.2), channel_id=1, source_target_pairs={{1,0},{2,1},{3,2},{4,3},{5,4},{6,5},{7,6},{9,8},{10,9},{11,10},{12... | collective-permute-start | bytes 6193160 | tf_op jit(solution)/shard_map/ppermute | solution.py:29
  110.2 3.9 copy-start.2
  114.1 2.0 copy-start.14
  122.6 5.2 %copy-start.15 = (pred[6,6]{1,0:T(8,128)(4,1)S(1)}, pred[6,6]{1,0:T(8,128)(4,1)}, u32[]{:S(2)}) copy-start(pred[6,6]{1,0:T(8,128)(4,1)} %copy-done.14) | copy-start | bytes 112 | tf_op jit(solution)/shard_map/while
  127.7 2.0 copy-start.14
  136.2 5.1 %copy-start.15 = (pred[6,6]{1,0:T(8,128)(4,1)S(1)}, pred[6,6]{1,0:T(8,128)(4,1)}, u32[]{:S(2)}) copy-start(pred[6,6]{1,0:T(8,128)(4,1)} %copy-done.14) | copy-start | bytes 112 | tf_op jit(solution)/shard_map/while
  141.3 2.0 copy-start.14
  149.7 5.1 %copy-start.15 = (pred[6,6]{1,0:T(8,128)(4,1)S(1)}, pred[6,6]{1,0:T(8,128)(4,1)}, u32[]{:S(2)}) copy-start(pred[6,6]{1,0:T(8,128)(4,1)} %copy-done.14) | copy-start | bytes 112 | tf_op jit(solution)/shard_map/while
  154.8 2.0 copy-start.14
  163.3 5.1 %copy-start.15 = (pred[6,6]{1,0:T(8,128)(4,1)S(1)}, pred[6,6]{1,0:T(8,128)(4,1)}, u32[]{:S(2)}) copy-start(pred[6,6]{1,0:T(8,128)(4,1)} %copy-done.14) | copy-start | bytes 112 | tf_op jit(solution)/shard_map/while
  168.4 2.0 copy-start.14
  176.9 5.2 %copy-start.15 = (pred[6,6]{1,0:T(8,128)(4,1)S(1)}, pred[6,6]{1,0:T(8,128)(4,1)}, u32[]{:S(2)}) copy-start(pred[6,6]{1,0:T(8,128)(4,1)} %copy-done.14) | copy-start | bytes 112 | tf_op jit(solution)/shard_map/while
  182.1 2.0 copy-start.14
  190.5 5.1 %copy-start.15 = (pred[6,6]{1,0:T(8,128)(4,1)S(1)}, pred[6,6]{1,0:T(8,128)(4,1)}, u32[]{:S(2)}) copy-start(pred[6,6]{1,0:T(8,128)(4,1)} %copy-done.14) | copy-start | bytes 112 | tf_op jit(solution)/shard_map/while
  218.9 2.9 copy-start.3
  225.3 17.8 %copy-start.13 = (f32[768]{0:T(1024)S(1)}, f32[768]{0:T(1024)}, u32[]{:S(2)}) copy-start(f32[768]{0:T(1024)} %get-tuple-element.462) | copy-start | bytes 9220
  229.9 17.8 %copy-start.12 = (f32[768]{0:T(1024)S(1)}, f32[768]{0:T(1024)}, u32[]{:S(2)}) copy-start(f32[768]{0:T(1024)} %get-tuple-element.461) | copy-start | bytes 9220
  233.2 19.1 %copy-start.11 = (f32[768]{0:T(1024)S(1)}, f32[768]{0:T(1024)}, u32[]{:S(2)}) copy-start(f32[768]{0:T(1024)} %get-tuple-element.460) | copy-start | bytes 9220
  316.1 9.9 %slice-start.2 = ((s8[6193152]{0:T(1024)(128)(4,1)}), s8[1998848]{0:T(1024)(128)(4,1)S(1)}, s32[]{:S(2)}) async-start(s8[6193152]{0:T(1024)(128)(4,1)} %bitcast.88), calls=%async_computation.2 | async-start | bytes 3997696
  319.5 6.4 %slice-start.3 = ((s8[6193152]{0:T(1024)(128)(4,1)}), s8[4194304]{0:T(1024)(128)(4,1)S(1)}, s32[]{:S(2)}) async-start(s8[6193152]{0:T(1024)(128)(4,1)} %bitcast.88), calls=%async_computation.3 | async-start | bytes 8388608
  338.5 48.3 %slice-start = ((s8[6193152]{0:T(1024)(128)(4,1)}), s8[1998848]{0:T(1024)(128)(4,1)S(1)}, s32[]{:S(2)}) async-start(s8[6193152]{0:T(1024)(128)(4,1)} %bitcast.85), calls=%async_computation | async-start | bytes 3997696
  347.6 39.3 %slice-start.1 = ((s8[6193152]{0:T(1024)(128)(4,1)}), s8[4194304]{0:T(1024)(128)(4,1)S(1)}, s32[]{:S(2)}) async-start(s8[6193152]{0:T(1024)(128)(4,1)} %bitcast.85), calls=%async_computation.1 | async-start | bytes 8388608
  355.8 31.1 %copy-start.4 = (f32[1,6,6,56,768]{4,3,2,1,0:T(8,128)S(1)}, f32[1,6,6,56,768]{4,3,2,1,0:T(8,128)}, u32[]{:S(2)}) copy-start(f32[1,6,6,56,768]{4,3,2,1,0:T(8,128)} %stack_reshape_reshape.3) | copy-start | bytes 18579460
  358.4 27.5 %collective-permute-start.4 = (bf16[2,2,6,56,768]{4,3,2,1,0:T(8,128)(2,1)S(1)}, bf16[2,2,6,56,768]{4,3,2,1,0:T(8,128)(2,1)S(1)}, u32[]{:S(2)}, u32[]{:S(2)}) collective-permute-start(bf16[2,2,6,56,768]{4,3,2,1,0:T(8,128)(2,1)S(1)} %get-tuple-element.501), channel_id=1, source_target_pairs={{8,0},{16,8},{24,16},{9,1},{17,9},{25,17},{10,2},{18,10},{26,18},{... | collective-permute-start | bytes 6193160 | tf_op jit(solution)/shard_map/ppermute | solution.py:16
  360.9 35.2 %copy-start.8 = (f32[6,224,128]{2,1,0:T(8,128)S(1)}, f32[6,224,128]{2,1,0:T(8,128)}, u32[]{:S(2)}) copy-start(f32[6,224,128]{2,1,0:T(8,128)} %get-tuple-element.388) | copy-start | bytes 2064388
  360.9 26.0 %collective-permute-start.5 = (bf16[2,2,6,56,768]{4,3,2,1,0:T(8,128)(2,1)S(1)}, bf16[2,2,6,56,768]{4,3,2,1,0:T(8,128)(2,1)S(1)}, u32[]{:S(2)}, u32[]{:S(2)}) collective-permute-start(bf16[2,2,6,56,768]{4,3,2,1,0:T(8,128)(2,1)S(1)} %get-tuple-element.502), channel_id=1, source_target_pairs={{0,8},{8,16},{16,24},{1,9},{9,17},{17,25},{2,10},{10,18},{18,26},{... | collective-permute-start | bytes 6193160 | tf_op jit(solution)/shard_map/ppermute | solution.py:16
  389.5 10.2 %copy-start.5 = (bf16[6,6,56,768]{3,2,1,0:T(8,128)(2,1)S(1)}, bf16[6,6,56,768]{3,2,1,0:T(8,128)(2,1)}, u32[]{:S(2)}) copy-start(bf16[6,6,56,768]{3,2,1,0:T(8,128)(2,1)} %get-tuple-element.503) | copy-start | bytes 9289732
  389.5 11.4 %copy-start.9 = (bf16[6,224,128]{2,1,0:T(8,128)(2,1)S(1)}, bf16[6,224,128]{2,1,0:T(8,128)(2,1)}, u32[]{:S(2)}) copy-start(bf16[6,224,128]{2,1,0:T(8,128)(2,1)} %get-tuple-element.389) | copy-start | bytes 1032196
  390.7 19.8 %collective-permute-start.6 = (bf16[2,2,2,56,768]{4,3,2,1,0:T(8,128)(2,1)}, bf16[2,2,2,56,768]{4,3,2,1,0:T(8,128)(2,1)}, u32[]{:S(2)}, u32[]{:S(2)}) collective-permute-start(bf16[2,2,2,56,768]{4,3,2,1,0:T(8,128)(2,1)} %get-tuple-element.506), channel_id=1, source_target_pairs={{1,0},{2,1},{3,2},{4,3},{5,4},{6,5},{7,6},{9,8},{10,9},{11,10},{12... | collective-permute-start | bytes 2064392 | tf_op jit(solution)/shard_map/ppermute | solution.py:16
  392.7 17.8 %collective-permute-start.7 = (bf16[2,2,2,56,768]{4,3,2,1,0:T(8,128)(2,1)}, bf16[2,2,2,56,768]{4,3,2,1,0:T(8,128)(2,1)}, u32[]{:S(2)}, u32[]{:S(2)}) collective-permute-start(bf16[2,2,2,56,768]{4,3,2,1,0:T(8,128)(2,1)} %get-tuple-element.507), channel_id=1, source_target_pairs={{0,1},{1,2},{2,3},{3,4},{4,5},{5,6},{6,7},{8,9},{9,10},{10,11},{11... | collective-permute-start | bytes 2064392 | tf_op jit(solution)/shard_map/ppermute | solution.py:16
  399.7 13.7 %copy-start.1 = (s32[4,8,9]{2,1,0:T(8,128)S(1)}, s32[4,8,9]{2,1,0:T(8,128)}, u32[]{:S(2)}) copy-start(s32[4,8,9]{2,1,0:T(8,128)} %param.68) | copy-start | bytes 3460
where the time goes:
time: 420 us; the launch traced here: 413 us
  local copies, waits for them, and re-layouts  142 us (34%)
  waiting for transfers between devices  109 us (26%)
  other arithmetic  73.4 us (17%)
  matrix products  61 us (15%)
  starting transfers between devices  23.3 us (6%)
  loops' own time  4.26 us (1%)
    ppermute x2, waiting for transfers between devices, padded(): lax.ppermute(tail, axis, [(i, (i + 1) % count) for i in range(ends)])  80 us
    scatter-add x18, local copies, waits for them, and re-layouts, shards(): value_padded = value_padded.at[first_t:first_t + tile_side, first_h:first...  60 us
    transpose x3, local copies, waits for them, and re-layouts, heads_to_rows(): return stacked.transpose(1, 0, 2).reshape(stacked.shape[1], -1)  24.7 us
    ppermute x4, waiting for transfers between devices, from_behind(): return lax.ppermute(x, axis, pairs)  22.4 us
    add x18, other arithmetic, shards(): value_padded = value_padded.at[first_t:first_t + tile_side, first_h:first...  21.3 us
    scatter-add x9, other arithmetic, shards(): value_padded = value_padded.at[first_t:first_t + tile_side, first_h:first...  16.4 us
    another operation x2, local copies, waits for them, and re-layouts, shards(): partials = jnp.stack([key_part.reshape(window_shape), value_part])  15.4 us
    dot_general x6, matrix products, forward_head(): lax.dot_general(dscores, query_head, CONTRACT_FIRST, preferred_element_ty...  14.1 us
  transfers between devices with their start and end apart: 8, of which 6 were waited for; matrix products, arithmetic and copies ran while one was open for 5% of the time, Pallas kernels for 0%

commit v1 on v0

v1 whole, which is shorter than its diff:
```python
import functools

import jax
import jax.numpy as jnp
from jax import lax
from jax.experimental import pallas as pl
from jax.experimental.pallas import tpu as pltpu
from jax.sharding import PartitionSpec as P

HEAD_DIM = 128
GROUPS = 2
LOG2E = 1.4426950408889634
ROW_DELTA = 8
STAT_ROWS = 16


CONTRACT_LAST = (((1,), (1,)), ((), ()))


def flip_pairs(count):
    return [(i, i ^ 1) for i in range(count)]


def other_pairs(count):
    pairs = []
    for i in range(count):
        to = i + 1 if i % 2 else i - 1
        pairs.append((i, to if 0 <= to < count else i))
    return pairs


def relay_pairs(count):
    pairs = []
    for i in range(count):
        to = i - 2 if i % 2 else i + 2
        if 0 <= to < count:
            pairs.append((i, to))
    return pairs


def ta_halo(x):
    count = lax.axis_size("ta")
    return lax.ppermute(x, "ta", other_pairs(count)), lax.ppermute(x, "ta", flip_pairs(count))


def window_of(x):
    count = lax.axis_size("ha")
    near = lax.ppermute(x, "ha", flip_pairs(count))
    own_b, own_a = ta_halo(x)
    far = lax.ppermute(near, "ha", relay_pairs(count))
    near_b, near_a = ta_halo(near)
    far_b, far_a = ta_halo(far)
    return [x, near, far, own_a, near_a, far_a, own_b, near_b, far_b]


def stats_window(x):
    count = lax.axis_size("ha")
    near = lax.ppermute(x, "ha", flip_pairs(count))
    far = lax.ppermute(x, "ha", other_pairs(count))
    column = jnp.stack([x, near, far])
    column_b, column_a = ta_halo(column)
    return [column, column_a, column_b]


def offsets(index):
    sign = 1 - 2 * lax.rem(index, 2)
    return (0, sign, -sign)


def inside(index, count):
    return (index >= 0) & (index < count)


def halo_slab(tiles, even_t, even_h, in_t, in_h, width):
    def cell(tile, frame, row):
        start = (2 * frame + row) * width
        return tiles[tile][start : start + width]

    def side_h(slot_t, frame, R):
        if R in (1, 2):
            return cell(3 * slot_t, frame, R - 1)
        row = 1 if R == 0 else 0
        near, far = cell(3 * slot_t + 1, frame, row), cell(3 * slot_t + 2, frame, row)
        picked = jnp.where(even_h, far, near) if R == 0 else jnp.where(even_h, near, far)
        return jnp.where(in_h[0 if R == 0 else 1], picked, 0.0)

    slab = []
    for F in range(4):
        line = []
        for R in range(4):
            if F in (1, 2):
                line.append(side_h(0, F - 1, R))
                continue
            frame = 1 if F == 0 else 0
            first, second = side_h(1, frame, R), side_h(2, frame, R)
            picked = jnp.where(even_t, second, first) if F == 0 else jnp.where(even_t, first, second)
            line.append(jnp.where(in_t[0 if F == 0 else 1], picked, 0.0))
        slab.append(line)
    return slab


def depthwise(slab, weight, flipped, width):
    column = lax.broadcasted_iota(jnp.int32, (width, HEAD_DIM), 0)
    rows = []
    for f in range(2):
        for r in range(2):
            parts = []
            for dw in range(3):
                total = None
                for dt in range(3):
                    for dh in range(3):
                        tap = 9 * dt + 3 * dh + dw
                        tap = 26 - tap if flipped else tap
                        term = weight[tap : tap + 1] * slab[f + dt][r + dh]
                        total = term if total is None else total + term
                parts.append(total)
            before = jnp.where(column == 0, 0.0, pltpu.roll(parts[0], 1, 0))
            after = jnp.where(column == width - 1, 0.0, pltpu.roll(parts[2], width - 1, 0))
            rows.append(parts[1] + before + after)
    return jnp.concatenate(rows, axis=0)


def place(count_t, count_h):
    index_t, index_h = lax.axis_index("ta"), lax.axis_index("ha")
    even_t, even_h = lax.rem(index_t, 2) == 0, lax.rem(index_h, 2) == 0
    in_t = (index_t > 0, index_t < count_t - 1)
    in_h = (index_h > 0, index_h < count_h - 1)
    return index_t, index_h, even_t, even_h, in_t, in_h


def query_kernel(counts, width, n_prev, mask_ref, clip_ref, q_ref, grad_ref, weight_ref, *rest):
    kv = rest[:9]
    out_ref, dq_ref, stat_ref, score = rest[9 + n_prev :]
    count_t, count_h = counts
    index_t, index_h, even_t, even_h, in_t, in_h = place(count_t, count_h)
    queries = q_ref.shape[0]
    head = pl.program_id(0)
    scale = HEAD_DIM**-0.5
    lane = lax.broadcasted_iota(jnp.int32, (1, queries), 1)
    frame = lane // (2 * width)
    column = lax.rem(lane, width)

    q = q_ref[...]
    grad = grad_ref[...]
    top = None
    for slot in range(9):
        a, b = offsets(index_t)[slot // 3], offsets(index_h)[slot % 3]
        t, h = index_t + a, index_h + b
        kept = (mask_ref[index_t, index_h, 3 * (a + 1) + (b + 1)] == 1) & inside(t, count_t) & inside(h, count_h)
        safe = jnp.clip(t, 0, count_t - 1)
        lens = [jnp.where(kept, clip_ref[2 * safe + f], 0) for f in range(2)]
        bias = jnp.where(column < jnp.where(frame == 0, lens[0], lens[1]), 0.0, -jnp.inf)
        s = lax.dot_general(q, kv[slot][0], CONTRACT_LAST, preferred_element_type=jnp.float32)
        s = s * (scale * LOG2E) + bias
        score[slot] = s
        top = s if top is None else jnp.maximum(top, s)
    row_max = jnp.max(top, axis=1, keepdims=True)
    total, acc = None, None
    for slot in range(9):
        e = jnp.exp2(score[slot] - row_max)
        score[slot] = e
        part = jnp.dot(e.astype(jnp.bfloat16), kv[slot][1], preferred_element_type=jnp.float32)
        total = e if total is None else total + e
        acc = part if acc is None else acc + part
    row_total = jnp.sum(total, axis=1, keepdims=True)
    inverse = 1.0 / row_total
    attention = acc * inverse
    delta = jnp.sum(grad.astype(jnp.float32) * attention, axis=1, keepdims=True)
    dq = None
    for slot in range(9):
        dp = lax.dot_general(grad, kv[slot][1], CONTRACT_LAST, preferred_element_type=jnp.float32)
        ds = (score[slot] * (dp - delta)).astype(jnp.bfloat16)
        part = jnp.dot(ds, kv[slot][0], preferred_element_type=jnp.float32)
        dq = part if dq is None else dq + part
    dq_ref[...] = (dq * (inverse * scale)).astype(jnp.bfloat16)

    log_total = row_max + jnp.log2(row_total)
    half = lax.broadcasted_iota(jnp.int32, (queries, HEAD_DIM), 1) < HEAD_DIM // 2
    both = jnp.where(half, log_total, delta)
    pad = -queries % HEAD_DIM
    both = jnp.concatenate([both, jnp.zeros((pad, HEAD_DIM), jnp.float32)], axis=0)
    turned = both.T
    stat_ref[pl.ds(head, 1), :] = turned[0:1, :queries]
    stat_ref[pl.ds(head + ROW_DELTA, 1), :] = turned[HEAD_DIM // 2 : HEAD_DIM // 2 + 1, :queries]

    tiles = [kv[slot][1].astype(jnp.float32) for slot in range(9)]
    slab = halo_slab(tiles, even_t, even_h, in_t, in_h, width)
    conv = depthwise(slab, weight_ref[...].astype(jnp.float32), False, width)
    out_ref[...] = (attention + conv).astype(jnp.bfloat16)


def key_kernel(counts, width, n_prev, mask_ref, clip_ref, kv_ref, weight_ref, *rest):
    qg = rest[:9]
    stats = rest[9:12]
    dk_ref, dv_ref = rest[12 + n_prev :]
    count_t, count_h = counts
    index_t, index_h, even_t, even_h, in_t, in_h = place(count_t, count_h)
    keys = kv_ref.shape[1]
    head = pl.program_id(0)
    scale = HEAD_DIM**-0.5
    k, v = kv_ref[0], kv_ref[1]
    dk, dv = None, None
    for slot in range(9):
        a, b = offsets(index_t)[slot // 3], offsets(index_h)[slot % 3]
        t, h = index_t + a, index_h + b
        safe_t, safe_h = jnp.clip(t, 0, count_t - 1), jnp.clip(h, 0, count_h - 1)
        kept = (mask_ref[safe_t, safe_h, 3 * (1 - a) + (1 - b)] == 1) & inside(t, count_t) & inside(h, count_h)
        log_total = stats[slot // 3][slot % 3, pl.ds(head, 1), :]
        log_total = jnp.where(kept, log_total, jnp.inf)
        delta = stats[slot // 3][slot % 3, pl.ds(head + ROW_DELTA, 1), :]
        q, grad = qg[slot][0], qg[slot][1]
        s = lax.dot_general(k, q, CONTRACT_LAST, preferred_element_type=jnp.float32)
        p = jnp.exp2(s * (scale * LOG2E) - log_total)
        dp = lax.dot_general(v, grad, CONTRACT_LAST, preferred_element_type=jnp.float32)
        ds = (p * (dp - delta)).astype(jnp.bfloat16)
        part_v = jnp.dot(p.astype(jnp.bfloat16), grad, preferred_element_type=jnp.float32)
        part_k = jnp.dot(ds, q, preferred_element_type=jnp.float32)
        dk = part_k if dk is None else dk + part_k
        dv = part_v if dv is None else dv + part_v
    row = lax.broadcasted_iota(jnp.int32, (keys, HEAD_DIM), 0)
    lens = [clip_ref[2 * index_t + f] for f in range(2)]
    live = lax.rem(row, width) < jnp.where(row < 2 * width, lens[0], lens[1])
    dk_ref[...] = jnp.where(live, dk * scale, 0.0).astype(jnp.bfloat16)

    tiles = [qg[slot][1].astype(jnp.float32) for slot in range(9)]
    slab = halo_slab(tiles, even_t, even_h, in_t, in_h, width)
    conv = depthwise(slab, weight_ref[...].astype(jnp.float32), True, width)
    dv_ref[...] = (jnp.where(live, dv, 0.0) + conv).astype(jnp.bfloat16)


def cost(heads, rows, matmuls):
    work = heads * rows * 9 * rows * HEAD_DIM * 2 * matmuls
    return pl.CostEstimate(flops=work, bytes_accessed=heads * rows * HEAD_DIM * 2 * 24, transcendentals=heads * rows * rows * 9)


def shards(query_states, key_states, value_states, conv_weight, out_grad, tile_mask, clip_lengths):
    width, channels = query_states.shape[2:]
    rows = query_states.shape[0] * query_states.shape[1] * width
    counts = (lax.axis_size("ta"), lax.axis_size("ha"))
    heads = channels // HEAD_DIM
    group_heads = heads // GROUPS
    group_width = group_heads * HEAD_DIM
    flat = [x.reshape(rows, channels) for x in (query_states, key_states, value_states, out_grad)]
    query, key, value, grad = flat
    smem = pl.BlockSpec(memory_space=pltpu.SMEM)
    anywhere = pl.BlockSpec(memory_space=pl.ANY)
    pair_spec = pl.BlockSpec((2, rows, HEAD_DIM), lambda h: (0, 0, h))
    params = pltpu.CompilerParams(vmem_limit_bytes=40 * 1024 * 1024)
    full = jax.ShapeDtypeStruct((rows, channels), jnp.bfloat16)

    def part(x, g):
        return x[:, g * group_width : (g + 1) * group_width]

    kvs = [jnp.stack([part(key, g), part(value, g)]) for g in range(GROUPS)]
    qgs = [jnp.stack([part(query, g), part(grad, g)]) for g in range(GROUPS)]
    kv_windows = [window_of(x) for x in kvs]
    qg_windows = [window_of(x) for x in qgs]

    layer_out = query_grad = None
    stats = []
    for g in range(GROUPS):
        first = g * group_heads
        col_spec = pl.BlockSpec((rows, HEAD_DIM), lambda h, first=first: (0, h + first))
        weight_spec = pl.BlockSpec((27, HEAD_DIM), lambda h, first=first: (0, h + first))
        previous = [] if g == 0 else [layer_out, query_grad]
        layer_out, query_grad, stat = pl.pallas_call(
            functools.partial(query_kernel, counts, width, len(previous)),
            grid=(group_heads,),
            in_specs=[smem, smem, col_spec, col_spec, weight_spec] + [pair_spec] * 9 + [anywhere] * len(previous),
            out_specs=[col_spec, col_spec, pl.BlockSpec((STAT_ROWS, rows), lambda h: (0, 0))],
            out_shape=[full, full, jax.ShapeDtypeStruct((STAT_ROWS, rows), jnp.float32)],
            scratch_shapes=[pltpu.VMEM((9, rows, rows), jnp.float32)],
            input_output_aliases={14 + i: i for i in range(len(previous))},
            compiler_params=params,
            cost_estimate=cost(group_heads, rows, 4),
            name="query_side",
        )(tile_mask, clip_lengths, query, grad, conv_weight, *kv_windows[g], *previous)
        stats.append(stats_window(stat))

    key_grad = value_grad = None
    stat_spec = pl.BlockSpec((3, STAT_ROWS, rows), lambda h: (0, 0, 0))
    for g in range(GROUPS):
        first = g * group_heads
        col_spec = pl.BlockSpec((rows, HEAD_DIM), lambda h, first=first: (0, h + first))
        weight_spec = pl.BlockSpec((27, HEAD_DIM), lambda h, first=first: (0, h + first))
        previous = [] if g == 0 else [key_grad, value_grad]
        key_grad, value_grad = pl.pallas_call(
            functools.partial(key_kernel, counts, width, len(previous)),
            grid=(group_heads,),
            in_specs=[smem, smem, pair_spec, weight_spec]
            + [pair_spec] * 9
            + [stat_spec] * 3
            + [anywhere] * len(previous),
            out_specs=[col_spec, col_spec],
            out_shape=[full, full],
            input_output_aliases={16 + i: i for i in range(len(previous))},
            compiler_params=params,
            cost_estimate=cost(group_heads, rows, 4),
            name="key_side",
        )(tile_mask, clip_lengths, kvs[g], conv_weight, *qg_windows[g], *stats[g], *previous)

    return tuple(x.reshape(query_states.shape) for x in (layer_out, query_grad, key_grad, value_grad))


def solution(mesh):
    placed = P("ta", "ha", None, None)
    return jax.shard_map(
        shards,
        mesh=mesh,
        in_specs=(placed, placed, placed, P(), placed, P(), P()),
        out_specs=(placed,) * 4,
        check_vma=False,
    )
```

time: 420 us -> 133 us (0.32); the launches traced: 413 us -> 133 us
  local copies, waits for them, and re-layouts: 142 us -> 1.34 us
  waiting for transfers between devices: 109 us -> 17.6 us
  other arithmetic: 73.4 us -> 0.19 us
  matrix products: 61 us -> 0 us
  starting transfers between devices: 23.3 us -> 74.7 us
  Pallas kernels: 0 us -> 37.6 us
  loops' own time: 4.26 us -> 0 us
    ppermute x8 -> x40, waiting for transfers between devices: 109 us -> 17.6 us  [the longest x4 5.21 us: window_of(): far = lax.ppermute(near, 'ha', relay_pairs(count))]
    dot_general x36 -> x0, matrix products: 61 us -> none  [the longest x6 14.1 us: forward_head(): lax.dot_general(dscores, query_head, CONTRACT_FIRST, preferred_element_ty...]
    scatter-add x18 -> x0, local copies, waits for them, and re-layouts: 60 us -> none  [shards(): value_padded = value_padded.at[first_t:first_t + tile_side, first_h:first...]
    ppermute x8 -> x40, starting transfers between devices: 23.3 us -> 74.7 us  [the longest x14 48.4 us: ta_halo(): lax.ppermute(x, 'ta', other_pairs(count))]
    pallas_call x0 -> x4, Pallas kernels: none -> 37.6 us  [the longest x2 19.9 us: shards(): pl.pallas_call(functools.partial(query_kernel, counts, width, len(previou...]
    another operation x5 -> x2, local copies, waits for them, and re-layouts: 26.6 us -> 1.31 us  [the longest x1 1.24 us: shards(): kvs = [jnp.stack([part(key, g), part(value, g)]) for g in range(GROUPS)]]
    transpose x3 -> x0, local copies, waits for them, and re-layouts: 24.7 us -> none  [heads_to_rows(): return stacked.transpose(1, 0, 2).reshape(stacked.shape[1], -1)]
    add x18 -> x0, other arithmetic: 21.3 us -> none  [shards(): value_padded = value_padded.at[first_t:first_t + tile_side, first_h:first...]
  transfers between devices with their start and end apart: 8 -> 40, of which waited for: 6 -> 9; matrix products, arithmetic and copies ran while one was open for 5% -> 0% of each run, Pallas kernels for 0% -> 22%
where the time goes in v1:
time: 133 us
  starting transfers between devices  74.7 us (56%)
  Pallas kernels  37.6 us (28%)
  waiting for transfers between devices  17.6 us (13%)
  local copies, waits for them, and re-layouts  1.34 us (1%)
    ppermute x14, starting transfers between devices, ta_halo(): lax.ppermute(x, 'ta', other_pairs(count))  48.4 us
    pallas_call x2, Pallas kernels, shards(): pl.pallas_call(functools.partial(query_kernel, counts, width, len(previou...  19.9 us
    pallas_call x2, Pallas kernels, shards(): pl.pallas_call(functools.partial(key_kernel, counts, width, len(previous)...  17.6 us
    ppermute x4, starting transfers between devices, window_of(): far = lax.ppermute(near, 'ha', relay_pairs(count))  12.3 us
    ppermute x4, waiting for transfers between devices, window_of(): far = lax.ppermute(near, 'ha', relay_pairs(count))  5.21 us
    ppermute x4, waiting for transfers between devices, window_of(): near = lax.ppermute(x, 'ha', flip_pairs(count))  5.08 us
    ppermute x4, starting transfers between devices, window_of(): near = lax.ppermute(x, 'ha', flip_pairs(count))  4.15 us
    ppermute x2, starting transfers between devices, stats_window(): near = lax.ppermute(x, 'ha', flip_pairs(count))  3.98 us
  transfers between devices with their start and end apart: 40, of which 9 were waited for; matrix products, arithmetic and copies ran while one was open for 0% of the time, Pallas kernels for 22%

profile of v1, /device:TPU:9, one launch (start us, length us, event | category | flops | bytes accessed | tf_op | source)
XLA Modules:
  0.0 132.5 jit_solution(15726629913905649978)
XLA Ops:
  0.6 1.2 slice_bitcast_fusion.4
  1.9 0.0 copy-start
  1.9 0.0 copy-start.1
  1.9 1.3 collective-permute-start.8
  3.2 1.0 collective-permute-start.10
  4.2 3.0 %collective-permute-start.13 = (bf16[2,224,384]{2,1,0:T(8,128)(2,1)S(1)}, bf16[2,224,384]{2,1,0:T(8,128)(2,1)S(1)}, u32[]{:S(2)}, u32[]{:S(2)}) collective-permute-start(bf16[2,224,384]{2,1,0:T(8,128)(2,1)S(1)} %pad_maximum_fusion.1.rest_0_.kv_ref), channel_id=1, source_target_pairs={{0,0},{8,16},{16,8},{24,24},{1,1},{9,17},{17,9},{25,25},{2,2},{10,... | collective-permute-start | bytes 1032200 | tf_op jit(solution)/shard_map/ppermute | solution.py:43
  7.2 0.1 slice_bitcast_fusion
  7.4 0.3 collective-permute-start.28
  7.7 3.3 %collective-permute-done.8.rest_1_ = bf16[2,224,384]{2,1,0:T(8,128)(2,1)S(1)} collective-permute-done((bf16[2,224,384]{2,1,0:T(8,128)(2,1)S(1)}, bf16[2,224,384]{2,1,0:T(8,128)(2,1)S(1)}, u32[]{:S(2)}, u32[]{:S(2)}) %collective-permute-start.8) | collective-permute-done | bytes 344096 | tf_op jit(solution)/shard_map/ppermute | solution.py:48
  10.9 5.7 %collective-permute-start.33 = (bf16[2,224,384]{2,1,0:T(8,128)(2,1)S(1)}, bf16[2,224,384]{2,1,0:T(8,128)(2,1)S(1)}, u32[]{:S(2)}, u32[]{:S(2)}) collective-permute-start(bf16[2,224,384]{2,1,0:T(8,128)(2,1)S(1)} %pad_maximum_fusion.3.rest_0_), channel_id=1, source_target_pairs={{0,0},{8,16},{16,8},{24,24},{1,1},{9,17},{17,9},{25,25},{2,2},{10,... | collective-permute-start | bytes 1032200 | tf_op jit(solution)/shard_map/ppermute | solution.py:43
  16.7 0.0 collective-permute-done.10.rest_3_
  16.7 1.3 collective-permute-start
  18.0 0.0 collective-permute-done.13.rest_6_
  18.0 0.0 collective-permute-start.2
  18.0 0.3 collective-permute-done.28.rest_1_
  18.3 5.7 %collective-permute-start.5 = (bf16[2,224,384]{2,1,0:T(8,128)(2,1)S(1)}, bf16[2,224,384]{2,1,0:T(8,128)(2,1)S(1)}, u32[]{:S(2)}, u32[]{:S(2)}) collective-permute-start(bf16[2,224,384]{2,1,0:T(8,128)(2,1)S(1)} %pad_maximum_fusion.rest_0_.kv_ref), channel_id=1, source_target_pairs={{0,0},{8,16},{16,8},{24,24},{1,1},{9,17},{17,9},{25,25},{2,2},{10,... | collective-permute-start | bytes 1032200 | tf_op jit(solution)/shard_map/ppermute | solution.py:43
  24.0 0.0 copy-start.2
  24.1 0.0 copy-start.3
  24.1 0.0 copy-start.4
  24.1 1.3 collective-permute-start.16
  25.4 0.0 collective-permute-done.33.rest_6_
  25.4 0.0 collective-permute-start.18
  25.4 1.5 %collective-permute-done.rest_1_ = bf16[2,224,384]{2,1,0:T(8,128)(2,1)S(1)} collective-permute-done((bf16[2,224,384]{2,1,0:T(8,128)(2,1)S(1)}, bf16[2,224,384]{2,1,0:T(8,128)(2,1)S(1)}, u32[]{:S(2)}, u32[]{:S(2)}) %collective-permute-start) | collective-permute-done | bytes 344096 | tf_op jit(solution)/shard_map/ppermute | solution.py:48
  26.9 4.5 %collective-permute-start.21 = (bf16[2,224,384]{2,1,0:T(8,128)(2,1)S(1)}, bf16[2,224,384]{2,1,0:T(8,128)(2,1)S(1)}, u32[]{:S(2)}, u32[]{:S(2)}) collective-permute-start(bf16[2,224,384]{2,1,0:T(8,128)(2,1)S(1)} %pad_maximum_fusion.2.rest_0_), channel_id=1, source_target_pairs={{0,0},{8,16},{16,8},{24,24},{1,1},{9,17},{17,9},{25,25},{2,2},{10,... | collective-permute-start | bytes 1032200 | tf_op jit(solution)/shard_map/ppermute | solution.py:43
  31.4 0.0 collective-permute-done.2.rest_3_
  31.4 3.2 %collective-permute-start.9 = (bf16[2,224,384]{2,1,0:T(8,128)(2,1)S(1)}, bf16[2,224,384]{2,1,0:T(8,128)(2,1)S(1)}, u32[]{:S(2)}, u32[]{:S(2)}) collective-permute-start(bf16[2,224,384]{2,1,0:T(8,128)(2,1)S(1)} %collective-permute-done.8.rest_1_), channel_id=1, source_target_pairs={{0,2},{2,4},{3,1},{4,6},{5,3},{7,5},{8,10},{10,12},{11,9},{12,14},... | collective-permute-start | bytes 1032200 | tf_op jit(solution)/shard_map/ppermute | solution.py:50
  34.6 0.0 collective-permute-done.5.rest_6_
  34.6 0.1 collective-permute-start.11
  34.7 2.9 %collective-permute-start.14 = (bf16[2,224,384]{2,1,0:T(8,128)(2,1)S(1)}, bf16[2,224,384]{2,1,0:T(8,128)(2,1)S(1)}, u32[]{:S(2)}, u32[]{:S(2)}) collective-permute-start(bf16[2,224,384]{2,1,0:T(8,128)(2,1)S(1)} %collective-permute-done.8.rest_1_), channel_id=1, source_target_pairs={{0,0},{8,16},{16,8},{24,24},{1,1},{9,17},{17,9},{25,25},{2,2},{10,... | collective-permute-start | bytes 1032200 | tf_op jit(solution)/shard_map/ppermute | solution.py:43
  37.6 0.0 collective-permute-done.18.rest_3_
  37.6 3.2 %collective-permute-start.29 = (bf16[2,224,384]{2,1,0:T(8,128)(2,1)S(1)}, bf16[2,224,384]{2,1,0:T(8,128)(2,1)S(1)}, u32[]{:S(2)}, u32[]{:S(2)}) collective-permute-start(bf16[2,224,384]{2,1,0:T(8,128)(2,1)S(1)} %collective-permute-done.28.rest_1_), channel_id=1, source_target_pairs={{0,2},{2,4},{3,1},{4,6},{5,3},{7,5},{8,10},{10,12},{11,9},{12,14},... | collective-permute-start | bytes 1032200 | tf_op jit(solution)/shard_map/ppermute | solution.py:50
  40.9 0.1 collective-permute-start.31
  41.0 2.9 %collective-permute-start.34 = (bf16[2,224,384]{2,1,0:T(8,128)(2,1)S(1)}, bf16[2,224,384]{2,1,0:T(8,128)(2,1)S(1)}, u32[]{:S(2)}, u32[]{:S(2)}) collective-permute-start(bf16[2,224,384]{2,1,0:T(8,128)(2,1)S(1)} %collective-permute-done.28.rest_1_), channel_id=1, source_target_pairs={{0,0},{8,16},{16,8},{24,24},{1,1},{9,17},{17,9},{25,25},{2,2},{10,... | collective-permute-start | bytes 1032200 | tf_op jit(solution)/shard_map/ppermute | solution.py:43
  43.9 2.7 %collective-permute-start.1 = (bf16[2,224,384]{2,1,0:T(8,128)(2,1)S(1)}, bf16[2,224,384]{2,1,0:T(8,128)(2,1)S(1)}, u32[]{:S(2)}, u32[]{:S(2)}) collective-permute-start(bf16[2,224,384]{2,1,0:T(8,128)(2,1)S(1)} %collective-permute-done.rest_1_), channel_id=1, source_target_pairs={{0,2},{2,4},{3,1},{4,6},{5,3},{7,5},{8,10},{10,12},{11,9},{12,14},... | collective-permute-start | bytes 1032200 | tf_op jit(solution)/shard_map/ppermute | solution.py:50
  46.6 0.1 collective-permute-start.3
  46.7 2.7 %collective-permute-done.29.rest_2_ = bf16[2,224,384]{2,1,0:T(8,128)(2,1)S(1)} collective-permute-done((bf16[2,224,384]{2,1,0:T(8,128)(2,1)S(1)}, bf16[2,224,384]{2,1,0:T(8,128)(2,1)S(1)}, u32[]{:S(2)}, u32[]{:S(2)}) %collective-permute-start.29) | collective-permute-done | bytes 344096 | tf_op jit(solution)/shard_map/ppermute | solution.py:50
  49.4 1.9 %collective-permute-start.6 = (bf16[2,224,384]{2,1,0:T(8,128)(2,1)S(1)}, bf16[2,224,384]{2,1,0:T(8,128)(2,1)S(1)}, u32[]{:S(2)}, u32[]{:S(2)}) collective-permute-start(bf16[2,224,384]{2,1,0:T(8,128)(2,1)S(1)} %collective-permute-done.rest_1_), channel_id=1, source_target_pairs={{0,0},{8,16},{16,8},{24,24},{1,1},{9,17},{17,9},{25,25},{2,2},{10,... | collective-permute-start | bytes 1032200 | tf_op jit(solution)/shard_map/ppermute | solution.py:43
  51.4 3.2 %collective-permute-start.17 = (bf16[2,224,384]{2,1,0:T(8,128)(2,1)S(1)}, bf16[2,224,384]{2,1,0:T(8,128)(2,1)S(1)}, u32[]{:S(2)}, u32[]{:S(2)}) collective-permute-start(bf16[2,224,384]{2,1,0:T(8,128)(2,1)S(1)} %collective-permute-done.16.rest_1_), channel_id=1, source_target_pairs={{0,2},{2,4},{3,1},{4,6},{5,3},{7,5},{8,10},{10,12},{11,9},{12,14},... | collective-permute-start | bytes 1032200 | tf_op jit(solution)/shard_map/ppermute | solution.py:50
  54.6 0.1 collective-permute-start.12
  54.7 2.1 %collective-permute-done.1.rest_2_ = bf16[2,224,384]{2,1,0:T(8,128)(2,1)S(1)} collective-permute-done((bf16[2,224,384]{2,1,0:T(8,128)(2,1)S(1)}, bf16[2,224,384]{2,1,0:T(8,128)(2,1)S(1)}, u32[]{:S(2)}, u32[]{:S(2)}) %collective-permute-start.1) | collective-permute-done | bytes 344096 | tf_op jit(solution)/shard_map/ppermute | solution.py:50
  56.8 2.0 %collective-permute-start.15 = (bf16[2,224,384]{2,1,0:T(8,128)(2,1)S(1)}, bf16[2,224,384]{2,1,0:T(8,128)(2,1)S(1)}, u32[]{:S(2)}, u32[]{:S(2)}) collective-permute-start(bf16[2,224,384]{2,1,0:T(8,128)(2,1)S(1)} %collective-permute-done.9.rest_2_), channel_id=1, source_target_pairs={{0,0},{8,16},{16,8},{24,24},{1,1},{9,17},{17,9},{25,25},{2,2},{10,... | collective-permute-start | bytes 1032200 | tf_op jit(solution)/shard_map/ppermute | solution.py:43
  58.8 0.1 collective-permute-start.4
  58.9 3.5 %collective-permute-start.7 = (bf16[2,224,384]{2,1,0:T(8,128)(2,1)S(1)}, bf16[2,224,384]{2,1,0:T(8,128)(2,1)S(1)}, u32[]{:S(2)}, u32[]{:S(2)}) collective-permute-start(bf16[2,224,384]{2,1,0:T(8,128)(2,1)S(1)} %collective-permute-done.1.rest_2_), channel_id=1, source_target_pairs={{0,0},{8,16},{16,8},{24,24},{1,1},{9,17},{17,9},{25,25},{2,2},{10,... | collective-permute-start | bytes 1032200 | tf_op jit(solution)/shard_map/ppermute | solution.py:43
  62.5 0.3 collective-permute-done.17.rest_2_
  62.8 0.5 collective-permute-start.32
  63.3 2.0 %collective-permute-done.15.rest_8_ = bf16[2,224,384]{2,1,0:T(8,128)(2,1)S(1)} collective-permute-done((bf16[2,224,384]{2,1,0:T(8,128)(2,1)S(1)}, bf16[2,224,384]{2,1,0:T(8,128)(2,1)S(1)}, u32[]{:S(2)}, u32[]{:S(2)}) %collective-permute-start.15) | collective-permute-done | bytes 344096 | tf_op jit(solution)/shard_map/ppermute | solution.py:43
  65.4 2.0 %collective-permute-start.35 = (bf16[2,224,384]{2,1,0:T(8,128)(2,1)S(1)}, bf16[2,224,384]{2,1,0:T(8,128)(2,1)S(1)}, u32[]{:S(2)}, u32[]{:S(2)}) collective-permute-start(bf16[2,224,384]{2,1,0:T(8,128)(2,1)S(1)} %collective-permute-done.29.rest_2_), channel_id=1, source_target_pairs={{0,0},{8,16},{16,8},{24,24},{1,1},{9,17},{17,9},{25,25},{2,2},{10,... | collective-permute-start | bytes 1032200 | tf_op jit(solution)/shard_map/ppermute | solution.py:43
  67.4 9.9 %query_side.2 = (bf16[224,768]{1,0:T(8,128)(2,1)}, bf16[224,768]{1,0:T(8,128)(2,1)}, f32[16,224]{1,0:T(8,128)S(1)}) custom-call(s32[4,8,9]{2,1,0:T(8,128)S(1)} %copy-done.3, s32[8]{0:T(128)S(1)} %copy-done.4, bf16[224,768]{1,0:T(8,128)(2,1)S(1)} %bitcast.31, bf16[224,768]{1,0:T(8,128)(2,1)S(1)} %bitcast.34, bf16[27,768]{1,0:T(8,128)(2,1)S(1)} %copy-done.2, ...), custom_call_target="tpu_custom_call" | custom-call | flops 1387266048 | bytes 4128768 | tf_op jit(solution)/shard_map/query_side/pallas_call | solution.py:266
  77.4 1.5 %collective-permute-start.36 = (f32[16,224]{1,0:T(8,128)S(1)}, f32[16,224]{1,0:T(8,128)S(1)}, u32[]{:S(2)}, u32[]{:S(2)}) collective-permute-start(f32[16,224]{1,0:T(8,128)S(1)} %get-tuple-element.19), channel_id=1, source_target_pairs={{0,1},{1,0},{2,3},{3,2},{4,5},{5,4},{6,7},{7,6},{8,9},{9,8},{10,11... | collective-permute-start | bytes 43016 | tf_op jit(solution)/shard_map/ppermute | solution.py:58
  78.9 2.0 %collective-permute-start.37 = (f32[16,224]{1,0:T(8,128)S(1)}, f32[16,224]{1,0:T(8,128)S(1)}, u32[]{:S(2)}, u32[]{:S(2)}) collective-permute-start(f32[16,224]{1,0:T(8,128)S(1)} %get-tuple-element.19), channel_id=1, source_target_pairs={{0,0},{1,2},{2,1},{3,4},{4,3},{5,6},{6,5},{7,7},{8,8},{9,10},{10,9... | collective-permute-start | bytes 43016 | tf_op jit(solution)/shard_map/ppermute | solution.py:59
  80.8 10.0 %query_side.3 = (bf16[224,768]{1,0:T(8,128)(2,1)}, bf16[224,768]{1,0:T(8,128)(2,1)}, f32[16,224]{1,0:T(8,128)S(1)}) custom-call(s32[4,8,9]{2,1,0:T(8,128)S(1)} %copy-done.3, s32[8]{0:T(128)S(1)} %copy-done.4, bf16[224,768]{1,0:T(8,128)(2,1)S(1)} %bitcast.32, bf16[224,768]{1,0:T(8,128)(2,1)S(1)} %bitcast.35, ...), custom_call_target="tpu_custom_call", output_to_operand_aliasing={{0}: (14, {}), {1}: (15, {})} | custom-call | flops 1387266048 | bytes 4128768 | tf_op jit(solution)/shard_map/query_side/pallas_call | solution.py:266
  90.8 3.5 %collective-permute-start.22 = (bf16[2,224,384]{2,1,0:T(8,128)(2,1)S(1)}, bf16[2,224,384]{2,1,0:T(8,128)(2,1)S(1)}, u32[]{:S(2)}, u32[]{:S(2)}) collective-permute-start(bf16[2,224,384]{2,1,0:T(8,128)(2,1)S(1)} %collective-permute-done.16.rest_1_), channel_id=1, source_target_pairs={{0,0},{8,16},{16,8},{24,24},{1,1},{9,17},{17,9},{25,25},{2,2},{10,... | collective-permute-start | bytes 1032200 | tf_op jit(solution)/shard_map/ppermute | solution.py:43
  94.3 0.1 collective-permute-start.20
  94.4 2.0 %collective-permute-start.23 = (bf16[2,224,384]{2,1,0:T(8,128)(2,1)S(1)}, bf16[2,224,384]{2,1,0:T(8,128)(2,1)S(1)}, u32[]{:S(2)}, u32[]{:S(2)}) collective-permute-start(bf16[2,224,384]{2,1,0:T(8,128)(2,1)S(1)} %collective-permute-done.17.rest_2_), channel_id=1, source_target_pairs={{0,0},{8,16},{16,8},{24,24},{1,1},{9,17},{17,9},{25,25},{2,2},{10,... | collective-permute-start | bytes 1032200 | tf_op jit(solution)/shard_map/ppermute | solution.py:43
  96.5 2.5 %collective-permute-start.24 = (f32[16,224]{1,0:T(8,128)S(1)}, f32[16,224]{1,0:T(8,128)S(1)}, u32[]{:S(2)}, u32[]{:S(2)}) collective-permute-start(f32[16,224]{1,0:T(8,128)S(1)} %get-tuple-element.18), channel_id=1, source_target_pairs={{0,1},{1,0},{2,3},{3,2},{4,5},{5,4},{6,7},{7,6},{8,9},{9,8},{10,11... | collective-permute-start | bytes 43016 | tf_op jit(solution)/shard_map/ppermute | solution.py:58
  99.0 1.9 %collective-permute-start.25 = (f32[16,224]{1,0:T(8,128)S(1)}, f32[16,224]{1,0:T(8,128)S(1)}, u32[]{:S(2)}, u32[]{:S(2)}) collective-permute-start(f32[16,224]{1,0:T(8,128)S(1)} %get-tuple-element.18), channel_id=1, source_target_pairs={{0,0},{1,2},{2,1},{3,4},{4,3},{5,6},{6,5},{7,7},{8,8},{9,10},{10,9... | collective-permute-start | bytes 43016 | tf_op jit(solution)/shard_map/ppermute | solution.py:59
  100.9 0.1 collective-permute-start.38
  101.0 3.5 %collective-permute-done.25 = f32[16,224]{1,0:T(8,128)S(1)} collective-permute-done((f32[16,224]{1,0:T(8,128)S(1)}, f32[16,224]{1,0:T(8,128)S(1)}, u32[]{:S(2)}, u32[]{:S(2)}) %collective-permute-start.25) | collective-permute-done | bytes 14368 | tf_op jit(solution)/shard_map/ppermute | solution.py:59
  104.5 4.8 %collective-permute-start.39 = (f32[3,16,224]{2,1,0:T(8,128)S(1)}, f32[3,16,224]{2,1,0:T(8,128)S(1)}, u32[]{:S(2)}, u32[]{:S(2)}) collective-permute-start(f32[3,16,224]{2,1,0:T(8,128)S(1)} %pad_maximum_fusion.5.rest_9_), channel_id=1, source_target_pairs={{0,0},{8,16},{16,8},{24,24},{1,1},{9,17},{17,9},{25,25},{2,2},{10,... | collective-permute-start | bytes 129032 | tf_op jit(solution)/shard_map/ppermute | solution.py:43
  109.3 0.1 collective-permute-start.26
  109.4 1.7 %collective-permute-done.39.rest_11_ = f32[3,16,224]{2,1,0:T(8,128)S(1)} collective-permute-done((f32[3,16,224]{2,1,0:T(8,128)S(1)}, f32[3,16,224]{2,1,0:T(8,128)S(1)}, u32[]{:S(2)}, u32[]{:S(2)}) %collective-permute-start.39) | collective-permute-done | bytes 43040 | tf_op jit(solution)/shard_map/ppermute | solution.py:43
  111.0 3.8 %collective-permute-start.27 = (f32[3,16,224]{2,1,0:T(8,128)S(1)}, f32[3,16,224]{2,1,0:T(8,128)S(1)}, u32[]{:S(2)}, u32[]{:S(2)}) collective-permute-start(f32[3,16,224]{2,1,0:T(8,128)S(1)} %pad_maximum_fusion.4.rest_9_), channel_id=1, source_target_pairs={{0,0},{8,16},{16,8},{24,24},{1,1},{9,17},{17,9},{25,25},{2,2},{10,... | collective-permute-start | bytes 129032 | tf_op jit(solution)/shard_map/ppermute | solution.py:43
  114.9 8.8 %key_side.2 = (bf16[224,768]{1,0:T(8,128)(2,1)}, bf16[224,768]{1,0:T(8,128)(2,1)}) custom-call(s32[4,8,9]{2,1,0:T(8,128)S(1)} %copy-done.3, s32[8]{0:T(128)S(1)} %copy-done.4, bf16[2,224,384]{2,1,0:T(8,128)(2,1)S(1)} %pad_maximum_fusion.1.rest_0_.kv_ref, bf16[27,768]{1,0:T(8,128)(2,1)S(1)} %copy-done.2, bf16[2,224,384]{2,1,0:T(8,128)(2,1)S(1)} %pad_maximum_fusion.3.rest_0_, ...), custom_call_target="tpu_custom_call" | custom-call | flops 1387266048 | bytes 4128768 | tf_op jit(solution)/shard_map/key_side/pallas_call | solution.py:287
  123.7 8.8 %key_side.3 = (bf16[224,768]{1,0:T(8,128)(2,1)}, bf16[224,768]{1,0:T(8,128)(2,1)}) custom-call(s32[4,8,9]{2,1,0:T(8,128)S(1)} %copy-done.3, s32[8]{0:T(128)S(1)} %copy-done.4, bf16[2,224,384]{2,1,0:T(8,128)(2,1)S(1)} %pad_maximum_fusion.rest_0_.kv_ref, bf16[27,768]{1,0:T(8,128)(2,1)S(1)} %copy-done.2, ...), custom_call_target="tpu_custom_call", output_to_operand_aliasing={{0}: (16, {}), {1}: (17, {})} | custom-call | flops 1387266048 | bytes 4128768 | tf_op jit(solution)/shard_map/key_side/pallas_call | solution.py:287
  (38 shorter events, 0.3 us)
Async XLA Ops:
  1.9 5.3 %copy-start = (bf16[2,2,56,768]{3,2,1,0:T(8,128)(2,1)S(1)}, bf16[2,2,56,768]{3,2,1,0:T(8,128)(2,1)}, u32[]{:S(2)}) copy-start(bf16[2,2,56,768]{3,2,1,0:T(8,128)(2,1)} %param.7) | copy-start | bytes 1032196
  1.9 5.3 %copy-start.1 = (bf16[2,2,56,768]{3,2,1,0:T(8,128)(2,1)S(1)}, bf16[2,2,56,768]{3,2,1,0:T(8,128)(2,1)}, u32[]{:S(2)}) copy-start(bf16[2,2,56,768]{3,2,1,0:T(8,128)(2,1)} %param.11) | copy-start | bytes 1032196
  1.9 9.0 %collective-permute-start.8 = (bf16[2,224,384]{2,1,0:T(8,128)(2,1)S(1)}, bf16[2,224,384]{2,1,0:T(8,128)(2,1)S(1)}, u32[]{:S(2)}, u32[]{:S(2)}) collective-permute-start(bf16[2,224,384]{2,1,0:T(8,128)(2,1)S(1)} %pad_maximum_fusion.1.rest_0_.kv_ref), channel_id=1, source_target_pairs={{0,1},{1,0},{2,3},{3,2},{4,5},{5,4},{6,7},{7,6},{8,9},{9,8},{10,11... | collective-permute-start | bytes 1032200 | tf_op jit(solution)/shard_map/ppermute | solution.py:48
  3.2 13.5 %collective-permute-start.10 = (bf16[2,224,384]{2,1,0:T(8,128)(2,1)S(1)}, bf16[2,224,384]{2,1,0:T(8,128)(2,1)S(1)}, u32[]{:S(2)}, u32[]{:S(2)}) collective-permute-start(bf16[2,224,384]{2,1,0:T(8,128)(2,1)S(1)} %pad_maximum_fusion.1.rest_0_.kv_ref), channel_id=1, source_target_pairs={{0,8},{8,0},{16,24},{24,16},{1,9},{9,1},{17,25},{25,17},{2,10},{10... | collective-permute-start | bytes 1032200 | tf_op jit(solution)/shard_map/ppermute | solution.py:43
  4.2 13.8 %collective-permute-start.13 = (bf16[2,224,384]{2,1,0:T(8,128)(2,1)S(1)}, bf16[2,224,384]{2,1,0:T(8,128)(2,1)S(1)}, u32[]{:S(2)}, u32[]{:S(2)}) collective-permute-start(bf16[2,224,384]{2,1,0:T(8,128)(2,1)S(1)} %pad_maximum_fusion.1.rest_0_.kv_ref), channel_id=1, source_target_pairs={{0,0},{8,16},{16,8},{24,24},{1,1},{9,17},{17,9},{25,25},{2,2},{10,... | collective-permute-start | bytes 1032200 | tf_op jit(solution)/shard_map/ppermute | solution.py:43
  7.4 11.0 %collective-permute-start.28 = (bf16[2,224,384]{2,1,0:T(8,128)(2,1)S(1)}, bf16[2,224,384]{2,1,0:T(8,128)(2,1)S(1)}, u32[]{:S(2)}, u32[]{:S(2)}) collective-permute-start(bf16[2,224,384]{2,1,0:T(8,128)(2,1)S(1)} %pad_maximum_fusion.3.rest_0_), channel_id=1, source_target_pairs={{0,1},{1,0},{2,3},{3,2},{4,5},{5,4},{6,7},{7,6},{8,9},{9,8},{10,11... | collective-permute-start | bytes 1032200 | tf_op jit(solution)/shard_map/ppermute | solution.py:48
  7.7 16.4 %collective-permute-start.30 = (bf16[2,224,384]{2,1,0:T(8,128)(2,1)S(1)}, bf16[2,224,384]{2,1,0:T(8,128)(2,1)S(1)}, u32[]{:S(2)}, u32[]{:S(2)}) collective-permute-start(bf16[2,224,384]{2,1,0:T(8,128)(2,1)S(1)} %pad_maximum_fusion.3.rest_0_), channel_id=1, source_target_pairs={{0,8},{8,0},{16,24},{24,16},{1,9},{9,1},{17,25},{25,17},{2,10},{10... | collective-permute-start | bytes 1032200 | tf_op jit(solution)/shard_map/ppermute | solution.py:43
  10.9 14.5 %collective-permute-start.33 = (bf16[2,224,384]{2,1,0:T(8,128)(2,1)S(1)}, bf16[2,224,384]{2,1,0:T(8,128)(2,1)S(1)}, u32[]{:S(2)}, u32[]{:S(2)}) collective-permute-start(bf16[2,224,384]{2,1,0:T(8,128)(2,1)S(1)} %pad_maximum_fusion.3.rest_0_), channel_id=1, source_target_pairs={{0,0},{8,16},{16,8},{24,24},{1,1},{9,17},{17,9},{25,25},{2,2},{10,... | collective-permute-start | bytes 1032200 | tf_op jit(solution)/shard_map/ppermute | solution.py:43
  16.7 10.2 %collective-permute-start = (bf16[2,224,384]{2,1,0:T(8,128)(2,1)S(1)}, bf16[2,224,384]{2,1,0:T(8,128)(2,1)S(1)}, u32[]{:S(2)}, u32[]{:S(2)}) collective-permute-start(bf16[2,224,384]{2,1,0:T(8,128)(2,1)S(1)} %pad_maximum_fusion.rest_0_.kv_ref), channel_id=1, source_target_pairs={{0,1},{1,0},{2,3},{3,2},{4,5},{5,4},{6,7},{7,6},{8,9},{9,8},{10,11... | collective-permute-start | bytes 1032200 | tf_op jit(solution)/shard_map/ppermute | solution.py:48
  18.0 13.4 %collective-permute-start.2 = (bf16[2,224,384]{2,1,0:T(8,128)(2,1)S(1)}, bf16[2,224,384]{2,1,0:T(8,128)(2,1)S(1)}, u32[]{:S(2)}, u32[]{:S(2)}) collective-permute-start(bf16[2,224,384]{2,1,0:T(8,128)(2,1)S(1)} %pad_maximum_fusion.rest_0_.kv_ref), channel_id=1, source_target_pairs={{0,8},{8,0},{16,24},{24,16},{1,9},{9,1},{17,25},{25,17},{2,10},{10... | collective-permute-start | bytes 1032200 | tf_op jit(solution)/shard_map/ppermute | solution.py:43
  18.3 16.3 %collective-permute-start.5 = (bf16[2,224,384]{2,1,0:T(8,128)(2,1)S(1)}, bf16[2,224,384]{2,1,0:T(8,128)(2,1)S(1)}, u32[]{:S(2)}, u32[]{:S(2)}) collective-permute-start(bf16[2,224,384]{2,1,0:T(8,128)(2,1)S(1)} %pad_maximum_fusion.rest_0_.kv_ref), channel_id=1, source_target_pairs={{0,0},{8,16},{16,8},{24,24},{1,1},{9,17},{17,9},{25,25},{2,2},{10,... | collective-permute-start | bytes 1032200 | tf_op jit(solution)/shard_map/ppermute | solution.py:43
  24.0 43.3 %copy-start.2 = (bf16[27,768]{1,0:T(8,128)(2,1)S(1)}, bf16[27,768]{1,0:T(8,128)(2,1)}, u32[]{:S(2)}) copy-start(bf16[27,768]{1,0:T(8,128)(2,1)} %weight_ref.7) | copy-start | bytes 124420
  24.1 43.3 %copy-start.3 = (s32[4,8,9]{2,1,0:T(8,128)S(1)}, s32[4,8,9]{2,1,0:T(8,128)}, u32[]{:S(2)}) copy-start(s32[4,8,9]{2,1,0:T(8,128)} %mask_ref.7) | copy-start | bytes 3460
  24.1 43.3 %copy-start.4 = (s32[8]{0:T(128)S(1)}, s32[8]{0:T(128)}, u32[]{:S(2)}) copy-start(s32[8]{0:T(128)} %clip_ref.7) | copy-start | bytes 100
  24.1 10.6 %collective-permute-start.16 = (bf16[2,224,384]{2,1,0:T(8,128)(2,1)S(1)}, bf16[2,224,384]{2,1,0:T(8,128)(2,1)S(1)}, u32[]{:S(2)}, u32[]{:S(2)}) collective-permute-start(bf16[2,224,384]{2,1,0:T(8,128)(2,1)S(1)} %pad_maximum_fusion.2.rest_0_), channel_id=1, source_target_pairs={{0,1},{1,0},{2,3},{3,2},{4,5},{5,4},{6,7},{7,6},{8,9},{9,8},{10,11... | collective-permute-start | bytes 1032200 | tf_op jit(solution)/shard_map/ppermute | solution.py:48
  25.4 12.2 %collective-permute-start.18 = (bf16[2,224,384]{2,1,0:T(8,128)(2,1)S(1)}, bf16[2,224,384]{2,1,0:T(8,128)(2,1)S(1)}, u32[]{:S(2)}, u32[]{:S(2)}) collective-permute-start(bf16[2,224,384]{2,1,0:T(8,128)(2,1)S(1)} %pad_maximum_fusion.2.rest_0_), channel_id=1, source_target_pairs={{0,8},{8,0},{16,24},{24,16},{1,9},{9,1},{17,25},{25,17},{2,10},{10... | collective-permute-start | bytes 1032200 | tf_op jit(solution)/shard_map/ppermute | solution.py:43
  26.9 13.9 %collective-permute-start.21 = (bf16[2,224,384]{2,1,0:T(8,128)(2,1)S(1)}, bf16[2,224,384]{2,1,0:T(8,128)(2,1)S(1)}, u32[]{:S(2)}, u32[]{:S(2)}) collective-permute-start(bf16[2,224,384]{2,1,0:T(8,128)(2,1)S(1)} %pad_maximum_fusion.2.rest_0_), channel_id=1, source_target_pairs={{0,0},{8,16},{16,8},{24,24},{1,1},{9,17},{17,9},{25,25},{2,2},{10,... | collective-permute-start | bytes 1032200 | tf_op jit(solution)/shard_map/ppermute | solution.py:43
  31.4 9.5 %collective-permute-start.9 = (bf16[2,224,384]{2,1,0:T(8,128)(2,1)S(1)}, bf16[2,224,384]{2,1,0:T(8,128)(2,1)S(1)}, u32[]{:S(2)}, u32[]{:S(2)}) collective-permute-start(bf16[2,224,384]{2,1,0:T(8,128)(2,1)S(1)} %collective-permute-done.8.rest_1_), channel_id=1, source_target_pairs={{0,2},{2,4},{3,1},{4,6},{5,3},{7,5},{8,10},{10,12},{11,9},{12,14},... | collective-permute-start | bytes 1032200 | tf_op jit(solution)/shard_map/ppermute | solution.py:50
  34.6 9.3 %collective-permute-start.11 = (bf16[2,224,384]{2,1,0:T(8,128)(2,1)S(1)}, bf16[2,224,384]{2,1,0:T(8,128)(2,1)S(1)}, u32[]{:S(2)}, u32[]{:S(2)}) collective-permute-start(bf16[2,224,384]{2,1,0:T(8,128)(2,1)S(1)} %collective-permute-done.8.rest_1_), channel_id=1, source_target_pairs={{0,8},{8,0},{16,24},{24,16},{1,9},{9,1},{17,25},{25,17},{2,10},{10... | collective-permute-start | bytes 1032200 | tf_op jit(solution)/shard_map/ppermute | solution.py:43
  34.7 11.9 %collective-permute-start.14 = (bf16[2,224,384]{2,1,0:T(8,128)(2,1)S(1)}, bf16[2,224,384]{2,1,0:T(8,128)(2,1)S(1)}, u32[]{:S(2)}, u32[]{:S(2)}) collective-permute-start(bf16[2,224,384]{2,1,0:T(8,128)(2,1)S(1)} %collective-permute-done.8.rest_1_), channel_id=1, source_target_pairs={{0,0},{8,16},{16,8},{24,24},{1,1},{9,17},{17,9},{25,25},{2,2},{10,... | collective-permute-start | bytes 1032200 | tf_op jit(solution)/shard_map/ppermute | solution.py:43
  37.6 11.8 %collective-permute-start.29 = (bf16[2,224,384]{2,1,0:T(8,128)(2,1)S(1)}, bf16[2,224,384]{2,1,0:T(8,128)(2,1)S(1)}, u32[]{:S(2)}, u32[]{:S(2)}) collective-permute-start(bf16[2,224,384]{2,1,0:T(8,128)(2,1)S(1)} %collective-permute-done.28.rest_1_), channel_id=1, source_target_pairs={{0,2},{2,4},{3,1},{4,6},{5,3},{7,5},{8,10},{10,12},{11,9},{12,14},... | collective-permute-start | bytes 1032200 | tf_op jit(solution)/shard_map/ppermute | solution.py:50
  40.9 10.5 %collective-permute-start.31 = (bf16[2,224,384]{2,1,0:T(8,128)(2,1)S(1)}, bf16[2,224,384]{2,1,0:T(8,128)(2,1)S(1)}, u32[]{:S(2)}, u32[]{:S(2)}) collective-permute-start(bf16[2,224,384]{2,1,0:T(8,128)(2,1)S(1)} %collective-permute-done.28.rest_1_), channel_id=1, source_target_pairs={{0,8},{8,0},{16,24},{24,16},{1,9},{9,1},{17,25},{25,17},{2,10},{10... | collective-permute-start | bytes 1032200 | tf_op jit(solution)/shard_map/ppermute | solution.py:43
  41.0 13.6 %collective-permute-start.34 = (bf16[2,224,384]{2,1,0:T(8,128)(2,1)S(1)}, bf16[2,224,384]{2,1,0:T(8,128)(2,1)S(1)}, u32[]{:S(2)}, u32[]{:S(2)}) collective-permute-start(bf16[2,224,384]{2,1,0:T(8,128)(2,1)S(1)} %collective-permute-done.28.rest_1_), channel_id=1, source_target_pairs={{0,0},{8,16},{16,8},{24,24},{1,1},{9,17},{17,9},{25,25},{2,2},{10,... | collective-permute-start | bytes 1032200 | tf_op jit(solution)/shard_map/ppermute | solution.py:43
  43.9 12.9 %collective-permute-start.1 = (bf16[2,224,384]{2,1,0:T(8,128)(2,1)S(1)}, bf16[2,224,384]{2,1,0:T(8,128)(2,1)S(1)}, u32[]{:S(2)}, u32[]{:S(2)}) collective-permute-start(bf16[2,224,384]{2,1,0:T(8,128)(2,1)S(1)} %collective-permute-done.rest_1_), channel_id=1, source_target_pairs={{0,2},{2,4},{3,1},{4,6},{5,3},{7,5},{8,10},{10,12},{11,9},{12,14},... | collective-permute-start | bytes 1032200 | tf_op jit(solution)/shard_map/ppermute | solution.py:50
  46.6 12.2 %collective-permute-start.3 = (bf16[2,224,384]{2,1,0:T(8,128)(2,1)S(1)}, bf16[2,224,384]{2,1,0:T(8,128)(2,1)S(1)}, u32[]{:S(2)}, u32[]{:S(2)}) collective-permute-start(bf16[2,224,384]{2,1,0:T(8,128)(2,1)S(1)} %collective-permute-done.rest_1_), channel_id=1, source_target_pairs={{0,8},{8,0},{16,24},{24,16},{1,9},{9,1},{17,25},{25,17},{2,10},{10... | collective-permute-start | bytes 1032200 | tf_op jit(solution)/shard_map/ppermute | solution.py:43
  49.4 9.5 %collective-permute-start.6 = (bf16[2,224,384]{2,1,0:T(8,128)(2,1)S(1)}, bf16[2,224,384]{2,1,0:T(8,128)(2,1)S(1)}, u32[]{:S(2)}, u32[]{:S(2)}) collective-permute-start(bf16[2,224,384]{2,1,0:T(8,128)(2,1)S(1)} %collective-permute-done.rest_1_), channel_id=1, source_target_pairs={{0,0},{8,16},{16,8},{24,24},{1,1},{9,17},{17,9},{25,25},{2,2},{10,... | collective-permute-start | bytes 1032200 | tf_op jit(solution)/shard_map/ppermute | solution.py:43
  51.4 11.4 %collective-permute-start.17 = (bf16[2,224,384]{2,1,0:T(8,128)(2,1)S(1)}, bf16[2,224,384]{2,1,0:T(8,128)(2,1)S(1)}, u32[]{:S(2)}, u32[]{:S(2)}) collective-permute-start(bf16[2,224,384]{2,1,0:T(8,128)(2,1)S(1)} %collective-permute-done.16.rest_1_), channel_id=1, source_target_pairs={{0,2},{2,4},{3,1},{4,6},{5,3},{7,5},{8,10},{10,12},{11,9},{12,14},... | collective-permute-start | bytes 1032200 | tf_op jit(solution)/shard_map/ppermute | solution.py:50
  54.6 8.2 %collective-permute-start.12 = (bf16[2,224,384]{2,1,0:T(8,128)(2,1)S(1)}, bf16[2,224,384]{2,1,0:T(8,128)(2,1)S(1)}, u32[]{:S(2)}, u32[]{:S(2)}) collective-permute-start(bf16[2,224,384]{2,1,0:T(8,128)(2,1)S(1)} %collective-permute-done.9.rest_2_), channel_id=1, source_target_pairs={{0,8},{8,0},{16,24},{24,16},{1,9},{9,1},{17,25},{25,17},{2,10},{10... | collective-permute-start | bytes 1032200 | tf_op jit(solution)/shard_map/ppermute | solution.py:43
  56.8 8.6 %collective-permute-start.15 = (bf16[2,224,384]{2,1,0:T(8,128)(2,1)S(1)}, bf16[2,224,384]{2,1,0:T(8,128)(2,1)S(1)}, u32[]{:S(2)}, u32[]{:S(2)}) collective-permute-start(bf16[2,224,384]{2,1,0:T(8,128)(2,1)S(1)} %collective-permute-done.9.rest_2_), channel_id=1, source_target_pairs={{0,0},{8,16},{16,8},{24,24},{1,1},{9,17},{17,9},{25,25},{2,2},{10,... | collective-permute-start | bytes 1032200 | tf_op jit(solution)/shard_map/ppermute | solution.py:43
  58.8 18.5 %collective-permute-start.4 = (bf16[2,224,384]{2,1,0:T(8,128)(2,1)S(1)}, bf16[2,224,384]{2,1,0:T(8,128)(2,1)S(1)}, u32[]{:S(2)}, u32[]{:S(2)}) collective-permute-start(bf16[2,224,384]{2,1,0:T(8,128)(2,1)S(1)} %collective-permute-done.1.rest_2_), channel_id=1, source_target_pairs={{0,8},{8,0},{16,24},{24,16},{1,9},{9,1},{17,25},{25,17},{2,10},{10... | collective-permute-start | bytes 1032200 | tf_op jit(solution)/shard_map/ppermute | solution.py:43
  58.9 19.9 %collective-permute-start.7 = (bf16[2,224,384]{2,1,0:T(8,128)(2,1)S(1)}, bf16[2,224,384]{2,1,0:T(8,128)(2,1)S(1)}, u32[]{:S(2)}, u32[]{:S(2)}) collective-permute-start(bf16[2,224,384]{2,1,0:T(8,128)(2,1)S(1)} %collective-permute-done.1.rest_2_), channel_id=1, source_target_pairs={{0,0},{8,16},{16,8},{24,24},{1,1},{9,17},{17,9},{25,25},{2,2},{10,... | collective-permute-start | bytes 1032200 | tf_op jit(solution)/shard_map/ppermute | solution.py:43
  62.8 28.0 %collective-permute-start.19 = (bf16[2,224,384]{2,1,0:T(8,128)(2,1)S(1)}, bf16[2,224,384]{2,1,0:T(8,128)(2,1)S(1)}, u32[]{:S(2)}, u32[]{:S(2)}) collective-permute-start(bf16[2,224,384]{2,1,0:T(8,128)(2,1)S(1)} %collective-permute-done.16.rest_1_), channel_id=1, source_target_pairs={{0,8},{8,0},{16,24},{24,16},{1,9},{9,1},{17,25},{25,17},{2,10},{10... | collective-permute-start | bytes 1032200 | tf_op jit(solution)/shard_map/ppermute | solution.py:43
  62.8 31.5 %collective-permute-start.32 = (bf16[2,224,384]{2,1,0:T(8,128)(2,1)S(1)}, bf16[2,224,384]{2,1,0:T(8,128)(2,1)S(1)}, u32[]{:S(2)}, u32[]{:S(2)}) collective-permute-start(bf16[2,224,384]{2,1,0:T(8,128)(2,1)S(1)} %collective-permute-done.29.rest_2_), channel_id=1, source_target_pairs={{0,8},{8,0},{16,24},{24,16},{1,9},{9,1},{17,25},{25,17},{2,10},{10... | collective-permute-start | bytes 1032200 | tf_op jit(solution)/shard_map/ppermute | solution.py:43
  65.4 29.1 %collective-permute-start.35 = (bf16[2,224,384]{2,1,0:T(8,128)(2,1)S(1)}, bf16[2,224,384]{2,1,0:T(8,128)(2,1)S(1)}, u32[]{:S(2)}, u32[]{:S(2)}) collective-permute-start(bf16[2,224,384]{2,1,0:T(8,128)(2,1)S(1)} %collective-permute-done.29.rest_2_), channel_id=1, source_target_pairs={{0,0},{8,16},{16,8},{24,24},{1,1},{9,17},{17,9},{25,25},{2,2},{10,... | collective-permute-start | bytes 1032200 | tf_op jit(solution)/shard_map/ppermute | solution.py:43
  77.4 19.1 %collective-permute-start.36 = (f32[16,224]{1,0:T(8,128)S(1)}, f32[16,224]{1,0:T(8,128)S(1)}, u32[]{:S(2)}, u32[]{:S(2)}) collective-permute-start(f32[16,224]{1,0:T(8,128)S(1)} %get-tuple-element.19), channel_id=1, source_target_pairs={{0,1},{1,0},{2,3},{3,2},{4,5},{5,4},{6,7},{7,6},{8,9},{9,8},{10,11... | collective-permute-start | bytes 43016 | tf_op jit(solution)/shard_map/ppermute | solution.py:58
  78.9 20.1 %collective-permute-start.37 = (f32[16,224]{1,0:T(8,128)S(1)}, f32[16,224]{1,0:T(8,128)S(1)}, u32[]{:S(2)}, u32[]{:S(2)}) collective-permute-start(f32[16,224]{1,0:T(8,128)S(1)} %get-tuple-element.19), channel_id=1, source_target_pairs={{0,0},{1,2},{2,1},{3,4},{4,3},{5,6},{6,5},{7,7},{8,8},{9,10},{10,9... | collective-permute-start | bytes 43016 | tf_op jit(solution)/shard_map/ppermute | solution.py:59
  90.8 32.9 %collective-permute-start.22 = (bf16[2,224,384]{2,1,0:T(8,128)(2,1)S(1)}, bf16[2,224,384]{2,1,0:T(8,128)(2,1)S(1)}, u32[]{:S(2)}, u32[]{:S(2)}) collective-permute-start(bf16[2,224,384]{2,1,0:T(8,128)(2,1)S(1)} %collective-permute-done.16.rest_1_), channel_id=1, source_target_pairs={{0,0},{8,16},{16,8},{24,24},{1,1},{9,17},{17,9},{25,25},{2,2},{10,... | collective-permute-start | bytes 1032200 | tf_op jit(solution)/shard_map/ppermute | solution.py:43
  94.3 29.3 %collective-permute-start.20 = (bf16[2,224,384]{2,1,0:T(8,128)(2,1)S(1)}, bf16[2,224,384]{2,1,0:T(8,128)(2,1)S(1)}, u32[]{:S(2)}, u32[]{:S(2)}) collective-permute-start(bf16[2,224,384]{2,1,0:T(8,128)(2,1)S(1)} %collective-permute-done.17.rest_2_), channel_id=1, source_target_pairs={{0,8},{8,0},{16,24},{24,16},{1,9},{9,1},{17,25},{25,17},{2,10},{10... | collective-permute-start | bytes 1032200 | tf_op jit(solution)/shard_map/ppermute | solution.py:43
  94.4 29.3 %collective-permute-start.23 = (bf16[2,224,384]{2,1,0:T(8,128)(2,1)S(1)}, bf16[2,224,384]{2,1,0:T(8,128)(2,1)S(1)}, u32[]{:S(2)}, u32[]{:S(2)}) collective-permute-start(bf16[2,224,384]{2,1,0:T(8,128)(2,1)S(1)} %collective-permute-done.17.rest_2_), channel_id=1, source_target_pairs={{0,0},{8,16},{16,8},{24,24},{1,1},{9,17},{17,9},{25,25},{2,2},{10,... | collective-permute-start | bytes 1032200 | tf_op jit(solution)/shard_map/ppermute | solution.py:43
  96.5 4.4 %collective-permute-start.24 = (f32[16,224]{1,0:T(8,128)S(1)}, f32[16,224]{1,0:T(8,128)S(1)}, u32[]{:S(2)}, u32[]{:S(2)}) collective-permute-start(f32[16,224]{1,0:T(8,128)S(1)} %get-tuple-element.18), channel_id=1, source_target_pairs={{0,1},{1,0},{2,3},{3,2},{4,5},{5,4},{6,7},{7,6},{8,9},{9,8},{10,11... | collective-permute-start | bytes 43016 | tf_op jit(solution)/shard_map/ppermute | solution.py:58
  99.0 5.5 %collective-permute-start.25 = (f32[16,224]{1,0:T(8,128)S(1)}, f32[16,224]{1,0:T(8,128)S(1)}, u32[]{:S(2)}, u32[]{:S(2)}) collective-permute-start(f32[16,224]{1,0:T(8,128)S(1)} %get-tuple-element.18), channel_id=1, source_target_pairs={{0,0},{1,2},{2,1},{3,4},{4,3},{5,6},{6,5},{7,7},{8,8},{9,10},{10,9... | collective-permute-start | bytes 43016 | tf_op jit(solution)/shard_map/ppermute | solution.py:59
  100.9 8.4 %collective-permute-start.38 = (f32[3,16,224]{2,1,0:T(8,128)S(1)}, f32[3,16,224]{2,1,0:T(8,128)S(1)}, u32[]{:S(2)}, u32[]{:S(2)}) collective-permute-start(f32[3,16,224]{2,1,0:T(8,128)S(1)} %pad_maximum_fusion.5.rest_9_), channel_id=1, source_target_pairs={{0,8},{8,0},{16,24},{24,16},{1,9},{9,1},{17,25},{25,17},{2,10},{10... | collective-permute-start | bytes 129032 | tf_op jit(solution)/shard_map/ppermute | solution.py:43
  104.5 6.5 %collective-permute-start.39 = (f32[3,16,224]{2,1,0:T(8,128)S(1)}, f32[3,16,224]{2,1,0:T(8,128)S(1)}, u32[]{:S(2)}, u32[]{:S(2)}) collective-permute-start(f32[3,16,224]{2,1,0:T(8,128)S(1)} %pad_maximum_fusion.5.rest_9_), channel_id=1, source_target_pairs={{0,0},{8,16},{16,8},{24,24},{1,1},{9,17},{17,9},{25,25},{2,2},{10,... | collective-permute-start | bytes 129032 | tf_op jit(solution)/shard_map/ppermute | solution.py:43
  109.3 14.4 %collective-permute-start.26 = (f32[3,16,224]{2,1,0:T(8,128)S(1)}, f32[3,16,224]{2,1,0:T(8,128)S(1)}, u32[]{:S(2)}, u32[]{:S(2)}) collective-permute-start(f32[3,16,224]{2,1,0:T(8,128)S(1)} %pad_maximum_fusion.4.rest_9_), channel_id=1, source_target_pairs={{0,8},{8,0},{16,24},{24,16},{1,9},{9,1},{17,25},{25,17},{2,10},{10... | collective-permute-start | bytes 129032 | tf_op jit(solution)/shard_map/ppermute | solution.py:43
  111.0 12.7 %collective-permute-start.27 = (f32[3,16,224]{2,1,0:T(8,128)S(1)}, f32[3,16,224]{2,1,0:T(8,128)S(1)}, u32[]{:S(2)}, u32[]{:S(2)}) collective-permute-start(f32[3,16,224]{2,1,0:T(8,128)S(1)} %pad_maximum_fusion.4.rest_9_), channel_id=1, source_target_pairs={{0,0},{8,16},{16,8},{24,24},{1,1},{9,17},{17,9},{25,25},{2,2},{10,... | collective-permute-start | bytes 129032 | tf_op jit(solution)/shard_map/ppermute | solution.py:43

commit v2 on v1

v2 whole, which is shorter than its diff:
```python
import functools

import jax
import jax.numpy as jnp
from jax import lax
from jax.experimental import pallas as pl
from jax.experimental.pallas import tpu as pltpu
from jax.sharding import PartitionSpec as P

HEAD_DIM = 128
LOG2E = 1.4426950408889634
ROW_DELTA = 8
STAT_ROWS = 16
UNROLL = 2


CONTRACT_LAST = (((1,), (1,)), ((), ()))


def flip_pairs(count):
    return [(i, i ^ 1) for i in range(count)]


def other_pairs(count):
    pairs = []
    for i in range(count):
        to = i + 1 if i % 2 else i - 1
        pairs.append((i, to if 0 <= to < count else i))
    return pairs


def relay_pairs(count):
    pairs = []
    for i in range(count):
        to = i - 2 if i % 2 else i + 2
        if 0 <= to < count:
            pairs.append((i, to))
    return pairs


def ha_near(x):
    return lax.ppermute(x, "ha", flip_pairs(lax.axis_size("ha")))


def ha_relay(near):
    return lax.ppermute(near, "ha", relay_pairs(lax.axis_size("ha")))


def ha_far(x):
    return lax.ppermute(x, "ha", other_pairs(lax.axis_size("ha")))


def ta_both(x):
    count = lax.axis_size("ta")
    other = lax.ppermute(x, "ta", other_pairs(count))
    return lax.ppermute(x, "ta", flip_pairs(count)), other


def after(x, *earlier):
    return lax.optimization_barrier((x, *earlier))[0]


def offsets(index):
    sign = 1 - 2 * lax.rem(index, 2)
    return (0, sign, -sign)


def inside(index, count):
    return (index >= 0) & (index < count)


def halo_slab(tile, place_now, width):
    even_t, even_h, in_t, in_h = place_now
    tiles = [tile(slot).astype(jnp.float32) for slot in range(9)]

    def cell(slot, frame, row):
        start = (2 * frame + row) * width
        return tiles[slot][start : start + width]

    def side_h(slot_t, frame, R):
        if R in (1, 2):
            return cell(3 * slot_t, frame, R - 1)
        row = 1 if R == 0 else 0
        near, far = cell(3 * slot_t + 1, frame, row), cell(3 * slot_t + 2, frame, row)
        picked = jnp.where(even_h, far, near) if R == 0 else jnp.where(even_h, near, far)
        return jnp.where(in_h[0 if R == 0 else 1], picked, 0.0)

    slab = []
    for F in range(4):
        line = []
        for R in range(4):
            if F in (1, 2):
                line.append(side_h(0, F - 1, R))
                continue
            frame = 1 if F == 0 else 0
            first, second = side_h(1, frame, R), side_h(2, frame, R)
            picked = jnp.where(even_t, second, first) if F == 0 else jnp.where(even_t, first, second)
            line.append(jnp.where(in_t[0 if F == 0 else 1], picked, 0.0))
        slab.append(line)
    return slab


def depthwise(slab, weight, flipped, width):
    column = lax.broadcasted_iota(jnp.int32, (width, HEAD_DIM), 0)
    rows = []
    for f in range(2):
        for r in range(2):
            parts = []
            for dw in range(3):
                total = None
                for dt in range(3):
                    for dh in range(3):
                        tap = 9 * dt + 3 * dh + dw
                        tap = 26 - tap if flipped else tap
                        term = weight[tap : tap + 1] * slab[f + dt][r + dh]
                        total = term if total is None else total + term
                parts.append(total)
            before = jnp.where(column == 0, 0.0, pltpu.roll(parts[0], 1, 0))
            after_ = jnp.where(column == width - 1, 0.0, pltpu.roll(parts[2], width - 1, 0))
            rows.append(parts[1] + before + after_)
    return jnp.concatenate(rows, axis=0)


def place(counts):
    index_t, index_h = lax.axis_index("ta"), lax.axis_index("ha")
    even_t, even_h = lax.rem(index_t, 2) == 0, lax.rem(index_h, 2) == 0
    in_t = (index_t > 0, index_t < counts[0] - 1)
    in_h = (index_h > 0, index_h < counts[1] - 1)
    return index_t, index_h, (even_t, even_h, in_t, in_h)


def head_columns(head):
    return pl.ds(pl.multiple_of(head * HEAD_DIM, HEAD_DIM), HEAD_DIM)


def dot_last(x, y):
    return lax.dot_general(x, y, CONTRACT_LAST, preferred_element_type=jnp.float32)


def dot(x, y):
    return jnp.dot(x, y, preferred_element_type=jnp.float32)


def query_kernel(counts, width, mask_ref, clip_ref, own, other_t, pair_t, weight_ref, near, far, near_a, far_a, near_b,
                 far_b, out_ref, dq_ref, stat_ref, score, bias, stat):
    index_t, index_h, place_now = place(counts)
    rows, channels = own.shape[1:]
    heads = channels // HEAD_DIM
    scale = HEAD_DIM**-0.5
    slots = [own, near, far, pair_t, near_a, far_a, other_t, near_b, far_b]
    lane = lax.broadcasted_iota(jnp.int32, (1, 9 * rows), 1)
    limit = jnp.zeros((1, 9 * rows), jnp.int32)
    for slot in range(9):
        a, b = offsets(index_t)[slot // 3], offsets(index_h)[slot % 3]
        t, h = index_t + a, index_h + b
        kept = (mask_ref[index_t, index_h, 3 * (a + 1) + (b + 1)] == 1) & inside(t, counts[0]) & inside(h, counts[1])
        safe = jnp.clip(t, 0, counts[0] - 1)
        for f in range(2):
            live = jnp.where(kept, clip_ref[2 * safe + f], 0)
            limit = jnp.where(lane >= slot * rows + f * (rows // 2), live, limit)
    bias[...] = jnp.where(lax.rem(lane, width) < limit, 0.0, -jnp.inf)
    which = lax.broadcasted_iota(jnp.int32, (rows, HEAD_DIM), 1)

    def body(step, _):
        hs = [step * UNROLL + u for u in range(UNROLL)]
        cols = [head_columns(h) for h in hs]
        every = range(UNROLL)
        row_max, row_total, acc, dp, dq = ([None] * UNROLL for _ in range(5))
        for u in every:
            keys = jnp.concatenate([ref[0, :, cols[u]] for ref in slots], axis=0)
            s = dot_last(own[2, :, cols[u]], keys) * (scale * LOG2E) + bias[...]
            score[u] = s
            row_max[u] = jnp.max(s, axis=1, keepdims=True)
        for u in every:
            e = jnp.exp2(score[u] - row_max[u])
            score[u] = e
            row_total[u] = jnp.sum(e, axis=1, keepdims=True)
            values = jnp.concatenate([ref[1, :, cols[u]] for ref in slots], axis=0)
            acc[u] = dot(e.astype(jnp.bfloat16), values)
        for u in every:
            grad = own[3, :, cols[u]]
            inverse = 1.0 / row_total[u]
            attention = acc[u] * inverse
            delta = jnp.sum(grad.astype(jnp.float32) * attention, axis=1, keepdims=True)
            values = jnp.concatenate([ref[1, :, cols[u]] for ref in slots], axis=0)
            ds = (score[u] * (dot_last(grad, values) - delta)).astype(jnp.bfloat16)
            keys = jnp.concatenate([ref[0, :, cols[u]] for ref in slots], axis=0)
            dq_ref[:, cols[u]] = (dot(ds, keys) * (inverse * scale)).astype(jnp.bfloat16)
            log_total = row_max[u] + jnp.log2(row_total[u])
            marked = jnp.where(which == hs[u], log_total, stat[...])
            stat[...] = jnp.where(which == hs[u] + ROW_DELTA, delta, marked)
            slab = halo_slab(lambda slot: slots[slot][1, :, cols[u]], place_now, width)
            conv = depthwise(slab, weight_ref[:, cols[u]].astype(jnp.float32), False, width)
            out_ref[:, cols[u]] = (attention + conv).astype(jnp.bfloat16)
        return 0

    stat[...] = jnp.zeros_like(stat)
    lax.fori_loop(0, heads // UNROLL, body, 0)
    pad = jnp.zeros((-rows % HEAD_DIM, HEAD_DIM), jnp.float32)
    turned = jnp.concatenate([stat[...], pad], axis=0).T
    stat_ref[...] = turned[:STAT_ROWS, :rows]


def key_kernel(counts, width, mask_ref, clip_ref, own, other_t, pair_t, weight_ref, near, far, near_a, far_a, near_b,
               far_b, stat_ref, dk_ref, dv_ref, stats):
    index_t, index_h, place_now = place(counts)
    rows, channels = own.shape[1:]
    heads = channels // HEAD_DIM
    scale = HEAD_DIM**-0.5
    slots = [own, near, far, pair_t, near_a, far_a, other_t, near_b, far_b]

    def part(slot, what, cols):
        return slots[slot][what + 2 if slot % 3 == 0 else what, :, cols]

    lane = lax.broadcasted_iota(jnp.int32, (STAT_ROWS, 9 * rows), 1)
    line = lax.broadcasted_iota(jnp.int32, (STAT_ROWS, 9 * rows), 0)
    use = jnp.zeros((STAT_ROWS, 9 * rows), jnp.int32)
    for slot in range(9):
        a, b = offsets(index_t)[slot // 3], offsets(index_h)[slot % 3]
        t, h = index_t + a, index_h + b
        safe_t, safe_h = jnp.clip(t, 0, counts[0] - 1), jnp.clip(h, 0, counts[1] - 1)
        kept = (mask_ref[safe_t, safe_h, 3 * (1 - a) + (1 - b)] == 1) & inside(t, counts[0]) & inside(h, counts[1])
        use = jnp.where(lane >= slot * rows, kept.astype(jnp.int32), use)
    stats[...] = jnp.where((use == 1) | (line >= ROW_DELTA), stat_ref[...], jnp.inf)
    row = lax.broadcasted_iota(jnp.int32, (rows, HEAD_DIM), 0)
    lens = [clip_ref[2 * index_t + f] for f in range(2)]
    live = lax.rem(row, width) < jnp.where(row < 2 * width, lens[0], lens[1])

    def body(step, _):
        for u in range(UNROLL):
            head = step * UNROLL + u
            cols = head_columns(head)
            queries = jnp.concatenate([part(slot, 0, cols) for slot in range(9)], axis=0)
            grads = jnp.concatenate([part(slot, 1, cols) for slot in range(9)], axis=0)
            s = dot_last(own[0, :, cols], queries)
            p = jnp.exp2(s * (scale * LOG2E) - stats[pl.ds(head, 1), :])
            dp = dot_last(own[1, :, cols], grads)
            ds = (p * (dp - stats[pl.ds(head + ROW_DELTA, 1), :])).astype(jnp.bfloat16)
            dv = jnp.where(live, dot(p.astype(jnp.bfloat16), grads), 0.0)
            dk = jnp.where(live, dot(ds, queries) * scale, 0.0)
            dk_ref[:, cols] = dk.astype(jnp.bfloat16)
            slab = halo_slab(lambda slot: part(slot, 1, cols), place_now, width)
            conv = depthwise(slab, weight_ref[:, cols].astype(jnp.float32), True, width)
            dv_ref[:, cols] = (dv + conv).astype(jnp.bfloat16)
        return 0

    lax.fori_loop(0, heads // UNROLL, body, 0)


def cost(heads, rows, matmuls):
    work = heads * rows * 9 * rows * HEAD_DIM * 2 * matmuls
    return pl.CostEstimate(flops=work, bytes_accessed=heads * rows * HEAD_DIM * 2 * 24, transcendentals=heads * rows * rows * 9)


def shards(query_states, key_states, value_states, conv_weight, out_grad, tile_mask, clip_lengths):
    width, channels = query_states.shape[2:]
    rows = query_states.shape[0] * query_states.shape[1] * width
    counts = (lax.axis_size("ta"), lax.axis_size("ha"))
    heads = channels // HEAD_DIM
    query, key, value, grad = [x.reshape(rows, channels) for x in (query_states, key_states, value_states, out_grad)]

    kv = jnp.stack([key, value])
    own = jnp.stack([key, value, query, grad])
    near_kv = ha_near(kv)
    pair_t, other_t = ta_both(own)
    far_kv = ha_relay(near_kv)
    near_kv_a, near_kv_b = ta_both(near_kv)
    near_qg = ha_near(after(jnp.stack([query, grad]), near_kv))
    far_kv_a, far_kv_b = ta_both(far_kv)
    far_qg = ha_relay(after(near_qg, far_kv))
    near_qg_a, near_qg_b = ta_both(near_qg)
    far_qg_a, far_qg_b = ta_both(far_qg)

    smem = pl.BlockSpec(memory_space=pltpu.SMEM)
    vmem = pl.BlockSpec(memory_space=pltpu.VMEM)
    params = pltpu.CompilerParams(vmem_limit_bytes=32 * 1024 * 1024)
    full = jax.ShapeDtypeStruct((rows, channels), jnp.bfloat16)
    layer_out, query_grad, stat = pl.pallas_call(
        functools.partial(query_kernel, counts, width),
        in_specs=[smem, smem] + [vmem] * 10,
        out_specs=[vmem] * 3,
        out_shape=[full, full, jax.ShapeDtypeStruct((STAT_ROWS, rows), jnp.float32)],
        scratch_shapes=[
            pltpu.VMEM((UNROLL, rows, 9 * rows), jnp.float32),
            pltpu.VMEM((1, 9 * rows), jnp.float32),
            pltpu.VMEM((rows, HEAD_DIM), jnp.float32),
        ],
        compiler_params=params,
        cost_estimate=cost(heads, rows, 4),
        name="query_side",
    )(tile_mask, clip_lengths, own, other_t, pair_t, conv_weight, near_kv, far_kv, near_kv_a, far_kv_a, near_kv_b, far_kv_b)

    column = jnp.concatenate([stat, ha_near(stat), ha_far(stat)], axis=1)
    column_a, column_b = ta_both(column)
    stats = jnp.concatenate([column, column_a, column_b], axis=1)
    key_grad, value_grad = pl.pallas_call(
        functools.partial(key_kernel, counts, width),
        in_specs=[smem, smem] + [vmem] * 11,
        out_specs=[vmem] * 2,
        out_shape=[full, full],
        scratch_shapes=[pltpu.VMEM((STAT_ROWS, 9 * rows), jnp.float32)],
        compiler_params=params,
        cost_estimate=cost(heads, rows, 4),
        name="key_side",
    )(tile_mask, clip_lengths, own, other_t, pair_t, conv_weight, near_qg, far_qg, near_qg_a, far_qg_a, near_qg_b, far_qg_b, stats)

    return tuple(x.reshape(query_states.shape) for x in (layer_out, query_grad, key_grad, value_grad))


def solution(mesh):
    placed = P("ta", "ha", None, None)
    return jax.shard_map(
        shards,
        mesh=mesh,
        in_specs=(placed, placed, placed, P(), placed, P(), P()),
        out_specs=(placed,) * 4,
        check_vma=False,
    )
```

time: 133 us -> 109 us (0.82)
  starting transfers between devices: 74.7 us -> 39.1 us
  waiting for transfers between devices: 17.6 us -> 41.7 us
  Pallas kernels: 37.6 us -> 23.2 us
  other arithmetic: 0.19 us -> 1.57 us
    ppermute x40 -> x18, starting transfers between devices: 74.7 us -> 39.1 us  [the longest x6 18.6 us: ta_both(): other = lax.ppermute(x, 'ta', other_pairs(count))]
    ppermute x40 -> x18, waiting for transfers between devices: 17.6 us -> 41.7 us  [the longest x2 17.9 us: ha_relay(): return lax.ppermute(near, 'ha', relay_pairs(lax.axis_size('ha')))]
    pallas_call x4 -> x2, Pallas kernels: 37.6 us -> 23.2 us  [the longest x1 11.7 us: shards(): pl.pallas_call(functools.partial(query_kernel, counts, width), in_specs=[...]
    unnamed x10 -> x18, local copies, waits for them, and re-layouts: 0.03 us -> 1.37 us
  transfers between devices with their start and end apart: 40 -> 18, of which waited for: 9 -> 8; matrix products, arithmetic and copies ran while one was open for 0% -> 0% of each run, Pallas kernels for 22% -> 11%
where the time goes in v2:
time: 109 us; the launch traced here: 108 us
  waiting for transfers between devices  41.7 us (38%)
  starting transfers between devices  39.1 us (36%)
  Pallas kernels  23.2 us (21%)
  other arithmetic  1.57 us (1%)
  local copies, waits for them, and re-layouts  1.48 us (1%)
    ppermute x6, starting transfers between devices, ta_both(): other = lax.ppermute(x, 'ta', other_pairs(count))  18.6 us
    ppermute x2, waiting for transfers between devices, ha_relay(): return lax.ppermute(near, 'ha', relay_pairs(lax.axis_size('ha')))  17.9 us
    ppermute x3, waiting for transfers between devices, ha_near(): return lax.ppermute(x, 'ha', flip_pairs(lax.axis_size('ha')))  12.9 us
    pallas_call x1, Pallas kernels, shards(): pl.pallas_call(functools.partial(query_kernel, counts, width), in_specs=[...  11.7 us
    pallas_call x1, Pallas kernels, shards(): pl.pallas_call(functools.partial(key_kernel, counts, width), in_specs=[sm...  11.6 us
    ppermute x6, starting transfers between devices, ta_both(): return (lax.ppermute(x, 'ta', flip_pairs(count)), other)  9.97 us
    ppermute x6, waiting for transfers between devices, ta_both(): other = lax.ppermute(x, 'ta', other_pairs(count))  6.86 us
    ppermute x2, starting transfers between devices, ha_relay(): return lax.ppermute(near, 'ha', relay_pairs(lax.axis_size('ha')))  6.4 us
  transfers between devices with their start and end apart: 18, of which 8 were waited for; matrix products, arithmetic and copies ran while one was open for 0% of the time, Pallas kernels for 11%

profile of v2, /device:TPU:9, one launch (start us, length us, event | category | flops | bytes accessed | tf_op | source)
XLA Modules:
  0.0 108.0 jit_solution(11592331556267461441)
XLA Ops:
  0.6 0.0 copy-start.5
  0.6 0.0 copy-start.6
  0.7 0.0 copy-start.7
  0.7 0.0 copy-start.8
  0.7 1.2 %pad_maximum_fusion.1 = bf16[2,224,768]{2,1,0:T(8,128)(2,1)S(1)} fusion(bf16[1,224,768]{2,1,0:T(8,128)(2,1)} %bitcast.8, bf16[1,224,768]{2,1,0:T(8,128)(2,1)} %bitcast.10), kind=kLoop, calls=%fused_computation.1 | loop fusion | flops 344064 | bytes 1376256 | tf_op jit(solution)/shard_map/stack | solution.py:262
  1.9 1.3 %collective-permute-start.2 = (bf16[2,224,768]{2,1,0:T(8,128)(2,1)S(1)}, bf16[2,224,768]{2,1,0:T(8,128)(2,1)S(1)}, u32[]{:S(2)}, u32[]{:S(2)}) collective-permute-start(bf16[2,224,768]{2,1,0:T(8,128)(2,1)S(1)} %pad_maximum_fusion.1), channel_id=1, source_target_pairs={{0,1},{1,0},{2,3},{3,2},{4,5},{5,4},{6,7},{7,6},{8,9},{9,8},{10,11... | collective-permute-start | bytes 2064392 | tf_op jit(solution)/shard_map/ppermute | solution.py:42
  3.2 0.0 copy-done.5
  3.2 0.0 copy-done.6
  3.2 0.0 copy-done.7
  3.2 0.0 copy-done.8
  3.2 0.0 copy-start.2
  3.2 0.0 copy-start.3
  3.2 0.0 copy-start.4
  3.2 0.2 pad_maximum_fusion.own
  3.4 4.0 %collective-permute-start = (bf16[4,224,768]{2,1,0:T(8,128)(2,1)S(1)}, bf16[4,224,768]{2,1,0:T(8,128)(2,1)S(1)}, u32[]{:S(2)}, u32[]{:S(2)}) collective-permute-start(bf16[4,224,768]{2,1,0:T(8,128)(2,1)S(1)} %pad_maximum_fusion.own), channel_id=1, source_target_pairs={{0,0},{8,16},{16,8},{24,24},{1,1},{9,17},{17,9},{25,25},{2,2},{10,... | collective-permute-start | bytes 4128776 | tf_op jit(solution)/shard_map/ppermute | solution.py:55
  7.4 0.1 collective-permute-start.1
  7.5 0.1 pad_maximum_fusion.2
  7.6 10.7 %collective-permute-done.2.near = bf16[2,224,768]{2,1,0:T(8,128)(2,1)S(1)} collective-permute-done((bf16[2,224,768]{2,1,0:T(8,128)(2,1)S(1)}, bf16[2,224,768]{2,1,0:T(8,128)(2,1)S(1)}, u32[]{:S(2)}, u32[]{:S(2)}) %collective-permute-start.2) | collective-permute-done | bytes 688160 | tf_op jit(solution)/shard_map/ppermute | solution.py:42
  18.3 3.2 %collective-permute-start.3 = (bf16[2,224,768]{2,1,0:T(8,128)(2,1)S(1)}, bf16[2,224,768]{2,1,0:T(8,128)(2,1)S(1)}, u32[]{:S(2)}, u32[]{:S(2)}) collective-permute-start(bf16[2,224,768]{2,1,0:T(8,128)(2,1)S(1)} %collective-permute-done.2.near), channel_id=1, source_target_pairs={{0,2},{2,4},{3,1},{4,6},{5,3},{7,5},{8,10},{10,12},{11,9},{12,14},... | collective-permute-start | bytes 2064392 | tf_op jit(solution)/shard_map/ppermute | solution.py:46
  21.5 0.1 collective-permute-start.8
  21.6 2.1 %collective-permute-start.4 = (bf16[2,224,768]{2,1,0:T(8,128)(2,1)S(1)}, bf16[2,224,768]{2,1,0:T(8,128)(2,1)S(1)}, u32[]{:S(2)}, u32[]{:S(2)}) collective-permute-start(bf16[2,224,768]{2,1,0:T(8,128)(2,1)S(1)} %collective-permute-done.2.near), channel_id=1, source_target_pairs={{0,8},{8,0},{16,24},{24,16},{1,9},{9,1},{17,25},{25,17},{2,10},{10... | collective-permute-start | bytes 2064392 | tf_op jit(solution)/shard_map/ppermute | solution.py:56
  23.7 11.9 %collective-permute-done.3.far = bf16[2,224,768]{2,1,0:T(8,128)(2,1)S(1)} collective-permute-done((bf16[2,224,768]{2,1,0:T(8,128)(2,1)S(1)}, bf16[2,224,768]{2,1,0:T(8,128)(2,1)S(1)}, u32[]{:S(2)}, u32[]{:S(2)}) %collective-permute-start.3) | collective-permute-done | bytes 688160 | tf_op jit(solution)/shard_map/ppermute | solution.py:46
  35.7 5.4 %collective-permute-start.6 = (bf16[2,224,768]{2,1,0:T(8,128)(2,1)S(1)}, bf16[2,224,768]{2,1,0:T(8,128)(2,1)S(1)}, u32[]{:S(2)}, u32[]{:S(2)}) collective-permute-start(bf16[2,224,768]{2,1,0:T(8,128)(2,1)S(1)} %collective-permute-done.2.near), channel_id=1, source_target_pairs={{0,0},{8,16},{16,8},{24,24},{1,1},{9,17},{17,9},{25,25},{2,2},{10,... | collective-permute-start | bytes 2064392 | tf_op jit(solution)/shard_map/ppermute | solution.py:55
  41.1 0.0 collective-permute-done.8.near
  41.1 3.2 %collective-permute-start.9 = (bf16[2,224,768]{2,1,0:T(8,128)(2,1)}, bf16[2,224,768]{2,1,0:T(8,128)(2,1)}, u32[]{:S(2)}, u32[]{:S(2)}) collective-permute-start(bf16[2,224,768]{2,1,0:T(8,128)(2,1)} %collective-permute-done.8.near), channel_id=1, source_target_pairs={{0,2},{2,4},{3,1},{4,6},{5,3},{7,5},{8,10},{10,12},{11,9},{12,14},... | collective-permute-start | bytes 2064392 | tf_op jit(solution)/shard_map/ppermute | solution.py:46
  44.3 0.0 collective-permute-done.other_t
  44.3 0.1 collective-permute-start.5
  44.4 0.0 collective-permute-done.1.pair_t
  44.4 0.0 copy-start
  44.4 2.2 %collective-permute-start.7 = (bf16[2,224,768]{2,1,0:T(8,128)(2,1)S(1)}, bf16[2,224,768]{2,1,0:T(8,128)(2,1)S(1)}, u32[]{:S(2)}, u32[]{:S(2)}) collective-permute-start(bf16[2,224,768]{2,1,0:T(8,128)(2,1)S(1)} %collective-permute-done.3.far), channel_id=1, source_target_pairs={{0,0},{8,16},{16,8},{24,24},{1,1},{9,17},{17,9},{25,25},{2,2},{10,... | collective-permute-start | bytes 2064392 | tf_op jit(solution)/shard_map/ppermute | solution.py:55
  46.6 0.0 collective-permute-done.4.near_a
  46.6 0.1 collective-permute-start.10
  46.7 3.4 %collective-permute-done.6.near_b = bf16[2,224,768]{2,1,0:T(8,128)(2,1)S(1)} collective-permute-done((bf16[2,224,768]{2,1,0:T(8,128)(2,1)S(1)}, bf16[2,224,768]{2,1,0:T(8,128)(2,1)S(1)}, u32[]{:S(2)}, u32[]{:S(2)}) %collective-permute-start.6) | collective-permute-done | bytes 688160 | tf_op jit(solution)/shard_map/ppermute | solution.py:55
  50.1 3.2 %collective-permute-start.12 = (bf16[2,224,768]{2,1,0:T(8,128)(2,1)}, bf16[2,224,768]{2,1,0:T(8,128)(2,1)}, u32[]{:S(2)}, u32[]{:S(2)}) collective-permute-start(bf16[2,224,768]{2,1,0:T(8,128)(2,1)} %collective-permute-done.8.near), channel_id=1, source_target_pairs={{0,0},{8,16},{16,8},{24,24},{1,1},{9,17},{17,9},{25,25},{2,2},{10,... | collective-permute-start | bytes 2064392 | tf_op jit(solution)/shard_map/ppermute | solution.py:55
  53.3 6.0 %collective-permute-done.9.far = bf16[2,224,768]{2,1,0:T(8,128)(2,1)} collective-permute-done((bf16[2,224,768]{2,1,0:T(8,128)(2,1)}, bf16[2,224,768]{2,1,0:T(8,128)(2,1)}, u32[]{:S(2)}, u32[]{:S(2)}) %collective-permute-start.9) | collective-permute-done | bytes 688160 | tf_op jit(solution)/shard_map/ppermute | solution.py:46
  59.3 0.0 collective-permute-start.11
  59.3 0.0 collective-permute-done.5.far_a
  59.3 1.9 %collective-permute-start.13 = (bf16[2,224,768]{2,1,0:T(8,128)(2,1)}, bf16[2,224,768]{2,1,0:T(8,128)(2,1)}, u32[]{:S(2)}, u32[]{:S(2)}) collective-permute-start(bf16[2,224,768]{2,1,0:T(8,128)(2,1)} %collective-permute-done.9.far), channel_id=1, source_target_pairs={{0,0},{8,16},{16,8},{24,24},{1,1},{9,17},{17,9},{25,25},{2,2},{10,... | collective-permute-start | bytes 2064392 | tf_op jit(solution)/shard_map/ppermute | solution.py:55
  61.3 0.0 collective-permute-done.7.far_b
  61.3 0.0 copy-done.2
  61.3 0.0 copy-done.3
  61.3 0.0 copy-done.4
  61.3 11.7 %query_side.1 = (bf16[224,768]{1,0:T(8,128)(2,1)}, bf16[224,768]{1,0:T(8,128)(2,1)}, f32[16,224]{1,0:T(8,128)S(1)}) custom-call(s32[4,8,9]{2,1,0:T(8,128)S(1)} %copy-done.3, s32[8]{0:T(128)S(1)} %copy-done.4, bf16[4,224,768]{2,1,0:T(8,128)(2,1)S(1)} %pad_maximum_fusion.own, bf16[4,224,768]{2,1,0:T(8,128)(2,1)S(1)} %collective-permute-done.other_t, ...), custom_call_target="tpu_custom_call" | custom-call | flops 2774532096 | bytes 8257536 | tf_op jit(solution)/shard_map/query_side/pallas_call | solution.py:278
  73.0 0.0 copy-done
  73.0 0.4 collective-permute-start.14
  73.4 2.1 %collective-permute-done.14 = f32[16,224]{1,0:T(8,128)S(1)} collective-permute-done((f32[16,224]{1,0:T(8,128)S(1)}, f32[16,224]{1,0:T(8,128)S(1)}, u32[]{:S(2)}, u32[]{:S(2)}) %collective-permute-start.14) | collective-permute-done | bytes 14368 | tf_op jit(solution)/shard_map/ppermute | solution.py:42
  75.6 2.2 %collective-permute-start.15 = (f32[16,224]{1,0:T(8,128)S(1)}, f32[16,224]{1,0:T(8,128)S(1)}, u32[]{:S(2)}, u32[]{:S(2)}) collective-permute-start(f32[16,224]{1,0:T(8,128)S(1)} %get-tuple-element.15), channel_id=1, source_target_pairs={{0,0},{1,2},{2,1},{3,4},{4,3},{5,6},{6,5},{7,7},{8,8},{9,10},{10,9... | collective-permute-start | bytes 43016 | tf_op jit(solution)/shard_map/ppermute | solution.py:50
  77.8 3.1 %collective-permute-done.15 = f32[16,224]{1,0:T(8,128)S(1)} collective-permute-done((f32[16,224]{1,0:T(8,128)S(1)}, f32[16,224]{1,0:T(8,128)S(1)}, u32[]{:S(2)}, u32[]{:S(2)}) %collective-permute-start.15) | collective-permute-done | bytes 14368 | tf_op jit(solution)/shard_map/ppermute | solution.py:50
  81.0 0.1 pad_maximum_fusion.3
  81.0 7.6 %collective-permute-start.16 = (f32[16,672]{1,0:T(8,128)S(1)}, f32[16,672]{1,0:T(8,128)S(1)}, u32[]{:S(2)}, u32[]{:S(2)}) collective-permute-start(f32[16,672]{1,0:T(8,128)S(1)} %pad_maximum_fusion.3), channel_id=1, source_target_pairs={{0,8},{8,0},{16,24},{24,16},{1,9},{9,1},{17,25},{25,17},{2,10},{10... | collective-permute-start | bytes 129032 | tf_op jit(solution)/shard_map/ppermute | solution.py:56
  88.7 0.9 collective-permute-done.16
  89.6 1.9 %collective-permute-start.17 = (f32[16,672]{1,0:T(8,128)S(1)}, f32[16,672]{1,0:T(8,128)S(1)}, u32[]{:S(2)}, u32[]{:S(2)}) collective-permute-start(f32[16,672]{1,0:T(8,128)S(1)} %pad_maximum_fusion.3), channel_id=1, source_target_pairs={{0,0},{8,16},{16,8},{24,24},{1,1},{9,17},{17,9},{25,25},{2,2},{10,... | collective-permute-start | bytes 129032 | tf_op jit(solution)/shard_map/ppermute | solution.py:55
  91.5 3.5 %collective-permute-done.17 = f32[16,672]{1,0:T(8,128)S(1)} collective-permute-done((f32[16,672]{1,0:T(8,128)S(1)}, f32[16,672]{1,0:T(8,128)S(1)}, u32[]{:S(2)}, u32[]{:S(2)}) %collective-permute-start.17) | collective-permute-done | bytes 43040 | tf_op jit(solution)/shard_map/ppermute | solution.py:55
  95.0 0.1 concatenate.8.stat_ref
  95.1 0.0 collective-permute-done.10.near_a
  95.1 0.0 collective-permute-done.12.near_b
  95.1 0.0 collective-permute-done.11.far_a
  95.1 0.0 collective-permute-done.13.far_b
  95.1 0.0 copy-start.1
  95.1 1.3 %copy-done.1 = bf16[4,224,768]{2,1,0:T(8,128)(2,1)S(1)} copy-done((bf16[4,224,768]{2,1,0:T(8,128)(2,1)S(1)}, bf16[4,224,768]{2,1,0:T(8,128)(2,1)}, u32[]{:S(2)}) %copy-start.1) | copy-done | bytes 1376280
  96.5 11.6 %key_side.1 = (bf16[224,768]{1,0:T(8,128)(2,1)}, bf16[224,768]{1,0:T(8,128)(2,1)}) custom-call(s32[4,8,9]{2,1,0:T(8,128)S(1)} %copy-done.3, s32[8]{0:T(128)S(1)} %copy-done.4, bf16[4,224,768]{2,1,0:T(8,128)(2,1)S(1)} %pad_maximum_fusion.own, bf16[4,224,768]{2,1,0:T(8,128)(2,1)S(1)} %collective-permute-done.other_t, bf16[4,224,768]{2,1,0:T(8,128)(2,1)S(1)} %copy-done.1, ...), custom_call_target="tpu_custom_call" | custom-call | flops 2774532096 | bytes 8257536 | tf_op jit(solution)/shard_map/key_side/pallas_call | solution.py:296
Async XLA Ops:
  0.6 2.6 %copy-start.5 = (bf16[2,2,56,768]{3,2,1,0:T(8,128)(2,1)S(1)}, bf16[2,2,56,768]{3,2,1,0:T(8,128)(2,1)}, u32[]{:S(2)}) copy-start(bf16[2,2,56,768]{3,2,1,0:T(8,128)(2,1)} %param.9) | copy-start | bytes 1032196
  0.6 2.6 %copy-start.6 = (bf16[2,2,56,768]{3,2,1,0:T(8,128)(2,1)S(1)}, bf16[2,2,56,768]{3,2,1,0:T(8,128)(2,1)}, u32[]{:S(2)}) copy-start(bf16[2,2,56,768]{3,2,1,0:T(8,128)(2,1)} %param.8) | copy-start | bytes 1032196
  0.7 2.6 %copy-start.7 = (bf16[2,2,56,768]{3,2,1,0:T(8,128)(2,1)S(1)}, bf16[2,2,56,768]{3,2,1,0:T(8,128)(2,1)}, u32[]{:S(2)}) copy-start(bf16[2,2,56,768]{3,2,1,0:T(8,128)(2,1)} %param.11) | copy-start | bytes 1032196
  0.7 2.5 %copy-start.8 = (bf16[2,2,56,768]{3,2,1,0:T(8,128)(2,1)S(1)}, bf16[2,2,56,768]{3,2,1,0:T(8,128)(2,1)}, u32[]{:S(2)}) copy-start(bf16[2,2,56,768]{3,2,1,0:T(8,128)(2,1)} %param.7) | copy-start | bytes 1032196
  1.9 16.4 %collective-permute-start.2 = (bf16[2,224,768]{2,1,0:T(8,128)(2,1)S(1)}, bf16[2,224,768]{2,1,0:T(8,128)(2,1)S(1)}, u32[]{:S(2)}, u32[]{:S(2)}) collective-permute-start(bf16[2,224,768]{2,1,0:T(8,128)(2,1)S(1)} %pad_maximum_fusion.1), channel_id=1, source_target_pairs={{0,1},{1,0},{2,3},{3,2},{4,5},{5,4},{6,7},{7,6},{8,9},{9,8},{10,11... | collective-permute-start | bytes 2064392 | tf_op jit(solution)/shard_map/ppermute | solution.py:42
  3.2 58.1 %copy-start.2 = (bf16[27,768]{1,0:T(8,128)(2,1)S(1)}, bf16[27,768]{1,0:T(8,128)(2,1)}, u32[]{:S(2)}) copy-start(bf16[27,768]{1,0:T(8,128)(2,1)} %weight_ref.3) | copy-start | bytes 124420
  3.2 58.1 %copy-start.3 = (s32[4,8,9]{2,1,0:T(8,128)S(1)}, s32[4,8,9]{2,1,0:T(8,128)}, u32[]{:S(2)}) copy-start(s32[4,8,9]{2,1,0:T(8,128)} %mask_ref.3) | copy-start | bytes 3460
  3.2 58.1 %copy-start.4 = (s32[8]{0:T(128)S(1)}, s32[8]{0:T(128)}, u32[]{:S(2)}) copy-start(s32[8]{0:T(128)} %clip_ref.3) | copy-start | bytes 100
  3.4 40.8 %collective-permute-start = (bf16[4,224,768]{2,1,0:T(8,128)(2,1)S(1)}, bf16[4,224,768]{2,1,0:T(8,128)(2,1)S(1)}, u32[]{:S(2)}, u32[]{:S(2)}) collective-permute-start(bf16[4,224,768]{2,1,0:T(8,128)(2,1)S(1)} %pad_maximum_fusion.own), channel_id=1, source_target_pairs={{0,0},{8,16},{16,8},{24,24},{1,1},{9,17},{17,9},{25,25},{2,2},{10,... | collective-permute-start | bytes 4128776 | tf_op jit(solution)/shard_map/ppermute | solution.py:55
  7.4 36.9 %collective-permute-start.1 = (bf16[4,224,768]{2,1,0:T(8,128)(2,1)S(1)}, bf16[4,224,768]{2,1,0:T(8,128)(2,1)S(1)}, u32[]{:S(2)}, u32[]{:S(2)}) collective-permute-start(bf16[4,224,768]{2,1,0:T(8,128)(2,1)S(1)} %pad_maximum_fusion.own), channel_id=1, source_target_pairs={{0,8},{8,0},{16,24},{24,16},{1,9},{9,1},{17,25},{25,17},{2,10},{10... | collective-permute-start | bytes 4128776 | tf_op jit(solution)/shard_map/ppermute | solution.py:56
  18.3 17.4 %collective-permute-start.3 = (bf16[2,224,768]{2,1,0:T(8,128)(2,1)S(1)}, bf16[2,224,768]{2,1,0:T(8,128)(2,1)S(1)}, u32[]{:S(2)}, u32[]{:S(2)}) collective-permute-start(bf16[2,224,768]{2,1,0:T(8,128)(2,1)S(1)} %collective-permute-done.2.near), channel_id=1, source_target_pairs={{0,2},{2,4},{3,1},{4,6},{5,3},{7,5},{8,10},{10,12},{11,9},{12,14},... | collective-permute-start | bytes 2064392 | tf_op jit(solution)/shard_map/ppermute | solution.py:46
  21.5 19.6 %collective-permute-start.8 = (bf16[2,224,768]{2,1,0:T(8,128)(2,1)S(1)}, bf16[2,224,768]{2,1,0:T(8,128)(2,1)}, u32[]{:S(2)}, u32[]{:S(2)}) collective-permute-start(bf16[2,224,768]{2,1,0:T(8,128)(2,1)S(1)} %pad_maximum_fusion.2), channel_id=1, source_target_pairs={{0,1},{1,0},{2,3},{3,2},{4,5},{5,4},{6,7},{7,6},{8,9},{9,8},{10,11... | collective-permute-start | bytes 2064392 | tf_op jit(solution)/shard_map/ppermute | solution.py:42
  21.6 25.0 %collective-permute-start.4 = (bf16[2,224,768]{2,1,0:T(8,128)(2,1)S(1)}, bf16[2,224,768]{2,1,0:T(8,128)(2,1)S(1)}, u32[]{:S(2)}, u32[]{:S(2)}) collective-permute-start(bf16[2,224,768]{2,1,0:T(8,128)(2,1)S(1)} %collective-permute-done.2.near), channel_id=1, source_target_pairs={{0,8},{8,0},{16,24},{24,16},{1,9},{9,1},{17,25},{25,17},{2,10},{10... | collective-permute-start | bytes 2064392 | tf_op jit(solution)/shard_map/ppermute | solution.py:56
  35.7 14.4 %collective-permute-start.6 = (bf16[2,224,768]{2,1,0:T(8,128)(2,1)S(1)}, bf16[2,224,768]{2,1,0:T(8,128)(2,1)S(1)}, u32[]{:S(2)}, u32[]{:S(2)}) collective-permute-start(bf16[2,224,768]{2,1,0:T(8,128)(2,1)S(1)} %collective-permute-done.2.near), channel_id=1, source_target_pairs={{0,0},{8,16},{16,8},{24,24},{1,1},{9,17},{17,9},{25,25},{2,2},{10,... | collective-permute-start | bytes 2064392 | tf_op jit(solution)/shard_map/ppermute | solution.py:55
  41.1 18.3 %collective-permute-start.9 = (bf16[2,224,768]{2,1,0:T(8,128)(2,1)}, bf16[2,224,768]{2,1,0:T(8,128)(2,1)}, u32[]{:S(2)}, u32[]{:S(2)}) collective-permute-start(bf16[2,224,768]{2,1,0:T(8,128)(2,1)} %collective-permute-done.8.near), channel_id=1, source_target_pairs={{0,2},{2,4},{3,1},{4,6},{5,3},{7,5},{8,10},{10,12},{11,9},{12,14},... | collective-permute-start | bytes 2064392 | tf_op jit(solution)/shard_map/ppermute | solution.py:46
  44.3 15.1 %collective-permute-start.5 = (bf16[2,224,768]{2,1,0:T(8,128)(2,1)S(1)}, bf16[2,224,768]{2,1,0:T(8,128)(2,1)S(1)}, u32[]{:S(2)}, u32[]{:S(2)}) collective-permute-start(bf16[2,224,768]{2,1,0:T(8,128)(2,1)S(1)} %collective-permute-done.3.far), channel_id=1, source_target_pairs={{0,8},{8,0},{16,24},{24,16},{1,9},{9,1},{17,25},{25,17},{2,10},{10... | collective-permute-start | bytes 2064392 | tf_op jit(solution)/shard_map/ppermute | solution.py:56
  44.4 28.6 %copy-start = (bf16[4,224,768]{2,1,0:T(8,128)(2,1)}, bf16[4,224,768]{2,1,0:T(8,128)(2,1)S(1)}, u32[]{:S(2)}) copy-start(bf16[4,224,768]{2,1,0:T(8,128)(2,1)S(1)} %collective-permute-done.1.pair_t) | copy-start | bytes 4128772
  44.4 16.9 %collective-permute-start.7 = (bf16[2,224,768]{2,1,0:T(8,128)(2,1)S(1)}, bf16[2,224,768]{2,1,0:T(8,128)(2,1)S(1)}, u32[]{:S(2)}, u32[]{:S(2)}) collective-permute-start(bf16[2,224,768]{2,1,0:T(8,128)(2,1)S(1)} %collective-permute-done.3.far), channel_id=1, source_target_pairs={{0,0},{8,16},{16,8},{24,24},{1,1},{9,17},{17,9},{25,25},{2,2},{10,... | collective-permute-start | bytes 2064392 | tf_op jit(solution)/shard_map/ppermute | solution.py:55
  46.6 48.5 %collective-permute-start.10 = (bf16[2,224,768]{2,1,0:T(8,128)(2,1)}, bf16[2,224,768]{2,1,0:T(8,128)(2,1)}, u32[]{:S(2)}, u32[]{:S(2)}) collective-permute-start(bf16[2,224,768]{2,1,0:T(8,128)(2,1)} %collective-permute-done.8.near), channel_id=1, source_target_pairs={{0,8},{8,0},{16,24},{24,16},{1,9},{9,1},{17,25},{25,17},{2,10},{10... | collective-permute-start | bytes 2064392 | tf_op jit(solution)/shard_map/ppermute | solution.py:56
  50.1 45.0 %collective-permute-start.12 = (bf16[2,224,768]{2,1,0:T(8,128)(2,1)}, bf16[2,224,768]{2,1,0:T(8,128)(2,1)}, u32[]{:S(2)}, u32[]{:S(2)}) collective-permute-start(bf16[2,224,768]{2,1,0:T(8,128)(2,1)} %collective-permute-done.8.near), channel_id=1, source_target_pairs={{0,0},{8,16},{16,8},{24,24},{1,1},{9,17},{17,9},{25,25},{2,2},{10,... | collective-permute-start | bytes 2064392 | tf_op jit(solution)/shard_map/ppermute | solution.py:55
  59.3 35.8 %collective-permute-start.11 = (bf16[2,224,768]{2,1,0:T(8,128)(2,1)}, bf16[2,224,768]{2,1,0:T(8,128)(2,1)}, u32[]{:S(2)}, u32[]{:S(2)}) collective-permute-start(bf16[2,224,768]{2,1,0:T(8,128)(2,1)} %collective-permute-done.9.far), channel_id=1, source_target_pairs={{0,8},{8,0},{16,24},{24,16},{1,9},{9,1},{17,25},{25,17},{2,10},{10... | collective-permute-start | bytes 2064392 | tf_op jit(solution)/shard_map/ppermute | solution.py:56
  59.3 35.8 %collective-permute-start.13 = (bf16[2,224,768]{2,1,0:T(8,128)(2,1)}, bf16[2,224,768]{2,1,0:T(8,128)(2,1)}, u32[]{:S(2)}, u32[]{:S(2)}) collective-permute-start(bf16[2,224,768]{2,1,0:T(8,128)(2,1)} %collective-permute-done.9.far), channel_id=1, source_target_pairs={{0,0},{8,16},{16,8},{24,24},{1,1},{9,17},{17,9},{25,25},{2,2},{10,... | collective-permute-start | bytes 2064392 | tf_op jit(solution)/shard_map/ppermute | solution.py:55
  73.0 2.6 %collective-permute-start.14 = (f32[16,224]{1,0:T(8,128)S(1)}, f32[16,224]{1,0:T(8,128)S(1)}, u32[]{:S(2)}, u32[]{:S(2)}) collective-permute-start(f32[16,224]{1,0:T(8,128)S(1)} %get-tuple-element.15), channel_id=1, source_target_pairs={{0,1},{1,0},{2,3},{3,2},{4,5},{5,4},{6,7},{7,6},{8,9},{9,8},{10,11... | collective-permute-start | bytes 43016 | tf_op jit(solution)/shard_map/ppermute | solution.py:42
  75.6 5.4 %collective-permute-start.15 = (f32[16,224]{1,0:T(8,128)S(1)}, f32[16,224]{1,0:T(8,128)S(1)}, u32[]{:S(2)}, u32[]{:S(2)}) collective-permute-start(f32[16,224]{1,0:T(8,128)S(1)} %get-tuple-element.15), channel_id=1, source_target_pairs={{0,0},{1,2},{2,1},{3,4},{4,3},{5,6},{6,5},{7,7},{8,8},{9,10},{10,9... | collective-permute-start | bytes 43016 | tf_op jit(solution)/shard_map/ppermute | solution.py:50
  81.0 8.5 %collective-permute-start.16 = (f32[16,672]{1,0:T(8,128)S(1)}, f32[16,672]{1,0:T(8,128)S(1)}, u32[]{:S(2)}, u32[]{:S(2)}) collective-permute-start(f32[16,672]{1,0:T(8,128)S(1)} %pad_maximum_fusion.3), channel_id=1, source_target_pairs={{0,8},{8,0},{16,24},{24,16},{1,9},{9,1},{17,25},{25,17},{2,10},{10... | collective-permute-start | bytes 129032 | tf_op jit(solution)/shard_map/ppermute | solution.py:56
  89.6 5.4 %collective-permute-start.17 = (f32[16,672]{1,0:T(8,128)S(1)}, f32[16,672]{1,0:T(8,128)S(1)}, u32[]{:S(2)}, u32[]{:S(2)}) collective-permute-start(f32[16,672]{1,0:T(8,128)S(1)} %pad_maximum_fusion.3), channel_id=1, source_target_pairs={{0,0},{8,16},{16,8},{24,24},{1,1},{9,17},{17,9},{25,25},{2,2},{10,... | collective-permute-start | bytes 129032 | tf_op jit(solution)/shard_map/ppermute | solution.py:55
  95.1 1.3 %copy-start.1 = (bf16[4,224,768]{2,1,0:T(8,128)(2,1)S(1)}, bf16[4,224,768]{2,1,0:T(8,128)(2,1)}, u32[]{:S(2)}) copy-start(bf16[4,224,768]{2,1,0:T(8,128)(2,1)} %copy-done) | copy-start | bytes 4128772

commit v3 on v2

v3 whole, which is shorter than its diff:
```python
import functools

import jax
import jax.numpy as jnp
from jax import lax
from jax.experimental import pallas as pl
from jax.experimental.pallas import tpu as pltpu
from jax.sharding import PartitionSpec as P

HEAD_DIM = 128
LOG2E = 1.4426950408889634
ROW_DELTA = 8
STAT_ROWS = 16
UNROLL = 2
FLOOR = -1e30


CONTRACT_LAST = (((1,), (1,)), ((), ()))


def flip_pairs(count):
    return [(i, i ^ 1) for i in range(count)]


def other_pairs(count):
    pairs = []
    for i in range(count):
        to = i + 1 if i % 2 else i - 1
        pairs.append((i, to if 0 <= to < count else i))
    return pairs


def relay_pairs(count):
    pairs = []
    for i in range(count):
        to = i - 2 if i % 2 else i + 2
        if 0 <= to < count:
            pairs.append((i, to))
    return pairs


def ha_near(x):
    return lax.ppermute(x, "ha", flip_pairs(lax.axis_size("ha")))


def ha_relay(near):
    return lax.ppermute(near, "ha", relay_pairs(lax.axis_size("ha")))


def ha_far(x):
    return lax.ppermute(x, "ha", other_pairs(lax.axis_size("ha")))


def ta_pair(x):
    return lax.ppermute(x, "ta", flip_pairs(lax.axis_size("ta")))


def ta_other(x):
    return lax.ppermute(x, "ta", other_pairs(lax.axis_size("ta")))


def offsets(index):
    sign = 1 - 2 * lax.rem(index, 2)
    return (0, sign, -sign)


def inside(index, count):
    return (index >= 0) & (index < count)


def halo_slab(tile, place_now, width):
    even_t, even_h, in_t, in_h = place_now
    tiles = [tile(slot).astype(jnp.float32) for slot in range(9)]

    def cell(slot, frame, row):
        start = (2 * frame + row) * width
        return tiles[slot][start : start + width]

    def side_h(slot_t, frame, R):
        if R in (1, 2):
            return cell(3 * slot_t, frame, R - 1)
        row = 1 if R == 0 else 0
        near, far = cell(3 * slot_t + 1, frame, row), cell(3 * slot_t + 2, frame, row)
        picked = jnp.where(even_h, far, near) if R == 0 else jnp.where(even_h, near, far)
        return jnp.where(in_h[0 if R == 0 else 1], picked, 0.0)

    slab = []
    for F in range(4):
        line = []
        for R in range(4):
            if F in (1, 2):
                line.append(side_h(0, F - 1, R))
                continue
            frame = 1 if F == 0 else 0
            first, second = side_h(1, frame, R), side_h(2, frame, R)
            picked = jnp.where(even_t, second, first) if F == 0 else jnp.where(even_t, first, second)
            line.append(jnp.where(in_t[0 if F == 0 else 1], picked, 0.0))
        slab.append(line)
    return slab


def depthwise(slab, weight, flipped, width):
    column = lax.broadcasted_iota(jnp.int32, (width, HEAD_DIM), 0)
    rows = []
    for f in range(2):
        for r in range(2):
            parts = []
            for dw in range(3):
                total = None
                for dt in range(3):
                    for dh in range(3):
                        tap = 9 * dt + 3 * dh + dw
                        tap = 26 - tap if flipped else tap
                        term = weight[tap : tap + 1] * slab[f + dt][r + dh]
                        total = term if total is None else total + term
                parts.append(total)
            before = jnp.where(column == 0, 0.0, pltpu.roll(parts[0], 1, 0))
            after_ = jnp.where(column == width - 1, 0.0, pltpu.roll(parts[2], width - 1, 0))
            rows.append(parts[1] + before + after_)
    return jnp.concatenate(rows, axis=0)


def place(counts):
    index_t, index_h = lax.axis_index("ta"), lax.axis_index("ha")
    even_t, even_h = lax.rem(index_t, 2) == 0, lax.rem(index_h, 2) == 0
    in_t = (index_t > 0, index_t < counts[0] - 1)
    in_h = (index_h > 0, index_h < counts[1] - 1)
    return index_t, index_h, (even_t, even_h, in_t, in_h)


def head_columns(head):
    return pl.ds(pl.multiple_of(head * HEAD_DIM, HEAD_DIM), HEAD_DIM)


def dot_last(x, y):
    return lax.dot_general(x, y, CONTRACT_LAST, preferred_element_type=jnp.float32)


def dot(x, y):
    return jnp.dot(x, y, preferred_element_type=jnp.float32)


def column_kernel(counts, width, column, last, mask_ref, clip_ref, query_ref, own, pair, other, *rest):
    slots = [own, pair, other]
    if last:
        grad_ref, sums, tops, totals = rest[0], (rest[1], rest[4]), (rest[2], rest[5]), (rest[3], rest[6])
        exp_ref, att_ref, fac_own, fac_near, fac_far, delta_ref, stat_ref, bias, stat = rest[7:]
    else:
        exp_ref, sum_ref, top_ref, total_ref, bias = rest
    index_t, index_h, _ = place(counts)
    rows, channels = query_ref.shape
    heads = channels // HEAD_DIM
    scale = HEAD_DIM**-0.5
    lane = lax.broadcasted_iota(jnp.int32, (1, 3 * rows), 1)
    limit = jnp.zeros((1, 3 * rows), jnp.int32)
    for slot in range(3):
        a, b = offsets(index_t)[slot], offsets(index_h)[column]
        t, h = index_t + a, index_h + b
        kept = (mask_ref[index_t, index_h, 3 * (a + 1) + (b + 1)] == 1) & inside(t, counts[0]) & inside(h, counts[1])
        safe = jnp.clip(t, 0, counts[0] - 1)
        for f in range(2):
            live = jnp.where(kept, clip_ref[2 * safe + f], 0)
            limit = jnp.where(lane >= slot * rows + f * (rows // 2), live, limit)
    bias[...] = jnp.where(lax.rem(lane, width) < limit, 0.0, -jnp.inf)
    which = lax.broadcasted_iota(jnp.int32, (rows, HEAD_DIM), 1)

    def body(step, _):
        hs = [step * UNROLL + u for u in range(UNROLL)]
        for h in hs:
            cols = head_columns(h)
            keys = jnp.concatenate([ref[0, :, cols] for ref in slots], axis=0)
            values = jnp.concatenate([ref[1, :, cols] for ref in slots], axis=0)
            s = dot_last(query_ref[:, cols], keys) * (scale * LOG2E) + bias[...]
            top = jnp.maximum(jnp.max(s, axis=1, keepdims=True), FLOOR)
            e = jnp.exp2(s - top)
            total = jnp.sum(e, axis=1, keepdims=True)
            e = e.astype(jnp.bfloat16)
            exp_ref[h] = e
            acc = dot(e, values)
            top = jnp.broadcast_to(top, (rows, HEAD_DIM))
            total = jnp.broadcast_to(total, (rows, HEAD_DIM))
            if not last:
                sum_ref[:, cols], top_ref[:, cols], total_ref[:, cols] = acc, top, total
                continue
            near_top, own_top = tops[1][:, cols], tops[0][:, cols]
            row_max = jnp.maximum(jnp.maximum(own_top, near_top), top)
            row_total = total * jnp.exp2(top - row_max) + totals[0][:, cols] * jnp.exp2(own_top - row_max)
            row_total = row_total + totals[1][:, cols] * jnp.exp2(near_top - row_max)
            log_total = row_max + jnp.log2(row_total)
            factors = [jnp.exp2(x - log_total) for x in (own_top, near_top, top)]
            for ref, factor in zip((fac_own, fac_near, fac_far), factors):
                ref[:, cols] = factor
            attention = sums[0][:, cols] * factors[0] + sums[1][:, cols] * factors[1] + acc * factors[2]
            att_ref[:, cols] = attention
            delta = jnp.sum(grad_ref[:, cols].astype(jnp.float32) * attention, axis=1, keepdims=True)
            delta = jnp.broadcast_to(delta, (rows, HEAD_DIM))
            delta_ref[:, cols] = delta
            marked = jnp.where(which == h, log_total, stat[...])
            stat[...] = jnp.where(which == h + ROW_DELTA, delta, marked)
        return 0

    if last:
        stat[...] = jnp.zeros_like(stat)
    lax.fori_loop(0, heads // UNROLL, body, 0)
    if last:
        pad = jnp.zeros((-rows % HEAD_DIM, HEAD_DIM), jnp.float32)
        turned = jnp.concatenate([stat[...], pad], axis=0).T
        stat_ref[...] = turned[:STAT_ROWS, :rows]


def query_kernel(counts, width, grad_ref, weight_ref, *rest):
    slots, exps, factors = rest[:9], rest[9:12], rest[12:15]
    att_ref, delta_ref, _, out_ref, dq_ref, done_ref = rest[15:]
    done_ref[...] = jnp.zeros_like(done_ref)
    _, _, place_now = place(counts)
    rows, channels = grad_ref.shape
    heads = channels // HEAD_DIM
    scale = HEAD_DIM**-0.5
    wide = -(-3 * rows // HEAD_DIM)

    def body(step, _):
        for u in range(UNROLL):
            h = step * UNROLL + u
            cols = head_columns(h)
            grad = grad_ref[:, cols]
            delta = jnp.concatenate([delta_ref[:, cols]] * wide, axis=1)[:, : 3 * rows]
            dq = None
            for column in range(3):
                refs = slots[column::3]
                values = jnp.concatenate([ref[1, :, cols] for ref in refs], axis=0)
                keys = jnp.concatenate([ref[0, :, cols] for ref in refs], axis=0)
                ds = exps[column][h].astype(jnp.float32) * (dot_last(grad, values) - delta)
                part = dot(ds.astype(jnp.bfloat16), keys) * (factors[column][:, cols] * scale)
                dq = part if dq is None else dq + part
            dq_ref[:, cols] = dq.astype(jnp.bfloat16)
            slab = halo_slab(lambda slot: slots[slot][1, :, cols], place_now, width)
            conv = depthwise(slab, weight_ref[:, cols].astype(jnp.float32), False, width)
            out_ref[:, cols] = (att_ref[:, cols] + conv).astype(jnp.bfloat16)
        return 0

    lax.fori_loop(0, heads // UNROLL, body, 0)


def key_kernel(counts, width, columns, last, mask_ref, clip_ref, own, stat_own, stat_pair, stat_other, *rest):
    count = 3 * len(columns)
    slots, rest = rest[:count], rest[count:]
    if last:
        weight_ref, *edges, dk_sum, dv_sum, dk_ref, dv_ref, stats = rest
    else:
        dk_ref, dv_ref, stats = rest
    index_t, index_h, place_now = place(counts)
    rows, channels = own.shape[1:]
    heads = channels // HEAD_DIM
    scale = HEAD_DIM**-0.5
    line = lax.broadcasted_iota(jnp.int32, (STAT_ROWS, rows), 0)
    pieces = []
    for column in columns:
        for slot, ref in enumerate((stat_own, stat_pair, stat_other)):
            a, b = offsets(index_t)[slot], offsets(index_h)[column]
            t, h = index_t + a, index_h + b
            safe_t, safe_h = jnp.clip(t, 0, counts[0] - 1), jnp.clip(h, 0, counts[1] - 1)
            kept = (mask_ref[safe_t, safe_h, 3 * (1 - a) + (1 - b)] == 1) & inside(t, counts[0]) & inside(h, counts[1])
            pieces.append(jnp.where(kept | (line >= ROW_DELTA), ref[column], jnp.inf))
    stats[...] = jnp.concatenate(pieces, axis=1)
    row = lax.broadcasted_iota(jnp.int32, (rows, HEAD_DIM), 0)
    lens = [clip_ref[2 * index_t + f] for f in range(2)]
    live = lax.rem(row, width) < jnp.where(row < 2 * width, lens[0], lens[1])

    def body(step, _):
        for u in range(UNROLL):
            head = step * UNROLL + u
            cols = head_columns(head)
            queries = jnp.concatenate([ref[0, :, cols] for ref in slots], axis=0)
            grads = jnp.concatenate([ref[1, :, cols] for ref in slots], axis=0)
            s = dot_last(own[0, :, cols], queries)
            p = jnp.exp2(s * (scale * LOG2E) - stats[pl.ds(head, 1), :])
            dp = dot_last(own[1, :, cols], grads)
            ds = (p * (dp - stats[pl.ds(head + ROW_DELTA, 1), :])).astype(jnp.bfloat16)
            dv = dot(p.astype(jnp.bfloat16), grads)
            dk = dot(ds, queries)
            if not last:
                dk_ref[:, cols], dv_ref[:, cols] = dk, dv
                continue
            dk = jnp.where(live, (dk + dk_sum[:, cols]) * scale, 0.0)
            dv = jnp.where(live, dv + dv_sum[:, cols], 0.0)
            dk_ref[:, cols] = dk.astype(jnp.bfloat16)
            around = [edges[0], edges[3], slots[0], edges[1], edges[4], slots[1], edges[2], edges[5], slots[2]]
            slab = halo_slab(lambda slot: around[slot][1, :, cols], place_now, width)
            conv = depthwise(slab, weight_ref[:, cols].astype(jnp.float32), True, width)
            dv_ref[:, cols] = (dv + conv).astype(jnp.bfloat16)
        return 0

    lax.fori_loop(0, heads // UNROLL, body, 0)


def cost(heads, rows, matmuls, columns):
    work = heads * rows * 3 * columns * rows * HEAD_DIM * 2 * matmuls
    moved = heads * rows * HEAD_DIM * 2 * 8 * columns
    return pl.CostEstimate(flops=work, bytes_accessed=moved, transcendentals=heads * rows * rows * 3 * columns)


def shards(query_states, key_states, value_states, conv_weight, out_grad, tile_mask, clip_lengths):
    width, channels = query_states.shape[2:]
    rows = query_states.shape[0] * query_states.shape[1] * width
    counts = (lax.axis_size("ta"), lax.axis_size("ha"))
    heads = channels // HEAD_DIM
    query, key, value, grad = [x.reshape(rows, channels) for x in (query_states, key_states, value_states, out_grad)]

    smem = pl.BlockSpec(memory_space=pltpu.SMEM)
    vmem = pl.BlockSpec(memory_space=pltpu.VMEM)
    params = pltpu.CompilerParams(vmem_limit_bytes=16 * 1024 * 1024)
    half = jax.ShapeDtypeStruct((rows, channels), jnp.bfloat16)
    full = jax.ShapeDtypeStruct((rows, channels), jnp.float32)
    exps = jax.ShapeDtypeStruct((heads, rows, 3 * rows), jnp.bfloat16)
    bias = pltpu.VMEM((1, 3 * rows), jnp.float32)

    def call(kernel, name, out_shape, scratch, work, *args):
        scalars = 2 if args[0] is tile_mask else 0
        return pl.pallas_call(
            kernel,
            in_specs=[smem] * scalars + [vmem] * (len(args) - scalars),
            out_specs=[vmem] * len(out_shape),
            out_shape=out_shape,
            scratch_shapes=scratch,
            compiler_params=params,
            cost_estimate=work,
            name=name,
        )(*args)

    def scores(column, tiles):
        kernel = functools.partial(column_kernel, counts, width, column, False)
        work = cost(heads, rows, 2, 1)
        return call(kernel, f"scores_{column}", [exps, full, full, full], [bias], work, tile_mask, clip_lengths, query, *tiles)

    def pair_up(x, y, *earlier):
        def kernel(x_ref, y_ref, *rest):
            rest[-1][0] = x_ref[...]
            rest[-1][1] = y_ref[...]

        return pl.pallas_call(
            kernel,
            in_specs=[vmem] * 2 + [pl.BlockSpec(memory_space=pl.ANY)] * len(earlier),
            out_specs=vmem,
            out_shape=jax.ShapeDtypeStruct((2,) + x.shape, x.dtype),
            name="pair_up",
        )(x, y, *earlier)

    def gate(x, *earlier):
        return pl.pallas_call(
            lambda *refs: None,
            in_specs=[pl.BlockSpec(memory_space=pl.ANY)] * (1 + len(earlier)),
            out_specs=pl.BlockSpec(memory_space=pl.ANY),
            out_shape=jax.ShapeDtypeStruct(x.shape, x.dtype),
            input_output_aliases={0: 0},
            name="gate",
        )(x, *earlier)

    near_k = ha_near(key)
    near_v = ha_near(gate(value, near_k))
    kv = pair_up(key, value)
    kv_b = ta_other(kv)
    far_k = ha_relay(near_k)
    kv_a = ta_pair(kv)
    qg = pair_up(query, grad, kv_a)
    qg_a, qg_b = ta_pair(qg), ta_other(qg)
    exp_own, *own_parts = scores(0, (kv, kv_a, kv_b))

    near_v = gate(near_v, own_parts[0])
    far_v = ha_relay(near_v)
    near_kv = pair_up(near_k, near_v, qg_a, qg_b)
    near_kv_a, near_kv_b = ta_pair(near_kv), ta_other(near_kv)
    near_qg = ha_near(pair_up(query, grad, near_v))
    far_kv = jnp.stack([far_k, far_v])
    far_kv_a, far_kv_b = ta_pair(far_kv), ta_other(far_kv)
    exp_near, *near_parts = scores(1, (near_kv, near_kv_a, near_kv_b))

    near_qg = gate(near_qg, near_parts[0])
    far_qg = ha_relay(near_qg)
    near_qg_a, near_qg_b = ta_pair(near_qg), ta_other(near_qg)
    exp_far, attention, fac_own, fac_near, fac_far, delta, stat = call(
        functools.partial(column_kernel, counts, width, 2, True),
        "scores_2",
        [exps] + [full] * 5 + [jax.ShapeDtypeStruct((STAT_ROWS, rows), jnp.float32)],
        [bias, pltpu.VMEM((rows, HEAD_DIM), jnp.float32)],
        cost(heads, rows, 2, 1),
        tile_mask, clip_lengths, query, far_kv, far_kv_a, far_kv_b, grad, *own_parts, *near_parts,
    )
    column = jnp.stack([stat, ha_near(stat), ha_far(stat)])
    column_a, column_b = ta_pair(column), ta_other(column)
    layer_out, query_grad, done = call(
        functools.partial(query_kernel, counts, width),
        "query_side",
        [half, half, jax.ShapeDtypeStruct((8, HEAD_DIM), jnp.float32)],
        [],
        cost(heads, rows, 2, 3),
        grad, conv_weight, kv, near_kv, far_kv, kv_a, near_kv_a, far_kv_a, kv_b, near_kv_b, far_kv_b,
        exp_own, exp_near, exp_far, fac_own, fac_near, fac_far, attention, delta, column,
    )
    far_qg = gate(far_qg, done, column_a, column_b)
    far_qg_a, far_qg_b = ta_pair(far_qg), ta_other(far_qg)

    first = (qg, qg_a, qg_b, near_qg, near_qg_a, near_qg_b)
    dk_sum, dv_sum = call(
        functools.partial(key_kernel, counts, width, (0, 1), False),
        "key_side_0",
        [full, full],
        [pltpu.VMEM((STAT_ROWS, 6 * rows), jnp.float32)],
        cost(heads, rows, 4, 2),
        tile_mask, clip_lengths, kv, column, column_a, column_b, *first,
    )
    key_grad, value_grad = call(
        functools.partial(key_kernel, counts, width, (2,), True),
        "key_side_1",
        [half, half],
        [pltpu.VMEM((STAT_ROWS, 3 * rows), jnp.float32)],
        cost(heads, rows, 4, 1),
        tile_mask, clip_lengths, kv, column, column_a, column_b, far_qg, far_qg_a, far_qg_b, conv_weight, *first, dk_sum, dv_sum,
    )
    return tuple(x.reshape(query_states.shape) for x in (layer_out, query_grad, key_grad, value_grad))


def solution(mesh):
    placed = P("ta", "ha", None, None)
    return jax.shard_map(
        shards,
        mesh=mesh,
        in_specs=(placed, placed, placed, P(), placed, P(), P()),
        out_specs=(placed,) * 4,
        check_vma=False,
    )
```

time: 109 us -> 126 us (1.16)
  the two profiles are of different devices: /device:TPU:9 before, /device:TPU:1 now
where the time goes in v3:
time: 126 us; the launch traced here: 124 us
  starting transfers between devices  49 us (39%)
  Pallas kernels  43.5 us (35%)
  local copies, waits for them, and re-layouts  27.6 us (22%)
  waiting for transfers between devices  1.9 us (2%)
    pallas_call x6, Pallas kernels, call(): pl.pallas_call(kernel, in_specs=[smem] * scalars + [vmem] * (len(args) -...  35.6 us
    unnamed x85, local copies, waits for them, and re-layouts  27.6 us
    ppermute x7, starting transfers between devices, ta_other(): return lax.ppermute(x, 'ta', other_pairs(lax.axis_size('ta')))  22.1 us
    ppermute x7, starting transfers between devices, ta_pair(): return lax.ppermute(x, 'ta', flip_pairs(lax.axis_size('ta')))  11.1 us
    ppermute x3, starting transfers between devices, ha_relay(): return lax.ppermute(near, 'ha', relay_pairs(lax.axis_size('ha')))  9.69 us
    pallas_call x4, Pallas kernels, pair_up(): pl.pallas_call(kernel, in_specs=[vmem] * 2 + [pl.BlockSpec(memory_space=p...  7.98 us
    ppermute x4, starting transfers between devices, ha_near(): return lax.ppermute(x, 'ha', flip_pairs(lax.axis_size('ha')))  5.49 us
  transfers between devices with their start and end apart: 22, of which 1 were waited for; matrix products, arithmetic and copies ran while one was open for 1% of the time, Pallas kernels for 28%

profile of v3, /device:TPU:1, one launch (start us, length us, event | category | flops | bytes accessed | tf_op | source)
XLA Modules:
  0.0 124.2 jit_solution(18436192262619859645)
XLA Ops:
  0.6 1.7 %copy.20 = bf16[2,2,56,768]{3,2,1,0:T(8,128)(2,1)} copy(bf16[2,2,56,768]{3,2,1,0:T(8,128)(2,1)} %param.9) | data formatting | bytes 688128
  2.4 2.0 %pair_up.4.own.rest_0_ = bf16[2,224,768]{2,1,0:T(8,128)(2,1)} custom-call(bf16[224,768]{1,0:T(8,128)(2,1)} %bitcast.1.x_ref, bf16[224,768]{1,0:T(8,128)(2,1)} %bitcast.23), custom_call_target="tpu_custom_call" | custom-call | tf_op jit(solution)/shard_map/pair_up/pallas_call | solution.py:340
  4.4 0.1 collective-permute-start.2
  4.5 4.6 %collective-permute-start.3 = (bf16[2,224,768]{2,1,0:T(8,128)(2,1)}, bf16[2,224,768]{2,1,0:T(8,128)(2,1)S(1)}, u32[]{:S(2)}, u32[]{:S(2)}) collective-permute-start(bf16[2,224,768]{2,1,0:T(8,128)(2,1)} %pair_up.4.own.rest_0_), channel_id=1, source_target_pairs={{0,0},{8,16},{16,8},{24,24},{1,1},{9,17},{17,9},{25,25},{2,2},{10,... | collective-permute-start | bytes 2064392 | tf_op jit(solution)/shard_map/ppermute | solution.py:59
  9.1 1.3 %collective-permute-start = (bf16[224,768]{1,0:T(8,128)(2,1)}, bf16[224,768]{1,0:T(8,128)(2,1)S(1)}, u32[]{:S(2)}, u32[]{:S(2)}) collective-permute-start(bf16[224,768]{1,0:T(8,128)(2,1)} %bitcast.1.x_ref), channel_id=1, source_target_pairs={{0,1},{1,0},{2,3},{3,2},{4,5},{5,4},{6,7},{7,6},{8,9},{9,8},{10,11... | collective-permute-start | bytes 1032200 | tf_op jit(solution)/shard_map/ppermute | solution.py:43
  10.4 0.8 copy-done.3
  11.2 2.0 %pair_up.5.rest_0_.rest_4_ = bf16[2,224,768]{2,1,0:T(8,128)(2,1)} custom-call(bf16[224,768]{1,0:T(8,128)(2,1)} %bitcast.13, bf16[224,768]{1,0:T(8,128)(2,1)} %bitcast.18, bf16[2,224,768]{2,1,0:T(8,128)(2,1)} %copy-done.3), custom_call_target="tpu_custom_call" | custom-call | tf_op jit(solution)/shard_map/pair_up/pallas_call | solution.py:340
  13.2 2.7 %collective-permute-start.5 = (bf16[2,224,768]{2,1,0:T(8,128)(2,1)}, bf16[2,224,768]{2,1,0:T(8,128)(2,1)S(1)}, u32[]{:S(2)}, u32[]{:S(2)}) collective-permute-start(bf16[2,224,768]{2,1,0:T(8,128)(2,1)} %pair_up.5.rest_0_.rest_4_), channel_id=1, source_target_pairs={{0,0},{8,16},{16,8},{24,24},{1,1},{9,17},{17,9},{25,25},{2,2},{10,... | collective-permute-start | bytes 2064392 | tf_op jit(solution)/shard_map/ppermute | solution.py:59
  15.9 1.8 %collective-permute-done.refs_1_.x_ref = bf16[224,768]{1,0:T(8,128)(2,1)S(1)} collective-permute-done((bf16[224,768]{1,0:T(8,128)(2,1)}, bf16[224,768]{1,0:T(8,128)(2,1)S(1)}, u32[]{:S(2)}, u32[]{:S(2)}) %collective-permute-start) | collective-permute-done | bytes 344096 | tf_op jit(solution)/shard_map/ppermute | solution.py:43
  17.7 0.7 copy-done.41
  18.4 1.7 %collective-permute-start.1 = (bf16[224,768]{1,0:T(8,128)(2,1)}, bf16[224,768]{1,0:T(8,128)(2,1)S(1)}, u32[]{:S(2)}, u32[]{:S(2)}) collective-permute-start(bf16[224,768]{1,0:T(8,128)(2,1)} %gate.4), channel_id=1, source_target_pairs={{0,1},{1,0},{2,3},{3,2},{4,5},{5,4},{6,7},{7,6},{8,9},{9,8},{10,11... | collective-permute-start | bytes 1032200 | tf_op jit(solution)/shard_map/ppermute | solution.py:43
  20.2 3.9 %collective-permute-start.6 = (bf16[224,768]{1,0:T(8,128)(2,1)}, bf16[224,768]{1,0:T(8,128)(2,1)}, u32[]{:S(2)}, u32[]{:S(2)}) collective-permute-start(bf16[224,768]{1,0:T(8,128)(2,1)} %copy-done.41), channel_id=1, source_target_pairs={{0,2},{2,4},{3,1},{4,6},{5,3},{7,5},{8,10},{10,12},{11,9},{12,14},... | collective-permute-start | bytes 1032200 | tf_op jit(solution)/shard_map/ppermute | solution.py:47
  24.1 0.0 collective-permute-done.3.other.rest_6_
  24.2 1.1 copy-done.4
  25.3 3.8 %scores_0.1 = (bf16[6,224,672]{2,1,0:T(8,128)(2,1)S(1)}, f32[224,768]{1,0:T(8,128)S(1)}, f32[224,768]{1,0:T(8,128)S(1)}, f32[224,768]{1,0:T(8,128)S(1)}) custom-call(s32[4,8,9]{2,1,0:T(8,128)S(1)} %copy-done.32, s32[8]{0:T(128)S(1)} %copy-done.38, bf16[224,768]{1,0:T(8,128)(2,1)S(1)} %bitcast.15, bf16[2,224,768]{2,1,0:T(8,128)(2,1)S(1)} %copy-done, ...), custom_call_target="tpu_custom_call" | custom-call | flops 462422016 | bytes 2752512 | tf_op jit(solution)/shard_map/scores_0/pallas_call | solution.py:319
  29.1 0.8 copy-done.14
  29.9 1.3 %copy-done.20 = bf16[6,224,672]{2,1,0:T(8,128)(2,1)} copy-done((bf16[6,224,672]{2,1,0:T(8,128)(2,1)}, bf16[6,224,672]{2,1,0:T(8,128)(2,1)S(1)}, u32[]{:S(2)}) %copy-start.20) | copy-done | bytes 1806360
  31.3 0.9 copy-done.24
  32.1 0.9 copy-done.26
  33.0 0.0 collective-permute-done.1.refs_0_
  33.0 0.7 copy-done.40
  33.7 3.2 %collective-permute-start.7 = (bf16[224,768]{1,0:T(8,128)(2,1)}, bf16[224,768]{1,0:T(8,128)(2,1)}, u32[]{:S(2)}, u32[]{:S(2)}) collective-permute-start(bf16[224,768]{1,0:T(8,128)(2,1)} %gate.5.y_ref.rest_0_), channel_id=1, source_target_pairs={{0,2},{2,4},{3,1},{4,6},{5,3},{7,5},{8,10},{10,12},{11,9},{12,14},... | collective-permute-start | bytes 1032200 | tf_op jit(solution)/shard_map/ppermute | solution.py:47
  37.0 0.9 copy-done.10
  37.8 0.9 copy-done.12
  38.7 2.0 %pair_up.6.own.rest_1_ = bf16[2,224,768]{2,1,0:T(8,128)(2,1)} custom-call(bf16[224,768]{1,0:T(8,128)(2,1)} %copy-done.41, bf16[224,768]{1,0:T(8,128)(2,1)} %gate.5.y_ref.rest_0_, bf16[2,224,768]{2,1,0:T(8,128)(2,1)} %copy-done.10, bf16[2,224,768]{2,1,0:T(8,128)(2,1)} %copy-done.12), custom_call_target="tpu_custom_call" | custom-call | tf_op jit(solution)/shard_map/pair_up/pallas_call | solution.py:340
  40.7 0.6 collective-permute-start.8
  41.3 3.5 %collective-permute-start.10 = (bf16[2,224,768]{2,1,0:T(8,128)(2,1)}, bf16[2,224,768]{2,1,0:T(8,128)(2,1)}, u32[]{:S(2)}, u32[]{:S(2)}) collective-permute-start(bf16[2,224,768]{2,1,0:T(8,128)(2,1)} %pair_up.6.own.rest_1_), channel_id=1, source_target_pairs={{0,0},{8,16},{16,8},{24,24},{1,1},{9,17},{17,9},{25,25},{2,2},{10,... | collective-permute-start | bytes 2064392 | tf_op jit(solution)/shard_map/ppermute | solution.py:59
  44.8 2.0 %pair_up.7 = bf16[2,224,768]{2,1,0:T(8,128)(2,1)} custom-call(bf16[224,768]{1,0:T(8,128)(2,1)} %bitcast.14, bf16[224,768]{1,0:T(8,128)(2,1)} %bitcast.19, bf16[224,768]{1,0:T(8,128)(2,1)} %gate.5.y_ref.rest_0_), custom_call_target="tpu_custom_call" | custom-call | tf_op jit(solution)/shard_map/pair_up/pallas_call | solution.py:340
  46.8 1.1 pad_maximum_fusion.own.rest_2_
  47.9 0.0 copy-start.7
  47.9 3.5 %collective-permute-start.9 = (bf16[2,224,768]{2,1,0:T(8,128)(2,1)S(1)}, bf16[2,224,768]{2,1,0:T(8,128)(2,1)}, u32[]{:S(2)}, u32[]{:S(2)}) collective-permute-start(bf16[2,224,768]{2,1,0:T(8,128)(2,1)S(1)} %pad_maximum_fusion.own.rest_2_), channel_id=1, source_target_pairs={{0,8},{8,0},{16,24},{24,16},{1,9},{9,1},{17,25},{25,17},{2,10},{10... | collective-permute-start | bytes 2064392 | tf_op jit(solution)/shard_map/ppermute | solution.py:55
  51.4 3.7 %collective-permute-start.11 = (bf16[2,224,768]{2,1,0:T(8,128)(2,1)S(1)}, bf16[2,224,768]{2,1,0:T(8,128)(2,1)}, u32[]{:S(2)}, u32[]{:S(2)}) collective-permute-start(bf16[2,224,768]{2,1,0:T(8,128)(2,1)S(1)} %pad_maximum_fusion.own.rest_2_), channel_id=1, source_target_pairs={{0,0},{8,16},{16,8},{24,24},{1,1},{9,17},{17,9},{25,25},{2,2},{10,... | collective-permute-start | bytes 2064392 | tf_op jit(solution)/shard_map/ppermute | solution.py:59
  55.1 4.4 %scores_1.1 = (bf16[6,224,672]{2,1,0:T(8,128)(2,1)S(1)}, f32[224,768]{1,0:T(8,128)S(1)}, f32[224,768]{1,0:T(8,128)S(1)}, f32[224,768]{1,0:T(8,128)S(1)}) custom-call(s32[4,8,9]{2,1,0:T(8,128)S(1)} %copy-done.32, s32[8]{0:T(128)S(1)} %copy-done.38, bf16[224,768]{1,0:T(8,128)(2,1)S(1)} %bitcast.16, bf16[2,224,768]{2,1,0:T(8,128)(2,1)S(1)} %copy-done.6, ...), custom_call_target="tpu_custom_call" | custom-call | flops 462422016 | bytes 2752512 | tf_op jit(solution)/shard_map/scores_1/pallas_call | solution.py:319
  59.5 0.8 copy-done.18
  60.3 1.3 %copy-done.22 = bf16[6,224,672]{2,1,0:T(8,128)(2,1)} copy-done((bf16[6,224,672]{2,1,0:T(8,128)(2,1)}, bf16[6,224,672]{2,1,0:T(8,128)(2,1)S(1)}, u32[]{:S(2)}) %copy-start.22) | copy-done | bytes 1806360
  61.7 0.8 copy-done.28
  62.5 0.8 copy-done.30
  63.4 2.5 %collective-permute-start.17 = (bf16[2,224,768]{2,1,0:T(8,128)(2,1)}, bf16[2,224,768]{2,1,0:T(8,128)(2,1)S(1)}, u32[]{:S(2)}, u32[]{:S(2)}) collective-permute-start(bf16[2,224,768]{2,1,0:T(8,128)(2,1)} %gate.6.rest_3_.rest_7_), channel_id=1, source_target_pairs={{0,2},{2,4},{3,1},{4,6},{5,3},{7,5},{8,10},{10,12},{11,9},{12,14},... | collective-permute-start | bytes 2064392 | tf_op jit(solution)/shard_map/ppermute | solution.py:47
  65.9 1.1 copy-done.15
  67.0 1.1 copy-done.19
  68.1 1.1 copy-done.25
  69.2 1.1 copy-done.27
  70.3 1.1 copy-done.29
  71.4 1.1 copy-done.31
  72.5 5.2 %scores_2.1 = (bf16[6,224,672]{2,1,0:T(8,128)(2,1)S(1)}, f32[224,768]{1,0:T(8,128)S(1)}, f32[224,768]{1,0:T(8,128)S(1)}, f32[224,768]{1,0:T(8,128)S(1)}, f32[224...) custom-call(s32[4,8,9]{2,1,0:T(8,128)S(1)} %copy-done.32, s32[8]{0:T(128)S(1)} %copy-done.38, ...), custom_call_target="tpu_custom_call" | custom-call | flops 462422016 | bytes 2752512 | tf_op jit(solution)/shard_map/scores_2/pallas_call | solution.py:319
  77.7 0.7 collective-permute-start.13
  78.4 2.5 %collective-permute-start.12 = (f32[16,224]{1,0:T(8,128)S(1)}, f32[16,224]{1,0:T(8,128)S(1)}, u32[]{:S(2)}, u32[]{:S(2)}) collective-permute-start(f32[16,224]{1,0:T(8,128)S(1)} %get-tuple-element.40), channel_id=1, source_target_pairs={{0,1},{1,0},{2,3},{3,2},{4,5},{5,4},{6,7},{7,6},{8,9},{9,8},{10,11... | collective-permute-start | bytes 43016 | tf_op jit(solution)/shard_map/ppermute | solution.py:43
  80.9 2.1 %collective-permute-start.20 = (bf16[2,224,768]{2,1,0:T(8,128)(2,1)}, bf16[2,224,768]{2,1,0:T(8,128)(2,1)}, u32[]{:S(2)}, u32[]{:S(2)}) collective-permute-start(bf16[2,224,768]{2,1,0:T(8,128)(2,1)} %gate.6.rest_3_.rest_7_), channel_id=1, source_target_pairs={{0,8},{8,0},{16,24},{24,16},{1,9},{9,1},{17,25},{25,17},{2,10},{10... | collective-permute-start | bytes 2064392 | tf_op jit(solution)/shard_map/ppermute | solution.py:55
  83.0 2.1 %collective-permute-start.21 = (bf16[2,224,768]{2,1,0:T(8,128)(2,1)}, bf16[2,224,768]{2,1,0:T(8,128)(2,1)}, u32[]{:S(2)}, u32[]{:S(2)}) collective-permute-start(bf16[2,224,768]{2,1,0:T(8,128)(2,1)} %gate.6.rest_3_.rest_7_), channel_id=1, source_target_pairs={{0,0},{8,16},{16,8},{24,24},{1,1},{9,17},{17,9},{25,25},{2,2},{10,... | collective-permute-start | bytes 2064392 | tf_op jit(solution)/shard_map/ppermute | solution.py:59
  85.1 4.7 %collective-permute-start.14 = (f32[3,16,224]{2,1,0:T(8,128)S(1)}, f32[3,16,224]{2,1,0:T(8,128)S(1)}, u32[]{:S(2)}, u32[]{:S(2)}) collective-permute-start(f32[3,16,224]{2,1,0:T(8,128)S(1)} %pad_maximum_fusion.1.rest_17_.stat_own), channel_id=1, source_target_pairs={{0,8},{8,0},{16,24},{24,16},{1,9},{9,1},{17,25},{25,17},{2,10},{10... | collective-permute-start | bytes 129032 | tf_op jit(solution)/shard_map/ppermute | solution.py:55
  89.8 2.1 %collective-permute-start.15 = (f32[3,16,224]{2,1,0:T(8,128)S(1)}, f32[3,16,224]{2,1,0:T(8,128)S(1)}, u32[]{:S(2)}, u32[]{:S(2)}) collective-permute-start(f32[3,16,224]{2,1,0:T(8,128)S(1)} %pad_maximum_fusion.1.rest_17_.stat_own), channel_id=1, source_target_pairs={{0,0},{8,16},{16,8},{24,24},{1,1},{9,17},{17,9},{25,25},{2,2},{10,... | collective-permute-start | bytes 129032 | tf_op jit(solution)/shard_map/ppermute | solution.py:59
  91.9 8.7 %query_side.1 = (bf16[224,768]{1,0:T(8,128)(2,1)}, bf16[224,768]{1,0:T(8,128)(2,1)}, f32[8,128]{1,0:T(8,128)S(1)}) custom-call(bf16[224,768]{1,0:T(8,128)(2,1)S(1)} %bitcast.21, bf16[27,768]{1,0:T(8,128)(2,1)S(1)} %copy-done.33, bf16[2,224,768]{2,1,0:T(8,128)(2,1)S(1)} %copy-done, bf16[2,224,768]{2,1,0:T(8,128)(2,1)S(1)} %copy-done.6, ...), custom_call_target="tpu_custom_call" | custom-call | flops 1387266048 | bytes 8257536 | tf_op jit(solution)/shard_map/query_side/pallas_call | solution.py:319
  100.6 0.6 copy-done.39
  101.2 0.0 copy-start.36
  101.2 0.8 copy-done.16
  102.1 0.1 collective-permute-start.18
  102.1 3.6 %collective-permute-start.19 = (bf16[2,224,768]{2,1,0:T(8,128)(2,1)}, bf16[2,224,768]{2,1,0:T(8,128)(2,1)S(1)}, u32[]{:S(2)}, u32[]{:S(2)}) collective-permute-start(bf16[2,224,768]{2,1,0:T(8,128)(2,1)} %gate.7.rest_0_), channel_id=1, source_target_pairs={{0,0},{8,16},{16,8},{24,24},{1,1},{9,17},{17,9},{25,25},{2,2},{10,... | collective-permute-start | bytes 2064392 | tf_op jit(solution)/shard_map/ppermute | solution.py:59
  105.8 1.1 copy-done.8
  106.9 1.1 copy-done.11
  108.0 1.1 copy-done.13
  109.1 0.8 copy-done.35
  109.9 0.8 copy-done.37
  110.7 6.5 %key_side_0.1 = (f32[224,768]{1,0:T(8,128)S(1)}, f32[224,768]{1,0:T(8,128)S(1)}) custom-call(s32[4,8,9]{2,1,0:T(8,128)S(1)} %copy-done.32, s32[8]{0:T(128)S(1)} %copy-done.38, bf16[2,224,768]{2,1,0:T(8,128)(2,1)S(1)} %copy-done, f32[3,16,224]{2,1,0:T(8,128)S(1)} %pad_maximum_fusion.1.rest_17_.stat_own, f32[3,16,224]{2,1,0:T(8,128)S(1)} %copy-done.35, ...), custom_call_target="tpu_custom_call" | custom-call | flops 1849688064 | bytes 5505024 | tf_op jit(solution)/shard_map/key_side_0/pallas_call | solution.py:319
  117.3 7.0 %key_side_1.1 = (bf16[224,768]{1,0:T(8,128)(2,1)}, bf16[224,768]{1,0:T(8,128)(2,1)}) custom-call(s32[4,8,9]{2,1,0:T(8,128)S(1)} %copy-done.32, s32[8]{0:T(128)S(1)} %copy-done.38, bf16[2,224,768]{2,1,0:T(8,128)(2,1)S(1)} %copy-done, f32[3,16,224]{2,1,0:T(8,128)S(1)} %pad_maximum_fusion.1.rest_17_.stat_own, f32[3,16,224]{2,1,0:T(8,128)S(1)} %copy-done.35, ...), custom_call_target="tpu_custom_call" | custom-call | flops 924844032 | bytes 2752512 | tf_op jit(solution)/shard_map/key_side_1/pallas_call | solution.py:319
  (81 shorter events, 0.2 us)
Async XLA Ops:
  2.4 21.8 %copy-start.1 = (bf16[2,2,56,768]{3,2,1,0:T(8,128)(2,1)S(1)}, bf16[2,2,56,768]{3,2,1,0:T(8,128)(2,1)}, u32[]{:S(2)}) copy-start(bf16[2,2,56,768]{3,2,1,0:T(8,128)(2,1)} %param.7) | copy-start | bytes 1032196
  2.4 21.8 %copy-start.32 = (s32[4,8,9]{2,1,0:T(8,128)S(1)}, s32[4,8,9]{2,1,0:T(8,128)}, u32[]{:S(2)}) copy-start(s32[4,8,9]{2,1,0:T(8,128)} %mask_ref.9) | copy-start | bytes 3460
  2.4 21.8 %copy-start.38 = (s32[8]{0:T(128)S(1)}, s32[8]{0:T(128)}, u32[]{:S(2)}) copy-start(s32[8]{0:T(128)} %clip_ref.9) | copy-start | bytes 100
  4.4 19.8 %copy-start = (bf16[2,224,768]{2,1,0:T(8,128)(2,1)S(1)}, bf16[2,224,768]{2,1,0:T(8,128)(2,1)}, u32[]{:S(2)}) copy-start(bf16[2,224,768]{2,1,0:T(8,128)(2,1)} %pair_up.4.own.rest_0_) | copy-start | bytes 2064388
  4.4 5.9 %collective-permute-start.2 = (bf16[2,224,768]{2,1,0:T(8,128)(2,1)}, bf16[2,224,768]{2,1,0:T(8,128)(2,1)S(1)}, u32[]{:S(2)}, u32[]{:S(2)}) collective-permute-start(bf16[2,224,768]{2,1,0:T(8,128)(2,1)} %pair_up.4.own.rest_0_), channel_id=1, source_target_pairs={{0,8},{8,0},{16,24},{24,16},{1,9},{9,1},{17,25},{25,17},{2,10},{10... | collective-permute-start | bytes 2064392 | tf_op jit(solution)/shard_map/ppermute | solution.py:55
  4.5 19.7 %collective-permute-start.3 = (bf16[2,224,768]{2,1,0:T(8,128)(2,1)}, bf16[2,224,768]{2,1,0:T(8,128)(2,1)S(1)}, u32[]{:S(2)}, u32[]{:S(2)}) collective-permute-start(bf16[2,224,768]{2,1,0:T(8,128)(2,1)} %pair_up.4.own.rest_0_), channel_id=1, source_target_pairs={{0,0},{8,16},{16,8},{24,24},{1,1},{9,17},{17,9},{25,25},{2,2},{10,... | collective-permute-start | bytes 2064392 | tf_op jit(solution)/shard_map/ppermute | solution.py:59
  9.1 8.6 %collective-permute-start = (bf16[224,768]{1,0:T(8,128)(2,1)}, bf16[224,768]{1,0:T(8,128)(2,1)S(1)}, u32[]{:S(2)}, u32[]{:S(2)}) collective-permute-start(bf16[224,768]{1,0:T(8,128)(2,1)} %bitcast.1.x_ref), channel_id=1, source_target_pairs={{0,1},{1,0},{2,3},{3,2},{4,5},{5,4},{6,7},{7,6},{8,9},{9,8},{10,11... | collective-permute-start | bytes 1032200 | tf_op jit(solution)/shard_map/ppermute | solution.py:43
  10.4 0.8 copy-start.3
  13.2 23.8 %collective-permute-start.4 = (bf16[2,224,768]{2,1,0:T(8,128)(2,1)}, bf16[2,224,768]{2,1,0:T(8,128)(2,1)S(1)}, u32[]{:S(2)}, u32[]{:S(2)}) collective-permute-start(bf16[2,224,768]{2,1,0:T(8,128)(2,1)} %pair_up.5.rest_0_.rest_4_), channel_id=1, source_target_pairs={{0,8},{8,0},{16,24},{24,16},{1,9},{9,1},{17,25},{25,17},{2,10},{10... | collective-permute-start | bytes 2064392 | tf_op jit(solution)/shard_map/ppermute | solution.py:55
  13.2 23.8 %collective-permute-start.5 = (bf16[2,224,768]{2,1,0:T(8,128)(2,1)}, bf16[2,224,768]{2,1,0:T(8,128)(2,1)S(1)}, u32[]{:S(2)}, u32[]{:S(2)}) collective-permute-start(bf16[2,224,768]{2,1,0:T(8,128)(2,1)} %pair_up.5.rest_0_.rest_4_), channel_id=1, source_target_pairs={{0,0},{8,16},{16,8},{24,24},{1,1},{9,17},{17,9},{25,25},{2,2},{10,... | collective-permute-start | bytes 2064392 | tf_op jit(solution)/shard_map/ppermute | solution.py:59
  17.7 0.7 copy-start.41
  18.4 14.6 %collective-permute-start.1 = (bf16[224,768]{1,0:T(8,128)(2,1)}, bf16[224,768]{1,0:T(8,128)(2,1)S(1)}, u32[]{:S(2)}, u32[]{:S(2)}) collective-permute-start(bf16[224,768]{1,0:T(8,128)(2,1)} %gate.4), channel_id=1, source_target_pairs={{0,1},{1,0},{2,3},{3,2},{4,5},{5,4},{6,7},{7,6},{8,9},{9,8},{10,11... | collective-permute-start | bytes 1032200 | tf_op jit(solution)/shard_map/ppermute | solution.py:43
  20.2 26.6 %collective-permute-start.6 = (bf16[224,768]{1,0:T(8,128)(2,1)}, bf16[224,768]{1,0:T(8,128)(2,1)}, u32[]{:S(2)}, u32[]{:S(2)}) collective-permute-start(bf16[224,768]{1,0:T(8,128)(2,1)} %copy-done.41), channel_id=1, source_target_pairs={{0,2},{2,4},{3,1},{4,6},{5,3},{7,5},{8,10},{10,12},{11,9},{12,14},... | collective-permute-start | bytes 1032200 | tf_op jit(solution)/shard_map/ppermute | solution.py:47
  24.2 1.1 copy-start.4
  29.1 0.8 copy-start.14
  29.9 1.3 %copy-start.20 = (bf16[6,224,672]{2,1,0:T(8,128)(2,1)}, bf16[6,224,672]{2,1,0:T(8,128)(2,1)S(1)}, u32[]{:S(2)}) copy-start(bf16[6,224,672]{2,1,0:T(8,128)(2,1)S(1)} %get-tuple-element.27.rest_9_) | copy-start | bytes 5419012
  31.3 0.9 copy-start.24
  32.1 0.9 copy-start.26
  33.0 0.7 copy-start.40
  33.7 13.0 %collective-permute-start.7 = (bf16[224,768]{1,0:T(8,128)(2,1)}, bf16[224,768]{1,0:T(8,128)(2,1)}, u32[]{:S(2)}, u32[]{:S(2)}) collective-permute-start(bf16[224,768]{1,0:T(8,128)(2,1)} %gate.5.y_ref.rest_0_), channel_id=1, source_target_pairs={{0,2},{2,4},{3,1},{4,6},{5,3},{7,5},{8,10},{10,12},{11,9},{12,14},... | collective-permute-start | bytes 1032200 | tf_op jit(solution)/shard_map/ppermute | solution.py:47
  37.0 0.9 copy-start.10
  37.8 0.9 copy-start.12
  40.7 14.4 %copy-start.2 = (bf16[2,2,56,768]{3,2,1,0:T(8,128)(2,1)S(1)}, bf16[2,2,56,768]{3,2,1,0:T(8,128)(2,1)}, u32[]{:S(2)}) copy-start(bf16[2,2,56,768]{3,2,1,0:T(8,128)(2,1)} %param.7) | copy-start | bytes 1032196
  40.7 14.4 %copy-start.6 = (bf16[2,224,768]{2,1,0:T(8,128)(2,1)S(1)}, bf16[2,224,768]{2,1,0:T(8,128)(2,1)}, u32[]{:S(2)}) copy-start(bf16[2,224,768]{2,1,0:T(8,128)(2,1)} %pair_up.6.own.rest_1_) | copy-start | bytes 2064388
  40.7 14.4 %collective-permute-start.8 = (bf16[2,224,768]{2,1,0:T(8,128)(2,1)}, bf16[2,224,768]{2,1,0:T(8,128)(2,1)}, u32[]{:S(2)}, u32[]{:S(2)}) collective-permute-start(bf16[2,224,768]{2,1,0:T(8,128)(2,1)} %pair_up.6.own.rest_1_), channel_id=1, source_target_pairs={{0,8},{8,0},{16,24},{24,16},{1,9},{9,1},{17,25},{25,17},{2,10},{10... | collective-permute-start | bytes 2064392 | tf_op jit(solution)/shard_map/ppermute | solution.py:55
  41.3 13.8 %collective-permute-start.10 = (bf16[2,224,768]{2,1,0:T(8,128)(2,1)}, bf16[2,224,768]{2,1,0:T(8,128)(2,1)}, u32[]{:S(2)}, u32[]{:S(2)}) collective-permute-start(bf16[2,224,768]{2,1,0:T(8,128)(2,1)} %pair_up.6.own.rest_1_), channel_id=1, source_target_pairs={{0,0},{8,16},{16,8},{24,24},{1,1},{9,17},{17,9},{25,25},{2,2},{10,... | collective-permute-start | bytes 2064392 | tf_op jit(solution)/shard_map/ppermute | solution.py:59
  46.7 16.6 %collective-permute-start.16 = (bf16[2,224,768]{2,1,0:T(8,128)(2,1)}, bf16[2,224,768]{2,1,0:T(8,128)(2,1)}, u32[]{:S(2)}, u32[]{:S(2)}) collective-permute-start(bf16[2,224,768]{2,1,0:T(8,128)(2,1)} %pair_up.7), channel_id=1, source_target_pairs={{0,1},{1,0},{2,3},{3,2},{4,5},{5,4},{6,7},{7,6},{8,9},{9,8},{10,11... | collective-permute-start | bytes 2064392 | tf_op jit(solution)/shard_map/ppermute | solution.py:43
  47.9 18.0 %copy-start.7 = (bf16[2,2,56,768]{3,2,1,0:T(8,128)(2,1)S(1)}, bf16[2,2,56,768]{3,2,1,0:T(8,128)(2,1)}, u32[]{:S(2)}) copy-start(bf16[2,2,56,768]{3,2,1,0:T(8,128)(2,1)} %param.11) | copy-start | bytes 1032196
  47.9 18.0 %collective-permute-start.9 = (bf16[2,224,768]{2,1,0:T(8,128)(2,1)S(1)}, bf16[2,224,768]{2,1,0:T(8,128)(2,1)}, u32[]{:S(2)}, u32[]{:S(2)}) collective-permute-start(bf16[2,224,768]{2,1,0:T(8,128)(2,1)S(1)} %pad_maximum_fusion.own.rest_2_), channel_id=1, source_target_pairs={{0,8},{8,0},{16,24},{24,16},{1,9},{9,1},{17,25},{25,17},{2,10},{10... | collective-permute-start | bytes 2064392 | tf_op jit(solution)/shard_map/ppermute | solution.py:55
  51.4 14.5 %collective-permute-start.11 = (bf16[2,224,768]{2,1,0:T(8,128)(2,1)S(1)}, bf16[2,224,768]{2,1,0:T(8,128)(2,1)}, u32[]{:S(2)}, u32[]{:S(2)}) collective-permute-start(bf16[2,224,768]{2,1,0:T(8,128)(2,1)S(1)} %pad_maximum_fusion.own.rest_2_), channel_id=1, source_target_pairs={{0,0},{8,16},{16,8},{24,24},{1,1},{9,17},{17,9},{25,25},{2,2},{10,... | collective-permute-start | bytes 2064392 | tf_op jit(solution)/shard_map/ppermute | solution.py:59
  59.5 0.9 copy-start.18
  60.3 1.4 %copy-start.22 = (bf16[6,224,672]{2,1,0:T(8,128)(2,1)}, bf16[6,224,672]{2,1,0:T(8,128)(2,1)S(1)}, u32[]{:S(2)}) copy-start(bf16[6,224,672]{2,1,0:T(8,128)(2,1)S(1)} %get-tuple-element.28.rest_10_) | copy-start | bytes 5419012
  61.7 0.8 copy-start.28
  62.5 0.8 copy-start.30
  63.4 37.8 %collective-permute-start.17 = (bf16[2,224,768]{2,1,0:T(8,128)(2,1)}, bf16[2,224,768]{2,1,0:T(8,128)(2,1)S(1)}, u32[]{:S(2)}, u32[]{:S(2)}) collective-permute-start(bf16[2,224,768]{2,1,0:T(8,128)(2,1)} %gate.6.rest_3_.rest_7_), channel_id=1, source_target_pairs={{0,2},{2,4},{3,1},{4,6},{5,3},{7,5},{8,10},{10,12},{11,9},{12,14},... | collective-permute-start | bytes 2064392 | tf_op jit(solution)/shard_map/ppermute | solution.py:47
  65.9 1.1 copy-start.15
  67.0 1.1 copy-start.19
  68.1 1.1 copy-start.25
  69.2 1.1 copy-start.27
  70.3 1.1 copy-start.29
  71.4 1.1 copy-start.31
  72.5 19.3 %copy-start.5 = (bf16[2,224,768]{2,1,0:T(8,128)(2,1)S(1)}, bf16[2,224,768]{2,1,0:T(8,128)(2,1)}, u32[]{:S(2)}) copy-start(bf16[2,224,768]{2,1,0:T(8,128)(2,1)} %copy-done.3) | copy-start | bytes 2064388
  72.5 19.3 %copy-start.21 = (bf16[6,224,672]{2,1,0:T(8,128)(2,1)S(1)}, bf16[6,224,672]{2,1,0:T(8,128)(2,1)}, u32[]{:S(2)}) copy-start(bf16[6,224,672]{2,1,0:T(8,128)(2,1)} %copy-done.20) | copy-start | bytes 5419012
  72.5 19.3 %copy-start.23 = (bf16[6,224,672]{2,1,0:T(8,128)(2,1)S(1)}, bf16[6,224,672]{2,1,0:T(8,128)(2,1)}, u32[]{:S(2)}) copy-start(bf16[6,224,672]{2,1,0:T(8,128)(2,1)} %copy-done.22) | copy-start | bytes 5419012
  72.5 19.3 %copy-start.33 = (bf16[27,768]{1,0:T(8,128)(2,1)S(1)}, bf16[27,768]{1,0:T(8,128)(2,1)}, u32[]{:S(2)}) copy-start(bf16[27,768]{1,0:T(8,128)(2,1)} %rest_3_.1) | copy-start | bytes 124420
  77.7 7.3 %collective-permute-start.13 = (f32[16,224]{1,0:T(8,128)S(1)}, f32[16,224]{1,0:T(8,128)S(1)}, u32[]{:S(2)}, u32[]{:S(2)}) collective-permute-start(f32[16,224]{1,0:T(8,128)S(1)} %get-tuple-element.40), channel_id=1, source_target_pairs={{0,0},{1,2},{2,1},{3,4},{4,3},{5,6},{6,5},{7,7},{8,8},{9,10},{10,9... | collective-permute-start | bytes 43016 | tf_op jit(solution)/shard_map/ppermute | solution.py:51
  78.4 6.6 %collective-permute-start.12 = (f32[16,224]{1,0:T(8,128)S(1)}, f32[16,224]{1,0:T(8,128)S(1)}, u32[]{:S(2)}, u32[]{:S(2)}) collective-permute-start(f32[16,224]{1,0:T(8,128)S(1)} %get-tuple-element.40), channel_id=1, source_target_pairs={{0,1},{1,0},{2,3},{3,2},{4,5},{5,4},{6,7},{7,6},{8,9},{9,8},{10,11... | collective-permute-start | bytes 43016 | tf_op jit(solution)/shard_map/ppermute | solution.py:43
  80.9 24.9 %collective-permute-start.20 = (bf16[2,224,768]{2,1,0:T(8,128)(2,1)}, bf16[2,224,768]{2,1,0:T(8,128)(2,1)}, u32[]{:S(2)}, u32[]{:S(2)}) collective-permute-start(bf16[2,224,768]{2,1,0:T(8,128)(2,1)} %gate.6.rest_3_.rest_7_), channel_id=1, source_target_pairs={{0,8},{8,0},{16,24},{24,16},{1,9},{9,1},{17,25},{25,17},{2,10},{10... | collective-permute-start | bytes 2064392 | tf_op jit(solution)/shard_map/ppermute | solution.py:55
  83.0 22.8 %collective-permute-start.21 = (bf16[2,224,768]{2,1,0:T(8,128)(2,1)}, bf16[2,224,768]{2,1,0:T(8,128)(2,1)}, u32[]{:S(2)}, u32[]{:S(2)}) collective-permute-start(bf16[2,224,768]{2,1,0:T(8,128)(2,1)} %gate.6.rest_3_.rest_7_), channel_id=1, source_target_pairs={{0,0},{8,16},{16,8},{24,24},{1,1},{9,17},{17,9},{25,25},{2,2},{10,... | collective-permute-start | bytes 2064392 | tf_op jit(solution)/shard_map/ppermute | solution.py:59
  85.1 16.1 %collective-permute-start.14 = (f32[3,16,224]{2,1,0:T(8,128)S(1)}, f32[3,16,224]{2,1,0:T(8,128)S(1)}, u32[]{:S(2)}, u32[]{:S(2)}) collective-permute-start(f32[3,16,224]{2,1,0:T(8,128)S(1)} %pad_maximum_fusion.1.rest_17_.stat_own), channel_id=1, source_target_pairs={{0,8},{8,0},{16,24},{24,16},{1,9},{9,1},{17,25},{25,17},{2,10},{10... | collective-permute-start | bytes 129032 | tf_op jit(solution)/shard_map/ppermute | solution.py:55
  89.8 11.4 %collective-permute-start.15 = (f32[3,16,224]{2,1,0:T(8,128)S(1)}, f32[3,16,224]{2,1,0:T(8,128)S(1)}, u32[]{:S(2)}, u32[]{:S(2)}) collective-permute-start(f32[3,16,224]{2,1,0:T(8,128)S(1)} %pad_maximum_fusion.1.rest_17_.stat_own), channel_id=1, source_target_pairs={{0,0},{8,16},{16,8},{24,24},{1,1},{9,17},{17,9},{25,25},{2,2},{10,... | collective-permute-start | bytes 129032 | tf_op jit(solution)/shard_map/ppermute | solution.py:59
  100.6 0.6 copy-start.39
  101.2 0.9 copy-start.34
  101.2 0.9 copy-start.36
  101.2 0.8 copy-start.16
  102.0 15.2 %copy-start.9 = (bf16[2,224,768]{2,1,0:T(8,128)(2,1)S(1)}, bf16[2,224,768]{2,1,0:T(8,128)(2,1)}, u32[]{:S(2)}) copy-start(bf16[2,224,768]{2,1,0:T(8,128)(2,1)} %pair_up.5.rest_0_.rest_4_) | copy-start | bytes 2064388
  102.1 15.2 %collective-permute-start.18 = (bf16[2,224,768]{2,1,0:T(8,128)(2,1)}, bf16[2,224,768]{2,1,0:T(8,128)(2,1)S(1)}, u32[]{:S(2)}, u32[]{:S(2)}) collective-permute-start(bf16[2,224,768]{2,1,0:T(8,128)(2,1)} %gate.7.rest_0_), channel_id=1, source_target_pairs={{0,8},{8,0},{16,24},{24,16},{1,9},{9,1},{17,25},{25,17},{2,10},{10... | collective-permute-start | bytes 2064392 | tf_op jit(solution)/shard_map/ppermute | solution.py:55
  102.1 15.1 %collective-permute-start.19 = (bf16[2,224,768]{2,1,0:T(8,128)(2,1)}, bf16[2,224,768]{2,1,0:T(8,128)(2,1)S(1)}, u32[]{:S(2)}, u32[]{:S(2)}) collective-permute-start(bf16[2,224,768]{2,1,0:T(8,128)(2,1)} %gate.7.rest_0_), channel_id=1, source_target_pairs={{0,0},{8,16},{16,8},{24,24},{1,1},{9,17},{17,9},{25,25},{2,2},{10,... | collective-permute-start | bytes 2064392 | tf_op jit(solution)/shard_map/ppermute | solution.py:59
  105.8 1.1 copy-start.8
  106.9 1.1 copy-start.11
  108.0 1.1 copy-start.13
  109.1 0.8 copy-start.35
  109.9 0.8 copy-start.37
  110.7 6.6 %copy-start.17 = (bf16[2,224,768]{2,1,0:T(8,128)(2,1)S(1)}, bf16[2,224,768]{2,1,0:T(8,128)(2,1)}, u32[]{:S(2)}) copy-start(bf16[2,224,768]{2,1,0:T(8,128)(2,1)} %gate.7.rest_0_) | copy-start | bytes 2064388

commit v4 on v3

--- a/solution.py
+++ b/solution.py
@@ -13,6 +13,8 @@
 STAT_ROWS = 16
 UNROLL = 2
 FLOOR = -1e30
+SMALL = 2 * 1024 * 1024
+LARGE = 8 * 1024 * 1024
 
 
 CONTRACT_LAST = (((1,), (1,)), ((), ()))
@@ -308,7 +310,7 @@
 
     smem = pl.BlockSpec(memory_space=pltpu.SMEM)
     vmem = pl.BlockSpec(memory_space=pltpu.VMEM)
-    params = pltpu.CompilerParams(vmem_limit_bytes=16 * 1024 * 1024)
+    params = pltpu.CompilerParams(vmem_limit_bytes=LARGE)
     half = jax.ShapeDtypeStruct((rows, channels), jnp.bfloat16)
     full = jax.ShapeDtypeStruct((rows, channels), jnp.float32)
     exps = jax.ShapeDtypeStruct((heads, rows, 3 * rows), jnp.bfloat16)
@@ -342,6 +344,7 @@
             in_specs=[vmem] * 2 + [pl.BlockSpec(memory_space=pl.ANY)] * len(earlier),
             out_specs=vmem,
             out_shape=jax.ShapeDtypeStruct((2,) + x.shape, x.dtype),
+            compiler_params=pltpu.CompilerParams(vmem_limit_bytes=SMALL),
             name="pair_up",
         )(x, y, *earlier)
 
@@ -352,6 +355,7 @@
             out_specs=pl.BlockSpec(memory_space=pl.ANY),
             out_shape=jax.ShapeDtypeStruct(x.shape, x.dtype),
             input_output_aliases={0: 0},
+            compiler_params=pltpu.CompilerParams(vmem_limit_bytes=SMALL),
             name="gate",
         )(x, *earlier)
 

time: 126 us -> 92.3 us (0.73); the launches traced: 124 us -> 91.9 us
  local copies, waits for them, and re-layouts: 27.6 us -> 1.07 us
  waiting for transfers between devices: 1.9 us -> 17.5 us
  Pallas kernels: 43.5 us -> 32.4 us
  starting transfers between devices: 49 us -> 39.9 us
    unnamed x85 -> x11, local copies, waits for them, and re-layouts: 27.6 us -> 1.07 us
    ppermute x7, starting transfers between devices: 11.1 us -> 2.14 us  [ta_pair(): return lax.ppermute(x, 'ta', flip_pairs(lax.axis_size('ta')))]
    ppermute x7, waiting for transfers between devices: 0.02 us -> 6.99 us  [ta_other(): return lax.ppermute(x, 'ta', other_pairs(lax.axis_size('ta')))]
    pallas_call x4, Pallas kernels: 7.98 us -> 1.19 us  [pair_up(): pl.pallas_call(kernel, in_specs=[vmem] * 2 + [pl.BlockSpec(memory_space=p...]
    pallas_call x6, Pallas kernels: 35.6 us -> 31.2 us  [call(): pl.pallas_call(kernel, in_specs=[smem] * scalars + [vmem] * (len(args) -...]
    ppermute x3, waiting for transfers between devices: 0.01 us -> 4.34 us  [ha_relay(): return lax.ppermute(near, 'ha', relay_pairs(lax.axis_size('ha')))]
    ppermute x4, waiting for transfers between devices: 1.85 us -> 6.17 us  [ha_near(): return lax.ppermute(x, 'ha', flip_pairs(lax.axis_size('ha')))]
    ppermute x7, starting transfers between devices: 22.1 us -> 19.8 us  [ta_other(): return lax.ppermute(x, 'ta', other_pairs(lax.axis_size('ta')))]
  transfers between devices with their start and end apart: 22 -> 22, of which waited for: 1 -> 7; matrix products, arithmetic and copies ran while one was open for 1% -> 0% of each run, Pallas kernels for 28% -> 27%
where the time goes in v4:
time: 92.3 us; the launch traced here: 91.9 us
  starting transfers between devices  39.9 us (43%)
  Pallas kernels  32.4 us (35%)
  waiting for transfers between devices  17.5 us (19%)
  local copies, waits for them, and re-layouts  1.07 us (1%)
  between operations  0.97 us (1%)
    pallas_call x6, Pallas kernels, call(): pl.pallas_call(kernel, in_specs=[smem] * scalars + [vmem] * (len(args) -...  31.2 us
    ppermute x7, starting transfers between devices, ta_other(): return lax.ppermute(x, 'ta', other_pairs(lax.axis_size('ta')))  19.8 us
    ppermute x3, starting transfers between devices, ha_relay(): return lax.ppermute(near, 'ha', relay_pairs(lax.axis_size('ha')))  10.5 us
    ppermute x7, waiting for transfers between devices, ta_other(): return lax.ppermute(x, 'ta', other_pairs(lax.axis_size('ta')))  6.99 us
    ppermute x4, starting transfers between devices, ha_near(): return lax.ppermute(x, 'ha', flip_pairs(lax.axis_size('ha')))  6.84 us
    ppermute x4, waiting for transfers between devices, ha_near(): return lax.ppermute(x, 'ha', flip_pairs(lax.axis_size('ha')))  6.17 us
    ppermute x3, waiting for transfers between devices, ha_relay(): return lax.ppermute(near, 'ha', relay_pairs(lax.axis_size('ha')))  4.34 us
    ppermute x7, starting transfers between devices, ta_pair(): return lax.ppermute(x, 'ta', flip_pairs(lax.axis_size('ta')))  2.14 us
  transfers between devices with their start and end apart: 22, of which 7 were waited for; matrix products, arithmetic and copies ran while one was open for 0% of the time, Pallas kernels for 27%

profile of v4, /device:TPU:1, one launch (start us, length us, event | category | flops | bytes accessed | tf_op | source)
XLA Modules:
  0.0 91.9 jit_solution(171142527163172169)
XLA Ops:
  0.6 0.0 copy-start
  0.6 0.0 copy-start.1
  0.7 1.0 %copy.20 = bf16[2,2,56,768]{3,2,1,0:T(8,128)(2,1)S(1)} copy(bf16[2,2,56,768]{3,2,1,0:T(8,128)(2,1)} %param.9) | data formatting | bytes 688128
  1.7 0.0 copy-start.2
  1.7 0.0 copy-start.4
  1.7 1.1 %pair_up.4.own.rest_0_ = bf16[2,224,768]{2,1,0:T(8,128)(2,1)S(1)} custom-call(bf16[224,768]{1,0:T(8,128)(2,1)} %bitcast.1.x_ref, bf16[224,768]{1,0:T(8,128)(2,1)S(1)} %bitcast.22), custom_call_target="tpu_custom_call" | custom-call | tf_op jit(solution)/shard_map/pair_up/pallas_call | solution.py:342
  2.8 0.1 collective-permute-start.2
  2.9 4.5 %collective-permute-start.3 = (bf16[2,224,768]{2,1,0:T(8,128)(2,1)S(1)}, bf16[2,224,768]{2,1,0:T(8,128)(2,1)S(1)}, u32[]{:S(2)}, u32[]{:S(2)}) collective-permute-start(bf16[2,224,768]{2,1,0:T(8,128)(2,1)S(1)} %pair_up.4.own.rest_0_), channel_id=1, source_target_pairs={{0,0},{8,16},{16,8},{24,24},{1,1},{9,17},{17,9},{25,25},{2,2},{10,... | collective-permute-start | bytes 2064392 | tf_op jit(solution)/shard_map/ppermute | solution.py:61
  7.4 1.3 %collective-permute-start = (bf16[224,768]{1,0:T(8,128)(2,1)}, bf16[224,768]{1,0:T(8,128)(2,1)S(1)}, u32[]{:S(2)}, u32[]{:S(2)}) collective-permute-start(bf16[224,768]{1,0:T(8,128)(2,1)} %bitcast.1.x_ref), channel_id=1, source_target_pairs={{0,1},{1,0},{2,3},{3,2},{4,5},{5,4},{6,7},{7,6},{8,9},{9,8},{10,11... | collective-permute-start | bytes 1032200 | tf_op jit(solution)/shard_map/ppermute | solution.py:45
  8.7 0.0 collective-permute-done.2.pair.rest_0_.rest_3_
  8.7 0.0 copy-done
  8.7 0.0 copy-done.1
  8.7 0.1 collective-permute-start.4
  8.8 2.8 %collective-permute-start.5 = (bf16[2,224,768]{2,1,0:T(8,128)(2,1)S(1)}, bf16[2,224,768]{2,1,0:T(8,128)(2,1)S(1)}, u32[]{:S(2)}, u32[]{:S(2)}) collective-permute-start(bf16[2,224,768]{2,1,0:T(8,128)(2,1)S(1)} %pair_up.5.rest_0_.rest_4_), channel_id=1, source_target_pairs={{0,0},{8,16},{16,8},{24,24},{1,1},{9,17},{17,9},{25,25},{2,2},{10,... | collective-permute-start | bytes 2064392 | tf_op jit(solution)/shard_map/ppermute | solution.py:61
  11.6 3.5 %collective-permute-done.refs_1_.x_ref = bf16[224,768]{1,0:T(8,128)(2,1)S(1)} collective-permute-done((bf16[224,768]{1,0:T(8,128)(2,1)}, bf16[224,768]{1,0:T(8,128)(2,1)S(1)}, u32[]{:S(2)}, u32[]{:S(2)}) %collective-permute-start) | collective-permute-done | bytes 344096 | tf_op jit(solution)/shard_map/ppermute | solution.py:45
  15.0 1.7 %collective-permute-start.1 = (bf16[224,768]{1,0:T(8,128)(2,1)S(1)}, bf16[224,768]{1,0:T(8,128)(2,1)S(1)}, u32[]{:S(2)}, u32[]{:S(2)}) collective-permute-start(bf16[224,768]{1,0:T(8,128)(2,1)S(1)} %gate.4), channel_id=1, source_target_pairs={{0,1},{1,0},{2,3},{3,2},{4,5},{5,4},{6,7},{7,6},{8,9},{9,8},{10,11... | collective-permute-start | bytes 1032200 | tf_op jit(solution)/shard_map/ppermute | solution.py:45
  16.8 3.2 %collective-permute-start.6 = (bf16[224,768]{1,0:T(8,128)(2,1)S(1)}, bf16[224,768]{1,0:T(8,128)(2,1)S(1)}, u32[]{:S(2)}, u32[]{:S(2)}) collective-permute-start(bf16[224,768]{1,0:T(8,128)(2,1)S(1)} %collective-permute-done.refs_1_.x_ref), channel_id=1, source_target_pairs={{0,2},{2,4},{3,1},{4,6},{5,3},{7,5},{8,10},{10,12},{11,9},{12,14},... | collective-permute-start | bytes 1032200 | tf_op jit(solution)/shard_map/ppermute | solution.py:49
  20.0 0.0 collective-permute-done.3.other.rest_6_
  20.0 0.0 copy-done.2
  20.0 0.0 copy-done.4
  20.0 3.8 %scores_0.1 = (bf16[6,224,672]{2,1,0:T(8,128)(2,1)S(1)}, f32[224,768]{1,0:T(8,128)S(1)}, f32[224,768]{1,0:T(8,128)S(1)}, f32[224,768]{1,0:T(8,128)S(1)}) custom-call(s32[4,8,9]{2,1,0:T(8,128)S(1)} %copy-done.2, s32[8]{0:T(128)S(1)} %copy-done.4, bf16[224,768]{1,0:T(8,128)(2,1)S(1)} %bitcast.14, bf16[2,224,768]{2,1,0:T(8,128)(2,1)S(1)} %pair_up.4.own.rest_0_, ...), custom_call_target="tpu_custom_call" | custom-call | flops 462422016 | bytes 2752512 | tf_op jit(solution)/shard_map/scores_0/pallas_call | solution.py:321
  23.9 0.2 collective-permute-done.1.refs_0_
  24.0 4.0 %collective-permute-start.7 = (bf16[224,768]{1,0:T(8,128)(2,1)S(1)}, bf16[224,768]{1,0:T(8,128)(2,1)S(1)}, u32[]{:S(2)}, u32[]{:S(2)}) collective-permute-start(bf16[224,768]{1,0:T(8,128)(2,1)S(1)} %gate.5.y_ref.rest_0_), channel_id=1, source_target_pairs={{0,2},{2,4},{3,1},{4,6},{5,3},{7,5},{8,10},{10,12},{11,9},{12,14},... | collective-permute-start | bytes 1032200 | tf_op jit(solution)/shard_map/ppermute | solution.py:49
  28.1 0.0 collective-permute-done.4.rest_0_.rest_1_.rest_5_
  28.1 0.0 collective-permute-done.5.rest_1_.rest_2_.rest_6_
  28.2 0.1 collective-permute-start.8
  28.2 3.1 %collective-permute-start.10 = (bf16[2,224,768]{2,1,0:T(8,128)(2,1)S(1)}, bf16[2,224,768]{2,1,0:T(8,128)(2,1)S(1)}, u32[]{:S(2)}, u32[]{:S(2)}) collective-permute-start(bf16[2,224,768]{2,1,0:T(8,128)(2,1)S(1)} %pair_up.6.own.rest_1_), channel_id=1, source_target_pairs={{0,0},{8,16},{16,8},{24,24},{1,1},{9,17},{17,9},{25,25},{2,2},{10,... | collective-permute-start | bytes 2064392 | tf_op jit(solution)/shard_map/ppermute | solution.py:61
  31.4 0.1 collective-permute-start.16
  31.5 0.0 collective-permute-done.6
  31.5 4.3 %collective-permute-done.7 = bf16[224,768]{1,0:T(8,128)(2,1)S(1)} collective-permute-done((bf16[224,768]{1,0:T(8,128)(2,1)S(1)}, bf16[224,768]{1,0:T(8,128)(2,1)S(1)}, u32[]{:S(2)}, u32[]{:S(2)}) %collective-permute-start.7) | collective-permute-done | bytes 344096 | tf_op jit(solution)/shard_map/ppermute | solution.py:49
  35.8 0.1 pad_maximum_fusion.own.rest_2_
  35.9 0.6 collective-permute-start.9
  36.5 1.9 %collective-permute-start.11 = (bf16[2,224,768]{2,1,0:T(8,128)(2,1)S(1)}, bf16[2,224,768]{2,1,0:T(8,128)(2,1)S(1)}, u32[]{:S(2)}, u32[]{:S(2)}) collective-permute-start(bf16[2,224,768]{2,1,0:T(8,128)(2,1)S(1)} %pad_maximum_fusion.own.rest_2_), channel_id=1, source_target_pairs={{0,0},{8,16},{16,8},{24,24},{1,1},{9,17},{17,9},{25,25},{2,2},{10,... | collective-permute-start | bytes 2064392 | tf_op jit(solution)/shard_map/ppermute | solution.py:61
  38.4 0.0 collective-permute-done.8.pair.rest_4_
  38.4 2.4 %collective-permute-done.10.other.rest_7_ = bf16[2,224,768]{2,1,0:T(8,128)(2,1)S(1)} collective-permute-done((bf16[2,224,768]{2,1,0:T(8,128)(2,1)S(1)}, bf16[2,224,768]{2,1,0:T(8,128)(2,1)S(1)}, u32[]{:S(2)}, u32[]{:S(2)}) %collective-permute-start.10) | collective-permute-done | bytes 688160 | tf_op jit(solution)/shard_map/ppermute | solution.py:61
  40.8 3.8 %scores_1.1 = (bf16[6,224,672]{2,1,0:T(8,128)(2,1)S(1)}, f32[224,768]{1,0:T(8,128)S(1)}, f32[224,768]{1,0:T(8,128)S(1)}, f32[224,768]{1,0:T(8,128)S(1)}) custom-call(s32[4,8,9]{2,1,0:T(8,128)S(1)} %copy-done.2, s32[8]{0:T(128)S(1)} %copy-done.4, bf16[224,768]{1,0:T(8,128)(2,1)S(1)} %bitcast.16, bf16[2,224,768]{2,1,0:T(8,128)(2,1)S(1)} %pair_up.6.own.rest_1_, ...), custom_call_target="tpu_custom_call" | custom-call | flops 462422016 | bytes 2752512 | tf_op jit(solution)/shard_map/scores_1/pallas_call | solution.py:321
  44.6 2.5 %collective-permute-done.16.refs_0_ = bf16[2,224,768]{2,1,0:T(8,128)(2,1)S(1)} collective-permute-done((bf16[2,224,768]{2,1,0:T(8,128)(2,1)S(1)}, bf16[2,224,768]{2,1,0:T(8,128)(2,1)S(1)}, u32[]{:S(2)}, u32[]{:S(2)}) %collective-permute-start.16) | collective-permute-done | bytes 688160 | tf_op jit(solution)/shard_map/ppermute | solution.py:45
  47.2 3.2 %collective-permute-start.17 = (bf16[2,224,768]{2,1,0:T(8,128)(2,1)S(1)}, bf16[2,224,768]{2,1,0:T(8,128)(2,1)S(1)}, u32[]{:S(2)}, u32[]{:S(2)}) collective-permute-start(bf16[2,224,768]{2,1,0:T(8,128)(2,1)S(1)} %gate.6.rest_3_.rest_7_), channel_id=1, source_target_pairs={{0,2},{2,4},{3,1},{4,6},{5,3},{7,5},{8,10},{10,12},{11,9},{12,14},... | collective-permute-start | bytes 2064392 | tf_op jit(solution)/shard_map/ppermute | solution.py:49
  50.4 0.0 collective-permute-done.9.pair.rest_5_
  50.4 0.0 collective-permute-done.11.other.rest_8_
  50.4 0.0 copy-start.3
  50.4 4.5 %scores_2.1 = (bf16[6,224,672]{2,1,0:T(8,128)(2,1)S(1)}, f32[224,768]{1,0:T(8,128)S(1)}, f32[224,768]{1,0:T(8,128)S(1)}, f32[224,768]{1,0:T(8,128)S(1)}, f32[224...) custom-call(s32[4,8,9]{2,1,0:T(8,128)S(1)} %copy-done.2, s32[8]{0:T(128)S(1)} %copy-done.4, ...), custom_call_target="tpu_custom_call" | custom-call | flops 462422016 | bytes 2752512 | tf_op jit(solution)/shard_map/scores_2/pallas_call | solution.py:321
  55.0 0.7 collective-permute-start.13
  55.6 3.8 %collective-permute-start.12 = (f32[16,224]{1,0:T(8,128)S(1)}, f32[16,224]{1,0:T(8,128)S(1)}, u32[]{:S(2)}, u32[]{:S(2)}) collective-permute-start(f32[16,224]{1,0:T(8,128)S(1)} %get-tuple-element.40), channel_id=1, source_target_pairs={{0,1},{1,0},{2,3},{3,2},{4,5},{5,4},{6,7},{7,6},{8,9},{9,8},{10,11... | collective-permute-start | bytes 43016 | tf_op jit(solution)/shard_map/ppermute | solution.py:45
  59.4 1.2 %collective-permute-start.20 = (bf16[2,224,768]{2,1,0:T(8,128)(2,1)S(1)}, bf16[2,224,768]{2,1,0:T(8,128)(2,1)S(1)}, u32[]{:S(2)}, u32[]{:S(2)}) collective-permute-start(bf16[2,224,768]{2,1,0:T(8,128)(2,1)S(1)} %gate.6.rest_3_.rest_7_), channel_id=1, source_target_pairs={{0,8},{8,0},{16,24},{24,16},{1,9},{9,1},{17,25},{25,17},{2,10},{10... | collective-permute-start | bytes 2064392 | tf_op jit(solution)/shard_map/ppermute | solution.py:57
  60.6 1.9 %collective-permute-start.21 = (bf16[2,224,768]{2,1,0:T(8,128)(2,1)S(1)}, bf16[2,224,768]{2,1,0:T(8,128)(2,1)S(1)}, u32[]{:S(2)}, u32[]{:S(2)}) collective-permute-start(bf16[2,224,768]{2,1,0:T(8,128)(2,1)S(1)} %gate.6.rest_3_.rest_7_), channel_id=1, source_target_pairs={{0,0},{8,16},{16,8},{24,24},{1,1},{9,17},{17,9},{25,25},{2,2},{10,... | collective-permute-start | bytes 2064392 | tf_op jit(solution)/shard_map/ppermute | solution.py:61
  62.5 0.0 collective-permute-done.13
  62.5 0.0 collective-permute-done.12
  62.6 0.1 collective-permute-start.14
  62.7 3.6 %collective-permute-start.15 = (f32[3,16,224]{2,1,0:T(8,128)S(1)}, f32[3,16,224]{2,1,0:T(8,128)S(1)}, u32[]{:S(2)}, u32[]{:S(2)}) collective-permute-start(f32[3,16,224]{2,1,0:T(8,128)S(1)} %pad_maximum_fusion.1.rest_17_.stat_own), channel_id=1, source_target_pairs={{0,0},{8,16},{16,8},{24,24},{1,1},{9,17},{17,9},{25,25},{2,2},{10,... | collective-permute-start | bytes 129032 | tf_op jit(solution)/shard_map/ppermute | solution.py:61
  66.3 0.0 copy-done.3
  66.3 7.0 %query_side.1 = (bf16[224,768]{1,0:T(8,128)(2,1)}, bf16[224,768]{1,0:T(8,128)(2,1)}, f32[8,128]{1,0:T(8,128)S(1)}) custom-call(bf16[224,768]{1,0:T(8,128)(2,1)S(1)} %bitcast.21, bf16[27,768]{1,0:T(8,128)(2,1)S(1)} %copy-done.3, bf16[2,224,768]{2,1,0:T(8,128)(2,1)S(1)} %pair_up.4.own.rest_0_, bf16[2,224,768]{2,1,0:T(8,128)(2,1)S(1)} %pair_up.6.own.rest_1_, ...), custom_call_target="tpu_custom_call" | custom-call | flops 1387266048 | bytes 8257536 | tf_op jit(solution)/shard_map/query_side/pallas_call | solution.py:321
  73.3 0.0 collective-permute-done.14.refs_2_.stat_pair
  73.3 0.1 collective-permute-done.15.refs_3_.stat_other
  73.4 0.0 collective-permute-done.17.refs_0_
  73.4 0.0 collective-permute-start.18
  73.4 1.9 %collective-permute-start.19 = (bf16[2,224,768]{2,1,0:T(8,128)(2,1)S(1)}, bf16[2,224,768]{2,1,0:T(8,128)(2,1)S(1)}, u32[]{:S(2)}, u32[]{:S(2)}) collective-permute-start(bf16[2,224,768]{2,1,0:T(8,128)(2,1)S(1)} %gate.7.rest_0_), channel_id=1, source_target_pairs={{0,0},{8,16},{16,8},{24,24},{1,1},{9,17},{17,9},{25,25},{2,2},{10,... | collective-permute-start | bytes 2064392 | tf_op jit(solution)/shard_map/ppermute | solution.py:61
  75.4 0.0 collective-permute-done.20.rest_4_.rest_8_
  75.4 0.0 collective-permute-done.21.rest_5_.rest_9_
  75.4 5.8 %key_side_0.1 = (f32[224,768]{1,0:T(8,128)S(1)}, f32[224,768]{1,0:T(8,128)S(1)}) custom-call(s32[4,8,9]{2,1,0:T(8,128)S(1)} %copy-done.2, s32[8]{0:T(128)S(1)} %copy-done.4, bf16[2,224,768]{2,1,0:T(8,128)(2,1)S(1)} %pair_up.4.own.rest_0_, f32[3,16,224]{2,1,0:T(8,128)S(1)} %pad_maximum_fusion.1.rest_17_.stat_own, ...), custom_call_target="tpu_custom_call" | custom-call | flops 1849688064 | bytes 5505024 | tf_op jit(solution)/shard_map/key_side_0/pallas_call | solution.py:321
  81.2 0.0 collective-permute-done.18.rest_1_
  81.2 4.5 %collective-permute-done.19.rest_2_ = bf16[2,224,768]{2,1,0:T(8,128)(2,1)S(1)} collective-permute-done((bf16[2,224,768]{2,1,0:T(8,128)(2,1)S(1)}, bf16[2,224,768]{2,1,0:T(8,128)(2,1)S(1)}, u32[]{:S(2)}, u32[]{:S(2)}) %collective-permute-start.19) | collective-permute-done | bytes 688160 | tf_op jit(solution)/shard_map/ppermute | solution.py:61
  85.7 6.2 %key_side_1.1 = (bf16[224,768]{1,0:T(8,128)(2,1)}, bf16[224,768]{1,0:T(8,128)(2,1)}) custom-call(s32[4,8,9]{2,1,0:T(8,128)S(1)} %copy-done.2, s32[8]{0:T(128)S(1)} %copy-done.4, bf16[2,224,768]{2,1,0:T(8,128)(2,1)S(1)} %pair_up.4.own.rest_0_, f32[3,16,224]{2,1,0:T(8,128)S(1)} %pad_maximum_fusion.1.rest_17_.stat_own, ...), custom_call_target="tpu_custom_call" | custom-call | flops 924844032 | bytes 2752512 | tf_op jit(solution)/shard_map/key_side_1/pallas_call | solution.py:321
  (8 shorter events, 0.2 us)
Async XLA Ops:
  0.6 8.0 %copy-start = (bf16[2,2,56,768]{3,2,1,0:T(8,128)(2,1)S(1)}, bf16[2,2,56,768]{3,2,1,0:T(8,128)(2,1)}, u32[]{:S(2)}) copy-start(bf16[2,2,56,768]{3,2,1,0:T(8,128)(2,1)} %param.7) | copy-start | bytes 1032196
  0.6 8.0 %copy-start.1 = (bf16[2,2,56,768]{3,2,1,0:T(8,128)(2,1)S(1)}, bf16[2,2,56,768]{3,2,1,0:T(8,128)(2,1)}, u32[]{:S(2)}) copy-start(bf16[2,2,56,768]{3,2,1,0:T(8,128)(2,1)} %param.11) | copy-start | bytes 1032196
  1.7 18.3 %copy-start.2 = (s32[4,8,9]{2,1,0:T(8,128)S(1)}, s32[4,8,9]{2,1,0:T(8,128)}, u32[]{:S(2)}) copy-start(s32[4,8,9]{2,1,0:T(8,128)} %mask_ref.9) | copy-start | bytes 3460
  1.7 18.3 %copy-start.4 = (s32[8]{0:T(128)S(1)}, s32[8]{0:T(128)}, u32[]{:S(2)}) copy-start(s32[8]{0:T(128)} %clip_ref.9) | copy-start | bytes 100
  2.8 5.9 %collective-permute-start.2 = (bf16[2,224,768]{2,1,0:T(8,128)(2,1)S(1)}, bf16[2,224,768]{2,1,0:T(8,128)(2,1)S(1)}, u32[]{:S(2)}, u32[]{:S(2)}) collective-permute-start(bf16[2,224,768]{2,1,0:T(8,128)(2,1)S(1)} %pair_up.4.own.rest_0_), channel_id=1, source_target_pairs={{0,8},{8,0},{16,24},{24,16},{1,9},{9,1},{17,25},{25,17},{2,10},{10... | collective-permute-start | bytes 2064392 | tf_op jit(solution)/shard_map/ppermute | solution.py:57
  2.9 17.1 %collective-permute-start.3 = (bf16[2,224,768]{2,1,0:T(8,128)(2,1)S(1)}, bf16[2,224,768]{2,1,0:T(8,128)(2,1)S(1)}, u32[]{:S(2)}, u32[]{:S(2)}) collective-permute-start(bf16[2,224,768]{2,1,0:T(8,128)(2,1)S(1)} %pair_up.4.own.rest_0_), channel_id=1, source_target_pairs={{0,0},{8,16},{16,8},{24,24},{1,1},{9,17},{17,9},{25,25},{2,2},{10,... | collective-permute-start | bytes 2064392 | tf_op jit(solution)/shard_map/ppermute | solution.py:61
  7.4 7.7 %collective-permute-start = (bf16[224,768]{1,0:T(8,128)(2,1)}, bf16[224,768]{1,0:T(8,128)(2,1)S(1)}, u32[]{:S(2)}, u32[]{:S(2)}) collective-permute-start(bf16[224,768]{1,0:T(8,128)(2,1)} %bitcast.1.x_ref), channel_id=1, source_target_pairs={{0,1},{1,0},{2,3},{3,2},{4,5},{5,4},{6,7},{7,6},{8,9},{9,8},{10,11... | collective-permute-start | bytes 1032200 | tf_op jit(solution)/shard_map/ppermute | solution.py:45
  8.7 19.4 %collective-permute-start.4 = (bf16[2,224,768]{2,1,0:T(8,128)(2,1)S(1)}, bf16[2,224,768]{2,1,0:T(8,128)(2,1)S(1)}, u32[]{:S(2)}, u32[]{:S(2)}) collective-permute-start(bf16[2,224,768]{2,1,0:T(8,128)(2,1)S(1)} %pair_up.5.rest_0_.rest_4_), channel_id=1, source_target_pairs={{0,8},{8,0},{16,24},{24,16},{1,9},{9,1},{17,25},{25,17},{2,10},{10... | collective-permute-start | bytes 2064392 | tf_op jit(solution)/shard_map/ppermute | solution.py:57
  8.8 19.3 %collective-permute-start.5 = (bf16[2,224,768]{2,1,0:T(8,128)(2,1)S(1)}, bf16[2,224,768]{2,1,0:T(8,128)(2,1)S(1)}, u32[]{:S(2)}, u32[]{:S(2)}) collective-permute-start(bf16[2,224,768]{2,1,0:T(8,128)(2,1)S(1)} %pair_up.5.rest_0_.rest_4_), channel_id=1, source_target_pairs={{0,0},{8,16},{16,8},{24,24},{1,1},{9,17},{17,9},{25,25},{2,2},{10,... | collective-permute-start | bytes 2064392 | tf_op jit(solution)/shard_map/ppermute | solution.py:61
  15.0 9.0 %collective-permute-start.1 = (bf16[224,768]{1,0:T(8,128)(2,1)S(1)}, bf16[224,768]{1,0:T(8,128)(2,1)S(1)}, u32[]{:S(2)}, u32[]{:S(2)}) collective-permute-start(bf16[224,768]{1,0:T(8,128)(2,1)S(1)} %gate.4), channel_id=1, source_target_pairs={{0,1},{1,0},{2,3},{3,2},{4,5},{5,4},{6,7},{7,6},{8,9},{9,8},{10,11... | collective-permute-start | bytes 1032200 | tf_op jit(solution)/shard_map/ppermute | solution.py:45
  16.8 14.7 %collective-permute-start.6 = (bf16[224,768]{1,0:T(8,128)(2,1)S(1)}, bf16[224,768]{1,0:T(8,128)(2,1)S(1)}, u32[]{:S(2)}, u32[]{:S(2)}) collective-permute-start(bf16[224,768]{1,0:T(8,128)(2,1)S(1)} %collective-permute-done.refs_1_.x_ref), channel_id=1, source_target_pairs={{0,2},{2,4},{3,1},{4,6},{5,3},{7,5},{8,10},{10,12},{11,9},{12,14},... | collective-permute-start | bytes 1032200 | tf_op jit(solution)/shard_map/ppermute | solution.py:49
  24.0 11.8 %collective-permute-start.7 = (bf16[224,768]{1,0:T(8,128)(2,1)S(1)}, bf16[224,768]{1,0:T(8,128)(2,1)S(1)}, u32[]{:S(2)}, u32[]{:S(2)}) collective-permute-start(bf16[224,768]{1,0:T(8,128)(2,1)S(1)} %gate.5.y_ref.rest_0_), channel_id=1, source_target_pairs={{0,2},{2,4},{3,1},{4,6},{5,3},{7,5},{8,10},{10,12},{11,9},{12,14},... | collective-permute-start | bytes 1032200 | tf_op jit(solution)/shard_map/ppermute | solution.py:49
  28.2 10.2 %collective-permute-start.8 = (bf16[2,224,768]{2,1,0:T(8,128)(2,1)S(1)}, bf16[2,224,768]{2,1,0:T(8,128)(2,1)S(1)}, u32[]{:S(2)}, u32[]{:S(2)}) collective-permute-start(bf16[2,224,768]{2,1,0:T(8,128)(2,1)S(1)} %pair_up.6.own.rest_1_), channel_id=1, source_target_pairs={{0,8},{8,0},{16,24},{24,16},{1,9},{9,1},{17,25},{25,17},{2,10},{10... | collective-permute-start | bytes 2064392 | tf_op jit(solution)/shard_map/ppermute | solution.py:57
  28.2 12.6 %collective-permute-start.10 = (bf16[2,224,768]{2,1,0:T(8,128)(2,1)S(1)}, bf16[2,224,768]{2,1,0:T(8,128)(2,1)S(1)}, u32[]{:S(2)}, u32[]{:S(2)}) collective-permute-start(bf16[2,224,768]{2,1,0:T(8,128)(2,1)S(1)} %pair_up.6.own.rest_1_), channel_id=1, source_target_pairs={{0,0},{8,16},{16,8},{24,24},{1,1},{9,17},{17,9},{25,25},{2,2},{10,... | collective-permute-start | bytes 2064392 | tf_op jit(solution)/shard_map/ppermute | solution.py:61
  31.4 15.8 %collective-permute-start.16 = (bf16[2,224,768]{2,1,0:T(8,128)(2,1)S(1)}, bf16[2,224,768]{2,1,0:T(8,128)(2,1)S(1)}, u32[]{:S(2)}, u32[]{:S(2)}) collective-permute-start(bf16[2,224,768]{2,1,0:T(8,128)(2,1)S(1)} %pair_up.7), channel_id=1, source_target_pairs={{0,1},{1,0},{2,3},{3,2},{4,5},{5,4},{6,7},{7,6},{8,9},{9,8},{10,11... | collective-permute-start | bytes 2064392 | tf_op jit(solution)/shard_map/ppermute | solution.py:45
  35.9 14.5 %collective-permute-start.9 = (bf16[2,224,768]{2,1,0:T(8,128)(2,1)S(1)}, bf16[2,224,768]{2,1,0:T(8,128)(2,1)S(1)}, u32[]{:S(2)}, u32[]{:S(2)}) collective-permute-start(bf16[2,224,768]{2,1,0:T(8,128)(2,1)S(1)} %pad_maximum_fusion.own.rest_2_), channel_id=1, source_target_pairs={{0,8},{8,0},{16,24},{24,16},{1,9},{9,1},{17,25},{25,17},{2,10},{10... | collective-permute-start | bytes 2064392 | tf_op jit(solution)/shard_map/ppermute | solution.py:57
  36.5 14.0 %collective-permute-start.11 = (bf16[2,224,768]{2,1,0:T(8,128)(2,1)S(1)}, bf16[2,224,768]{2,1,0:T(8,128)(2,1)S(1)}, u32[]{:S(2)}, u32[]{:S(2)}) collective-permute-start(bf16[2,224,768]{2,1,0:T(8,128)(2,1)S(1)} %pad_maximum_fusion.own.rest_2_), channel_id=1, source_target_pairs={{0,0},{8,16},{16,8},{24,24},{1,1},{9,17},{17,9},{25,25},{2,2},{10,... | collective-permute-start | bytes 2064392 | tf_op jit(solution)/shard_map/ppermute | solution.py:61
  47.2 26.2 %collective-permute-start.17 = (bf16[2,224,768]{2,1,0:T(8,128)(2,1)S(1)}, bf16[2,224,768]{2,1,0:T(8,128)(2,1)S(1)}, u32[]{:S(2)}, u32[]{:S(2)}) collective-permute-start(bf16[2,224,768]{2,1,0:T(8,128)(2,1)S(1)} %gate.6.rest_3_.rest_7_), channel_id=1, source_target_pairs={{0,2},{2,4},{3,1},{4,6},{5,3},{7,5},{8,10},{10,12},{11,9},{12,14},... | collective-permute-start | bytes 2064392 | tf_op jit(solution)/shard_map/ppermute | solution.py:49
  50.4 15.9 %copy-start.3 = (bf16[27,768]{1,0:T(8,128)(2,1)S(1)}, bf16[27,768]{1,0:T(8,128)(2,1)}, u32[]{:S(2)}) copy-start(bf16[27,768]{1,0:T(8,128)(2,1)} %rest_3_.1) | copy-start | bytes 124420
  55.0 7.6 %collective-permute-start.13 = (f32[16,224]{1,0:T(8,128)S(1)}, f32[16,224]{1,0:T(8,128)S(1)}, u32[]{:S(2)}, u32[]{:S(2)}) collective-permute-start(f32[16,224]{1,0:T(8,128)S(1)} %get-tuple-element.40), channel_id=1, source_target_pairs={{0,0},{1,2},{2,1},{3,4},{4,3},{5,6},{6,5},{7,7},{8,8},{9,10},{10,9... | collective-permute-start | bytes 43016 | tf_op jit(solution)/shard_map/ppermute | solution.py:53
  55.6 6.9 %collective-permute-start.12 = (f32[16,224]{1,0:T(8,128)S(1)}, f32[16,224]{1,0:T(8,128)S(1)}, u32[]{:S(2)}, u32[]{:S(2)}) collective-permute-start(f32[16,224]{1,0:T(8,128)S(1)} %get-tuple-element.40), channel_id=1, source_target_pairs={{0,1},{1,0},{2,3},{3,2},{4,5},{5,4},{6,7},{7,6},{8,9},{9,8},{10,11... | collective-permute-start | bytes 43016 | tf_op jit(solution)/shard_map/ppermute | solution.py:45
  59.4 16.0 %collective-permute-start.20 = (bf16[2,224,768]{2,1,0:T(8,128)(2,1)S(1)}, bf16[2,224,768]{2,1,0:T(8,128)(2,1)S(1)}, u32[]{:S(2)}, u32[]{:S(2)}) collective-permute-start(bf16[2,224,768]{2,1,0:T(8,128)(2,1)S(1)} %gate.6.rest_3_.rest_7_), channel_id=1, source_target_pairs={{0,8},{8,0},{16,24},{24,16},{1,9},{9,1},{17,25},{25,17},{2,10},{10... | collective-permute-start | bytes 2064392 | tf_op jit(solution)/shard_map/ppermute | solution.py:57
  60.6 14.7 %collective-permute-start.21 = (bf16[2,224,768]{2,1,0:T(8,128)(2,1)S(1)}, bf16[2,224,768]{2,1,0:T(8,128)(2,1)S(1)}, u32[]{:S(2)}, u32[]{:S(2)}) collective-permute-start(bf16[2,224,768]{2,1,0:T(8,128)(2,1)S(1)} %gate.6.rest_3_.rest_7_), channel_id=1, source_target_pairs={{0,0},{8,16},{16,8},{24,24},{1,1},{9,17},{17,9},{25,25},{2,2},{10,... | collective-permute-start | bytes 2064392 | tf_op jit(solution)/shard_map/ppermute | solution.py:61
  62.6 10.8 %collective-permute-start.14 = (f32[3,16,224]{2,1,0:T(8,128)S(1)}, f32[3,16,224]{2,1,0:T(8,128)S(1)}, u32[]{:S(2)}, u32[]{:S(2)}) collective-permute-start(f32[3,16,224]{2,1,0:T(8,128)S(1)} %pad_maximum_fusion.1.rest_17_.stat_own), channel_id=1, source_target_pairs={{0,8},{8,0},{16,24},{24,16},{1,9},{9,1},{17,25},{25,17},{2,10},{10... | collective-permute-start | bytes 129032 | tf_op jit(solution)/shard_map/ppermute | solution.py:57
  62.7 10.7 %collective-permute-start.15 = (f32[3,16,224]{2,1,0:T(8,128)S(1)}, f32[3,16,224]{2,1,0:T(8,128)S(1)}, u32[]{:S(2)}, u32[]{:S(2)}) collective-permute-start(f32[3,16,224]{2,1,0:T(8,128)S(1)} %pad_maximum_fusion.1.rest_17_.stat_own), channel_id=1, source_target_pairs={{0,0},{8,16},{16,8},{24,24},{1,1},{9,17},{17,9},{25,25},{2,2},{10,... | collective-permute-start | bytes 129032 | tf_op jit(solution)/shard_map/ppermute | solution.py:61
  73.4 7.8 %collective-permute-start.18 = (bf16[2,224,768]{2,1,0:T(8,128)(2,1)S(1)}, bf16[2,224,768]{2,1,0:T(8,128)(2,1)S(1)}, u32[]{:S(2)}, u32[]{:S(2)}) collective-permute-start(bf16[2,224,768]{2,1,0:T(8,128)(2,1)S(1)} %gate.7.rest_0_), channel_id=1, source_target_pairs={{0,8},{8,0},{16,24},{24,16},{1,9},{9,1},{17,25},{25,17},{2,10},{10... | collective-permute-start | bytes 2064392 | tf_op jit(solution)/shard_map/ppermute | solution.py:57
  73.4 12.3 %collective-permute-start.19 = (bf16[2,224,768]{2,1,0:T(8,128)(2,1)S(1)}, bf16[2,224,768]{2,1,0:T(8,128)(2,1)S(1)}, u32[]{:S(2)}, u32[]{:S(2)}) collective-permute-start(bf16[2,224,768]{2,1,0:T(8,128)(2,1)S(1)} %gate.7.rest_0_), channel_id=1, source_target_pairs={{0,0},{8,16},{16,8},{24,24},{1,1},{9,17},{17,9},{25,25},{2,2},{10,... | collective-permute-start | bytes 2064392 | tf_op jit(solution)/shard_map/ppermute | solution.py:61

commit v5 on v4

--- a/solution.py
+++ b/solution.py
@@ -212,7 +212,7 @@
 
 def query_kernel(counts, width, grad_ref, weight_ref, *rest):
     slots, exps, factors = rest[:9], rest[9:12], rest[12:15]
-    att_ref, delta_ref, _, out_ref, dq_ref, done_ref = rest[15:]
+    att_ref, delta_ref, out_ref, dq_ref, done_ref = rest[15:]
     done_ref[...] = jnp.zeros_like(done_ref)
     _, _, place_now = place(counts)
     rows, channels = grad_ref.shape
@@ -243,26 +243,33 @@
     lax.fori_loop(0, heads // UNROLL, body, 0)
 
 
-def key_kernel(counts, width, columns, last, mask_ref, clip_ref, own, stat_own, stat_pair, stat_other, *rest):
+def key_kernel(counts, width, columns, last, mask_ref, clip_ref, own, stat_ref, *rest):
     count = 3 * len(columns)
     slots, rest = rest[:count], rest[count:]
     if last:
-        weight_ref, *edges, dk_sum, dv_sum, dk_ref, dv_ref, stats = rest
+        weight_ref, *edges, dk_sum, dv_sum, dk_ref, dv_ref, stats, landed, sems = rest
     else:
-        dk_ref, dv_ref, stats = rest
+        dk_ref, dv_ref, stats, landed, sems = rest
     index_t, index_h, place_now = place(counts)
     rows, channels = own.shape[1:]
     heads = channels // HEAD_DIM
     scale = HEAD_DIM**-0.5
     line = lax.broadcasted_iota(jnp.int32, (STAT_ROWS, rows), 0)
-    pieces = []
+    copies, kept = [], []
     for column in columns:
-        for slot, ref in enumerate((stat_own, stat_pair, stat_other)):
+        for slot in range(3):
             a, b = offsets(index_t)[slot], offsets(index_h)[column]
             t, h = index_t + a, index_h + b
             safe_t, safe_h = jnp.clip(t, 0, counts[0] - 1), jnp.clip(h, 0, counts[1] - 1)
-            kept = (mask_ref[safe_t, safe_h, 3 * (1 - a) + (1 - b)] == 1) & inside(t, counts[0]) & inside(h, counts[1])
-            pieces.append(jnp.where(kept | (line >= ROW_DELTA), ref[column], jnp.inf))
+            keep = mask_ref[safe_t, safe_h, 3 * (1 - a) + (1 - b)] == 1
+            kept.append(keep & inside(t, counts[0]) & inside(h, counts[1]))
+            i = len(copies)
+            copies.append(pltpu.make_async_copy(stat_ref.at[safe_t * counts[1] + safe_h], landed.at[i], sems.at[i]))
+    for copy in copies:
+        copy.start()
+    for copy in copies:
+        copy.wait()
+    pieces = [jnp.where(kept[i] | (line >= ROW_DELTA), landed[i], jnp.inf) for i in range(len(copies))]
     stats[...] = jnp.concatenate(pieces, axis=1)
     row = lax.broadcasted_iota(jnp.int32, (rows, HEAD_DIM), 0)
     lens = [clip_ref[2 * index_t + f] for f in range(2)]
@@ -316,11 +323,13 @@
     exps = jax.ShapeDtypeStruct((heads, rows, 3 * rows), jnp.bfloat16)
     bias = pltpu.VMEM((1, 3 * rows), jnp.float32)
 
+    stats = None
+
     def call(kernel, name, out_shape, scratch, work, *args):
         scalars = 2 if args[0] is tile_mask else 0
         return pl.pallas_call(
             kernel,
-            in_specs=[smem] * scalars + [vmem] * (len(args) - scalars),
+            in_specs=[smem] * scalars + [pl.BlockSpec(memory_space=pl.ANY) if x is stats else vmem for x in args[scalars:]],
             out_specs=[vmem] * len(out_shape),
             out_shape=out_shape,
             scratch_shapes=scratch,
@@ -333,6 +342,19 @@
         kernel = functools.partial(column_kernel, counts, width, column, False)
         work = cost(heads, rows, 2, 1)
         return call(kernel, f"scores_{column}", [exps, full, full, full], [bias], work, tile_mask, clip_lengths, query, *tiles)
+
+    def later(x, *earlier):
+        def kernel(x_ref, *rest):
+            rest[-1][...] = x_ref[...]
+
+        return pl.pallas_call(
+            kernel,
+            in_specs=[vmem] + [pl.BlockSpec(memory_space=pl.ANY)] * len(earlier),
+            out_specs=vmem,
+            out_shape=jax.ShapeDtypeStruct(x.shape, x.dtype),
+            compiler_params=pltpu.CompilerParams(vmem_limit_bytes=SMALL),
+            name="later",
+        )(x, *earlier)
 
     def pair_up(x, y, *earlier):
         def kernel(x_ref, y_ref, *rest):
@@ -359,25 +381,21 @@
             name="gate",
         )(x, *earlier)
 
-    near_k = ha_near(key)
-    near_v = ha_near(gate(value, near_k))
-    kv = pair_up(key, value)
-    kv_b = ta_other(kv)
-    far_k = ha_relay(near_k)
-    kv_a = ta_pair(kv)
+    kv = jnp.stack([key, value])
+    near_kv = ha_near(kv)
+    kv_a, kv_b = ta_pair(kv), ta_other(kv)
     qg = pair_up(query, grad, kv_a)
     qg_a, qg_b = ta_pair(qg), ta_other(qg)
     exp_own, *own_parts = scores(0, (kv, kv_a, kv_b))
 
-    near_v = gate(near_v, own_parts[0])
-    far_v = ha_relay(near_v)
-    near_kv = pair_up(near_k, near_v, qg_a, qg_b)
-    near_kv_a, near_kv_b = ta_pair(near_kv), ta_other(near_kv)
-    near_qg = ha_near(pair_up(query, grad, near_v))
-    far_kv = jnp.stack([far_k, far_v])
+    far_kv = ha_relay(near_kv)
+    near_kv_again = later(near_kv, qg_a, qg_b)
+    near_kv_a, near_kv_b = ta_pair(near_kv_again), ta_other(near_kv_again)
+    near_qg = ha_near(pair_up(query, grad, near_kv))
+    exp_near, *near_parts = scores(1, (near_kv, near_kv_a, near_kv_b))
+
+    far_kv = gate(far_kv, own_parts[0])
     far_kv_a, far_kv_b = ta_pair(far_kv), ta_other(far_kv)
-    exp_near, *near_parts = scores(1, (near_kv, near_kv_a, near_kv_b))
-
     near_qg = gate(near_qg, near_parts[0])
     far_qg = ha_relay(near_qg)
     near_qg_a, near_qg_b = ta_pair(near_qg), ta_other(near_qg)
@@ -389,8 +407,7 @@
         cost(heads, rows, 2, 1),
         tile_mask, clip_lengths, query, far_kv, far_kv_a, far_kv_b, grad, *own_parts, *near_parts,
     )
-    column = jnp.stack([stat, ha_near(stat), ha_far(stat)])
-    column_a, column_b = ta_pair(column), ta_other(column)
+    stats = lax.all_gather(stat, ("ta", "ha"))
     layer_out, query_grad, done = call(
         functools.partial(query_kernel, counts, width),
         "query_side",
@@ -398,27 +415,34 @@
         [],
         cost(heads, rows, 2, 3),
         grad, conv_weight, kv, near_kv, far_kv, kv_a, near_kv_a, far_kv_a, kv_b, near_kv_b, far_kv_b,
-        exp_own, exp_near, exp_far, fac_own, fac_near, fac_far, attention, delta, column,
+        exp_own, exp_near, exp_far, fac_own, fac_near, fac_far, attention, delta,
     )
-    far_qg = gate(far_qg, done, column_a, column_b)
+    far_qg = gate(far_qg, done)
     far_qg_a, far_qg_b = ta_pair(far_qg), ta_other(far_qg)
+
+    def stat_scratch(count):
+        return [
+            pltpu.VMEM((STAT_ROWS, count * rows), jnp.float32),
+            pltpu.VMEM((count, STAT_ROWS, rows), jnp.float32),
+            pltpu.SemaphoreType.DMA((count,)),
+        ]
 
     first = (qg, qg_a, qg_b, near_qg, near_qg_a, near_qg_b)
     dk_sum, dv_sum = call(
         functools.partial(key_kernel, counts, width, (0, 1), False),
         "key_side_0",
         [full, full],
-        [pltpu.VMEM((STAT_ROWS, 6 * rows), jnp.float32)],
+        stat_scratch(6),
         cost(heads, rows, 4, 2),
-        tile_mask, clip_lengths, kv, column, column_a, column_b, *first,
+        tile_mask, clip_lengths, kv, stats, *first,
     )
     key_grad, value_grad = call(
         functools.partial(key_kernel, counts, width, (2,), True),
         "key_side_1",
         [half, half],
-        [pltpu.VMEM((STAT_ROWS, 3 * rows), jnp.float32)],
+        stat_scratch(3),
         cost(heads, rows, 4, 1),
-        tile_mask, clip_lengths, kv, column, column_a, column_b, far_qg, far_qg_a, far_qg_b, conv_weight, *first, dk_sum, dv_sum,
+        tile_mask, clip_lengths, kv, stats, far_qg, far_qg_a, far_qg_b, conv_weight, *first, dk_sum, dv_sum,
     )
     return tuple(x.reshape(query_states.shape) for x in (layer_out, query_grad, key_grad, value_grad))
 

time: 92.3 us -> 149 us (1.61)
  the two profiles are of different devices: /device:TPU:1 before, /device:TPU:0 now
where the time goes in v5:
time: 149 us; the launch traced here: 148 us
  blocking collectives  70 us (47%)
  Pallas kernels  31.7 us (21%)
  waiting for transfers between devices  21.9 us (15%)
  starting transfers between devices  20.6 us (14%)
  local copies, waits for them, and re-layouts  1.99 us (1%)
    all_gather x1, blocking collectives, shards(): stats = lax.all_gather(stat, ('ta', 'ha'))  70 us
    pallas_call x6, Pallas kernels, call(): pl.pallas_call(kernel, in_specs=[smem] * scalars + [pl.BlockSpec(memory_s...  31.6 us
    ppermute x2, waiting for transfers between devices, ha_near(): return lax.ppermute(x, 'ha', flip_pairs(lax.axis_size('ha')))  12.3 us
    ppermute x2, waiting for transfers between devices, ha_relay(): return lax.ppermute(near, 'ha', relay_pairs(lax.axis_size('ha')))  9.58 us
    ppermute x2, starting transfers between devices, ha_relay(): return lax.ppermute(near, 'ha', relay_pairs(lax.axis_size('ha')))  8.21 us
    ppermute x6, starting transfers between devices, ta_pair(): return lax.ppermute(x, 'ta', flip_pairs(lax.axis_size('ta')))  5.44 us
    ppermute x6, starting transfers between devices, ta_other(): return lax.ppermute(x, 'ta', other_pairs(lax.axis_size('ta')))  4.31 us
  transfers between devices with their start and end apart: 16, of which 2 were waited for; matrix products, arithmetic and copies ran while one was open for 0% of the time, Pallas kernels for 17%

profile of v5, /device:TPU:0, one launch (start us, length us, event | category | flops | bytes accessed | tf_op | source)
XLA Modules:
  0.0 148.3 jit_solution(12325462683984038437)
XLA Ops:
  0.6 1.1 pad_maximum_fusion.own.rest_0_
  1.8 0.5 collective-permute-start.2
  2.3 2.6 %collective-permute-start = (bf16[2,224,768]{2,1,0:T(8,128)(2,1)S(1)}, bf16[2,224,768]{2,1,0:T(8,128)(2,1)S(1)}, u32[]{:S(2)}, u32[]{:S(2)}) collective-permute-start(bf16[2,224,768]{2,1,0:T(8,128)(2,1)S(1)} %pad_maximum_fusion.own.rest_0_), channel_id=1, source_target_pairs={{0,1},{1,0},{2,3},{3,2},{4,5},{5,4},{6,7},{7,6},{8,9},{9,8},{10,11... | collective-permute-start | bytes 2064392 | tf_op jit(solution)/shard_map/ppermute | solution.py:45
  4.9 0.0 collective-permute-done.2.pair.rest_0_.rest_3_
  4.9 0.0 copy-start
  4.9 1.0 copy-done
  5.8 0.0 copy-start.2
  5.8 1.0 copy-done.2
  6.9 0.0 copy-start.1
  6.9 0.0 copy-start.4
  6.9 0.0 copy-start.6
  6.9 0.2 collective-permute-start.4
  7.1 0.7 collective-permute-start.5
  7.8 0.7 collective-permute-start.3
  8.6 12.3 %collective-permute-done.x_ref.own.rest_1_.rest_0_ = bf16[2,224,768]{2,1,0:T(8,128)(2,1)S(1)} collective-permute-done((bf16[2,224,768]{2,1,0:T(8,128)(2,1)S(1)}, bf16[2,224,768]{2,1,0:T(8,128)(2,1)S(1)}, u32[]{:S(2)}, u32[]{:S(2)}) %collective-permute-start) | collective-permute-done | bytes 688160 | tf_op jit(solution)/shard_map/ppermute | solution.py:45
  20.9 3.8 %collective-permute-start.1 = (bf16[2,224,768]{2,1,0:T(8,128)(2,1)S(1)}, bf16[2,224,768]{2,1,0:T(8,128)(2,1)S(1)}, u32[]{:S(2)}, u32[]{:S(2)}) collective-permute-start(bf16[2,224,768]{2,1,0:T(8,128)(2,1)S(1)} %collective-permute-done.x_ref.own.rest_1_.rest_0_), channel_id=1, source_target_pairs={{0,2},{2,4},{3,1},{4,6},{5,3},{7,5},{8,10},{10,12},{11,9},{12,14},... | collective-permute-start | bytes 2064392 | tf_op jit(solution)/shard_map/ppermute | solution.py:49
  24.7 0.0 collective-permute-done.4.rest_0_.rest_1_.rest_5_
  24.7 0.0 collective-permute-done.5.rest_1_.rest_2_.rest_6_
  24.8 0.1 collective-permute-start.6
  24.8 0.7 collective-permute-start.8
  25.6 0.1 collective-permute-start.10
  25.7 0.0 collective-permute-done.3.other.rest_6_
  25.7 0.0 copy-done.1
  25.7 0.0 copy-done.4
  25.7 0.0 copy-done.6
  25.7 3.8 %scores_0.1 = (bf16[6,224,672]{2,1,0:T(8,128)(2,1)S(1)}, f32[224,768]{1,0:T(8,128)S(1)}, f32[224,768]{1,0:T(8,128)S(1)}, f32[224,768]{1,0:T(8,128)S(1)}) custom-call(s32[4,8,9]{2,1,0:T(8,128)S(1)} %copy-done.4, s32[8]{0:T(128)S(1)} %copy-done.6, bf16[224,768]{1,0:T(8,128)(2,1)S(1)} %bitcast.11, bf16[2,224,768]{2,1,0:T(8,128)(2,1)S(1)} %pad_maximum_fusion.own.rest_0_, ...), custom_call_target="tpu_custom_call" | custom-call | flops 462422016 | bytes 2752512 | tf_op jit(solution)/shard_map/scores_0/pallas_call | solution.py:330
  29.6 9.6 %collective-permute-done.1.refs_0_ = bf16[2,224,768]{2,1,0:T(8,128)(2,1)S(1)} collective-permute-done((bf16[2,224,768]{2,1,0:T(8,128)(2,1)S(1)}, bf16[2,224,768]{2,1,0:T(8,128)(2,1)S(1)}, u32[]{:S(2)}, u32[]{:S(2)}) %collective-permute-start.1) | collective-permute-done | bytes 688160 | tf_op jit(solution)/shard_map/ppermute | solution.py:49
  39.1 0.0 copy-start.3
  39.1 0.0 collective-permute-start.7
  39.1 0.8 collective-permute-start.9
  40.0 0.0 collective-permute-done.6.pair.rest_4_
  40.0 0.0 collective-permute-done.8.other.rest_7_
  40.0 3.8 %scores_1.1 = (bf16[6,224,672]{2,1,0:T(8,128)(2,1)S(1)}, f32[224,768]{1,0:T(8,128)S(1)}, f32[224,768]{1,0:T(8,128)S(1)}, f32[224,768]{1,0:T(8,128)S(1)}) custom-call(s32[4,8,9]{2,1,0:T(8,128)S(1)} %copy-done.4, s32[8]{0:T(128)S(1)} %copy-done.6, bf16[224,768]{1,0:T(8,128)(2,1)S(1)} %bitcast.12, ...), custom_call_target="tpu_custom_call" | custom-call | flops 462422016 | bytes 2752512 | tf_op jit(solution)/shard_map/scores_1/pallas_call | solution.py:330
  43.8 0.0 collective-permute-done.10.refs_0_
  43.9 4.4 %collective-permute-start.11 = (bf16[2,224,768]{2,1,0:T(8,128)(2,1)S(1)}, bf16[2,224,768]{2,1,0:T(8,128)(2,1)S(1)}, u32[]{:S(2)}, u32[]{:S(2)}) collective-permute-start(bf16[2,224,768]{2,1,0:T(8,128)(2,1)S(1)} %gate.4.rest_3_.rest_7_), channel_id=1, source_target_pairs={{0,2},{2,4},{3,1},{4,6},{5,3},{7,5},{8,10},{10,12},{11,9},{12,14},... | collective-permute-start | bytes 2064392 | tf_op jit(solution)/shard_map/ppermute | solution.py:49
  48.3 2.6 %collective-permute-start.14 = (bf16[2,224,768]{2,1,0:T(8,128)(2,1)S(1)}, bf16[2,224,768]{2,1,0:T(8,128)(2,1)S(1)}, u32[]{:S(2)}, u32[]{:S(2)}) collective-permute-start(bf16[2,224,768]{2,1,0:T(8,128)(2,1)S(1)} %gate.4.rest_3_.rest_7_), channel_id=1, source_target_pairs={{0,8},{8,0},{16,24},{24,16},{1,9},{9,1},{17,25},{25,17},{2,10},{10... | collective-permute-start | bytes 2064392 | tf_op jit(solution)/shard_map/ppermute | solution.py:57
  50.9 0.7 collective-permute-start.15
  51.6 0.0 collective-permute-done.7.pair.rest_5_
  51.6 0.0 collective-permute-done.9.other.rest_8_
  51.6 0.0 copy-done.3
  51.7 0.0 copy-start.5
  51.7 4.5 %scores_2.1 = (bf16[6,224,672]{2,1,0:T(8,128)(2,1)S(1)}, f32[224,768]{1,0:T(8,128)S(1)}, f32[224,768]{1,0:T(8,128)S(1)}, f32[224,768]{1,0:T(8,128)S(1)}, f32[224...) custom-call(s32[4,8,9]{2,1,0:T(8,128)S(1)} %copy-done.4, s32[8]{0:T(128)S(1)} %copy-done.6, ...), custom_call_target="tpu_custom_call" | custom-call | flops 462422016 | bytes 2752512 | tf_op jit(solution)/shard_map/scores_2/pallas_call | solution.py:330
  56.2 0.0 copy-done.5
  56.2 7.0 %query_side.1 = (bf16[224,768]{1,0:T(8,128)(2,1)}, bf16[224,768]{1,0:T(8,128)(2,1)}, f32[8,128]{1,0:T(8,128)S(1)}) custom-call(bf16[224,768]{1,0:T(8,128)(2,1)S(1)} %bitcast.17, bf16[27,768]{1,0:T(8,128)(2,1)S(1)} %copy-done.5, bf16[2,224,768]{2,1,0:T(8,128)(2,1)S(1)} %pad_maximum_fusion.own.rest_0_, ...), custom_call_target="tpu_custom_call" | custom-call | flops 1387266048 | bytes 8257536 | tf_op jit(solution)/shard_map/query_side/pallas_call | solution.py:330
  63.2 0.0 collective-permute-done.11.refs_0_
  63.2 2.0 %collective-permute-start.12 = (bf16[2,224,768]{2,1,0:T(8,128)(2,1)S(1)}, bf16[2,224,768]{2,1,0:T(8,128)(2,1)S(1)}, u32[]{:S(2)}, u32[]{:S(2)}) collective-permute-start(bf16[2,224,768]{2,1,0:T(8,128)(2,1)S(1)} %gate.5.rest_0_), channel_id=1, source_target_pairs={{0,8},{8,0},{16,24},{24,16},{1,9},{9,1},{17,25},{25,17},{2,10},{10... | collective-permute-start | bytes 2064392 | tf_op jit(solution)/shard_map/ppermute | solution.py:57
  65.2 0.7 collective-permute-start.13
  65.9 70.0 %all-gather = f32[512,224]{1,0:T(8,128)S(1)} all-gather(f32[16,224]{1,0:T(8,128)S(1)} %get-tuple-element.42), channel_id=2, replica_groups=mesh['ta'=4,'ha'=8] {'ta','ha'}, dimensions={0}, use_global_device_ids=true | all-gather | bytes 473088 | tf_op jit(solution)/shard_map/all_gather | solution.py:410
  135.9 0.0 collective-permute-done.14.rest_4_.rest_8_
  135.9 0.0 collective-permute-done.15.rest_5_.rest_9_
  135.9 6.0 %key_side_0.1 = (f32[224,768]{1,0:T(8,128)S(1)}, f32[224,768]{1,0:T(8,128)S(1)}) custom-call(s32[4,8,9]{2,1,0:T(8,128)S(1)} %copy-done.4, s32[8]{0:T(128)S(1)} %copy-done.6, bf16[2,224,768]{2,1,0:T(8,128)(2,1)S(1)} %pad_maximum_fusion.own.rest_0_, f32[32,16,224]{2,1,0:T(8,128)S(1)} %bitcast.18, bf16[2,224,768]{2,1,0:T(8,128)(2,1)S(1)} %pair_up.2.rest_0_.rest_4_, ...), custom_call_target="tpu_custom_call" | custom-call | flops 1849688064 | bytes 5505024 | tf_op jit(solution)/shard_map/key_side_0/pallas_call | solution.py:330
  141.9 0.0 collective-permute-done.12.rest_1_
  141.9 0.0 collective-permute-done.13.rest_2_
  142.0 6.4 %key_side_1.1 = (bf16[224,768]{1,0:T(8,128)(2,1)}, bf16[224,768]{1,0:T(8,128)(2,1)}) custom-call(s32[4,8,9]{2,1,0:T(8,128)S(1)} %copy-done.4, s32[8]{0:T(128)S(1)} %copy-done.6, bf16[2,224,768]{2,1,0:T(8,128)(2,1)S(1)} %pad_maximum_fusion.own.rest_0_, f32[32,16,224]{2,1,0:T(8,128)S(1)} %bitcast.19, bf16[2,224,768]{2,1,0:T(8,128)(2,1)S(1)} %gate.5.rest_0_, ...), custom_call_target="tpu_custom_call" | custom-call | flops 924844032 | bytes 2752512 | tf_op jit(solution)/shard_map/key_side_1/pallas_call | solution.py:330
  (6 shorter events, 0.1 us)
Async XLA Ops:
  1.8 3.1 %collective-permute-start.2 = (bf16[2,224,768]{2,1,0:T(8,128)(2,1)S(1)}, bf16[2,224,768]{2,1,0:T(8,128)(2,1)S(1)}, u32[]{:S(2)}, u32[]{:S(2)}) collective-permute-start(bf16[2,224,768]{2,1,0:T(8,128)(2,1)S(1)} %pad_maximum_fusion.own.rest_0_), channel_id=1, source_target_pairs={{0,8},{8,0},{16,24},{24,16},{1,9},{9,1},{17,25},{25,17},{2,10},{10... | collective-permute-start | bytes 2064392 | tf_op jit(solution)/shard_map/ppermute | solution.py:57
  2.3 18.6 %collective-permute-start = (bf16[2,224,768]{2,1,0:T(8,128)(2,1)S(1)}, bf16[2,224,768]{2,1,0:T(8,128)(2,1)S(1)}, u32[]{:S(2)}, u32[]{:S(2)}) collective-permute-start(bf16[2,224,768]{2,1,0:T(8,128)(2,1)S(1)} %pad_maximum_fusion.own.rest_0_), channel_id=1, source_target_pairs={{0,1},{1,0},{2,3},{3,2},{4,5},{5,4},{6,7},{7,6},{8,9},{9,8},{10,11... | collective-permute-start | bytes 2064392 | tf_op jit(solution)/shard_map/ppermute | solution.py:45
  4.9 1.0 copy-start
  5.8 1.0 copy-start.2
  6.9 18.8 %copy-start.1 = (bf16[2,2,56,768]{3,2,1,0:T(8,128)(2,1)S(1)}, bf16[2,2,56,768]{3,2,1,0:T(8,128)(2,1)}, u32[]{:S(2)}) copy-start(bf16[2,2,56,768]{3,2,1,0:T(8,128)(2,1)} %param.7) | copy-start | bytes 1032196
  6.9 18.8 %copy-start.4 = (s32[4,8,9]{2,1,0:T(8,128)S(1)}, s32[4,8,9]{2,1,0:T(8,128)}, u32[]{:S(2)}) copy-start(s32[4,8,9]{2,1,0:T(8,128)} %mask_ref.9) | copy-start | bytes 3460
  6.9 18.8 %copy-start.6 = (s32[8]{0:T(128)S(1)}, s32[8]{0:T(128)}, u32[]{:S(2)}) copy-start(s32[8]{0:T(128)} %clip_ref.9) | copy-start | bytes 100
  6.9 17.8 %collective-permute-start.4 = (bf16[2,224,768]{2,1,0:T(8,128)(2,1)S(1)}, bf16[2,224,768]{2,1,0:T(8,128)(2,1)S(1)}, u32[]{:S(2)}, u32[]{:S(2)}) collective-permute-start(bf16[2,224,768]{2,1,0:T(8,128)(2,1)S(1)} %pair_up.2.rest_0_.rest_4_), channel_id=1, source_target_pairs={{0,8},{8,0},{16,24},{24,16},{1,9},{9,1},{17,25},{25,17},{2,10},{10... | collective-permute-start | bytes 2064392 | tf_op jit(solution)/shard_map/ppermute | solution.py:57
  7.1 17.5 %collective-permute-start.5 = (bf16[2,224,768]{2,1,0:T(8,128)(2,1)S(1)}, bf16[2,224,768]{2,1,0:T(8,128)(2,1)S(1)}, u32[]{:S(2)}, u32[]{:S(2)}) collective-permute-start(bf16[2,224,768]{2,1,0:T(8,128)(2,1)S(1)} %pair_up.2.rest_0_.rest_4_), channel_id=1, source_target_pairs={{0,0},{8,16},{16,8},{24,24},{1,1},{9,17},{17,9},{25,25},{2,2},{10,... | collective-permute-start | bytes 2064392 | tf_op jit(solution)/shard_map/ppermute | solution.py:61
  7.8 17.8 %collective-permute-start.3 = (bf16[2,224,768]{2,1,0:T(8,128)(2,1)S(1)}, bf16[2,224,768]{2,1,0:T(8,128)(2,1)S(1)}, u32[]{:S(2)}, u32[]{:S(2)}) collective-permute-start(bf16[2,224,768]{2,1,0:T(8,128)(2,1)S(1)} %pad_maximum_fusion.own.rest_0_), channel_id=1, source_target_pairs={{0,0},{8,16},{16,8},{24,24},{1,1},{9,17},{17,9},{25,25},{2,2},{10,... | collective-permute-start | bytes 2064392 | tf_op jit(solution)/shard_map/ppermute | solution.py:61
  20.9 18.2 %collective-permute-start.1 = (bf16[2,224,768]{2,1,0:T(8,128)(2,1)S(1)}, bf16[2,224,768]{2,1,0:T(8,128)(2,1)S(1)}, u32[]{:S(2)}, u32[]{:S(2)}) collective-permute-start(bf16[2,224,768]{2,1,0:T(8,128)(2,1)S(1)} %collective-permute-done.x_ref.own.rest_1_.rest_0_), channel_id=1, source_target_pairs={{0,2},{2,4},{3,1},{4,6},{5,3},{7,5},{8,10},{10,12},{11,9},{12,14},... | collective-permute-start | bytes 2064392 | tf_op jit(solution)/shard_map/ppermute | solution.py:49
  24.8 15.2 %collective-permute-start.6 = (bf16[2,224,768]{2,1,0:T(8,128)(2,1)S(1)}, bf16[2,224,768]{2,1,0:T(8,128)(2,1)S(1)}, u32[]{:S(2)}, u32[]{:S(2)}) collective-permute-start(bf16[2,224,768]{2,1,0:T(8,128)(2,1)S(1)} %later.1), channel_id=1, source_target_pairs={{0,8},{8,0},{16,24},{24,16},{1,9},{9,1},{17,25},{25,17},{2,10},{10... | collective-permute-start | bytes 2064392 | tf_op jit(solution)/shard_map/ppermute | solution.py:57
  24.8 15.2 %collective-permute-start.8 = (bf16[2,224,768]{2,1,0:T(8,128)(2,1)S(1)}, bf16[2,224,768]{2,1,0:T(8,128)(2,1)S(1)}, u32[]{:S(2)}, u32[]{:S(2)}) collective-permute-start(bf16[2,224,768]{2,1,0:T(8,128)(2,1)S(1)} %later.1), channel_id=1, source_target_pairs={{0,0},{8,16},{16,8},{24,24},{1,1},{9,17},{17,9},{25,25},{2,2},{10,... | collective-permute-start | bytes 2064392 | tf_op jit(solution)/shard_map/ppermute | solution.py:61
  25.6 18.2 %collective-permute-start.10 = (bf16[2,224,768]{2,1,0:T(8,128)(2,1)S(1)}, bf16[2,224,768]{2,1,0:T(8,128)(2,1)S(1)}, u32[]{:S(2)}, u32[]{:S(2)}) collective-permute-start(bf16[2,224,768]{2,1,0:T(8,128)(2,1)S(1)} %pair_up.3), channel_id=1, source_target_pairs={{0,1},{1,0},{2,3},{3,2},{4,5},{5,4},{6,7},{7,6},{8,9},{9,8},{10,11... | collective-permute-start | bytes 2064392 | tf_op jit(solution)/shard_map/ppermute | solution.py:45
  39.1 12.5 %copy-start.3 = (bf16[2,2,56,768]{3,2,1,0:T(8,128)(2,1)S(1)}, bf16[2,2,56,768]{3,2,1,0:T(8,128)(2,1)}, u32[]{:S(2)}) copy-start(bf16[2,2,56,768]{3,2,1,0:T(8,128)(2,1)} %param.11) | copy-start | bytes 1032196
  39.1 12.5 %collective-permute-start.7 = (bf16[2,224,768]{2,1,0:T(8,128)(2,1)S(1)}, bf16[2,224,768]{2,1,0:T(8,128)(2,1)S(1)}, u32[]{:S(2)}, u32[]{:S(2)}) collective-permute-start(bf16[2,224,768]{2,1,0:T(8,128)(2,1)S(1)} %gate.3.own.rest_2_), channel_id=1, source_target_pairs={{0,8},{8,0},{16,24},{24,16},{1,9},{9,1},{17,25},{25,17},{2,10},{10... | collective-permute-start | bytes 2064392 | tf_op jit(solution)/shard_map/ppermute | solution.py:57
  39.1 12.5 %collective-permute-start.9 = (bf16[2,224,768]{2,1,0:T(8,128)(2,1)S(1)}, bf16[2,224,768]{2,1,0:T(8,128)(2,1)S(1)}, u32[]{:S(2)}, u32[]{:S(2)}) collective-permute-start(bf16[2,224,768]{2,1,0:T(8,128)(2,1)S(1)} %gate.3.own.rest_2_), channel_id=1, source_target_pairs={{0,0},{8,16},{16,8},{24,24},{1,1},{9,17},{17,9},{25,25},{2,2},{10,... | collective-permute-start | bytes 2064392 | tf_op jit(solution)/shard_map/ppermute | solution.py:61
  43.9 19.3 %collective-permute-start.11 = (bf16[2,224,768]{2,1,0:T(8,128)(2,1)S(1)}, bf16[2,224,768]{2,1,0:T(8,128)(2,1)S(1)}, u32[]{:S(2)}, u32[]{:S(2)}) collective-permute-start(bf16[2,224,768]{2,1,0:T(8,128)(2,1)S(1)} %gate.4.rest_3_.rest_7_), channel_id=1, source_target_pairs={{0,2},{2,4},{3,1},{4,6},{5,3},{7,5},{8,10},{10,12},{11,9},{12,14},... | collective-permute-start | bytes 2064392 | tf_op jit(solution)/shard_map/ppermute | solution.py:49
  48.3 87.6 %collective-permute-start.14 = (bf16[2,224,768]{2,1,0:T(8,128)(2,1)S(1)}, bf16[2,224,768]{2,1,0:T(8,128)(2,1)S(1)}, u32[]{:S(2)}, u32[]{:S(2)}) collective-permute-start(bf16[2,224,768]{2,1,0:T(8,128)(2,1)S(1)} %gate.4.rest_3_.rest_7_), channel_id=1, source_target_pairs={{0,8},{8,0},{16,24},{24,16},{1,9},{9,1},{17,25},{25,17},{2,10},{10... | collective-permute-start | bytes 2064392 | tf_op jit(solution)/shard_map/ppermute | solution.py:57
  50.9 85.0 %collective-permute-start.15 = (bf16[2,224,768]{2,1,0:T(8,128)(2,1)S(1)}, bf16[2,224,768]{2,1,0:T(8,128)(2,1)S(1)}, u32[]{:S(2)}, u32[]{:S(2)}) collective-permute-start(bf16[2,224,768]{2,1,0:T(8,128)(2,1)S(1)} %gate.4.rest_3_.rest_7_), channel_id=1, source_target_pairs={{0,0},{8,16},{16,8},{24,24},{1,1},{9,17},{17,9},{25,25},{2,2},{10,... | collective-permute-start | bytes 2064392 | tf_op jit(solution)/shard_map/ppermute | solution.py:61
  51.7 4.5 %copy-start.5 = (bf16[27,768]{1,0:T(8,128)(2,1)S(1)}, bf16[27,768]{1,0:T(8,128)(2,1)}, u32[]{:S(2)}) copy-start(bf16[27,768]{1,0:T(8,128)(2,1)} %rest_3_.1) | copy-start | bytes 124420
  63.2 78.7 %collective-permute-start.12 = (bf16[2,224,768]{2,1,0:T(8,128)(2,1)S(1)}, bf16[2,224,768]{2,1,0:T(8,128)(2,1)S(1)}, u32[]{:S(2)}, u32[]{:S(2)}) collective-permute-start(bf16[2,224,768]{2,1,0:T(8,128)(2,1)S(1)} %gate.5.rest_0_), channel_id=1, source_target_pairs={{0,8},{8,0},{16,24},{24,16},{1,9},{9,1},{17,25},{25,17},{2,10},{10... | collective-permute-start | bytes 2064392 | tf_op jit(solution)/shard_map/ppermute | solution.py:57
  65.2 76.8 %collective-permute-start.13 = (bf16[2,224,768]{2,1,0:T(8,128)(2,1)S(1)}, bf16[2,224,768]{2,1,0:T(8,128)(2,1)S(1)}, u32[]{:S(2)}, u32[]{:S(2)}) collective-permute-start(bf16[2,224,768]{2,1,0:T(8,128)(2,1)S(1)} %gate.5.rest_0_), channel_id=1, source_target_pairs={{0,0},{8,16},{16,8},{24,24},{1,1},{9,17},{17,9},{25,25},{2,2},{10,... | collective-permute-start | bytes 2064392 | tf_op jit(solution)/shard_map/ppermute | solution.py:61

commit v6 on v4

--- a/solution.py
+++ b/solution.py
@@ -11,6 +11,7 @@
 LOG2E = 1.4426950408889634
 ROW_DELTA = 8
 STAT_ROWS = 16
+STAT_LANES = 256
 UNROLL = 2
 FLOOR = -1e30
 SMALL = 2 * 1024 * 1024
@@ -212,7 +213,7 @@
 
 def query_kernel(counts, width, grad_ref, weight_ref, *rest):
     slots, exps, factors = rest[:9], rest[9:12], rest[12:15]
-    att_ref, delta_ref, _, out_ref, dq_ref, done_ref = rest[15:]
+    att_ref, delta_ref, _, _, out_ref, dq_ref, done_ref = rest[15:]
     done_ref[...] = jnp.zeros_like(done_ref)
     _, _, place_now = place(counts)
     rows, channels = grad_ref.shape
@@ -243,26 +244,49 @@
     lax.fori_loop(0, heads // UNROLL, body, 0)
 
 
-def key_kernel(counts, width, columns, last, mask_ref, clip_ref, own, stat_own, stat_pair, stat_other, *rest):
-    count = 3 * len(columns)
-    slots, rest = rest[:count], rest[count:]
-    if last:
-        weight_ref, *edges, dk_sum, dv_sum, dk_ref, dv_ref, stats = rest
-    else:
-        dk_ref, dv_ref, stats = rest
+def pack_kernel(rows, qg_ref, own_ref, near_ref, far_ref, *rest):
+    out_ref = rest[-1]
+    out_ref[:rows] = qg_ref[0]
+    out_ref[rows : 2 * rows] = qg_ref[1]
+    first = 2 * rows
+    out_ref[first:] = jnp.zeros(out_ref[first:].shape, jnp.bfloat16)
+    for i, ref in enumerate((own_ref, near_ref, far_ref)):
+        left = ref[...]
+        for part in range(3):
+            high = left.astype(jnp.bfloat16)
+            out_ref[first + part * STAT_ROWS : first + (part + 1) * STAT_ROWS, i * STAT_LANES : i * STAT_LANES + rows] = high
+            left = left - high.astype(jnp.float32)
+
+
+def key_kernel(counts, width, slot_t, mask_ref, clip_ref, own, own_ref, near_ref, far_ref, *rest):
+    first, last = slot_t == 0, slot_t == 2
     index_t, index_h, place_now = place(counts)
     rows, channels = own.shape[1:]
     heads = channels // HEAD_DIM
     scale = HEAD_DIM**-0.5
+
+    def packed(ref, what, cols):
+        return ref[what * rows : (what + 1) * rows, cols] if len(ref.shape) == 2 else ref[what, :, cols]
+
+    if first:
+        *stat_refs, dk_ref, dv_ref, stats = rest
+        pieces = [ref[...] for ref in stat_refs]
+    else:
+        dk_sum, dv_sum, *edges, dk_ref, dv_ref, stats = rest
+        pieces = []
+        for i in range(3):
+            parts = []
+            for part in range(3):
+                start = 2 * rows + part * STAT_ROWS
+                parts.append(far_ref[start : start + STAT_ROWS, i * STAT_LANES : i * STAT_LANES + rows].astype(jnp.float32))
+            pieces.append(parts[0] + (parts[1] + parts[2]))
     line = lax.broadcasted_iota(jnp.int32, (STAT_ROWS, rows), 0)
-    pieces = []
-    for column in columns:
-        for slot, ref in enumerate((stat_own, stat_pair, stat_other)):
-            a, b = offsets(index_t)[slot], offsets(index_h)[column]
-            t, h = index_t + a, index_h + b
-            safe_t, safe_h = jnp.clip(t, 0, counts[0] - 1), jnp.clip(h, 0, counts[1] - 1)
-            kept = (mask_ref[safe_t, safe_h, 3 * (1 - a) + (1 - b)] == 1) & inside(t, counts[0]) & inside(h, counts[1])
-            pieces.append(jnp.where(kept | (line >= ROW_DELTA), ref[column], jnp.inf))
+    for column in range(3):
+        a, b = offsets(index_t)[slot_t], offsets(index_h)[column]
+        t, h = index_t + a, index_h + b
+        safe_t, safe_h = jnp.clip(t, 0, counts[0] - 1), jnp.clip(h, 0, counts[1] - 1)
+        kept = (mask_ref[safe_t, safe_h, 3 * (1 - a) + (1 - b)] == 1) & inside(t, counts[0]) & inside(h, counts[1])
+        pieces[column] = jnp.where(kept | (line >= ROW_DELTA), pieces[column], jnp.inf)
     stats[...] = jnp.concatenate(pieces, axis=1)
     row = lax.broadcasted_iota(jnp.int32, (rows, HEAD_DIM), 0)
     lens = [clip_ref[2 * index_t + f] for f in range(2)]
@@ -272,24 +296,24 @@
         for u in range(UNROLL):
             head = step * UNROLL + u
             cols = head_columns(head)
-            queries = jnp.concatenate([ref[0, :, cols] for ref in slots], axis=0)
-            grads = jnp.concatenate([ref[1, :, cols] for ref in slots], axis=0)
+            queries = jnp.concatenate([packed(ref, 0, cols) for ref in (own_ref, near_ref, far_ref)], axis=0)
+            grads = jnp.concatenate([packed(ref, 1, cols) for ref in (own_ref, near_ref, far_ref)], axis=0)
             s = dot_last(own[0, :, cols], queries)
             p = jnp.exp2(s * (scale * LOG2E) - stats[pl.ds(head, 1), :])
             dp = dot_last(own[1, :, cols], grads)
             ds = (p * (dp - stats[pl.ds(head + ROW_DELTA, 1), :])).astype(jnp.bfloat16)
             dv = dot(p.astype(jnp.bfloat16), grads)
             dk = dot(ds, queries)
+            if not first:
+                dk, dv = dk + dk_sum[:, cols], dv + dv_sum[:, cols]
             if not last:
                 dk_ref[:, cols], dv_ref[:, cols] = dk, dv
                 continue
-            dk = jnp.where(live, (dk + dk_sum[:, cols]) * scale, 0.0)
-            dv = jnp.where(live, dv + dv_sum[:, cols], 0.0)
-            dk_ref[:, cols] = dk.astype(jnp.bfloat16)
-            around = [edges[0], edges[3], slots[0], edges[1], edges[4], slots[1], edges[2], edges[5], slots[2]]
-            slab = halo_slab(lambda slot: around[slot][1, :, cols], place_now, width)
-            conv = depthwise(slab, weight_ref[:, cols].astype(jnp.float32), True, width)
-            dv_ref[:, cols] = (dv + conv).astype(jnp.bfloat16)
+            dk_ref[:, cols] = jnp.where(live, dk * scale, 0.0).astype(jnp.bfloat16)
+            around = (*edges[1:], own_ref, near_ref, far_ref)
+            slab = halo_slab(lambda slot: packed(around[slot], 1, cols), place_now, width)
+            conv = depthwise(slab, edges[0][:, cols].astype(jnp.float32), True, width)
+            dv_ref[:, cols] = (jnp.where(live, dv, 0.0) + conv).astype(jnp.bfloat16)
         return 0
 
     lax.fori_loop(0, heads // UNROLL, body, 0)
@@ -334,6 +358,19 @@
         work = cost(heads, rows, 2, 1)
         return call(kernel, f"scores_{column}", [exps, full, full, full], [bias], work, tile_mask, clip_lengths, query, *tiles)
 
+    def later(x, *earlier):
+        def kernel(x_ref, *rest):
+            rest[-1][...] = x_ref[...]
+
+        return pl.pallas_call(
+            kernel,
+            in_specs=[vmem] + [pl.BlockSpec(memory_space=pl.ANY)] * len(earlier),
+            out_specs=vmem,
+            out_shape=jax.ShapeDtypeStruct(x.shape, x.dtype),
+            compiler_params=pltpu.CompilerParams(vmem_limit_bytes=SMALL),
+            name="later",
+        )(x, *earlier)
+
     def pair_up(x, y, *earlier):
         def kernel(x_ref, y_ref, *rest):
             rest[-1][0] = x_ref[...]
@@ -360,18 +397,17 @@
         )(x, *earlier)
 
     near_k = ha_near(key)
-    near_v = ha_near(gate(value, near_k))
-    kv = pair_up(key, value)
-    kv_b = ta_other(kv)
-    far_k = ha_relay(near_k)
-    kv_a = ta_pair(kv)
+    kv = jnp.stack([key, value])
+    kv_a, kv_b = ta_pair(kv), ta_other(kv)
     qg = pair_up(query, grad, kv_a)
     qg_a, qg_b = ta_pair(qg), ta_other(qg)
+    near_v = ha_near(later(value, near_k))
+    far_k = ha_relay(near_k)
     exp_own, *own_parts = scores(0, (kv, kv_a, kv_b))
 
     near_v = gate(near_v, own_parts[0])
     far_v = ha_relay(near_v)
-    near_kv = pair_up(near_k, near_v, qg_a, qg_b)
+    near_kv = pair_up(near_k, near_v, qg_a, qg_b, far_k)
     near_kv_a, near_kv_b = ta_pair(near_kv), ta_other(near_kv)
     near_qg = ha_near(pair_up(query, grad, near_v))
     far_kv = jnp.stack([far_k, far_v])
@@ -389,8 +425,7 @@
         cost(heads, rows, 2, 1),
         tile_mask, clip_lengths, query, far_kv, far_kv_a, far_kv_b, grad, *own_parts, *near_parts,
     )
-    column = jnp.stack([stat, ha_near(stat), ha_far(stat)])
-    column_a, column_b = ta_pair(column), ta_other(column)
+    near_stat, far_stat = ha_near(stat), ha_far(stat)
     layer_out, query_grad, done = call(
         functools.partial(query_kernel, counts, width),
         "query_side",
@@ -398,27 +433,32 @@
         [],
         cost(heads, rows, 2, 3),
         grad, conv_weight, kv, near_kv, far_kv, kv_a, near_kv_a, far_kv_a, kv_b, near_kv_b, far_kv_b,
-        exp_own, exp_near, exp_far, fac_own, fac_near, fac_far, attention, delta, column,
-    )
-    far_qg = gate(far_qg, done, column_a, column_b)
-    far_qg_a, far_qg_b = ta_pair(far_qg), ta_other(far_qg)
-
-    first = (qg, qg_a, qg_b, near_qg, near_qg_a, near_qg_b)
-    dk_sum, dv_sum = call(
-        functools.partial(key_kernel, counts, width, (0, 1), False),
-        "key_side_0",
-        [full, full],
-        [pltpu.VMEM((STAT_ROWS, 6 * rows), jnp.float32)],
-        cost(heads, rows, 4, 2),
-        tile_mask, clip_lengths, kv, column, column_a, column_b, *first,
+        exp_own, exp_near, exp_far, fac_own, fac_near, fac_far, attention, delta, near_stat, far_stat,
+    )
+    message = pl.pallas_call(
+        functools.partial(pack_kernel, rows),
+        in_specs=[vmem] * 4 + [pl.BlockSpec(memory_space=pl.ANY)] * 3,
+        out_specs=vmem,
+        out_shape=jax.ShapeDtypeStruct((2 * rows + 3 * STAT_ROWS, channels), jnp.bfloat16),
+        compiler_params=pltpu.CompilerParams(vmem_limit_bytes=SMALL),
+        name="pack",
+    )(far_qg, stat, near_stat, far_stat, done, near_qg_a, near_qg_b)
+    message_a, message_b = ta_pair(message), ta_other(message)
+
+    scratch = [pltpu.VMEM((STAT_ROWS, 3 * rows), jnp.float32)]
+    work = cost(heads, rows, 4, 1)
+    sums = call(
+        functools.partial(key_kernel, counts, width, 0), "key_side_0", [full, full], scratch, work,
+        tile_mask, clip_lengths, kv, qg, near_qg, far_qg, stat, near_stat, far_stat,
+    )
+    sums = call(
+        functools.partial(key_kernel, counts, width, 1), "key_side_1", [full, full], scratch, work,
+        tile_mask, clip_lengths, kv, qg_a, near_qg_a, message_a, *sums,
     )
     key_grad, value_grad = call(
-        functools.partial(key_kernel, counts, width, (2,), True),
-        "key_side_1",
-        [half, half],
-        [pltpu.VMEM((STAT_ROWS, 3 * rows), jnp.float32)],
-        cost(heads, rows, 4, 1),
-        tile_mask, clip_lengths, kv, column, column_a, column_b, far_qg, far_qg_a, far_qg_b, conv_weight, *first, dk_sum, dv_sum,
+        functools.partial(key_kernel, counts, width, 2), "key_side_2", [half, half], scratch, work,
+        tile_mask, clip_lengths, kv, qg_b, near_qg_b, message_b, *sums,
+        conv_weight, qg, near_qg, far_qg, qg_a, near_qg_a, message_a,
     )
     return tuple(x.reshape(query_states.shape) for x in (layer_out, query_grad, key_grad, value_grad))
 

time: 92.3 us -> 92.9 us (level)
  the two profiles are of different devices: /device:TPU:1 before, /device:TPU:9 now
where the time goes in v6:
time: 92.9 us; the launch traced here: 92.1 us
  starting transfers between devices  33.6 us (36%)
  Pallas kernels  33.1 us (36%)
  waiting for transfers between devices  21.1 us (23%)
  local copies, waits for them, and re-layouts  1.99 us (2%)
  other arithmetic  1.27 us (1%)
  between operations  0.95 us (1%)
    pallas_call x7, Pallas kernels, call(): pl.pallas_call(kernel, in_specs=[smem] * scalars + [vmem] * (len(args) -...  32.9 us
    ppermute x6, starting transfers between devices, ta_other(): return lax.ppermute(x, 'ta', other_pairs(lax.axis_size('ta')))  15.5 us
    ppermute x3, waiting for transfers between devices, ha_relay(): return lax.ppermute(near, 'ha', relay_pairs(lax.axis_size('ha')))  11.6 us
    ppermute x3, starting transfers between devices, ha_relay(): return lax.ppermute(near, 'ha', relay_pairs(lax.axis_size('ha')))  9.59 us
    ppermute x4, starting transfers between devices, ha_near(): return lax.ppermute(x, 'ha', flip_pairs(lax.axis_size('ha')))  3.87 us
    ppermute x6, waiting for transfers between devices, ta_other(): return lax.ppermute(x, 'ta', other_pairs(lax.axis_size('ta')))  3.39 us
    ppermute x4, waiting for transfers between devices, ha_near(): return lax.ppermute(x, 'ha', flip_pairs(lax.axis_size('ha')))  3.04 us
    ppermute x1, waiting for transfers between devices, ha_far(): return lax.ppermute(x, 'ha', other_pairs(lax.axis_size('ha')))  3.02 us
  transfers between devices with their start and end apart: 20, of which 6 were waited for; matrix products, arithmetic and copies ran while one was open for 0% of the time, Pallas kernels for 29%

profile of v6, /device:TPU:9, one launch (start us, length us, event | category | flops | bytes accessed | tf_op | source)
XLA Modules:
  0.0 92.1 jit_solution(7452430497723986180)
XLA Ops:
  0.6 0.0 copy-start.4
  0.6 0.0 copy-start.1
  0.7 0.0 copy-start.5
  0.7 0.0 copy-start.7
  0.7 1.2 %pad_maximum_fusion.own.rest_0_ = bf16[2,224,768]{2,1,0:T(8,128)(2,1)S(1)} fusion(bf16[1,224,768]{2,1,0:T(8,128)(2,1)} %bitcast.22, bf16[1,224,768]{2,1,0:T(8,128)(2,1)} %bitcast.24), kind=kLoop, calls=%fused_computation | loop fusion | flops 344064 | bytes 1376256 | tf_op jit(solution)/shard_map/stack | solution.py:400
  1.9 0.7 collective-permute-start.2
  2.6 3.0 %collective-permute-start.3 = (bf16[2,224,768]{2,1,0:T(8,128)(2,1)S(1)}, bf16[2,224,768]{2,1,0:T(8,128)(2,1)S(1)}, u32[]{:S(2)}, u32[]{:S(2)}) collective-permute-start(bf16[2,224,768]{2,1,0:T(8,128)(2,1)S(1)} %pad_maximum_fusion.own.rest_0_), channel_id=1, source_target_pairs={{0,0},{8,16},{16,8},{24,24},{1,1},{9,17},{17,9},{25,25},{2,2},{10,... | collective-permute-start | bytes 2064392 | tf_op jit(solution)/shard_map/ppermute | solution.py:62
  5.7 1.3 %collective-permute-start = (bf16[224,768]{1,0:T(8,128)(2,1)}, bf16[224,768]{1,0:T(8,128)(2,1)S(1)}, u32[]{:S(2)}, u32[]{:S(2)}) collective-permute-start(bf16[224,768]{1,0:T(8,128)(2,1)} %bitcast.25), channel_id=1, source_target_pairs={{0,1},{1,0},{2,3},{3,2},{4,5},{5,4},{6,7},{7,6},{8,9},{9,8},{10,11... | collective-permute-start | bytes 1032200 | tf_op jit(solution)/shard_map/ppermute | solution.py:46
  7.0 0.0 collective-permute-done.2.pair.rest_0_.rest_3_
  7.0 0.0 copy-start
  7.0 1.0 %copy-done = bf16[2,2,56,768]{3,2,1,0:T(8,128)(2,1)S(1)} copy-done((bf16[2,2,56,768]{3,2,1,0:T(8,128)(2,1)S(1)}, bf16[2,2,56,768]{3,2,1,0:T(8,128)(2,1)}, u32[]{:S(2)}) %copy-start) | copy-done | bytes 344088
  7.9 1.0 %copy-done.2 = bf16[2,2,56,768]{3,2,1,0:T(8,128)(2,1)S(1)} copy-done((bf16[2,2,56,768]{3,2,1,0:T(8,128)(2,1)S(1)}, bf16[2,2,56,768]{3,2,1,0:T(8,128)(2,1)}, u32[]{:S(2)}) %copy-start.2) | copy-done | bytes 344088
  9.0 0.1 collective-permute-start.4
  9.0 2.8 %collective-permute-start.5 = (bf16[2,224,768]{2,1,0:T(8,128)(2,1)S(1)}, bf16[2,224,768]{2,1,0:T(8,128)(2,1)S(1)}, u32[]{:S(2)}, u32[]{:S(2)}) collective-permute-start(bf16[2,224,768]{2,1,0:T(8,128)(2,1)S(1)} %pair_up.3.own_ref.rest_3_), channel_id=1, source_target_pairs={{0,0},{8,16},{16,8},{24,24},{1,1},{9,17},{17,9},{25,25},{2,2},{10,... | collective-permute-start | bytes 2064392 | tf_op jit(solution)/shard_map/ppermute | solution.py:62
  11.8 2.0 %collective-permute-done.rest_0_.x_ref = bf16[224,768]{1,0:T(8,128)(2,1)S(1)} collective-permute-done((bf16[224,768]{1,0:T(8,128)(2,1)}, bf16[224,768]{1,0:T(8,128)(2,1)S(1)}, u32[]{:S(2)}, u32[]{:S(2)}) %collective-permute-start) | collective-permute-done | bytes 344096 | tf_op jit(solution)/shard_map/ppermute | solution.py:46
  13.9 0.0 copy-done.4
  13.9 1.3 %collective-permute-start.1 = (bf16[224,768]{1,0:T(8,128)(2,1)S(1)}, bf16[224,768]{1,0:T(8,128)(2,1)S(1)}, u32[]{:S(2)}, u32[]{:S(2)}) collective-permute-start(bf16[224,768]{1,0:T(8,128)(2,1)S(1)} %later.1), channel_id=1, source_target_pairs={{0,1},{1,0},{2,3},{3,2},{4,5},{5,4},{6,7},{7,6},{8,9},{9,8},{10,11... | collective-permute-start | bytes 1032200 | tf_op jit(solution)/shard_map/ppermute | solution.py:46
  15.2 3.2 %collective-permute-start.6 = (bf16[224,768]{1,0:T(8,128)(2,1)S(1)}, bf16[224,768]{1,0:T(8,128)(2,1)S(1)}, u32[]{:S(2)}, u32[]{:S(2)}) collective-permute-start(bf16[224,768]{1,0:T(8,128)(2,1)S(1)} %collective-permute-done.rest_0_.x_ref), channel_id=1, source_target_pairs={{0,2},{2,4},{3,1},{4,6},{5,3},{7,5},{8,10},{10,12},{11,9},{12,14},... | collective-permute-start | bytes 1032200 | tf_op jit(solution)/shard_map/ppermute | solution.py:50
  18.4 0.0 collective-permute-done.3.other.rest_6_
  18.4 0.0 copy-done.1
  18.4 0.0 copy-done.5
  18.4 0.0 copy-done.7
  18.4 3.8 %scores_0.1 = (bf16[6,224,672]{2,1,0:T(8,128)(2,1)S(1)}, f32[224,768]{1,0:T(8,128)S(1)}, f32[224,768]{1,0:T(8,128)S(1)}, f32[224,768]{1,0:T(8,128)S(1)}) custom-call(s32[4,8,9]{2,1,0:T(8,128)S(1)} %copy-done.5, s32[8]{0:T(128)S(1)} %copy-done.7, bf16[224,768]{1,0:T(8,128)(2,1)S(1)} %bitcast.13, bf16[2,224,768]{2,1,0:T(8,128)(2,1)S(1)} %pad_maximum_fusion.own.rest_0_, ...), custom_call_target="tpu_custom_call" | custom-call | flops 462422016 | bytes 2752512 | tf_op jit(solution)/shard_map/scores_0/pallas_call | solution.py:345
  22.3 1.0 %collective-permute-done.1.refs_0_ = bf16[224,768]{1,0:T(8,128)(2,1)S(1)} collective-permute-done((bf16[224,768]{1,0:T(8,128)(2,1)S(1)}, bf16[224,768]{1,0:T(8,128)(2,1)S(1)}, u32[]{:S(2)}, u32[]{:S(2)}) %collective-permute-start.1) | collective-permute-done | bytes 344096 | tf_op jit(solution)/shard_map/ppermute | solution.py:46
  23.3 3.1 %collective-permute-done.6.rest_2_ = bf16[224,768]{1,0:T(8,128)(2,1)S(1)} collective-permute-done((bf16[224,768]{1,0:T(8,128)(2,1)S(1)}, bf16[224,768]{1,0:T(8,128)(2,1)S(1)}, u32[]{:S(2)}, u32[]{:S(2)}) %collective-permute-start.6) | collective-permute-done | bytes 344096 | tf_op jit(solution)/shard_map/ppermute | solution.py:50
  26.3 0.0 collective-permute-done.4.rest_0_.own_ref.rest_6_
  26.3 0.0 collective-permute-done.5.rest_1_.own_ref
  26.4 0.3 collective-permute-start.8
  26.7 1.9 %collective-permute-start.10 = (bf16[2,224,768]{2,1,0:T(8,128)(2,1)S(1)}, bf16[2,224,768]{2,1,0:T(8,128)(2,1)S(1)}, u32[]{:S(2)}, u32[]{:S(2)}) collective-permute-start(bf16[2,224,768]{2,1,0:T(8,128)(2,1)S(1)} %pair_up.4.own.rest_1_), channel_id=1, source_target_pairs={{0,0},{8,16},{16,8},{24,24},{1,1},{9,17},{17,9},{25,25},{2,2},{10,... | collective-permute-start | bytes 2064392 | tf_op jit(solution)/shard_map/ppermute | solution.py:62
  28.6 0.0 copy-done.3
  28.7 0.3 collective-permute-start.14
  29.0 3.2 %collective-permute-start.7 = (bf16[224,768]{1,0:T(8,128)(2,1)S(1)}, bf16[224,768]{1,0:T(8,128)(2,1)S(1)}, u32[]{:S(2)}, u32[]{:S(2)}) collective-permute-start(bf16[224,768]{1,0:T(8,128)(2,1)S(1)} %gate.2.y_ref.rest_0_), channel_id=1, source_target_pairs={{0,2},{2,4},{3,1},{4,6},{5,3},{7,5},{8,10},{10,12},{11,9},{12,14},... | collective-permute-start | bytes 1032200 | tf_op jit(solution)/shard_map/ppermute | solution.py:50
  32.2 8.5 %collective-permute-done.7 = bf16[224,768]{1,0:T(8,128)(2,1)S(1)} collective-permute-done((bf16[224,768]{1,0:T(8,128)(2,1)S(1)}, bf16[224,768]{1,0:T(8,128)(2,1)S(1)}, u32[]{:S(2)}, u32[]{:S(2)}) %collective-permute-start.7) | collective-permute-done | bytes 344096 | tf_op jit(solution)/shard_map/ppermute | solution.py:50
  40.8 0.1 pad_maximum_fusion.1.own.rest_2_
  40.8 0.2 collective-permute-start.9
  41.1 1.9 %collective-permute-start.11 = (bf16[2,224,768]{2,1,0:T(8,128)(2,1)S(1)}, bf16[2,224,768]{2,1,0:T(8,128)(2,1)S(1)}, u32[]{:S(2)}, u32[]{:S(2)}) collective-permute-start(bf16[2,224,768]{2,1,0:T(8,128)(2,1)S(1)} %pad_maximum_fusion.1.own.rest_2_), channel_id=1, source_target_pairs={{0,0},{8,16},{16,8},{24,24},{1,1},{9,17},{17,9},{25,25},{2,2},{10,... | collective-permute-start | bytes 2064392 | tf_op jit(solution)/shard_map/ppermute | solution.py:62
  43.0 0.0 collective-permute-done.8.pair.rest_4_
  43.0 0.0 collective-permute-done.10.other.rest_7_
  43.0 3.8 %scores_1.1 = (bf16[6,224,672]{2,1,0:T(8,128)(2,1)S(1)}, f32[224,768]{1,0:T(8,128)S(1)}, f32[224,768]{1,0:T(8,128)S(1)}, f32[224,768]{1,0:T(8,128)S(1)}) custom-call(s32[4,8,9]{2,1,0:T(8,128)S(1)} %copy-done.5, s32[8]{0:T(128)S(1)} %copy-done.7, bf16[224,768]{1,0:T(8,128)(2,1)S(1)} %bitcast.15, bf16[2,224,768]{2,1,0:T(8,128)(2,1)S(1)} %pair_up.4.own.rest_1_, ...), custom_call_target="tpu_custom_call" | custom-call | flops 462422016 | bytes 2752512 | tf_op jit(solution)/shard_map/scores_1/pallas_call | solution.py:345
  46.9 0.0 collective-permute-done.14.refs_0_
  46.9 3.6 %collective-permute-start.15 = (bf16[2,224,768]{2,1,0:T(8,128)(2,1)S(1)}, bf16[2,224,768]{2,1,0:T(8,128)(2,1)S(1)}, u32[]{:S(2)}, u32[]{:S(2)}) collective-permute-start(bf16[2,224,768]{2,1,0:T(8,128)(2,1)S(1)} %gate.3.near_ref.rest_4_), channel_id=1, source_target_pairs={{0,0},{8,16},{16,8},{24,24},{1,1},{9,17},{17,9},{25,25},{2,2},{10,... | collective-permute-start | bytes 2064392 | tf_op jit(solution)/shard_map/ppermute | solution.py:62
  50.5 3.2 %collective-permute-start.16 = (bf16[2,224,768]{2,1,0:T(8,128)(2,1)S(1)}, bf16[2,224,768]{2,1,0:T(8,128)(2,1)S(1)}, u32[]{:S(2)}, u32[]{:S(2)}) collective-permute-start(bf16[2,224,768]{2,1,0:T(8,128)(2,1)S(1)} %gate.3.near_ref.rest_4_), channel_id=1, source_target_pairs={{0,2},{2,4},{3,1},{4,6},{5,3},{7,5},{8,10},{10,12},{11,9},{12,14},... | collective-permute-start | bytes 2064392 | tf_op jit(solution)/shard_map/ppermute | solution.py:50
  53.7 0.1 collective-permute-start.17
  53.8 0.0 collective-permute-done.9.pair.rest_5_
  53.8 0.0 collective-permute-done.11.other.rest_8_
  53.8 0.0 copy-start.6
  53.9 4.6 %scores_2.1 = (bf16[6,224,672]{2,1,0:T(8,128)(2,1)S(1)}, f32[224,768]{1,0:T(8,128)S(1)}, f32[224,768]{1,0:T(8,128)S(1)}, f32[224,768]{1,0:T(8,128)S(1)}, f32[224...) custom-call(s32[4,8,9]{2,1,0:T(8,128)S(1)} %copy-done.5, s32[8]{0:T(128)S(1)} %copy-done.7, ...), custom_call_target="tpu_custom_call" | custom-call | flops 462422016 | bytes 2752512 | tf_op jit(solution)/shard_map/scores_2/pallas_call | solution.py:345
  58.4 1.0 %collective-permute-start.12 = (f32[16,224]{1,0:T(8,128)S(1)}, f32[16,224]{1,0:T(8,128)S(1)}, u32[]{:S(2)}, u32[]{:S(2)}) collective-permute-start(f32[16,224]{1,0:T(8,128)S(1)} %get-tuple-element.42.own_ref.rest_0_), channel_id=1, source_target_pairs={{0,1},{1,0},{2,3},{3,2},{4,5},{5,4},{6,7},{7,6},{8,9},{9,8},{10,11... | collective-permute-start | bytes 43016 | tf_op jit(solution)/shard_map/ppermute | solution.py:46
  59.4 2.3 %collective-permute-start.13 = (f32[16,224]{1,0:T(8,128)S(1)}, f32[16,224]{1,0:T(8,128)S(1)}, u32[]{:S(2)}, u32[]{:S(2)}) collective-permute-start(f32[16,224]{1,0:T(8,128)S(1)} %get-tuple-element.42.own_ref.rest_0_), channel_id=1, source_target_pairs={{0,0},{1,2},{2,1},{3,4},{4,3},{5,6},{6,5},{7,7},{8,8},{9,10},{10,9... | collective-permute-start | bytes 43016 | tf_op jit(solution)/shard_map/ppermute | solution.py:54
  61.7 0.0 collective-permute-done.12.rest_17_.near_ref.rest_1_
  61.7 3.0 %collective-permute-done.13.rest_18_.far_ref.rest_2_ = f32[16,224]{1,0:T(8,128)S(1)} collective-permute-done((f32[16,224]{1,0:T(8,128)S(1)}, f32[16,224]{1,0:T(8,128)S(1)}, u32[]{:S(2)}, u32[]{:S(2)}) %collective-permute-start.13) | collective-permute-done | bytes 14368 | tf_op jit(solution)/shard_map/ppermute | solution.py:54
  64.8 0.0 copy-done.6
  64.8 7.0 %query_side.1 = (bf16[224,768]{1,0:T(8,128)(2,1)}, bf16[224,768]{1,0:T(8,128)(2,1)}, f32[8,128]{1,0:T(8,128)S(1)}) custom-call(bf16[224,768]{1,0:T(8,128)(2,1)S(1)} %bitcast.20, bf16[27,768]{1,0:T(8,128)(2,1)S(1)} %copy-done.6, bf16[2,224,768]{2,1,0:T(8,128)(2,1)S(1)} %pad_maximum_fusion.own.rest_0_, bf16[2,224,768]{2,1,0:T(8,128)(2,1)S(1)} %pair_up.4.own.rest_1_, ...), custom_call_target="tpu_custom_call" | custom-call | flops 1387266048 | bytes 8257536 | tf_op jit(solution)/shard_map/query_side/pallas_call | solution.py:345
  71.8 0.0 collective-permute-done.15.rest_2_.near_ref
  71.8 0.0 collective-permute-done.16.qg_ref.far_ref.rest_5_
  71.8 0.0 collective-permute-done.17.rest_1_.near_ref.rest_7_
  71.8 0.1 pack.1
  71.8 0.9 %collective-permute-start.19 = (bf16[496,768]{1,0:T(8,128)(2,1)S(1)}, bf16[496,768]{1,0:T(8,128)(2,1)S(1)}, u32[]{:S(2)}, u32[]{:S(2)}) collective-permute-start(bf16[496,768]{1,0:T(8,128)(2,1)S(1)} %pack.1), channel_id=1, source_target_pairs={{0,8},{8,0},{16,24},{24,16},{1,9},{9,1},{17,25},{25,17},{2,10},{10... | collective-permute-start | bytes 2285576 | tf_op jit(solution)/shard_map/ppermute | solution.py:58
  72.8 2.2 %collective-permute-start.18 = (bf16[496,768]{1,0:T(8,128)(2,1)S(1)}, bf16[496,768]{1,0:T(8,128)(2,1)S(1)}, u32[]{:S(2)}, u32[]{:S(2)}) collective-permute-start(bf16[496,768]{1,0:T(8,128)(2,1)S(1)} %pack.1), channel_id=1, source_target_pairs={{0,0},{8,16},{16,8},{24,24},{1,1},{9,17},{17,9},{25,25},{2,2},{10,... | collective-permute-start | bytes 2285576 | tf_op jit(solution)/shard_map/ppermute | solution.py:62
  75.0 3.6 %key_side_0.1 = (f32[224,768]{1,0:T(8,128)S(1)}, f32[224,768]{1,0:T(8,128)S(1)}) custom-call(s32[4,8,9]{2,1,0:T(8,128)S(1)} %copy-done.5, s32[8]{0:T(128)S(1)} %copy-done.7, bf16[2,224,768]{2,1,0:T(8,128)(2,1)S(1)} %pad_maximum_fusion.own.rest_0_, bf16[2,224,768]{2,1,0:T(8,128)(2,1)S(1)} %pair_up.3.own_ref.rest_3_, ...), custom_call_target="tpu_custom_call" | custom-call | flops 924844032 | bytes 2752512 | tf_op jit(solution)/shard_map/key_side_0/pallas_call | solution.py:345
  78.6 0.0 collective-permute-done.19.far_ref.rest_8_
  78.6 3.8 %key_side_1.1 = (f32[224,768]{1,0:T(8,128)S(1)}, f32[224,768]{1,0:T(8,128)S(1)}) custom-call(s32[4,8,9]{2,1,0:T(8,128)S(1)} %copy-done.5, s32[8]{0:T(128)S(1)} %copy-done.7, bf16[2,224,768]{2,1,0:T(8,128)(2,1)S(1)} %pad_maximum_fusion.own.rest_0_, bf16[2,224,768]{2,1,0:T(8,128)(2,1)S(1)} %collective-permute-done.4.rest_0_.own_ref.rest_6_, ...), custom_call_target="tpu_custom_call" | custom-call | flops 924844032 | bytes 2752512 | tf_op jit(solution)/shard_map/key_side_1/pallas_call | solution.py:345
  82.4 3.4 %collective-permute-done.18.far_ref = bf16[496,768]{1,0:T(8,128)(2,1)S(1)} collective-permute-done((bf16[496,768]{1,0:T(8,128)(2,1)S(1)}, bf16[496,768]{1,0:T(8,128)(2,1)S(1)}, u32[]{:S(2)}, u32[]{:S(2)}) %collective-permute-start.18) | collective-permute-done | bytes 761888 | tf_op jit(solution)/shard_map/ppermute | solution.py:62
  85.8 6.2 %key_side_2.1 = (bf16[224,768]{1,0:T(8,128)(2,1)}, bf16[224,768]{1,0:T(8,128)(2,1)}) custom-call(s32[4,8,9]{2,1,0:T(8,128)S(1)} %copy-done.5, s32[8]{0:T(128)S(1)} %copy-done.7, bf16[2,224,768]{2,1,0:T(8,128)(2,1)S(1)} %pad_maximum_fusion.own.rest_0_, bf16[2,224,768]{2,1,0:T(8,128)(2,1)S(1)} %collective-permute-done.5.rest_1_.own_ref, ...), custom_call_target="tpu_custom_call" | custom-call | flops 924844032 | bytes 2752512 | tf_op jit(solution)/shard_map/key_side_2/pallas_call | solution.py:345
  (8 shorter events, 0.2 us)
Async XLA Ops:
  0.6 13.2 %copy-start.4 = (bf16[2,2,56,768]{3,2,1,0:T(8,128)(2,1)S(1)}, bf16[2,2,56,768]{3,2,1,0:T(8,128)(2,1)}, u32[]{:S(2)}) copy-start(bf16[2,2,56,768]{3,2,1,0:T(8,128)(2,1)} %param.9) | copy-start | bytes 1032196
  0.6 17.8 %copy-start.1 = (bf16[2,2,56,768]{3,2,1,0:T(8,128)(2,1)S(1)}, bf16[2,2,56,768]{3,2,1,0:T(8,128)(2,1)}, u32[]{:S(2)}) copy-start(bf16[2,2,56,768]{3,2,1,0:T(8,128)(2,1)} %param.7) | copy-start | bytes 1032196
  0.7 17.8 %copy-start.5 = (s32[4,8,9]{2,1,0:T(8,128)S(1)}, s32[4,8,9]{2,1,0:T(8,128)}, u32[]{:S(2)}) copy-start(s32[4,8,9]{2,1,0:T(8,128)} %mask_ref.11) | copy-start | bytes 3460
  0.7 17.8 %copy-start.7 = (s32[8]{0:T(128)S(1)}, s32[8]{0:T(128)}, u32[]{:S(2)}) copy-start(s32[8]{0:T(128)} %clip_ref.11) | copy-start | bytes 100
  1.9 5.1 %collective-permute-start.2 = (bf16[2,224,768]{2,1,0:T(8,128)(2,1)S(1)}, bf16[2,224,768]{2,1,0:T(8,128)(2,1)S(1)}, u32[]{:S(2)}, u32[]{:S(2)}) collective-permute-start(bf16[2,224,768]{2,1,0:T(8,128)(2,1)S(1)} %pad_maximum_fusion.own.rest_0_), channel_id=1, source_target_pairs={{0,8},{8,0},{16,24},{24,16},{1,9},{9,1},{17,25},{25,17},{2,10},{10... | collective-permute-start | bytes 2064392 | tf_op jit(solution)/shard_map/ppermute | solution.py:58
  2.6 15.8 %collective-permute-start.3 = (bf16[2,224,768]{2,1,0:T(8,128)(2,1)S(1)}, bf16[2,224,768]{2,1,0:T(8,128)(2,1)S(1)}, u32[]{:S(2)}, u32[]{:S(2)}) collective-permute-start(bf16[2,224,768]{2,1,0:T(8,128)(2,1)S(1)} %pad_maximum_fusion.own.rest_0_), channel_id=1, source_target_pairs={{0,0},{8,16},{16,8},{24,24},{1,1},{9,17},{17,9},{25,25},{2,2},{10,... | collective-permute-start | bytes 2064392 | tf_op jit(solution)/shard_map/ppermute | solution.py:62
  5.7 8.2 %collective-permute-start = (bf16[224,768]{1,0:T(8,128)(2,1)}, bf16[224,768]{1,0:T(8,128)(2,1)S(1)}, u32[]{:S(2)}, u32[]{:S(2)}) collective-permute-start(bf16[224,768]{1,0:T(8,128)(2,1)} %bitcast.25), channel_id=1, source_target_pairs={{0,1},{1,0},{2,3},{3,2},{4,5},{5,4},{6,7},{7,6},{8,9},{9,8},{10,11... | collective-permute-start | bytes 1032200 | tf_op jit(solution)/shard_map/ppermute | solution.py:46
  7.0 1.0 %copy-start = (bf16[2,2,56,768]{3,2,1,0:T(8,128)(2,1)S(1)}, bf16[2,2,56,768]{3,2,1,0:T(8,128)(2,1)}, u32[]{:S(2)}) copy-start(bf16[2,2,56,768]{3,2,1,0:T(8,128)(2,1)} %param.7) | copy-start | bytes 1032196
  7.9 1.0 %copy-start.2 = (bf16[2,2,56,768]{3,2,1,0:T(8,128)(2,1)S(1)}, bf16[2,2,56,768]{3,2,1,0:T(8,128)(2,1)}, u32[]{:S(2)}) copy-start(bf16[2,2,56,768]{3,2,1,0:T(8,128)(2,1)} %param.11) | copy-start | bytes 1032196
  9.0 17.4 %collective-permute-start.4 = (bf16[2,224,768]{2,1,0:T(8,128)(2,1)S(1)}, bf16[2,224,768]{2,1,0:T(8,128)(2,1)S(1)}, u32[]{:S(2)}, u32[]{:S(2)}) collective-permute-start(bf16[2,224,768]{2,1,0:T(8,128)(2,1)S(1)} %pair_up.3.own_ref.rest_3_), channel_id=1, source_target_pairs={{0,8},{8,0},{16,24},{24,16},{1,9},{9,1},{17,25},{25,17},{2,10},{10... | collective-permute-start | bytes 2064392 | tf_op jit(solution)/shard_map/ppermute | solution.py:58
  9.0 17.3 %collective-permute-start.5 = (bf16[2,224,768]{2,1,0:T(8,128)(2,1)S(1)}, bf16[2,224,768]{2,1,0:T(8,128)(2,1)S(1)}, u32[]{:S(2)}, u32[]{:S(2)}) collective-permute-start(bf16[2,224,768]{2,1,0:T(8,128)(2,1)S(1)} %pair_up.3.own_ref.rest_3_), channel_id=1, source_target_pairs={{0,0},{8,16},{16,8},{24,24},{1,1},{9,17},{17,9},{25,25},{2,2},{10,... | collective-permute-start | bytes 2064392 | tf_op jit(solution)/shard_map/ppermute | solution.py:62
  13.9 9.4 %collective-permute-start.1 = (bf16[224,768]{1,0:T(8,128)(2,1)S(1)}, bf16[224,768]{1,0:T(8,128)(2,1)S(1)}, u32[]{:S(2)}, u32[]{:S(2)}) collective-permute-start(bf16[224,768]{1,0:T(8,128)(2,1)S(1)} %later.1), channel_id=1, source_target_pairs={{0,1},{1,0},{2,3},{3,2},{4,5},{5,4},{6,7},{7,6},{8,9},{9,8},{10,11... | collective-permute-start | bytes 1032200 | tf_op jit(solution)/shard_map/ppermute | solution.py:46
  15.2 11.2 %collective-permute-start.6 = (bf16[224,768]{1,0:T(8,128)(2,1)S(1)}, bf16[224,768]{1,0:T(8,128)(2,1)S(1)}, u32[]{:S(2)}, u32[]{:S(2)}) collective-permute-start(bf16[224,768]{1,0:T(8,128)(2,1)S(1)} %collective-permute-done.rest_0_.x_ref), channel_id=1, source_target_pairs={{0,2},{2,4},{3,1},{4,6},{5,3},{7,5},{8,10},{10,12},{11,9},{12,14},... | collective-permute-start | bytes 1032200 | tf_op jit(solution)/shard_map/ppermute | solution.py:50
  23.3 5.4 %copy-start.3 = (bf16[2,2,56,768]{3,2,1,0:T(8,128)(2,1)S(1)}, bf16[2,2,56,768]{3,2,1,0:T(8,128)(2,1)}, u32[]{:S(2)}) copy-start(bf16[2,2,56,768]{3,2,1,0:T(8,128)(2,1)} %param.11) | copy-start | bytes 1032196
  26.4 16.6 %collective-permute-start.8 = (bf16[2,224,768]{2,1,0:T(8,128)(2,1)S(1)}, bf16[2,224,768]{2,1,0:T(8,128)(2,1)S(1)}, u32[]{:S(2)}, u32[]{:S(2)}) collective-permute-start(bf16[2,224,768]{2,1,0:T(8,128)(2,1)S(1)} %pair_up.4.own.rest_1_), channel_id=1, source_target_pairs={{0,8},{8,0},{16,24},{24,16},{1,9},{9,1},{17,25},{25,17},{2,10},{10... | collective-permute-start | bytes 2064392 | tf_op jit(solution)/shard_map/ppermute | solution.py:58
  26.7 16.3 %collective-permute-start.10 = (bf16[2,224,768]{2,1,0:T(8,128)(2,1)S(1)}, bf16[2,224,768]{2,1,0:T(8,128)(2,1)S(1)}, u32[]{:S(2)}, u32[]{:S(2)}) collective-permute-start(bf16[2,224,768]{2,1,0:T(8,128)(2,1)S(1)} %pair_up.4.own.rest_1_), channel_id=1, source_target_pairs={{0,0},{8,16},{16,8},{24,24},{1,1},{9,17},{17,9},{25,25},{2,2},{10,... | collective-permute-start | bytes 2064392 | tf_op jit(solution)/shard_map/ppermute | solution.py:62
  28.7 18.2 %collective-permute-start.14 = (bf16[2,224,768]{2,1,0:T(8,128)(2,1)S(1)}, bf16[2,224,768]{2,1,0:T(8,128)(2,1)S(1)}, u32[]{:S(2)}, u32[]{:S(2)}) collective-permute-start(bf16[2,224,768]{2,1,0:T(8,128)(2,1)S(1)} %pair_up.5), channel_id=1, source_target_pairs={{0,1},{1,0},{2,3},{3,2},{4,5},{5,4},{6,7},{7,6},{8,9},{9,8},{10,11... | collective-permute-start | bytes 2064392 | tf_op jit(solution)/shard_map/ppermute | solution.py:46
  29.0 11.7 %collective-permute-start.7 = (bf16[224,768]{1,0:T(8,128)(2,1)S(1)}, bf16[224,768]{1,0:T(8,128)(2,1)S(1)}, u32[]{:S(2)}, u32[]{:S(2)}) collective-permute-start(bf16[224,768]{1,0:T(8,128)(2,1)S(1)} %gate.2.y_ref.rest_0_), channel_id=1, source_target_pairs={{0,2},{2,4},{3,1},{4,6},{5,3},{7,5},{8,10},{10,12},{11,9},{12,14},... | collective-permute-start | bytes 1032200 | tf_op jit(solution)/shard_map/ppermute | solution.py:50
  40.8 13.0 %collective-permute-start.9 = (bf16[2,224,768]{2,1,0:T(8,128)(2,1)S(1)}, bf16[2,224,768]{2,1,0:T(8,128)(2,1)S(1)}, u32[]{:S(2)}, u32[]{:S(2)}) collective-permute-start(bf16[2,224,768]{2,1,0:T(8,128)(2,1)S(1)} %pad_maximum_fusion.1.own.rest_2_), channel_id=1, source_target_pairs={{0,8},{8,0},{16,24},{24,16},{1,9},{9,1},{17,25},{25,17},{2,10},{10... | collective-permute-start | bytes 2064392 | tf_op jit(solution)/shard_map/ppermute | solution.py:58
  41.1 12.8 %collective-permute-start.11 = (bf16[2,224,768]{2,1,0:T(8,128)(2,1)S(1)}, bf16[2,224,768]{2,1,0:T(8,128)(2,1)S(1)}, u32[]{:S(2)}, u32[]{:S(2)}) collective-permute-start(bf16[2,224,768]{2,1,0:T(8,128)(2,1)S(1)} %pad_maximum_fusion.1.own.rest_2_), channel_id=1, source_target_pairs={{0,0},{8,16},{16,8},{24,24},{1,1},{9,17},{17,9},{25,25},{2,2},{10,... | collective-permute-start | bytes 2064392 | tf_op jit(solution)/shard_map/ppermute | solution.py:62
  46.9 24.9 %collective-permute-start.15 = (bf16[2,224,768]{2,1,0:T(8,128)(2,1)S(1)}, bf16[2,224,768]{2,1,0:T(8,128)(2,1)S(1)}, u32[]{:S(2)}, u32[]{:S(2)}) collective-permute-start(bf16[2,224,768]{2,1,0:T(8,128)(2,1)S(1)} %gate.3.near_ref.rest_4_), channel_id=1, source_target_pairs={{0,0},{8,16},{16,8},{24,24},{1,1},{9,17},{17,9},{25,25},{2,2},{10,... | collective-permute-start | bytes 2064392 | tf_op jit(solution)/shard_map/ppermute | solution.py:62
  50.5 21.2 %collective-permute-start.16 = (bf16[2,224,768]{2,1,0:T(8,128)(2,1)S(1)}, bf16[2,224,768]{2,1,0:T(8,128)(2,1)S(1)}, u32[]{:S(2)}, u32[]{:S(2)}) collective-permute-start(bf16[2,224,768]{2,1,0:T(8,128)(2,1)S(1)} %gate.3.near_ref.rest_4_), channel_id=1, source_target_pairs={{0,2},{2,4},{3,1},{4,6},{5,3},{7,5},{8,10},{10,12},{11,9},{12,14},... | collective-permute-start | bytes 2064392 | tf_op jit(solution)/shard_map/ppermute | solution.py:50
  53.7 18.0 %collective-permute-start.17 = (bf16[2,224,768]{2,1,0:T(8,128)(2,1)S(1)}, bf16[2,224,768]{2,1,0:T(8,128)(2,1)S(1)}, u32[]{:S(2)}, u32[]{:S(2)}) collective-permute-start(bf16[2,224,768]{2,1,0:T(8,128)(2,1)S(1)} %gate.3.near_ref.rest_4_), channel_id=1, source_target_pairs={{0,8},{8,0},{16,24},{24,16},{1,9},{9,1},{17,25},{25,17},{2,10},{10... | collective-permute-start | bytes 2064392 | tf_op jit(solution)/shard_map/ppermute | solution.py:58
  53.8 10.9 %copy-start.6 = (bf16[27,768]{1,0:T(8,128)(2,1)S(1)}, bf16[27,768]{1,0:T(8,128)(2,1)}, u32[]{:S(2)}) copy-start(bf16[27,768]{1,0:T(8,128)(2,1)} %rest_2_.1) | copy-start | bytes 124420
  58.4 3.3 %collective-permute-start.12 = (f32[16,224]{1,0:T(8,128)S(1)}, f32[16,224]{1,0:T(8,128)S(1)}, u32[]{:S(2)}, u32[]{:S(2)}) collective-permute-start(f32[16,224]{1,0:T(8,128)S(1)} %get-tuple-element.42.own_ref.rest_0_), channel_id=1, source_target_pairs={{0,1},{1,0},{2,3},{3,2},{4,5},{5,4},{6,7},{7,6},{8,9},{9,8},{10,11... | collective-permute-start | bytes 43016 | tf_op jit(solution)/shard_map/ppermute | solution.py:46
  59.4 5.4 %collective-permute-start.13 = (f32[16,224]{1,0:T(8,128)S(1)}, f32[16,224]{1,0:T(8,128)S(1)}, u32[]{:S(2)}, u32[]{:S(2)}) collective-permute-start(f32[16,224]{1,0:T(8,128)S(1)} %get-tuple-element.42.own_ref.rest_0_), channel_id=1, source_target_pairs={{0,0},{1,2},{2,1},{3,4},{4,3},{5,6},{6,5},{7,7},{8,8},{9,10},{10,9... | collective-permute-start | bytes 43016 | tf_op jit(solution)/shard_map/ppermute | solution.py:54
  71.8 6.8 %collective-permute-start.19 = (bf16[496,768]{1,0:T(8,128)(2,1)S(1)}, bf16[496,768]{1,0:T(8,128)(2,1)S(1)}, u32[]{:S(2)}, u32[]{:S(2)}) collective-permute-start(bf16[496,768]{1,0:T(8,128)(2,1)S(1)} %pack.1), channel_id=1, source_target_pairs={{0,8},{8,0},{16,24},{24,16},{1,9},{9,1},{17,25},{25,17},{2,10},{10... | collective-permute-start | bytes 2285576 | tf_op jit(solution)/shard_map/ppermute | solution.py:58
  72.8 13.0 %collective-permute-start.18 = (bf16[496,768]{1,0:T(8,128)(2,1)S(1)}, bf16[496,768]{1,0:T(8,128)(2,1)S(1)}, u32[]{:S(2)}, u32[]{:S(2)}) collective-permute-start(bf16[496,768]{1,0:T(8,128)(2,1)S(1)} %pack.1), channel_id=1, source_target_pairs={{0,0},{8,16},{16,8},{24,24},{1,1},{9,17},{17,9},{25,25},{2,2},{10,... | collective-permute-start | bytes 2285576 | tf_op jit(solution)/shard_map/ppermute | solution.py:62

commit v7 on v6

--- a/solution.py
+++ b/solution.py
@@ -71,55 +71,80 @@
     return (index >= 0) & (index < count)
 
 
-def halo_slab(tile, place_now, width):
-    even_t, even_h, in_t, in_h = place_now
-    tiles = [tile(slot).astype(jnp.float32) for slot in range(9)]
-
-    def cell(slot, frame, row):
-        start = (2 * frame + row) * width
-        return tiles[slot][start : start + width]
-
-    def side_h(slot_t, frame, R):
+def row_of(tile, frame, row, width):
+    start = (2 * frame + row) * width
+    return tile[start : start + width]
+
+
+def shifted_sum(parts, width):
+    column = lax.broadcasted_iota(jnp.int32, (width, HEAD_DIM), 0)
+    before = jnp.where(column == 0, 0.0, pltpu.roll(parts[0], 1, 0))
+    behind = jnp.where(column == width - 1, 0.0, pltpu.roll(parts[2], width - 1, 0))
+    return parts[1] + before + behind
+
+
+def total_of(terms):
+    return functools.reduce(lambda x, y: x + y, terms)
+
+
+def along_t(own, pair, other, place_now):
+    even_t, _, in_t, _ = place_now
+    ahead = jnp.where(in_t[0], jnp.where(even_t, other(1), pair(1)), 0.0)
+    behind = jnp.where(in_t[1], jnp.where(even_t, pair(0), other(0)), 0.0)
+    return [ahead, own(0), own(1), behind]
+
+
+def conv_inner(tiles, weight, flipped, place_now, width):
+    _, even_h, _, in_h = place_now
+    tiles = [[x.astype(jnp.float32) for x in pair] for pair in tiles]
+
+    def cell(slot, R):
         if R in (1, 2):
-            return cell(3 * slot_t, frame, R - 1)
-        row = 1 if R == 0 else 0
-        near, far = cell(3 * slot_t + 1, frame, row), cell(3 * slot_t + 2, frame, row)
-        picked = jnp.where(even_h, far, near) if R == 0 else jnp.where(even_h, near, far)
-        return jnp.where(in_h[0 if R == 0 else 1], picked, 0.0)
-
-    slab = []
-    for F in range(4):
-        line = []
-        for R in range(4):
-            if F in (1, 2):
-                line.append(side_h(0, F - 1, R))
-                continue
-            frame = 1 if F == 0 else 0
-            first, second = side_h(1, frame, R), side_h(2, frame, R)
-            picked = jnp.where(even_t, second, first) if F == 0 else jnp.where(even_t, first, second)
-            line.append(jnp.where(in_t[0 if F == 0 else 1], picked, 0.0))
-        slab.append(line)
-    return slab
-
-
-def depthwise(slab, weight, flipped, width):
-    column = lax.broadcasted_iota(jnp.int32, (width, HEAD_DIM), 0)
+            return lambda frame: row_of(tiles[slot][0], frame, R - 1, width)
+        if R == 0:
+            return lambda frame: jnp.where(even_h | ~in_h[0], 0.0, row_of(tiles[slot][1], frame, 1, width))
+        return lambda frame: jnp.where(even_h & in_h[1], row_of(tiles[slot][1], frame, 0, width), 0.0)
+
+    slab = [along_t(cell(0, R), cell(1, R), cell(2, R), place_now) for R in range(4)]
     rows = []
     for f in range(2):
         for r in range(2):
             parts = []
             for dw in range(3):
-                total = None
-                for dt in range(3):
-                    for dh in range(3):
-                        tap = 9 * dt + 3 * dh + dw
-                        tap = 26 - tap if flipped else tap
-                        term = weight[tap : tap + 1] * slab[f + dt][r + dh]
-                        total = term if total is None else total + term
-                parts.append(total)
-            before = jnp.where(column == 0, 0.0, pltpu.roll(parts[0], 1, 0))
-            after_ = jnp.where(column == width - 1, 0.0, pltpu.roll(parts[2], width - 1, 0))
-            rows.append(parts[1] + before + after_)
+                taps = [(dt, dh, 9 * dt + 3 * dh + dw) for dt in range(3) for dh in range(3)]
+                taps = [(dt, dh, 26 - tap if flipped else tap) for dt, dh, tap in taps]
+                parts.append(total_of([weight[tap : tap + 1] * slab[r + dh][f + dt] for dt, dh, tap in taps]))
+            rows.append(shifted_sum(parts, width))
+    return jnp.concatenate(rows, axis=0)
+
+
+def conv_far(tiles, weight, flipped, place_now, width):
+    _, even_h, _, in_h = place_now
+    tiles = [x.astype(jnp.float32) for x in tiles]
+    there = (even_h & in_h[0]) | (~even_h & in_h[1])
+
+    def cell(slot):
+        def of(frame):
+            row = jnp.where(even_h, row_of(tiles[slot], frame, 1, width), row_of(tiles[slot], frame, 0, width))
+            return jnp.where(there, row, 0.0)
+
+        return of
+
+    line = along_t(cell(0), cell(1), cell(2), place_now)
+    rows = []
+    for f in range(2):
+        parts = []
+        for dw in range(3):
+            terms = []
+            for dt in range(3):
+                up, down = 9 * dt + dw, 9 * dt + 6 + dw
+                if flipped:
+                    up, down = 26 - up, 26 - down
+                tap = jnp.where(even_h, weight[up : up + 1], weight[down : down + 1])
+                terms.append(tap * line[f + dt])
+            parts.append(total_of(terms))
+        beside = shifted_sum(parts, width)
+        rows += [jnp.where(even_h, beside, 0.0), jnp.where(even_h, 0.0, beside)]
     return jnp.concatenate(rows, axis=0)
 
 
@@ -147,7 +172,7 @@
     slots = [own, pair, other]
     if last:
         grad_ref, sums, tops, totals = rest[0], (rest[1], rest[4]), (rest[2], rest[5]), (rest[3], rest[6])
-        exp_ref, att_ref, fac_own, fac_near, fac_far, delta_ref, stat_ref, bias, stat = rest[7:]
+        exp_ref, att_ref, fac_own, fac_near, fac_far, delta_ref, stat_ref, bias, stat = rest[8:]
     else:
         exp_ref, sum_ref, top_ref, total_ref, bias = rest
     index_t, index_h, _ = place(counts)
@@ -211,9 +236,22 @@
         stat_ref[...] = turned[:STAT_ROWS, :rows]
 
 
+def conv_kernel(counts, width, flipped, own, near, pair, near_pair, other, near_other, weight_ref, out_ref):
+    _, _, place_now = place(counts)
+    rows, channels = out_ref.shape
+
+    def body(head, _):
+        cols = head_columns(head)
+        tiles = [(x[1, :, cols], y[1, :, cols]) for x, y in ((own, near), (pair, near_pair), (other, near_other))]
+        out_ref[:, cols] = conv_inner(tiles, weight_ref[:, cols].astype(jnp.float32), flipped, place_now, width)
+        return 0
+
+    lax.fori_loop(0, channels // HEAD_DIM, body, 0)
+
+
 def query_kernel(counts, width, grad_ref, weight_ref, *rest):
     slots, exps, factors = rest[:9], rest[9:12], rest[12:15]
-    att_ref, delta_ref, _, _, out_ref, dq_ref, done_ref = rest[15:]
+    att_ref, delta_ref, conv_ref, out_ref, dq_ref, done_ref = rest[15:]
     done_ref[...] = jnp.zeros_like(done_ref)
     _, _, place_now = place(counts)
     rows, channels = grad_ref.shape
@@ -236,8 +274,8 @@
                 part = dot(ds.astype(jnp.bfloat16), keys) * (factors[column][:, cols] * scale)
                 dq = part if dq is None else dq + part
             dq_ref[:, cols] = dq.astype(jnp.bfloat16)
-            slab = halo_slab(lambda slot: slots[slot][1, :, cols], place_now, width)
-            conv = depthwise(slab, weight_ref[:, cols].astype(jnp.float32), False, width)
+            tiles = [slots[i][1, :, cols] for i in (2, 5, 8)]
+            conv = conv_ref[:, cols] + conv_far(tiles, weight_ref[:, cols].astype(jnp.float32), False, place_now, width)
             out_ref[:, cols] = (att_ref[:, cols] + conv).astype(jnp.bfloat16)
         return 0
 
@@ -310,9 +348,9 @@
                 dk_ref[:, cols], dv_ref[:, cols] = dk, dv
                 continue
             dk_ref[:, cols] = jnp.where(live, dk * scale, 0.0).astype(jnp.bfloat16)
-            around = (*edges[1:], own_ref, near_ref, far_ref)
-            slab = halo_slab(lambda slot: packed(around[slot], 1, cols), place_now, width)
-            conv = depthwise(slab, edges[0][:, cols].astype(jnp.float32), True, width)
+            weight_ref, conv_ref, *far_refs = edges
+            tiles = [packed(ref, 1, cols) for ref in (*far_refs, far_ref)]
+            conv = conv_ref[:, cols] + conv_far(tiles, weight_ref[:, cols].astype(jnp.float32), True, place_now, width)
             dv_ref[:, cols] = (jnp.where(live, dv, 0.0) + conv).astype(jnp.bfloat16)
         return 0
 
@@ -353,6 +391,10 @@
             name=name,
         )(*args)
 
+    def convolution(flipped, *tiles):
+        kernel = functools.partial(conv_kernel, counts, width, flipped)
+        return call(kernel, "convolution", [full], [], cost(heads, rows, 1, 1), *tiles, conv_weight)[0]
+
     def scores(column, tiles):
         kernel = functools.partial(column_kernel, counts, width, column, False)
         work = cost(heads, rows, 2, 1)
@@ -405,14 +447,15 @@
     far_k = ha_relay(near_k)
     exp_own, *own_parts = scores(0, (kv, kv_a, kv_b))
 
-    near_v = gate(near_v, own_parts[0])
     far_v = ha_relay(near_v)
-    near_kv = pair_up(near_k, near_v, qg_a, qg_b, far_k)
+    near_kv = pair_up(near_k, near_v, qg_a, qg_b)
     near_kv_a, near_kv_b = ta_pair(near_kv), ta_other(near_kv)
-    near_qg = ha_near(pair_up(query, grad, near_v))
-    far_kv = jnp.stack([far_k, far_v])
+    near_qg = ha_near(pair_up(query, grad, near_v, far_k))
+    far_kv = pair_up(far_k, far_v, own_parts[0])
     far_kv_a, far_kv_b = ta_pair(far_kv), ta_other(far_kv)
     exp_near, *near_parts = scores(1, (near_kv, near_kv_a, near_kv_b))
+
+    conv_value = convolution(False, kv, near_kv, kv_a, near_kv_a, kv_b, near_kv_b)
 
     near_qg = gate(near_qg, near_parts[0])
     far_qg = ha_relay(near_qg)
@@ -423,7 +466,7 @@
         [exps] + [full] * 5 + [jax.ShapeDtypeStruct((STAT_ROWS, rows), jnp.float32)],
         [bias, pltpu.VMEM((rows, HEAD_DIM), jnp.float32)],
         cost(heads, rows, 2, 1),
-        tile_mask, clip_lengths, query, far_kv, far_kv_a, far_kv_b, grad, *own_parts, *near_parts,
+        tile_mask, clip_lengths, query, far_kv, far_kv_a, far_kv_b, grad, *own_parts, *near_parts, conv_value,
     )
     near_stat, far_stat = ha_near(stat), ha_far(stat)
     layer_out, query_grad, done = call(
@@ -433,7 +476,7 @@
         [],
         cost(heads, rows, 2, 3),
         grad, conv_weight, kv, near_kv, far_kv, kv_a, near_kv_a, far_kv_a, kv_b, near_kv_b, far_kv_b,
-        exp_own, exp_near, exp_far, fac_own, fac_near, fac_far, attention, delta, near_stat, far_stat,
+        exp_own, exp_near, exp_far, fac_own, fac_near, fac_far, attention, delta, conv_value,
     )
     message = pl.pallas_call(
         functools.partial(pack_kernel, rows),
@@ -445,6 +488,7 @@
     )(far_qg, stat, near_stat, far_stat, done, near_qg_a, near_qg_b)
     message_a, message_b = ta_pair(message), ta_other(message)
 
+    conv_grad = convolution(True, qg, near_qg, qg_a, near_qg_a, qg_b, near_qg_b)
     scratch = [pltpu.VMEM((STAT_ROWS, 3 * rows), jnp.float32)]
     work = cost(heads, rows, 4, 1)
     sums = call(
@@ -458,7 +502,7 @@
     key_grad, value_grad = call(
         functools.partial(key_kernel, counts, width, 2), "key_side_2", [half, half], scratch, work,
         tile_mask, clip_lengths, kv, qg_b, near_qg_b, message_b, *sums,
-        conv_weight, qg, near_qg, far_qg, qg_a, near_qg_a, message_a,
+        conv_weight, conv_grad, far_qg, message_a,
     )
     return tuple(x.reshape(query_states.shape) for x in (layer_out, query_grad, key_grad, value_grad))
 

time: 92.9 us -> 86.9 us (0.935)
  waiting for transfers between devices: 21.1 us -> 9.5 us
  starting transfers between devices: 33.6 us -> 38.9 us
    ppermute x3, waiting for transfers between devices: 11.6 us -> 4.57 us  [ha_relay(): return lax.ppermute(near, 'ha', relay_pairs(lax.axis_size('ha')))]
    ppermute x1, waiting for transfers between devices: 3.02 us -> 0.01 us  [ha_far(): return lax.ppermute(x, 'ha', other_pairs(lax.axis_size('ha')))]
    ppermute x6, starting transfers between devices: 15.5 us -> 18.1 us  [ta_other(): return lax.ppermute(x, 'ta', other_pairs(lax.axis_size('ta')))]
    ppermute x6, starting transfers between devices: 2.38 us -> 4.13 us  [ta_pair(): return lax.ppermute(x, 'ta', flip_pairs(lax.axis_size('ta')))]
    ppermute x6, waiting for transfers between devices: 3.39 us -> 1.92 us  [ta_other(): return lax.ppermute(x, 'ta', other_pairs(lax.axis_size('ta')))]
    ppermute x1, starting transfers between devices: 2.33 us -> 3.28 us  [ha_far(): return lax.ppermute(x, 'ha', other_pairs(lax.axis_size('ha')))]
    pallas_call x7 -> x9, Pallas kernels: 32.9 us -> 33.5 us  [call(): pl.pallas_call(kernel, in_specs=[smem] * scalars + [vmem] * (len(args) -...]
  transfers between devices with their start and end apart: 20 -> 20, of which waited for: 6 -> 4; matrix products, arithmetic and copies ran while one was open for 0% -> 0% of each run, Pallas kernels for 29% -> 34%
where the time goes in v7:
time: 86.9 us; the launch traced here: 86.4 us
  starting transfers between devices  38.9 us (45%)
  Pallas kernels  33.8 us (39%)
  waiting for transfers between devices  9.5 us (11%)
  local copies, waits for them, and re-layouts  1.99 us (2%)
  other arithmetic  1.19 us (1%)
  between operations  1 us (1%)
    pallas_call x9, Pallas kernels, call(): pl.pallas_call(kernel, in_specs=[smem] * scalars + [vmem] * (len(args) -...  33.5 us
    ppermute x6, starting transfers between devices, ta_other(): return lax.ppermute(x, 'ta', other_pairs(lax.axis_size('ta')))  18.1 us
    ppermute x3, starting transfers between devices, ha_relay(): return lax.ppermute(near, 'ha', relay_pairs(lax.axis_size('ha')))  9.59 us
    ppermute x3, waiting for transfers between devices, ha_relay(): return lax.ppermute(near, 'ha', relay_pairs(lax.axis_size('ha')))  4.57 us
    ppermute x6, starting transfers between devices, ta_pair(): return lax.ppermute(x, 'ta', flip_pairs(lax.axis_size('ta')))  4.13 us
    ppermute x4, starting transfers between devices, ha_near(): return lax.ppermute(x, 'ha', flip_pairs(lax.axis_size('ha')))  3.81 us
    ppermute x1, starting transfers between devices, ha_far(): return lax.ppermute(x, 'ha', other_pairs(lax.axis_size('ha')))  3.28 us
    ppermute x4, waiting for transfers between devices, ha_near(): return lax.ppermute(x, 'ha', flip_pairs(lax.axis_size('ha')))  2.45 us
  transfers between devices with their start and end apart: 20, of which 4 were waited for; matrix products, arithmetic and copies ran while one was open for 0% of the time, Pallas kernels for 34%

profile of v7, /device:TPU:9, one launch (start us, length us, event | category | flops | bytes accessed | tf_op | source)
XLA Modules:
  0.0 86.4 jit_solution(13186818986900045285)
XLA Ops:
  0.6 0.0 copy-start.4
  0.6 1.2 %pad_maximum_fusion.own.rest_0_ = bf16[2,224,768]{2,1,0:T(8,128)(2,1)S(1)} fusion(bf16[1,224,768]{2,1,0:T(8,128)(2,1)} %bitcast.19, bf16[1,224,768]{2,1,0:T(8,128)(2,1)} %bitcast.21), kind=kLoop, calls=%fused_computation | loop fusion | flops 344064 | bytes 1376256 | tf_op jit(solution)/shard_map/stack | solution.py:442
  1.8 0.7 collective-permute-start.2
  2.6 1.2 %collective-permute-start = (bf16[224,768]{1,0:T(8,128)(2,1)}, bf16[224,768]{1,0:T(8,128)(2,1)S(1)}, u32[]{:S(2)}, u32[]{:S(2)}) collective-permute-start(bf16[224,768]{1,0:T(8,128)(2,1)} %bitcast.22), channel_id=1, source_target_pairs={{0,1},{1,0},{2,3},{3,2},{4,5},{5,4},{6,7},{7,6},{8,9},{9,8},{10,11... | collective-permute-start | bytes 1032200 | tf_op jit(solution)/shard_map/ppermute | solution.py:46
  3.8 0.5 collective-permute-done.2.rest_0_.pair.rest_3_
  4.4 1.0 %copy-done = bf16[2,2,56,768]{3,2,1,0:T(8,128)(2,1)S(1)} copy-done((bf16[2,2,56,768]{3,2,1,0:T(8,128)(2,1)S(1)}, bf16[2,2,56,768]{3,2,1,0:T(8,128)(2,1)}, u32[]{:S(2)}) %copy-start) | copy-done | bytes 344088
  5.3 1.0 %copy-done.2 = bf16[2,2,56,768]{3,2,1,0:T(8,128)(2,1)S(1)} copy-done((bf16[2,2,56,768]{3,2,1,0:T(8,128)(2,1)S(1)}, bf16[2,2,56,768]{3,2,1,0:T(8,128)(2,1)}, u32[]{:S(2)}) %copy-start.2) | copy-done | bytes 344088
  6.4 0.0 copy-start.1
  6.4 0.0 copy-start.3
  6.4 0.4 collective-permute-start.3
  6.8 3.2 %collective-permute-start.4 = (bf16[2,224,768]{2,1,0:T(8,128)(2,1)S(1)}, bf16[2,224,768]{2,1,0:T(8,128)(2,1)S(1)}, u32[]{:S(2)}, u32[]{:S(2)}) collective-permute-start(bf16[2,224,768]{2,1,0:T(8,128)(2,1)S(1)} %pair_up.4.own_ref.own), channel_id=1, source_target_pairs={{0,0},{8,16},{16,8},{24,24},{1,1},{9,17},{17,9},{25,25},{2,2},{10,... | collective-permute-start | bytes 2064392 | tf_op jit(solution)/shard_map/ppermute | solution.py:62
  10.0 2.4 %collective-permute-done.rest_0_.x_ref = bf16[224,768]{1,0:T(8,128)(2,1)S(1)} collective-permute-done((bf16[224,768]{1,0:T(8,128)(2,1)}, bf16[224,768]{1,0:T(8,128)(2,1)S(1)}, u32[]{:S(2)}, u32[]{:S(2)}) %collective-permute-start) | collective-permute-done | bytes 344096 | tf_op jit(solution)/shard_map/ppermute | solution.py:46
  12.4 0.0 copy-done.4
  12.5 0.0 copy-start.6
  12.5 0.0 copy-start.7
  12.5 1.3 %collective-permute-start.1 = (bf16[224,768]{1,0:T(8,128)(2,1)S(1)}, bf16[224,768]{1,0:T(8,128)(2,1)S(1)}, u32[]{:S(2)}, u32[]{:S(2)}) collective-permute-start(bf16[224,768]{1,0:T(8,128)(2,1)S(1)} %later.1), channel_id=1, source_target_pairs={{0,1},{1,0},{2,3},{3,2},{4,5},{5,4},{6,7},{7,6},{8,9},{9,8},{10,11... | collective-permute-start | bytes 1032200 | tf_op jit(solution)/shard_map/ppermute | solution.py:46
  13.8 3.2 %collective-permute-start.5 = (bf16[224,768]{1,0:T(8,128)(2,1)S(1)}, bf16[224,768]{1,0:T(8,128)(2,1)S(1)}, u32[]{:S(2)}, u32[]{:S(2)}) collective-permute-start(bf16[224,768]{1,0:T(8,128)(2,1)S(1)} %collective-permute-done.rest_0_.x_ref), channel_id=1, source_target_pairs={{0,2},{2,4},{3,1},{4,6},{5,3},{7,5},{8,10},{10,12},{11,9},{12,14},... | collective-permute-start | bytes 1032200 | tf_op jit(solution)/shard_map/ppermute | solution.py:50
  17.0 4.4 %collective-permute-start.7 = (bf16[2,224,768]{2,1,0:T(8,128)(2,1)S(1)}, bf16[2,224,768]{2,1,0:T(8,128)(2,1)S(1)}, u32[]{:S(2)}, u32[]{:S(2)}) collective-permute-start(bf16[2,224,768]{2,1,0:T(8,128)(2,1)S(1)} %pad_maximum_fusion.own.rest_0_), channel_id=1, source_target_pairs={{0,0},{8,16},{16,8},{24,24},{1,1},{9,17},{17,9},{25,25},{2,2},{10,... | collective-permute-start | bytes 2064392 | tf_op jit(solution)/shard_map/ppermute | solution.py:62
  21.4 0.0 collective-permute-done.1.y_ref.rest_0_
  21.4 0.0 collective-permute-done.3.rest_0_.own_ref.pair
  21.4 0.0 collective-permute-done.4.rest_1_.other.own_ref
  21.5 1.6 %collective-permute-start.8 = (bf16[2,224,768]{2,1,0:T(8,128)(2,1)S(1)}, bf16[2,224,768]{2,1,0:T(8,128)(2,1)S(1)}, u32[]{:S(2)}, u32[]{:S(2)}) collective-permute-start(bf16[2,224,768]{2,1,0:T(8,128)(2,1)S(1)} %pair_up.5.own.near.rest_1_), channel_id=1, source_target_pairs={{0,8},{8,0},{16,24},{24,16},{1,9},{9,1},{17,25},{25,17},{2,10},{10... | collective-permute-start | bytes 2064392 | tf_op jit(solution)/shard_map/ppermute | solution.py:58
  23.1 3.0 %collective-permute-start.10 = (bf16[2,224,768]{2,1,0:T(8,128)(2,1)S(1)}, bf16[2,224,768]{2,1,0:T(8,128)(2,1)S(1)}, u32[]{:S(2)}, u32[]{:S(2)}) collective-permute-start(bf16[2,224,768]{2,1,0:T(8,128)(2,1)S(1)} %pair_up.5.own.near.rest_1_), channel_id=1, source_target_pairs={{0,0},{8,16},{16,8},{24,24},{1,1},{9,17},{17,9},{25,25},{2,2},{10,... | collective-permute-start | bytes 2064392 | tf_op jit(solution)/shard_map/ppermute | solution.py:62
  26.2 0.0 collective-permute-done.5.x_ref.rest_1_
  26.2 0.0 copy-done.1
  26.2 0.0 copy-done.3
  26.3 1.3 %collective-permute-start.12 = (bf16[2,224,768]{2,1,0:T(8,128)(2,1)S(1)}, bf16[2,224,768]{2,1,0:T(8,128)(2,1)S(1)}, u32[]{:S(2)}, u32[]{:S(2)}) collective-permute-start(bf16[2,224,768]{2,1,0:T(8,128)(2,1)S(1)} %pair_up.7), channel_id=1, source_target_pairs={{0,1},{1,0},{2,3},{3,2},{4,5},{5,4},{6,7},{7,6},{8,9},{9,8},{10,11... | collective-permute-start | bytes 2064392 | tf_op jit(solution)/shard_map/ppermute | solution.py:46
  27.6 3.2 %collective-permute-start.6 = (bf16[224,768]{1,0:T(8,128)(2,1)S(1)}, bf16[224,768]{1,0:T(8,128)(2,1)S(1)}, u32[]{:S(2)}, u32[]{:S(2)}) collective-permute-start(bf16[224,768]{1,0:T(8,128)(2,1)S(1)} %collective-permute-done.1.y_ref.rest_0_), channel_id=1, source_target_pairs={{0,2},{2,4},{3,1},{4,6},{5,3},{7,5},{8,10},{10,12},{11,9},{12,14},... | collective-permute-start | bytes 1032200 | tf_op jit(solution)/shard_map/ppermute | solution.py:50
  30.8 0.0 collective-permute-done.7.other.rest_6_
  30.8 0.0 copy-done.6
  30.8 0.0 copy-done.7
  30.8 3.8 %scores_0.1 = (bf16[6,224,672]{2,1,0:T(8,128)(2,1)S(1)}, f32[224,768]{1,0:T(8,128)S(1)}, f32[224,768]{1,0:T(8,128)S(1)}, f32[224,768]{1,0:T(8,128)S(1)}) custom-call(s32[4,8,9]{2,1,0:T(8,128)S(1)} %copy-done.6, s32[8]{0:T(128)S(1)} %copy-done.7, bf16[224,768]{1,0:T(8,128)(2,1)S(1)} %bitcast.12, bf16[2,224,768]{2,1,0:T(8,128)(2,1)S(1)} %pad_maximum_fusion.own.rest_0_, ...), custom_call_target="tpu_custom_call" | custom-call | flops 462422016 | bytes 2752512 | tf_op jit(solution)/shard_map/scores_0/pallas_call | solution.py:383
  34.6 4.6 %collective-permute-done.6.y_ref = bf16[224,768]{1,0:T(8,128)(2,1)S(1)} collective-permute-done((bf16[224,768]{1,0:T(8,128)(2,1)S(1)}, bf16[224,768]{1,0:T(8,128)(2,1)S(1)}, u32[]{:S(2)}, u32[]{:S(2)}) %collective-permute-start.6) | collective-permute-done | bytes 344096 | tf_op jit(solution)/shard_map/ppermute | solution.py:50
  39.2 0.0 copy-start.5
  39.3 0.1 collective-permute-start.9
  39.4 1.9 %collective-permute-start.11 = (bf16[2,224,768]{2,1,0:T(8,128)(2,1)S(1)}, bf16[2,224,768]{2,1,0:T(8,128)(2,1)S(1)}, u32[]{:S(2)}, u32[]{:S(2)}) collective-permute-start(bf16[2,224,768]{2,1,0:T(8,128)(2,1)S(1)} %pair_up.6.own.rest_2_), channel_id=1, source_target_pairs={{0,0},{8,16},{16,8},{24,24},{1,1},{9,17},{17,9},{25,25},{2,2},{10,... | collective-permute-start | bytes 2064392 | tf_op jit(solution)/shard_map/ppermute | solution.py:62
  41.3 0.0 collective-permute-done.8.pair.near_pair.rest_4_
  41.3 0.0 collective-permute-done.10.other.near_other.rest_7_
  41.3 3.8 %scores_1.1 = (bf16[6,224,672]{2,1,0:T(8,128)(2,1)S(1)}, f32[224,768]{1,0:T(8,128)S(1)}, f32[224,768]{1,0:T(8,128)S(1)}, f32[224,768]{1,0:T(8,128)S(1)}) custom-call(s32[4,8,9]{2,1,0:T(8,128)S(1)} %copy-done.6, s32[8]{0:T(128)S(1)} %copy-done.7, bf16[224,768]{1,0:T(8,128)(2,1)S(1)} %bitcast.13, bf16[2,224,768]{2,1,0:T(8,128)(2,1)S(1)} %pair_up.5.own.near.rest_1_, ...), custom_call_target="tpu_custom_call" | custom-call | flops 462422016 | bytes 2752512 | tf_op jit(solution)/shard_map/scores_1/pallas_call | solution.py:383
  45.2 0.0 collective-permute-done.12.refs_0_
  45.2 3.6 %collective-permute-start.13 = (bf16[2,224,768]{2,1,0:T(8,128)(2,1)S(1)}, bf16[2,224,768]{2,1,0:T(8,128)(2,1)S(1)}, u32[]{:S(2)}, u32[]{:S(2)}) collective-permute-start(bf16[2,224,768]{2,1,0:T(8,128)(2,1)S(1)} %gate.1.near_ref.near), channel_id=1, source_target_pairs={{0,0},{8,16},{16,8},{24,24},{1,1},{9,17},{17,9},{25,25},{2,2},{10,... | collective-permute-start | bytes 2064392 | tf_op jit(solution)/shard_map/ppermute | solution.py:62
  48.8 3.2 %collective-permute-start.14 = (bf16[2,224,768]{2,1,0:T(8,128)(2,1)S(1)}, bf16[2,224,768]{2,1,0:T(8,128)(2,1)S(1)}, u32[]{:S(2)}, u32[]{:S(2)}) collective-permute-start(bf16[2,224,768]{2,1,0:T(8,128)(2,1)S(1)} %gate.1.near_ref.near), channel_id=1, source_target_pairs={{0,2},{2,4},{3,1},{4,6},{5,3},{7,5},{8,10},{10,12},{11,9},{12,14},... | collective-permute-start | bytes 2064392 | tf_op jit(solution)/shard_map/ppermute | solution.py:50
  52.1 0.1 collective-permute-start.17
  52.1 1.8 %convolution.2.rest_7_.rest_17_ = f32[224,768]{1,0:T(8,128)S(1)} custom-call(bf16[2,224,768]{2,1,0:T(8,128)(2,1)S(1)} %pad_maximum_fusion.own.rest_0_, bf16[2,224,768]{2,1,0:T(8,128)(2,1)S(1)} %pair_up.5.own.near.rest_1_, bf16[2,224,768]{2,1,0:T(8,128)(2,1)S(1)} %collective-permute-done.2.rest_0_.pair.rest_3_, ...), custom_call_target="tpu_custom_call" | custom-call | flops 231211008 | bytes 2752512 | tf_op jit(solution)/shard_map/convolution/pallas_call | solution.py:383
  53.9 0.0 collective-permute-done.9.pair.rest_5_
  53.9 0.0 collective-permute-done.11.other.rest_8_
  53.9 4.5 %scores_2.1 = (bf16[6,224,672]{2,1,0:T(8,128)(2,1)S(1)}, f32[224,768]{1,0:T(8,128)S(1)}, f32[224,768]{1,0:T(8,128)S(1)}, f32[224,768]{1,0:T(8,128)S(1)}, f32[224...) custom-call(s32[4,8,9]{2,1,0:T(8,128)S(1)} %copy-done.6, s32[8]{0:T(128)S(1)} %copy-done.7, ...), custom_call_target="tpu_custom_call" | custom-call | flops 462422016 | bytes 2752512 | tf_op jit(solution)/shard_map/scores_2/pallas_call | solution.py:383
  58.5 0.0 collective-permute-start.15
  58.5 3.3 %collective-permute-start.16 = (f32[16,224]{1,0:T(8,128)S(1)}, f32[16,224]{1,0:T(8,128)S(1)}, u32[]{:S(2)}, u32[]{:S(2)}) collective-permute-start(f32[16,224]{1,0:T(8,128)S(1)} %get-tuple-element.44.own_ref.rest_0_), channel_id=1, source_target_pairs={{0,0},{1,2},{2,1},{3,4},{4,3},{5,6},{6,5},{7,7},{8,8},{9,10},{10,9... | collective-permute-start | bytes 43016 | tf_op jit(solution)/shard_map/ppermute | solution.py:54
  61.8 5.7 %query_side.1 = (bf16[224,768]{1,0:T(8,128)(2,1)}, bf16[224,768]{1,0:T(8,128)(2,1)}, f32[8,128]{1,0:T(8,128)S(1)}) custom-call(bf16[224,768]{1,0:T(8,128)(2,1)S(1)} %bitcast.18, bf16[27,768]{1,0:T(8,128)(2,1)S(1)} %copy-done.5, bf16[2,224,768]{2,1,0:T(8,128)(2,1)S(1)} %pad_maximum_fusion.own.rest_0_, bf16[2,224,768]{2,1,0:T(8,128)(2,1)S(1)} %pair_up.5.own.near.rest_1_, ...), custom_call_target="tpu_custom_call" | custom-call | flops 1387266048 | bytes 8257536 | tf_op jit(solution)/shard_map/query_side/pallas_call | solution.py:383
  67.5 0.0 collective-permute-done.15.near_ref.rest_1_
  67.5 0.0 collective-permute-done.16.far_ref.rest_2_
  67.5 0.0 collective-permute-done.13.rest_2_.near_other.near_ref
  67.5 0.0 collective-permute-done.14.qg_ref.far_ref.rest_4_
  67.5 0.0 collective-permute-done.17.rest_1_.near_ref.near_pair
  67.5 0.1 pack.1
  67.6 1.1 %collective-permute-start.19 = (bf16[496,768]{1,0:T(8,128)(2,1)S(1)}, bf16[496,768]{1,0:T(8,128)(2,1)S(1)}, u32[]{:S(2)}, u32[]{:S(2)}) collective-permute-start(bf16[496,768]{1,0:T(8,128)(2,1)S(1)} %pack.1), channel_id=1, source_target_pairs={{0,8},{8,0},{16,24},{24,16},{1,9},{9,1},{17,25},{25,17},{2,10},{10... | collective-permute-start | bytes 2285576 | tf_op jit(solution)/shard_map/ppermute | solution.py:58
  68.7 1.9 %collective-permute-start.18 = (bf16[496,768]{1,0:T(8,128)(2,1)S(1)}, bf16[496,768]{1,0:T(8,128)(2,1)S(1)}, u32[]{:S(2)}, u32[]{:S(2)}) collective-permute-start(bf16[496,768]{1,0:T(8,128)(2,1)S(1)} %pack.1), channel_id=1, source_target_pairs={{0,0},{8,16},{16,8},{24,24},{1,1},{9,17},{17,9},{25,25},{2,2},{10,... | collective-permute-start | bytes 2285576 | tf_op jit(solution)/shard_map/ppermute | solution.py:62
  70.6 1.8 %convolution.3.rest_3_ = f32[224,768]{1,0:T(8,128)S(1)} custom-call(bf16[2,224,768]{2,1,0:T(8,128)(2,1)S(1)} %pair_up.4.own_ref.own, bf16[2,224,768]{2,1,0:T(8,128)(2,1)S(1)} %gate.1.near_ref.near, bf16[2,224,768]{2,1,0:T(8,128)(2,1)S(1)} %collective-permute-done.3.rest_0_.own_ref.pair, ...), custom_call_target="tpu_custom_call" | custom-call | flops 231211008 | bytes 2752512 | tf_op jit(solution)/shard_map/convolution/pallas_call | solution.py:383
  72.4 3.6 %key_side_0.1 = (f32[224,768]{1,0:T(8,128)S(1)}, f32[224,768]{1,0:T(8,128)S(1)}) custom-call(s32[4,8,9]{2,1,0:T(8,128)S(1)} %copy-done.6, s32[8]{0:T(128)S(1)} %copy-done.7, bf16[2,224,768]{2,1,0:T(8,128)(2,1)S(1)} %pad_maximum_fusion.own.rest_0_, bf16[2,224,768]{2,1,0:T(8,128)(2,1)S(1)} %pair_up.4.own_ref.own, bf16[2,224,768]{2,1,0:T(8,128)(2,1)S(1)} %gate.1.near_ref.near, ...), custom_call_target="tpu_custom_call" | custom-call | flops 924844032 | bytes 2752512 | tf_op jit(solution)/shard_map/key_side_0/pallas_call | solution.py:383
  76.0 0.0 collective-permute-done.19.far_ref.rest_5_
  76.0 3.8 %key_side_1.1 = (f32[224,768]{1,0:T(8,128)S(1)}, f32[224,768]{1,0:T(8,128)S(1)}) custom-call(s32[4,8,9]{2,1,0:T(8,128)S(1)} %copy-done.6, s32[8]{0:T(128)S(1)} %copy-done.7, bf16[2,224,768]{2,1,0:T(8,128)(2,1)S(1)} %pad_maximum_fusion.own.rest_0_, bf16[2,224,768]{2,1,0:T(8,128)(2,1)S(1)} %collective-permute-done.3.rest_0_.own_ref.pair, ...), custom_call_target="tpu_custom_call" | custom-call | flops 924844032 | bytes 2752512 | tf_op jit(solution)/shard_map/key_side_1/pallas_call | solution.py:383
  79.8 1.9 %collective-permute-done.18.far_ref = bf16[496,768]{1,0:T(8,128)(2,1)S(1)} collective-permute-done((bf16[496,768]{1,0:T(8,128)(2,1)S(1)}, bf16[496,768]{1,0:T(8,128)(2,1)S(1)}, u32[]{:S(2)}, u32[]{:S(2)}) %collective-permute-start.18) | collective-permute-done | bytes 761888 | tf_op jit(solution)/shard_map/ppermute | solution.py:62
  81.7 4.7 %key_side_2.1 = (bf16[224,768]{1,0:T(8,128)(2,1)}, bf16[224,768]{1,0:T(8,128)(2,1)}) custom-call(s32[4,8,9]{2,1,0:T(8,128)S(1)} %copy-done.6, s32[8]{0:T(128)S(1)} %copy-done.7, bf16[2,224,768]{2,1,0:T(8,128)(2,1)S(1)} %pad_maximum_fusion.own.rest_0_, bf16[2,224,768]{2,1,0:T(8,128)(2,1)S(1)} %collective-permute-done.4.rest_1_.other.own_ref, ...), custom_call_target="tpu_custom_call" | custom-call | flops 924844032 | bytes 2752512 | tf_op jit(solution)/shard_map/key_side_2/pallas_call | solution.py:383
  (9 shorter events, 0.2 us)
Async XLA Ops:
  0.6 11.8 %copy-start.4 = (bf16[2,2,56,768]{3,2,1,0:T(8,128)(2,1)S(1)}, bf16[2,2,56,768]{3,2,1,0:T(8,128)(2,1)}, u32[]{:S(2)}) copy-start(bf16[2,2,56,768]{3,2,1,0:T(8,128)(2,1)} %param.9) | copy-start | bytes 1032196
  1.8 2.5 %collective-permute-start.2 = (bf16[2,224,768]{2,1,0:T(8,128)(2,1)S(1)}, bf16[2,224,768]{2,1,0:T(8,128)(2,1)S(1)}, u32[]{:S(2)}, u32[]{:S(2)}) collective-permute-start(bf16[2,224,768]{2,1,0:T(8,128)(2,1)S(1)} %pad_maximum_fusion.own.rest_0_), channel_id=1, source_target_pairs={{0,8},{8,0},{16,24},{24,16},{1,9},{9,1},{17,25},{25,17},{2,10},{10... | collective-permute-start | bytes 2064392 | tf_op jit(solution)/shard_map/ppermute | solution.py:58
  2.6 9.9 %collective-permute-start = (bf16[224,768]{1,0:T(8,128)(2,1)}, bf16[224,768]{1,0:T(8,128)(2,1)S(1)}, u32[]{:S(2)}, u32[]{:S(2)}) collective-permute-start(bf16[224,768]{1,0:T(8,128)(2,1)} %bitcast.22), channel_id=1, source_target_pairs={{0,1},{1,0},{2,3},{3,2},{4,5},{5,4},{6,7},{7,6},{8,9},{9,8},{10,11... | collective-permute-start | bytes 1032200 | tf_op jit(solution)/shard_map/ppermute | solution.py:46
  4.3 1.0 %copy-start = (bf16[2,2,56,768]{3,2,1,0:T(8,128)(2,1)S(1)}, bf16[2,2,56,768]{3,2,1,0:T(8,128)(2,1)}, u32[]{:S(2)}) copy-start(bf16[2,2,56,768]{3,2,1,0:T(8,128)(2,1)} %param.7) | copy-start | bytes 1032196
  5.3 1.0 %copy-start.2 = (bf16[2,2,56,768]{3,2,1,0:T(8,128)(2,1)S(1)}, bf16[2,2,56,768]{3,2,1,0:T(8,128)(2,1)}, u32[]{:S(2)}) copy-start(bf16[2,2,56,768]{3,2,1,0:T(8,128)(2,1)} %param.11) | copy-start | bytes 1032196
  6.4 19.9 %copy-start.1 = (bf16[2,2,56,768]{3,2,1,0:T(8,128)(2,1)S(1)}, bf16[2,2,56,768]{3,2,1,0:T(8,128)(2,1)}, u32[]{:S(2)}) copy-start(bf16[2,2,56,768]{3,2,1,0:T(8,128)(2,1)} %param.7) | copy-start | bytes 1032196
  6.4 19.9 %copy-start.3 = (bf16[2,2,56,768]{3,2,1,0:T(8,128)(2,1)S(1)}, bf16[2,2,56,768]{3,2,1,0:T(8,128)(2,1)}, u32[]{:S(2)}) copy-start(bf16[2,2,56,768]{3,2,1,0:T(8,128)(2,1)} %param.11) | copy-start | bytes 1032196
  6.4 15.0 %collective-permute-start.3 = (bf16[2,224,768]{2,1,0:T(8,128)(2,1)S(1)}, bf16[2,224,768]{2,1,0:T(8,128)(2,1)S(1)}, u32[]{:S(2)}, u32[]{:S(2)}) collective-permute-start(bf16[2,224,768]{2,1,0:T(8,128)(2,1)S(1)} %pair_up.4.own_ref.own), channel_id=1, source_target_pairs={{0,8},{8,0},{16,24},{24,16},{1,9},{9,1},{17,25},{25,17},{2,10},{10... | collective-permute-start | bytes 2064392 | tf_op jit(solution)/shard_map/ppermute | solution.py:58
  6.8 14.6 %collective-permute-start.4 = (bf16[2,224,768]{2,1,0:T(8,128)(2,1)S(1)}, bf16[2,224,768]{2,1,0:T(8,128)(2,1)S(1)}, u32[]{:S(2)}, u32[]{:S(2)}) collective-permute-start(bf16[2,224,768]{2,1,0:T(8,128)(2,1)S(1)} %pair_up.4.own_ref.own), channel_id=1, source_target_pairs={{0,0},{8,16},{16,8},{24,24},{1,1},{9,17},{17,9},{25,25},{2,2},{10,... | collective-permute-start | bytes 2064392 | tf_op jit(solution)/shard_map/ppermute | solution.py:62
  12.5 18.3 %copy-start.6 = (s32[4,8,9]{2,1,0:T(8,128)S(1)}, s32[4,8,9]{2,1,0:T(8,128)}, u32[]{:S(2)}) copy-start(s32[4,8,9]{2,1,0:T(8,128)} %mask_ref.11) | copy-start | bytes 3460
  12.5 18.3 %copy-start.7 = (s32[8]{0:T(128)S(1)}, s32[8]{0:T(128)}, u32[]{:S(2)}) copy-start(s32[8]{0:T(128)} %clip_ref.11) | copy-start | bytes 100
  12.5 8.9 %collective-permute-start.1 = (bf16[224,768]{1,0:T(8,128)(2,1)S(1)}, bf16[224,768]{1,0:T(8,128)(2,1)S(1)}, u32[]{:S(2)}, u32[]{:S(2)}) collective-permute-start(bf16[224,768]{1,0:T(8,128)(2,1)S(1)} %later.1), channel_id=1, source_target_pairs={{0,1},{1,0},{2,3},{3,2},{4,5},{5,4},{6,7},{7,6},{8,9},{9,8},{10,11... | collective-permute-start | bytes 1032200 | tf_op jit(solution)/shard_map/ppermute | solution.py:46
  13.8 12.4 %collective-permute-start.5 = (bf16[224,768]{1,0:T(8,128)(2,1)S(1)}, bf16[224,768]{1,0:T(8,128)(2,1)S(1)}, u32[]{:S(2)}, u32[]{:S(2)}) collective-permute-start(bf16[224,768]{1,0:T(8,128)(2,1)S(1)} %collective-permute-done.rest_0_.x_ref), channel_id=1, source_target_pairs={{0,2},{2,4},{3,1},{4,6},{5,3},{7,5},{8,10},{10,12},{11,9},{12,14},... | collective-permute-start | bytes 1032200 | tf_op jit(solution)/shard_map/ppermute | solution.py:50
  17.0 13.8 %collective-permute-start.7 = (bf16[2,224,768]{2,1,0:T(8,128)(2,1)S(1)}, bf16[2,224,768]{2,1,0:T(8,128)(2,1)S(1)}, u32[]{:S(2)}, u32[]{:S(2)}) collective-permute-start(bf16[2,224,768]{2,1,0:T(8,128)(2,1)S(1)} %pad_maximum_fusion.own.rest_0_), channel_id=1, source_target_pairs={{0,0},{8,16},{16,8},{24,24},{1,1},{9,17},{17,9},{25,25},{2,2},{10,... | collective-permute-start | bytes 2064392 | tf_op jit(solution)/shard_map/ppermute | solution.py:62
  21.5 19.8 %collective-permute-start.8 = (bf16[2,224,768]{2,1,0:T(8,128)(2,1)S(1)}, bf16[2,224,768]{2,1,0:T(8,128)(2,1)S(1)}, u32[]{:S(2)}, u32[]{:S(2)}) collective-permute-start(bf16[2,224,768]{2,1,0:T(8,128)(2,1)S(1)} %pair_up.5.own.near.rest_1_), channel_id=1, source_target_pairs={{0,8},{8,0},{16,24},{24,16},{1,9},{9,1},{17,25},{25,17},{2,10},{10... | collective-permute-start | bytes 2064392 | tf_op jit(solution)/shard_map/ppermute | solution.py:58
  23.1 18.2 %collective-permute-start.10 = (bf16[2,224,768]{2,1,0:T(8,128)(2,1)S(1)}, bf16[2,224,768]{2,1,0:T(8,128)(2,1)S(1)}, u32[]{:S(2)}, u32[]{:S(2)}) collective-permute-start(bf16[2,224,768]{2,1,0:T(8,128)(2,1)S(1)} %pair_up.5.own.near.rest_1_), channel_id=1, source_target_pairs={{0,0},{8,16},{16,8},{24,24},{1,1},{9,17},{17,9},{25,25},{2,2},{10,... | collective-permute-start | bytes 2064392 | tf_op jit(solution)/shard_map/ppermute | solution.py:62
  26.3 18.9 %collective-permute-start.12 = (bf16[2,224,768]{2,1,0:T(8,128)(2,1)S(1)}, bf16[2,224,768]{2,1,0:T(8,128)(2,1)S(1)}, u32[]{:S(2)}, u32[]{:S(2)}) collective-permute-start(bf16[2,224,768]{2,1,0:T(8,128)(2,1)S(1)} %pair_up.7), channel_id=1, source_target_pairs={{0,1},{1,0},{2,3},{3,2},{4,5},{5,4},{6,7},{7,6},{8,9},{9,8},{10,11... | collective-permute-start | bytes 2064392 | tf_op jit(solution)/shard_map/ppermute | solution.py:46
  27.6 11.6 %collective-permute-start.6 = (bf16[224,768]{1,0:T(8,128)(2,1)S(1)}, bf16[224,768]{1,0:T(8,128)(2,1)S(1)}, u32[]{:S(2)}, u32[]{:S(2)}) collective-permute-start(bf16[224,768]{1,0:T(8,128)(2,1)S(1)} %collective-permute-done.1.y_ref.rest_0_), channel_id=1, source_target_pairs={{0,2},{2,4},{3,1},{4,6},{5,3},{7,5},{8,10},{10,12},{11,9},{12,14},... | collective-permute-start | bytes 1032200 | tf_op jit(solution)/shard_map/ppermute | solution.py:50
  39.2 12.9 %copy-start.5 = (bf16[27,768]{1,0:T(8,128)(2,1)S(1)}, bf16[27,768]{1,0:T(8,128)(2,1)}, u32[]{:S(2)}) copy-start(bf16[27,768]{1,0:T(8,128)(2,1)} %rest_2_.1) | copy-start | bytes 124420
  39.3 14.6 %collective-permute-start.9 = (bf16[2,224,768]{2,1,0:T(8,128)(2,1)S(1)}, bf16[2,224,768]{2,1,0:T(8,128)(2,1)S(1)}, u32[]{:S(2)}, u32[]{:S(2)}) collective-permute-start(bf16[2,224,768]{2,1,0:T(8,128)(2,1)S(1)} %pair_up.6.own.rest_2_), channel_id=1, source_target_pairs={{0,8},{8,0},{16,24},{24,16},{1,9},{9,1},{17,25},{25,17},{2,10},{10... | collective-permute-start | bytes 2064392 | tf_op jit(solution)/shard_map/ppermute | solution.py:58
  39.4 14.5 %collective-permute-start.11 = (bf16[2,224,768]{2,1,0:T(8,128)(2,1)S(1)}, bf16[2,224,768]{2,1,0:T(8,128)(2,1)S(1)}, u32[]{:S(2)}, u32[]{:S(2)}) collective-permute-start(bf16[2,224,768]{2,1,0:T(8,128)(2,1)S(1)} %pair_up.6.own.rest_2_), channel_id=1, source_target_pairs={{0,0},{8,16},{16,8},{24,24},{1,1},{9,17},{17,9},{25,25},{2,2},{10,... | collective-permute-start | bytes 2064392 | tf_op jit(solution)/shard_map/ppermute | solution.py:62
  45.2 22.3 %collective-permute-start.13 = (bf16[2,224,768]{2,1,0:T(8,128)(2,1)S(1)}, bf16[2,224,768]{2,1,0:T(8,128)(2,1)S(1)}, u32[]{:S(2)}, u32[]{:S(2)}) collective-permute-start(bf16[2,224,768]{2,1,0:T(8,128)(2,1)S(1)} %gate.1.near_ref.near), channel_id=1, source_target_pairs={{0,0},{8,16},{16,8},{24,24},{1,1},{9,17},{17,9},{25,25},{2,2},{10,... | collective-permute-start | bytes 2064392 | tf_op jit(solution)/shard_map/ppermute | solution.py:62
  48.8 18.7 %collective-permute-start.14 = (bf16[2,224,768]{2,1,0:T(8,128)(2,1)S(1)}, bf16[2,224,768]{2,1,0:T(8,128)(2,1)S(1)}, u32[]{:S(2)}, u32[]{:S(2)}) collective-permute-start(bf16[2,224,768]{2,1,0:T(8,128)(2,1)S(1)} %gate.1.near_ref.near), channel_id=1, source_target_pairs={{0,2},{2,4},{3,1},{4,6},{5,3},{7,5},{8,10},{10,12},{11,9},{12,14},... | collective-permute-start | bytes 2064392 | tf_op jit(solution)/shard_map/ppermute | solution.py:50
  52.1 15.5 %collective-permute-start.17 = (bf16[2,224,768]{2,1,0:T(8,128)(2,1)S(1)}, bf16[2,224,768]{2,1,0:T(8,128)(2,1)S(1)}, u32[]{:S(2)}, u32[]{:S(2)}) collective-permute-start(bf16[2,224,768]{2,1,0:T(8,128)(2,1)S(1)} %gate.1.near_ref.near), channel_id=1, source_target_pairs={{0,8},{8,0},{16,24},{24,16},{1,9},{9,1},{17,25},{25,17},{2,10},{10... | collective-permute-start | bytes 2064392 | tf_op jit(solution)/shard_map/ppermute | solution.py:58
  58.5 9.0 %collective-permute-start.15 = (f32[16,224]{1,0:T(8,128)S(1)}, f32[16,224]{1,0:T(8,128)S(1)}, u32[]{:S(2)}, u32[]{:S(2)}) collective-permute-start(f32[16,224]{1,0:T(8,128)S(1)} %get-tuple-element.44.own_ref.rest_0_), channel_id=1, source_target_pairs={{0,1},{1,0},{2,3},{3,2},{4,5},{5,4},{6,7},{7,6},{8,9},{9,8},{10,11... | collective-permute-start | bytes 43016 | tf_op jit(solution)/shard_map/ppermute | solution.py:46
  58.5 9.0 %collective-permute-start.16 = (f32[16,224]{1,0:T(8,128)S(1)}, f32[16,224]{1,0:T(8,128)S(1)}, u32[]{:S(2)}, u32[]{:S(2)}) collective-permute-start(f32[16,224]{1,0:T(8,128)S(1)} %get-tuple-element.44.own_ref.rest_0_), channel_id=1, source_target_pairs={{0,0},{1,2},{2,1},{3,4},{4,3},{5,6},{6,5},{7,7},{8,8},{9,10},{10,9... | collective-permute-start | bytes 43016 | tf_op jit(solution)/shard_map/ppermute | solution.py:54
  67.6 8.4 %collective-permute-start.19 = (bf16[496,768]{1,0:T(8,128)(2,1)S(1)}, bf16[496,768]{1,0:T(8,128)(2,1)S(1)}, u32[]{:S(2)}, u32[]{:S(2)}) collective-permute-start(bf16[496,768]{1,0:T(8,128)(2,1)S(1)} %pack.1), channel_id=1, source_target_pairs={{0,8},{8,0},{16,24},{24,16},{1,9},{9,1},{17,25},{25,17},{2,10},{10... | collective-permute-start | bytes 2285576 | tf_op jit(solution)/shard_map/ppermute | solution.py:58
  68.7 13.0 %collective-permute-start.18 = (bf16[496,768]{1,0:T(8,128)(2,1)S(1)}, bf16[496,768]{1,0:T(8,128)(2,1)S(1)}, u32[]{:S(2)}, u32[]{:S(2)}) collective-permute-start(bf16[496,768]{1,0:T(8,128)(2,1)S(1)} %pack.1), channel_id=1, source_target_pairs={{0,0},{8,16},{16,8},{24,24},{1,1},{9,17},{17,9},{25,25},{2,2},{10,... | collective-permute-start | bytes 2285576 | tf_op jit(solution)/shard_map/ppermute | solution.py:62

commit v8 on v7

--- a/solution.py
+++ b/solution.py
@@ -194,19 +194,24 @@
 
     def body(step, _):
         hs = [step * UNROLL + u for u in range(UNROLL)]
+        tops_, accs, sums_ = [], [], []
+        scored = []
         for h in hs:
+            keys = jnp.concatenate([ref[0, :, head_columns(h)] for ref in slots], axis=0)
+            s = dot_last(query_ref[:, head_columns(h)], keys) * (scale * LOG2E) + bias[...]
+            scored.append(s)
+            tops_.append(jnp.maximum(jnp.max(s, axis=1, keepdims=True), FLOOR))
+        for u, h in enumerate(hs):
+            e = jnp.exp2(scored[u] - tops_[u]).astype(jnp.bfloat16)
+            exp_ref[h] = e
+            values = jnp.concatenate([ref[1, :, head_columns(h)] for ref in slots], axis=0)
+            both = dot(e, jnp.concatenate([values, jnp.ones_like(values)], axis=1))
+            accs.append(both[:, :HEAD_DIM])
+            sums_.append(both[:, HEAD_DIM:])
+        for u, h in enumerate(hs):
             cols = head_columns(h)
-            keys = jnp.concatenate([ref[0, :, cols] for ref in slots], axis=0)
-            values = jnp.concatenate([ref[1, :, cols] for ref in slots], axis=0)
-            s = dot_last(query_ref[:, cols], keys) * (scale * LOG2E) + bias[...]
-            top = jnp.maximum(jnp.max(s, axis=1, keepdims=True), FLOOR)
-            e = jnp.exp2(s - top)
-            total = jnp.sum(e, axis=1, keepdims=True)
-            e = e.astype(jnp.bfloat16)
-            exp_ref[h] = e
-            acc = dot(e, values)
-            top = jnp.broadcast_to(top, (rows, HEAD_DIM))
-            total = jnp.broadcast_to(total, (rows, HEAD_DIM))
+            acc, total = accs[u], sums_[u]
+            top = jnp.broadcast_to(tops_[u], (rows, HEAD_DIM))
             if not last:
                 sum_ref[:, cols], top_ref[:, cols], total_ref[:, cols] = acc, top, total
                 continue
@@ -451,9 +456,9 @@
     near_kv = pair_up(near_k, near_v, qg_a, qg_b)
     near_kv_a, near_kv_b = ta_pair(near_kv), ta_other(near_kv)
     near_qg = ha_near(pair_up(query, grad, near_v, far_k))
-    far_kv = pair_up(far_k, far_v, own_parts[0])
+    exp_near, *near_parts = scores(1, (near_kv, near_kv_a, near_kv_b))
+    far_kv = pair_up(far_k, far_v, own_parts[0], near_parts[0])
     far_kv_a, far_kv_b = ta_pair(far_kv), ta_other(far_kv)
-    exp_near, *near_parts = scores(1, (near_kv, near_kv_a, near_kv_b))
 
     conv_value = convolution(False, kv, near_kv, kv_a, near_kv_a, kv_b, near_kv_b)
 

time: 86.9 us -> 84.8 us (0.976)
  Pallas kernels: 33.8 us -> 31.8 us
    ppermute x3, waiting for transfers between devices: 4.57 us -> 0.01 us  [ha_relay(): return lax.ppermute(near, 'ha', relay_pairs(lax.axis_size('ha')))]
    ppermute x6, waiting for transfers between devices: 1.92 us -> 5.82 us  [ta_other(): return lax.ppermute(x, 'ta', other_pairs(lax.axis_size('ta')))]
    pallas_call x9, Pallas kernels: 33.5 us -> 31.5 us  [call(): pl.pallas_call(kernel, in_specs=[smem] * scalars + [vmem] * (len(args) -...]
    ppermute x6, starting transfers between devices: 18.1 us -> 20.1 us  [ta_other(): return lax.ppermute(x, 'ta', other_pairs(lax.axis_size('ta')))]
    ppermute x6, starting transfers between devices: 4.13 us -> 3.04 us  [ta_pair(): return lax.ppermute(x, 'ta', flip_pairs(lax.axis_size('ta')))]
  transfers between devices with their start and end apart: 20 -> 20, of which waited for: 4 -> 5; matrix products, arithmetic and copies ran while one was open for 0% -> 0% of each run, Pallas kernels for 34% -> 32%
where the time goes in v8:
time: 84.8 us; the launch traced here: 84.3 us
  starting transfers between devices  39.5 us (47%)
  Pallas kernels  31.8 us (38%)
  waiting for transfers between devices  8.84 us (10%)
  local copies, waits for them, and re-layouts  1.99 us (2%)
  other arithmetic  1.19 us (1%)
  between operations  1.02 us (1%)
    pallas_call x9, Pallas kernels, call(): pl.pallas_call(kernel, in_specs=[smem] * scalars + [vmem] * (len(args) -...  31.5 us
    ppermute x6, starting transfers between devices, ta_other(): return lax.ppermute(x, 'ta', other_pairs(lax.axis_size('ta')))  20.1 us
    ppermute x3, starting transfers between devices, ha_relay(): return lax.ppermute(near, 'ha', relay_pairs(lax.axis_size('ha')))  9.59 us
    ppermute x6, waiting for transfers between devices, ta_other(): return lax.ppermute(x, 'ta', other_pairs(lax.axis_size('ta')))  5.82 us
    ppermute x4, starting transfers between devices, ha_near(): return lax.ppermute(x, 'ha', flip_pairs(lax.axis_size('ha')))  3.81 us
    ppermute x6, starting transfers between devices, ta_pair(): return lax.ppermute(x, 'ta', flip_pairs(lax.axis_size('ta')))  3.04 us
    ppermute x1, starting transfers between devices, ha_far(): return lax.ppermute(x, 'ha', other_pairs(lax.axis_size('ha')))  2.96 us
    ppermute x4, waiting for transfers between devices, ha_near(): return lax.ppermute(x, 'ha', flip_pairs(lax.axis_size('ha')))  2.45 us
  transfers between devices with their start and end apart: 20, of which 5 were waited for; matrix products, arithmetic and copies ran while one was open for 0% of the time, Pallas kernels for 32%

profile of v8, /device:TPU:9, one launch (start us, length us, event | category | flops | bytes accessed | tf_op | source)
XLA Modules:
  0.0 84.3 jit_solution(16628965209052058671)
XLA Ops:
  0.6 0.0 copy-start.4
  0.6 1.2 %pad_maximum_fusion.own.rest_0_ = bf16[2,224,768]{2,1,0:T(8,128)(2,1)S(1)} fusion(bf16[1,224,768]{2,1,0:T(8,128)(2,1)} %bitcast.19, bf16[1,224,768]{2,1,0:T(8,128)(2,1)} %bitcast.21), kind=kLoop, calls=%fused_computation | loop fusion | flops 344064 | bytes 1376256 | tf_op jit(solution)/shard_map/stack | solution.py:447
  1.8 0.7 collective-permute-start.2
  2.6 1.2 %collective-permute-start = (bf16[224,768]{1,0:T(8,128)(2,1)}, bf16[224,768]{1,0:T(8,128)(2,1)S(1)}, u32[]{:S(2)}, u32[]{:S(2)}) collective-permute-start(bf16[224,768]{1,0:T(8,128)(2,1)} %bitcast.22), channel_id=1, source_target_pairs={{0,1},{1,0},{2,3},{3,2},{4,5},{5,4},{6,7},{7,6},{8,9},{9,8},{10,11... | collective-permute-start | bytes 1032200 | tf_op jit(solution)/shard_map/ppermute | solution.py:46
  3.8 0.5 collective-permute-done.2.rest_0_.pair.rest_3_
  4.4 1.0 %copy-done = bf16[2,2,56,768]{3,2,1,0:T(8,128)(2,1)S(1)} copy-done((bf16[2,2,56,768]{3,2,1,0:T(8,128)(2,1)S(1)}, bf16[2,2,56,768]{3,2,1,0:T(8,128)(2,1)}, u32[]{:S(2)}) %copy-start) | copy-done | bytes 344088
  5.3 1.0 %copy-done.2 = bf16[2,2,56,768]{3,2,1,0:T(8,128)(2,1)S(1)} copy-done((bf16[2,2,56,768]{3,2,1,0:T(8,128)(2,1)S(1)}, bf16[2,2,56,768]{3,2,1,0:T(8,128)(2,1)}, u32[]{:S(2)}) %copy-start.2) | copy-done | bytes 344088
  6.4 0.0 copy-start.1
  6.4 0.0 copy-start.3
  6.4 0.4 collective-permute-start.3
  6.8 3.2 %collective-permute-start.4 = (bf16[2,224,768]{2,1,0:T(8,128)(2,1)S(1)}, bf16[2,224,768]{2,1,0:T(8,128)(2,1)S(1)}, u32[]{:S(2)}, u32[]{:S(2)}) collective-permute-start(bf16[2,224,768]{2,1,0:T(8,128)(2,1)S(1)} %pair_up.4.own_ref.own), channel_id=1, source_target_pairs={{0,0},{8,16},{16,8},{24,24},{1,1},{9,17},{17,9},{25,25},{2,2},{10,... | collective-permute-start | bytes 2064392 | tf_op jit(solution)/shard_map/ppermute | solution.py:62
  10.0 2.4 %collective-permute-done.rest_0_.x_ref = bf16[224,768]{1,0:T(8,128)(2,1)S(1)} collective-permute-done((bf16[224,768]{1,0:T(8,128)(2,1)}, bf16[224,768]{1,0:T(8,128)(2,1)S(1)}, u32[]{:S(2)}, u32[]{:S(2)}) %collective-permute-start) | collective-permute-done | bytes 344096 | tf_op jit(solution)/shard_map/ppermute | solution.py:46
  12.4 0.0 copy-done.4
  12.5 0.0 copy-start.6
  12.5 0.0 copy-start.7
  12.5 1.3 %collective-permute-start.1 = (bf16[224,768]{1,0:T(8,128)(2,1)S(1)}, bf16[224,768]{1,0:T(8,128)(2,1)S(1)}, u32[]{:S(2)}, u32[]{:S(2)}) collective-permute-start(bf16[224,768]{1,0:T(8,128)(2,1)S(1)} %later.1), channel_id=1, source_target_pairs={{0,1},{1,0},{2,3},{3,2},{4,5},{5,4},{6,7},{7,6},{8,9},{9,8},{10,11... | collective-permute-start | bytes 1032200 | tf_op jit(solution)/shard_map/ppermute | solution.py:46
  13.8 3.2 %collective-permute-start.5 = (bf16[224,768]{1,0:T(8,128)(2,1)S(1)}, bf16[224,768]{1,0:T(8,128)(2,1)S(1)}, u32[]{:S(2)}, u32[]{:S(2)}) collective-permute-start(bf16[224,768]{1,0:T(8,128)(2,1)S(1)} %collective-permute-done.rest_0_.x_ref), channel_id=1, source_target_pairs={{0,2},{2,4},{3,1},{4,6},{5,3},{7,5},{8,10},{10,12},{11,9},{12,14},... | collective-permute-start | bytes 1032200 | tf_op jit(solution)/shard_map/ppermute | solution.py:50
  17.0 4.4 %collective-permute-start.7 = (bf16[2,224,768]{2,1,0:T(8,128)(2,1)S(1)}, bf16[2,224,768]{2,1,0:T(8,128)(2,1)S(1)}, u32[]{:S(2)}, u32[]{:S(2)}) collective-permute-start(bf16[2,224,768]{2,1,0:T(8,128)(2,1)S(1)} %pad_maximum_fusion.own.rest_0_), channel_id=1, source_target_pairs={{0,0},{8,16},{16,8},{24,24},{1,1},{9,17},{17,9},{25,25},{2,2},{10,... | collective-permute-start | bytes 2064392 | tf_op jit(solution)/shard_map/ppermute | solution.py:62
  21.4 0.0 collective-permute-done.1.y_ref.rest_0_
  21.4 0.0 collective-permute-done.3.rest_0_.own_ref.pair
  21.4 0.0 collective-permute-done.4.rest_1_.other.own_ref
  21.5 1.6 %collective-permute-start.8 = (bf16[2,224,768]{2,1,0:T(8,128)(2,1)S(1)}, bf16[2,224,768]{2,1,0:T(8,128)(2,1)S(1)}, u32[]{:S(2)}, u32[]{:S(2)}) collective-permute-start(bf16[2,224,768]{2,1,0:T(8,128)(2,1)S(1)} %pair_up.5.own.near.rest_1_), channel_id=1, source_target_pairs={{0,8},{8,0},{16,24},{24,16},{1,9},{9,1},{17,25},{25,17},{2,10},{10... | collective-permute-start | bytes 2064392 | tf_op jit(solution)/shard_map/ppermute | solution.py:58
  23.1 3.0 %collective-permute-start.9 = (bf16[2,224,768]{2,1,0:T(8,128)(2,1)S(1)}, bf16[2,224,768]{2,1,0:T(8,128)(2,1)S(1)}, u32[]{:S(2)}, u32[]{:S(2)}) collective-permute-start(bf16[2,224,768]{2,1,0:T(8,128)(2,1)S(1)} %pair_up.5.own.near.rest_1_), channel_id=1, source_target_pairs={{0,0},{8,16},{16,8},{24,24},{1,1},{9,17},{17,9},{25,25},{2,2},{10,... | collective-permute-start | bytes 2064392 | tf_op jit(solution)/shard_map/ppermute | solution.py:62
  26.2 0.0 collective-permute-done.5.x_ref.rest_1_
  26.2 0.0 copy-done.1
  26.2 0.0 copy-done.3
  26.3 1.3 %collective-permute-start.12 = (bf16[2,224,768]{2,1,0:T(8,128)(2,1)S(1)}, bf16[2,224,768]{2,1,0:T(8,128)(2,1)S(1)}, u32[]{:S(2)}, u32[]{:S(2)}) collective-permute-start(bf16[2,224,768]{2,1,0:T(8,128)(2,1)S(1)} %pair_up.7), channel_id=1, source_target_pairs={{0,1},{1,0},{2,3},{3,2},{4,5},{5,4},{6,7},{7,6},{8,9},{9,8},{10,11... | collective-permute-start | bytes 2064392 | tf_op jit(solution)/shard_map/ppermute | solution.py:46
  27.6 3.2 %collective-permute-start.6 = (bf16[224,768]{1,0:T(8,128)(2,1)S(1)}, bf16[224,768]{1,0:T(8,128)(2,1)S(1)}, u32[]{:S(2)}, u32[]{:S(2)}) collective-permute-start(bf16[224,768]{1,0:T(8,128)(2,1)S(1)} %collective-permute-done.1.y_ref.rest_0_), channel_id=1, source_target_pairs={{0,2},{2,4},{3,1},{4,6},{5,3},{7,5},{8,10},{10,12},{11,9},{12,14},... | collective-permute-start | bytes 1032200 | tf_op jit(solution)/shard_map/ppermute | solution.py:50
  30.8 0.0 collective-permute-done.7.other.rest_6_
  30.8 0.0 copy-done.6
  30.8 0.0 copy-done.7
  30.8 3.1 %scores_0.1 = (bf16[6,224,672]{2,1,0:T(8,128)(2,1)S(1)}, f32[224,768]{1,0:T(8,128)S(1)}, f32[224,768]{1,0:T(8,128)S(1)}, f32[224,768]{1,0:T(8,128)S(1)}) custom-call(s32[4,8,9]{2,1,0:T(8,128)S(1)} %copy-done.6, s32[8]{0:T(128)S(1)} %copy-done.7, bf16[224,768]{1,0:T(8,128)(2,1)S(1)} %bitcast.12, bf16[2,224,768]{2,1,0:T(8,128)(2,1)S(1)} %pad_maximum_fusion.own.rest_0_, ...), custom_call_target="tpu_custom_call" | custom-call | flops 462422016 | bytes 2752512 | tf_op jit(solution)/shard_map/scores_0/pallas_call | solution.py:388
  33.9 0.0 collective-permute-done.8.pair.near_pair.rest_4_
  33.9 3.8 %collective-permute-done.9.other.near_other.rest_7_ = bf16[2,224,768]{2,1,0:T(8,128)(2,1)S(1)} collective-permute-done((bf16[2,224,768]{2,1,0:T(8,128)(2,1)S(1)}, bf16[2,224,768]{2,1,0:T(8,128)(2,1)S(1)}, u32[]{:S(2)}, u32[]{:S(2)}) %collective-permute-start.9) | collective-permute-done | bytes 688160 | tf_op jit(solution)/shard_map/ppermute | solution.py:62
  37.7 3.1 %scores_1.1 = (bf16[6,224,672]{2,1,0:T(8,128)(2,1)S(1)}, f32[224,768]{1,0:T(8,128)S(1)}, f32[224,768]{1,0:T(8,128)S(1)}, f32[224,768]{1,0:T(8,128)S(1)}) custom-call(s32[4,8,9]{2,1,0:T(8,128)S(1)} %copy-done.6, s32[8]{0:T(128)S(1)} %copy-done.7, bf16[224,768]{1,0:T(8,128)(2,1)S(1)} %bitcast.13, bf16[2,224,768]{2,1,0:T(8,128)(2,1)S(1)} %pair_up.5.own.near.rest_1_, ...), custom_call_target="tpu_custom_call" | custom-call | flops 462422016 | bytes 2752512 | tf_op jit(solution)/shard_map/scores_1/pallas_call | solution.py:388
  40.8 0.0 collective-permute-done.6.y_ref
  40.8 0.0 copy-start.5
  40.9 0.1 collective-permute-start.10
  41.0 3.3 %collective-permute-start.11 = (bf16[2,224,768]{2,1,0:T(8,128)(2,1)S(1)}, bf16[2,224,768]{2,1,0:T(8,128)(2,1)S(1)}, u32[]{:S(2)}, u32[]{:S(2)}) collective-permute-start(bf16[2,224,768]{2,1,0:T(8,128)(2,1)S(1)} %pair_up.6.own.rest_2_), channel_id=1, source_target_pairs={{0,0},{8,16},{16,8},{24,24},{1,1},{9,17},{17,9},{25,25},{2,2},{10,... | collective-permute-start | bytes 2064392 | tf_op jit(solution)/shard_map/ppermute | solution.py:62
  44.3 0.0 collective-permute-done.12.refs_0_
  44.3 2.2 %collective-permute-start.13 = (bf16[2,224,768]{2,1,0:T(8,128)(2,1)S(1)}, bf16[2,224,768]{2,1,0:T(8,128)(2,1)S(1)}, u32[]{:S(2)}, u32[]{:S(2)}) collective-permute-start(bf16[2,224,768]{2,1,0:T(8,128)(2,1)S(1)} %gate.1.near_ref.near), channel_id=1, source_target_pairs={{0,0},{8,16},{16,8},{24,24},{1,1},{9,17},{17,9},{25,25},{2,2},{10,... | collective-permute-start | bytes 2064392 | tf_op jit(solution)/shard_map/ppermute | solution.py:62
  46.6 3.2 %collective-permute-start.14 = (bf16[2,224,768]{2,1,0:T(8,128)(2,1)S(1)}, bf16[2,224,768]{2,1,0:T(8,128)(2,1)S(1)}, u32[]{:S(2)}, u32[]{:S(2)}) collective-permute-start(bf16[2,224,768]{2,1,0:T(8,128)(2,1)S(1)} %gate.1.near_ref.near), channel_id=1, source_target_pairs={{0,2},{2,4},{3,1},{4,6},{5,3},{7,5},{8,10},{10,12},{11,9},{12,14},... | collective-permute-start | bytes 2064392 | tf_op jit(solution)/shard_map/ppermute | solution.py:50
  49.8 0.1 collective-permute-start.17
  49.9 1.8 %convolution.2.rest_7_.rest_17_ = f32[224,768]{1,0:T(8,128)S(1)} custom-call(bf16[2,224,768]{2,1,0:T(8,128)(2,1)S(1)} %pad_maximum_fusion.own.rest_0_, bf16[2,224,768]{2,1,0:T(8,128)(2,1)S(1)} %pair_up.5.own.near.rest_1_, bf16[2,224,768]{2,1,0:T(8,128)(2,1)S(1)} %collective-permute-done.2.rest_0_.pair.rest_3_, ...), custom_call_target="tpu_custom_call" | custom-call | flops 231211008 | bytes 2752512 | tf_op jit(solution)/shard_map/convolution/pallas_call | solution.py:388
  51.6 0.0 collective-permute-done.10.pair.rest_5_
  51.6 1.9 %collective-permute-done.11.other.rest_8_ = bf16[2,224,768]{2,1,0:T(8,128)(2,1)S(1)} collective-permute-done((bf16[2,224,768]{2,1,0:T(8,128)(2,1)S(1)}, bf16[2,224,768]{2,1,0:T(8,128)(2,1)S(1)}, u32[]{:S(2)}, u32[]{:S(2)}) %collective-permute-start.11) | collective-permute-done | bytes 688160 | tf_op jit(solution)/shard_map/ppermute | solution.py:62
  53.5 3.9 %scores_2.1 = (bf16[6,224,672]{2,1,0:T(8,128)(2,1)S(1)}, f32[224,768]{1,0:T(8,128)S(1)}, f32[224,768]{1,0:T(8,128)S(1)}, f32[224,768]{1,0:T(8,128)S(1)}, f32[224...) custom-call(s32[4,8,9]{2,1,0:T(8,128)S(1)} %copy-done.6, s32[8]{0:T(128)S(1)} %copy-done.7, ...), custom_call_target="tpu_custom_call" | custom-call | flops 462422016 | bytes 2752512 | tf_op jit(solution)/shard_map/scores_2/pallas_call | solution.py:388
  57.4 0.0 collective-permute-start.15
  57.5 3.0 %collective-permute-start.16 = (f32[16,224]{1,0:T(8,128)S(1)}, f32[16,224]{1,0:T(8,128)S(1)}, u32[]{:S(2)}, u32[]{:S(2)}) collective-permute-start(f32[16,224]{1,0:T(8,128)S(1)} %get-tuple-element.44.own_ref.rest_0_), channel_id=1, source_target_pairs={{0,0},{1,2},{2,1},{3,4},{4,3},{5,6},{6,5},{7,7},{8,8},{9,10},{10,9... | collective-permute-start | bytes 43016 | tf_op jit(solution)/shard_map/ppermute | solution.py:54
  60.5 5.7 %query_side.1 = (bf16[224,768]{1,0:T(8,128)(2,1)}, bf16[224,768]{1,0:T(8,128)(2,1)}, f32[8,128]{1,0:T(8,128)S(1)}) custom-call(bf16[224,768]{1,0:T(8,128)(2,1)S(1)} %bitcast.18, bf16[27,768]{1,0:T(8,128)(2,1)S(1)} %copy-done.5, bf16[2,224,768]{2,1,0:T(8,128)(2,1)S(1)} %pad_maximum_fusion.own.rest_0_, bf16[2,224,768]{2,1,0:T(8,128)(2,1)S(1)} %pair_up.5.own.near.rest_1_, ...), custom_call_target="tpu_custom_call" | custom-call | flops 1387266048 | bytes 8257536 | tf_op jit(solution)/shard_map/query_side/pallas_call | solution.py:388
  66.1 0.0 collective-permute-done.13.rest_2_.near_other.near_ref
  66.1 0.0 collective-permute-done.14.qg_ref.far_ref.rest_4_
  66.2 0.0 collective-permute-done.17.rest_1_.near_ref.near_pair
  66.2 0.0 collective-permute-done.15.near_ref.rest_1_
  66.2 0.0 collective-permute-done.16.far_ref.rest_2_
  66.2 0.1 pack.1
  66.2 0.1 collective-permute-start.19
  66.3 3.9 %collective-permute-start.18 = (bf16[496,768]{1,0:T(8,128)(2,1)S(1)}, bf16[496,768]{1,0:T(8,128)(2,1)S(1)}, u32[]{:S(2)}, u32[]{:S(2)}) collective-permute-start(bf16[496,768]{1,0:T(8,128)(2,1)S(1)} %pack.1), channel_id=1, source_target_pairs={{0,0},{8,16},{16,8},{24,24},{1,1},{9,17},{17,9},{25,25},{2,2},{10,... | collective-permute-start | bytes 2285576 | tf_op jit(solution)/shard_map/ppermute | solution.py:62
  70.2 1.8 %convolution.3.rest_3_ = f32[224,768]{1,0:T(8,128)S(1)} custom-call(bf16[2,224,768]{2,1,0:T(8,128)(2,1)S(1)} %pair_up.4.own_ref.own, bf16[2,224,768]{2,1,0:T(8,128)(2,1)S(1)} %gate.1.near_ref.near, bf16[2,224,768]{2,1,0:T(8,128)(2,1)S(1)} %collective-permute-done.3.rest_0_.own_ref.pair, ...), custom_call_target="tpu_custom_call" | custom-call | flops 231211008 | bytes 2752512 | tf_op jit(solution)/shard_map/convolution/pallas_call | solution.py:388
  72.0 3.6 %key_side_0.1 = (f32[224,768]{1,0:T(8,128)S(1)}, f32[224,768]{1,0:T(8,128)S(1)}) custom-call(s32[4,8,9]{2,1,0:T(8,128)S(1)} %copy-done.6, s32[8]{0:T(128)S(1)} %copy-done.7, bf16[2,224,768]{2,1,0:T(8,128)(2,1)S(1)} %pad_maximum_fusion.own.rest_0_, bf16[2,224,768]{2,1,0:T(8,128)(2,1)S(1)} %pair_up.4.own_ref.own, bf16[2,224,768]{2,1,0:T(8,128)(2,1)S(1)} %gate.1.near_ref.near, ...), custom_call_target="tpu_custom_call" | custom-call | flops 924844032 | bytes 2752512 | tf_op jit(solution)/shard_map/key_side_0/pallas_call | solution.py:388
  75.6 0.0 collective-permute-done.19.far_ref.rest_5_
  75.6 3.8 %key_side_1.1 = (f32[224,768]{1,0:T(8,128)S(1)}, f32[224,768]{1,0:T(8,128)S(1)}) custom-call(s32[4,8,9]{2,1,0:T(8,128)S(1)} %copy-done.6, s32[8]{0:T(128)S(1)} %copy-done.7, bf16[2,224,768]{2,1,0:T(8,128)(2,1)S(1)} %pad_maximum_fusion.own.rest_0_, bf16[2,224,768]{2,1,0:T(8,128)(2,1)S(1)} %collective-permute-done.3.rest_0_.own_ref.pair, ...), custom_call_target="tpu_custom_call" | custom-call | flops 924844032 | bytes 2752512 | tf_op jit(solution)/shard_map/key_side_1/pallas_call | solution.py:388
  79.5 0.2 collective-permute-done.18.far_ref
  79.6 4.7 %key_side_2.1 = (bf16[224,768]{1,0:T(8,128)(2,1)}, bf16[224,768]{1,0:T(8,128)(2,1)}) custom-call(s32[4,8,9]{2,1,0:T(8,128)S(1)} %copy-done.6, s32[8]{0:T(128)S(1)} %copy-done.7, bf16[2,224,768]{2,1,0:T(8,128)(2,1)S(1)} %pad_maximum_fusion.own.rest_0_, bf16[2,224,768]{2,1,0:T(8,128)(2,1)S(1)} %collective-permute-done.4.rest_1_.other.own_ref, ...), custom_call_target="tpu_custom_call" | custom-call | flops 924844032 | bytes 2752512 | tf_op jit(solution)/shard_map/key_side_2/pallas_call | solution.py:388
  (9 shorter events, 0.2 us)
Async XLA Ops:
  0.6 11.8 %copy-start.4 = (bf16[2,2,56,768]{3,2,1,0:T(8,128)(2,1)S(1)}, bf16[2,2,56,768]{3,2,1,0:T(8,128)(2,1)}, u32[]{:S(2)}) copy-start(bf16[2,2,56,768]{3,2,1,0:T(8,128)(2,1)} %param.9) | copy-start | bytes 1032196
  1.8 2.5 %collective-permute-start.2 = (bf16[2,224,768]{2,1,0:T(8,128)(2,1)S(1)}, bf16[2,224,768]{2,1,0:T(8,128)(2,1)S(1)}, u32[]{:S(2)}, u32[]{:S(2)}) collective-permute-start(bf16[2,224,768]{2,1,0:T(8,128)(2,1)S(1)} %pad_maximum_fusion.own.rest_0_), channel_id=1, source_target_pairs={{0,8},{8,0},{16,24},{24,16},{1,9},{9,1},{17,25},{25,17},{2,10},{10... | collective-permute-start | bytes 2064392 | tf_op jit(solution)/shard_map/ppermute | solution.py:58
  2.6 9.9 %collective-permute-start = (bf16[224,768]{1,0:T(8,128)(2,1)}, bf16[224,768]{1,0:T(8,128)(2,1)S(1)}, u32[]{:S(2)}, u32[]{:S(2)}) collective-permute-start(bf16[224,768]{1,0:T(8,128)(2,1)} %bitcast.22), channel_id=1, source_target_pairs={{0,1},{1,0},{2,3},{3,2},{4,5},{5,4},{6,7},{7,6},{8,9},{9,8},{10,11... | collective-permute-start | bytes 1032200 | tf_op jit(solution)/shard_map/ppermute | solution.py:46
  4.3 1.0 %copy-start = (bf16[2,2,56,768]{3,2,1,0:T(8,128)(2,1)S(1)}, bf16[2,2,56,768]{3,2,1,0:T(8,128)(2,1)}, u32[]{:S(2)}) copy-start(bf16[2,2,56,768]{3,2,1,0:T(8,128)(2,1)} %param.7) | copy-start | bytes 1032196
  5.3 1.0 %copy-start.2 = (bf16[2,2,56,768]{3,2,1,0:T(8,128)(2,1)S(1)}, bf16[2,2,56,768]{3,2,1,0:T(8,128)(2,1)}, u32[]{:S(2)}) copy-start(bf16[2,2,56,768]{3,2,1,0:T(8,128)(2,1)} %param.11) | copy-start | bytes 1032196
  6.4 19.9 %copy-start.1 = (bf16[2,2,56,768]{3,2,1,0:T(8,128)(2,1)S(1)}, bf16[2,2,56,768]{3,2,1,0:T(8,128)(2,1)}, u32[]{:S(2)}) copy-start(bf16[2,2,56,768]{3,2,1,0:T(8,128)(2,1)} %param.7) | copy-start | bytes 1032196
  6.4 19.9 %copy-start.3 = (bf16[2,2,56,768]{3,2,1,0:T(8,128)(2,1)S(1)}, bf16[2,2,56,768]{3,2,1,0:T(8,128)(2,1)}, u32[]{:S(2)}) copy-start(bf16[2,2,56,768]{3,2,1,0:T(8,128)(2,1)} %param.11) | copy-start | bytes 1032196
  6.4 15.0 %collective-permute-start.3 = (bf16[2,224,768]{2,1,0:T(8,128)(2,1)S(1)}, bf16[2,224,768]{2,1,0:T(8,128)(2,1)S(1)}, u32[]{:S(2)}, u32[]{:S(2)}) collective-permute-start(bf16[2,224,768]{2,1,0:T(8,128)(2,1)S(1)} %pair_up.4.own_ref.own), channel_id=1, source_target_pairs={{0,8},{8,0},{16,24},{24,16},{1,9},{9,1},{17,25},{25,17},{2,10},{10... | collective-permute-start | bytes 2064392 | tf_op jit(solution)/shard_map/ppermute | solution.py:58
  6.8 14.6 %collective-permute-start.4 = (bf16[2,224,768]{2,1,0:T(8,128)(2,1)S(1)}, bf16[2,224,768]{2,1,0:T(8,128)(2,1)S(1)}, u32[]{:S(2)}, u32[]{:S(2)}) collective-permute-start(bf16[2,224,768]{2,1,0:T(8,128)(2,1)S(1)} %pair_up.4.own_ref.own), channel_id=1, source_target_pairs={{0,0},{8,16},{16,8},{24,24},{1,1},{9,17},{17,9},{25,25},{2,2},{10,... | collective-permute-start | bytes 2064392 | tf_op jit(solution)/shard_map/ppermute | solution.py:62
  12.5 18.3 %copy-start.6 = (s32[4,8,9]{2,1,0:T(8,128)S(1)}, s32[4,8,9]{2,1,0:T(8,128)}, u32[]{:S(2)}) copy-start(s32[4,8,9]{2,1,0:T(8,128)} %mask_ref.11) | copy-start | bytes 3460
  12.5 18.3 %copy-start.7 = (s32[8]{0:T(128)S(1)}, s32[8]{0:T(128)}, u32[]{:S(2)}) copy-start(s32[8]{0:T(128)} %clip_ref.11) | copy-start | bytes 100
  12.5 8.9 %collective-permute-start.1 = (bf16[224,768]{1,0:T(8,128)(2,1)S(1)}, bf16[224,768]{1,0:T(8,128)(2,1)S(1)}, u32[]{:S(2)}, u32[]{:S(2)}) collective-permute-start(bf16[224,768]{1,0:T(8,128)(2,1)S(1)} %later.1), channel_id=1, source_target_pairs={{0,1},{1,0},{2,3},{3,2},{4,5},{5,4},{6,7},{7,6},{8,9},{9,8},{10,11... | collective-permute-start | bytes 1032200 | tf_op jit(solution)/shard_map/ppermute | solution.py:46
  13.8 12.4 %collective-permute-start.5 = (bf16[224,768]{1,0:T(8,128)(2,1)S(1)}, bf16[224,768]{1,0:T(8,128)(2,1)S(1)}, u32[]{:S(2)}, u32[]{:S(2)}) collective-permute-start(bf16[224,768]{1,0:T(8,128)(2,1)S(1)} %collective-permute-done.rest_0_.x_ref), channel_id=1, source_target_pairs={{0,2},{2,4},{3,1},{4,6},{5,3},{7,5},{8,10},{10,12},{11,9},{12,14},... | collective-permute-start | bytes 1032200 | tf_op jit(solution)/shard_map/ppermute | solution.py:50
  17.0 13.8 %collective-permute-start.7 = (bf16[2,224,768]{2,1,0:T(8,128)(2,1)S(1)}, bf16[2,224,768]{2,1,0:T(8,128)(2,1)S(1)}, u32[]{:S(2)}, u32[]{:S(2)}) collective-permute-start(bf16[2,224,768]{2,1,0:T(8,128)(2,1)S(1)} %pad_maximum_fusion.own.rest_0_), channel_id=1, source_target_pairs={{0,0},{8,16},{16,8},{24,24},{1,1},{9,17},{17,9},{25,25},{2,2},{10,... | collective-permute-start | bytes 2064392 | tf_op jit(solution)/shard_map/ppermute | solution.py:62
  21.5 12.4 %collective-permute-start.8 = (bf16[2,224,768]{2,1,0:T(8,128)(2,1)S(1)}, bf16[2,224,768]{2,1,0:T(8,128)(2,1)S(1)}, u32[]{:S(2)}, u32[]{:S(2)}) collective-permute-start(bf16[2,224,768]{2,1,0:T(8,128)(2,1)S(1)} %pair_up.5.own.near.rest_1_), channel_id=1, source_target_pairs={{0,8},{8,0},{16,24},{24,16},{1,9},{9,1},{17,25},{25,17},{2,10},{10... | collective-permute-start | bytes 2064392 | tf_op jit(solution)/shard_map/ppermute | solution.py:58
  23.1 14.5 %collective-permute-start.9 = (bf16[2,224,768]{2,1,0:T(8,128)(2,1)S(1)}, bf16[2,224,768]{2,1,0:T(8,128)(2,1)S(1)}, u32[]{:S(2)}, u32[]{:S(2)}) collective-permute-start(bf16[2,224,768]{2,1,0:T(8,128)(2,1)S(1)} %pair_up.5.own.near.rest_1_), channel_id=1, source_target_pairs={{0,0},{8,16},{16,8},{24,24},{1,1},{9,17},{17,9},{25,25},{2,2},{10,... | collective-permute-start | bytes 2064392 | tf_op jit(solution)/shard_map/ppermute | solution.py:62
  26.3 18.0 %collective-permute-start.12 = (bf16[2,224,768]{2,1,0:T(8,128)(2,1)S(1)}, bf16[2,224,768]{2,1,0:T(8,128)(2,1)S(1)}, u32[]{:S(2)}, u32[]{:S(2)}) collective-permute-start(bf16[2,224,768]{2,1,0:T(8,128)(2,1)S(1)} %pair_up.7), channel_id=1, source_target_pairs={{0,1},{1,0},{2,3},{3,2},{4,5},{5,4},{6,7},{7,6},{8,9},{9,8},{10,11... | collective-permute-start | bytes 2064392 | tf_op jit(solution)/shard_map/ppermute | solution.py:46
  27.6 13.2 %collective-permute-start.6 = (bf16[224,768]{1,0:T(8,128)(2,1)S(1)}, bf16[224,768]{1,0:T(8,128)(2,1)S(1)}, u32[]{:S(2)}, u32[]{:S(2)}) collective-permute-start(bf16[224,768]{1,0:T(8,128)(2,1)S(1)} %collective-permute-done.1.y_ref.rest_0_), channel_id=1, source_target_pairs={{0,2},{2,4},{3,1},{4,6},{5,3},{7,5},{8,10},{10,12},{11,9},{12,14},... | collective-permute-start | bytes 1032200 | tf_op jit(solution)/shard_map/ppermute | solution.py:50
  40.8 9.0 %copy-start.5 = (bf16[27,768]{1,0:T(8,128)(2,1)S(1)}, bf16[27,768]{1,0:T(8,128)(2,1)}, u32[]{:S(2)}) copy-start(bf16[27,768]{1,0:T(8,128)(2,1)} %rest_2_.1) | copy-start | bytes 124420
  40.9 10.7 %collective-permute-start.10 = (bf16[2,224,768]{2,1,0:T(8,128)(2,1)S(1)}, bf16[2,224,768]{2,1,0:T(8,128)(2,1)S(1)}, u32[]{:S(2)}, u32[]{:S(2)}) collective-permute-start(bf16[2,224,768]{2,1,0:T(8,128)(2,1)S(1)} %pair_up.6.own.rest_2_), channel_id=1, source_target_pairs={{0,8},{8,0},{16,24},{24,16},{1,9},{9,1},{17,25},{25,17},{2,10},{10... | collective-permute-start | bytes 2064392 | tf_op jit(solution)/shard_map/ppermute | solution.py:58
  41.0 12.6 %collective-permute-start.11 = (bf16[2,224,768]{2,1,0:T(8,128)(2,1)S(1)}, bf16[2,224,768]{2,1,0:T(8,128)(2,1)S(1)}, u32[]{:S(2)}, u32[]{:S(2)}) collective-permute-start(bf16[2,224,768]{2,1,0:T(8,128)(2,1)S(1)} %pair_up.6.own.rest_2_), channel_id=1, source_target_pairs={{0,0},{8,16},{16,8},{24,24},{1,1},{9,17},{17,9},{25,25},{2,2},{10,... | collective-permute-start | bytes 2064392 | tf_op jit(solution)/shard_map/ppermute | solution.py:62
  44.3 21.8 %collective-permute-start.13 = (bf16[2,224,768]{2,1,0:T(8,128)(2,1)S(1)}, bf16[2,224,768]{2,1,0:T(8,128)(2,1)S(1)}, u32[]{:S(2)}, u32[]{:S(2)}) collective-permute-start(bf16[2,224,768]{2,1,0:T(8,128)(2,1)S(1)} %gate.1.near_ref.near), channel_id=1, source_target_pairs={{0,0},{8,16},{16,8},{24,24},{1,1},{9,17},{17,9},{25,25},{2,2},{10,... | collective-permute-start | bytes 2064392 | tf_op jit(solution)/shard_map/ppermute | solution.py:62
  46.6 19.6 %collective-permute-start.14 = (bf16[2,224,768]{2,1,0:T(8,128)(2,1)S(1)}, bf16[2,224,768]{2,1,0:T(8,128)(2,1)S(1)}, u32[]{:S(2)}, u32[]{:S(2)}) collective-permute-start(bf16[2,224,768]{2,1,0:T(8,128)(2,1)S(1)} %gate.1.near_ref.near), channel_id=1, source_target_pairs={{0,2},{2,4},{3,1},{4,6},{5,3},{7,5},{8,10},{10,12},{11,9},{12,14},... | collective-permute-start | bytes 2064392 | tf_op jit(solution)/shard_map/ppermute | solution.py:50
  49.8 16.4 %collective-permute-start.17 = (bf16[2,224,768]{2,1,0:T(8,128)(2,1)S(1)}, bf16[2,224,768]{2,1,0:T(8,128)(2,1)S(1)}, u32[]{:S(2)}, u32[]{:S(2)}) collective-permute-start(bf16[2,224,768]{2,1,0:T(8,128)(2,1)S(1)} %gate.1.near_ref.near), channel_id=1, source_target_pairs={{0,8},{8,0},{16,24},{24,16},{1,9},{9,1},{17,25},{25,17},{2,10},{10... | collective-permute-start | bytes 2064392 | tf_op jit(solution)/shard_map/ppermute | solution.py:58
  57.4 8.7 %collective-permute-start.15 = (f32[16,224]{1,0:T(8,128)S(1)}, f32[16,224]{1,0:T(8,128)S(1)}, u32[]{:S(2)}, u32[]{:S(2)}) collective-permute-start(f32[16,224]{1,0:T(8,128)S(1)} %get-tuple-element.44.own_ref.rest_0_), channel_id=1, source_target_pairs={{0,1},{1,0},{2,3},{3,2},{4,5},{5,4},{6,7},{7,6},{8,9},{9,8},{10,11... | collective-permute-start | bytes 43016 | tf_op jit(solution)/shard_map/ppermute | solution.py:46
  57.5 8.7 %collective-permute-start.16 = (f32[16,224]{1,0:T(8,128)S(1)}, f32[16,224]{1,0:T(8,128)S(1)}, u32[]{:S(2)}, u32[]{:S(2)}) collective-permute-start(f32[16,224]{1,0:T(8,128)S(1)} %get-tuple-element.44.own_ref.rest_0_), channel_id=1, source_target_pairs={{0,0},{1,2},{2,1},{3,4},{4,3},{5,6},{6,5},{7,7},{8,8},{9,10},{10,9... | collective-permute-start | bytes 43016 | tf_op jit(solution)/shard_map/ppermute | solution.py:54
  66.2 9.4 %collective-permute-start.19 = (bf16[496,768]{1,0:T(8,128)(2,1)S(1)}, bf16[496,768]{1,0:T(8,128)(2,1)S(1)}, u32[]{:S(2)}, u32[]{:S(2)}) collective-permute-start(bf16[496,768]{1,0:T(8,128)(2,1)S(1)} %pack.1), channel_id=1, source_target_pairs={{0,8},{8,0},{16,24},{24,16},{1,9},{9,1},{17,25},{25,17},{2,10},{10... | collective-permute-start | bytes 2285576 | tf_op jit(solution)/shard_map/ppermute | solution.py:58
  66.3 13.3 %collective-permute-start.18 = (bf16[496,768]{1,0:T(8,128)(2,1)S(1)}, bf16[496,768]{1,0:T(8,128)(2,1)S(1)}, u32[]{:S(2)}, u32[]{:S(2)}) collective-permute-start(bf16[496,768]{1,0:T(8,128)(2,1)S(1)} %pack.1), channel_id=1, source_target_pairs={{0,0},{8,16},{16,8},{24,24},{1,1},{9,17},{17,9},{25,25},{2,2},{10,... | collective-permute-start | bytes 2285576 | tf_op jit(solution)/shard_map/ppermute | solution.py:62

commit v9 on v8

--- a/solution.py
+++ b/solution.py
@@ -12,7 +12,8 @@
 ROW_DELTA = 8
 STAT_ROWS = 16
 STAT_LANES = 256
-UNROLL = 2
+UNROLL = 3
+SCORE_UNROLL = 6
 FLOOR = -1e30
 SMALL = 2 * 1024 * 1024
 LARGE = 8 * 1024 * 1024
@@ -193,7 +194,7 @@
     which = lax.broadcasted_iota(jnp.int32, (rows, HEAD_DIM), 1)
 
     def body(step, _):
-        hs = [step * UNROLL + u for u in range(UNROLL)]
+        hs = [step * SCORE_UNROLL + u for u in range(SCORE_UNROLL)]
         tops_, accs, sums_ = [], [], []
         scored = []
         for h in hs:
@@ -234,7 +235,7 @@
 
     if last:
         stat[...] = jnp.zeros_like(stat)
-    lax.fori_loop(0, heads // UNROLL, body, 0)
+    lax.fori_loop(0, heads // SCORE_UNROLL, body, 0)
     if last:
         pad = jnp.zeros((-rows % HEAD_DIM, HEAD_DIM), jnp.float32)
         turned = jnp.concatenate([stat[...], pad], axis=0).T
@@ -443,24 +444,21 @@
             name="gate",
         )(x, *earlier)
 
-    near_k = ha_near(key)
     kv = jnp.stack([key, value])
+    near_kv = ha_near(kv)
     kv_a, kv_b = ta_pair(kv), ta_other(kv)
     qg = pair_up(query, grad, kv_a)
     qg_a, qg_b = ta_pair(qg), ta_other(qg)
-    near_v = ha_near(later(value, near_k))
-    far_k = ha_relay(near_k)
     exp_own, *own_parts = scores(0, (kv, kv_a, kv_b))
 
-    far_v = ha_relay(near_v)
-    near_kv = pair_up(near_k, near_v, qg_a, qg_b)
-    near_kv_a, near_kv_b = ta_pair(near_kv), ta_other(near_kv)
-    near_qg = ha_near(pair_up(query, grad, near_v, far_k))
+    far_kv = ha_relay(near_kv)
+    near_kv_again = later(near_kv, qg_a, qg_b, kv_b)
+    near_kv_a, near_kv_b = ta_pair(near_kv_again), ta_other(near_kv_again)
+    near_qg = ha_near(pair_up(query, grad, near_kv))
     exp_near, *near_parts = scores(1, (near_kv, near_kv_a, near_kv_b))
-    far_kv = pair_up(far_k, far_v, own_parts[0], near_parts[0])
+    conv_value = convolution(False, kv, near_kv, kv_a, near_kv_a, kv_b, near_kv_b)
+    far_kv = later(far_kv, near_parts[0], own_parts[0], conv_value)
     far_kv_a, far_kv_b = ta_pair(far_kv), ta_other(far_kv)
-
-    conv_value = convolution(False, kv, near_kv, kv_a, near_kv_a, kv_b, near_kv_b)
 
     near_qg = gate(near_qg, near_parts[0])
     far_qg = ha_relay(near_qg)

time: 84.8 us -> 87.6 us (1.033); the launches traced: 84.3 us -> 86 us
  waiting for transfers between devices: 8.84 us -> 23.2 us
  starting transfers between devices: 39.5 us -> 29 us
  Pallas kernels: 31.8 us -> 29.6 us
    ppermute x4 -> x3, waiting for transfers between devices: 2.45 us -> 7.96 us  [ha_near(): return lax.ppermute(x, 'ha', flip_pairs(lax.axis_size('ha')))]
    ppermute x6, waiting for transfers between devices: 5.82 us -> 11.2 us  [ta_other(): return lax.ppermute(x, 'ta', other_pairs(lax.axis_size('ta')))]
    ppermute x3 -> x2, waiting for transfers between devices: 0.01 us -> 4.06 us  [ha_relay(): return lax.ppermute(near, 'ha', relay_pairs(lax.axis_size('ha')))]
    ppermute x3 -> x2, starting transfers between devices: 9.59 us -> 6.41 us  [ha_relay(): return lax.ppermute(near, 'ha', relay_pairs(lax.axis_size('ha')))]
    ppermute x4 -> x3, starting transfers between devices: 3.81 us -> 1.33 us  [ha_near(): return lax.ppermute(x, 'ha', flip_pairs(lax.axis_size('ha')))]
    pallas_call x9, Pallas kernels: 31.5 us -> 29.4 us  [call(): pl.pallas_call(kernel, in_specs=[smem] * scalars + [vmem] * (len(args) -...]
    ppermute x6, starting transfers between devices: 20.1 us -> 18.2 us  [ta_other(): return lax.ppermute(x, 'ta', other_pairs(lax.axis_size('ta')))]
    ppermute x6, starting transfers between devices: 3.04 us -> 1.1 us  [ta_pair(): return lax.ppermute(x, 'ta', flip_pairs(lax.axis_size('ta')))]
  transfers between devices with their start and end apart: 20 -> 18, of which waited for: 5 -> 6; matrix products, arithmetic and copies ran while one was open for 0% -> 0% of each run, Pallas kernels for 32% -> 29%
where the time goes in v9:
time: 87.6 us; the launch traced here: 86 us
  Pallas kernels  29.6 us (34%)
  starting transfers between devices  29 us (33%)
  waiting for transfers between devices  23.2 us (26%)
  local copies, waits for them, and re-layouts  1.98 us (2%)
  other arithmetic  1.15 us (1%)
  between operations  0.96 us (1%)
    pallas_call x9, Pallas kernels, call(): pl.pallas_call(kernel, in_specs=[smem] * scalars + [vmem] * (len(args) -...  29.4 us
    ppermute x6, starting transfers between devices, ta_other(): return lax.ppermute(x, 'ta', other_pairs(lax.axis_size('ta')))  18.2 us
    ppermute x6, waiting for transfers between devices, ta_other(): return lax.ppermute(x, 'ta', other_pairs(lax.axis_size('ta')))  11.2 us
    ppermute x3, waiting for transfers between devices, ha_near(): return lax.ppermute(x, 'ha', flip_pairs(lax.axis_size('ha')))  7.96 us
    ppermute x2, starting transfers between devices, ha_relay(): return lax.ppermute(near, 'ha', relay_pairs(lax.axis_size('ha')))  6.41 us
    ppermute x2, waiting for transfers between devices, ha_relay(): return lax.ppermute(near, 'ha', relay_pairs(lax.axis_size('ha')))  4.06 us
    ppermute x1, starting transfers between devices, ha_far(): return lax.ppermute(x, 'ha', other_pairs(lax.axis_size('ha')))  2.03 us
    unnamed x14, local copies, waits for them, and re-layouts  1.98 us
  transfers between devices with their start and end apart: 18, of which 6 were waited for; matrix products, arithmetic and copies ran while one was open for 0% of the time, Pallas kernels for 29%

profile of v9, /device:TPU:9, one launch (start us, length us, event | category | flops | bytes accessed | tf_op | source)
XLA Modules:
  0.0 86.0 jit_solution(1297733647450734370)
XLA Ops:
  0.6 1.1 %pad_maximum_fusion.own.rest_0_ = bf16[2,224,768]{2,1,0:T(8,128)(2,1)S(1)} fusion(bf16[1,224,768]{2,1,0:T(8,128)(2,1)} %bitcast.17, bf16[1,224,768]{2,1,0:T(8,128)(2,1)} %bitcast.18), kind=kLoop, calls=%fused_computation | loop fusion | flops 344064 | bytes 1376256 | tf_op jit(solution)/shard_map/stack | solution.py:447
  1.8 0.7 collective-permute-start.2
  2.5 1.2 %collective-permute-start = (bf16[2,224,768]{2,1,0:T(8,128)(2,1)S(1)}, bf16[2,224,768]{2,1,0:T(8,128)(2,1)S(1)}, u32[]{:S(2)}, u32[]{:S(2)}) collective-permute-start(bf16[2,224,768]{2,1,0:T(8,128)(2,1)S(1)} %pad_maximum_fusion.own.rest_0_), channel_id=1, source_target_pairs={{0,1},{1,0},{2,3},{3,2},{4,5},{5,4},{6,7},{7,6},{8,9},{9,8},{10,11... | collective-permute-start | bytes 2064392 | tf_op jit(solution)/shard_map/ppermute | solution.py:47
  3.7 3.4 %collective-permute-start.5 = (bf16[2,224,768]{2,1,0:T(8,128)(2,1)S(1)}, bf16[2,224,768]{2,1,0:T(8,128)(2,1)S(1)}, u32[]{:S(2)}, u32[]{:S(2)}) collective-permute-start(bf16[2,224,768]{2,1,0:T(8,128)(2,1)S(1)} %pad_maximum_fusion.own.rest_0_), channel_id=1, source_target_pairs={{0,0},{8,16},{16,8},{24,24},{1,1},{9,17},{17,9},{25,25},{2,2},{10,... | collective-permute-start | bytes 2064392 | tf_op jit(solution)/shard_map/ppermute | solution.py:63
  7.1 0.0 collective-permute-done.2.rest_0_.pair.rest_3_
  7.1 0.0 copy-start
  7.1 1.0 %copy-done = bf16[2,2,56,768]{3,2,1,0:T(8,128)(2,1)S(1)} copy-done((bf16[2,2,56,768]{3,2,1,0:T(8,128)(2,1)S(1)}, bf16[2,2,56,768]{3,2,1,0:T(8,128)(2,1)}, u32[]{:S(2)}) %copy-start) | copy-done | bytes 344088
  8.1 0.0 copy-start.2
  8.1 1.0 %copy-done.2 = bf16[2,2,56,768]{3,2,1,0:T(8,128)(2,1)S(1)} copy-done((bf16[2,2,56,768]{3,2,1,0:T(8,128)(2,1)S(1)}, bf16[2,2,56,768]{3,2,1,0:T(8,128)(2,1)}, u32[]{:S(2)}) %copy-start.2) | copy-done | bytes 344088
  9.1 0.0 copy-start.1
  9.2 0.0 copy-start.5
  9.2 0.0 copy-start.6
  9.2 0.1 collective-permute-start.3
  9.3 2.3 %collective-permute-start.4 = (bf16[2,224,768]{2,1,0:T(8,128)(2,1)S(1)}, bf16[2,224,768]{2,1,0:T(8,128)(2,1)S(1)}, u32[]{:S(2)}, u32[]{:S(2)}) collective-permute-start(bf16[2,224,768]{2,1,0:T(8,128)(2,1)S(1)} %pair_up.2.own_ref.own), channel_id=1, source_target_pairs={{0,0},{8,16},{16,8},{24,24},{1,1},{9,17},{17,9},{25,25},{2,2},{10,... | collective-permute-start | bytes 2064392 | tf_op jit(solution)/shard_map/ppermute | solution.py:63
  11.6 8.0 %collective-permute-done.x_ref.own.near.rest_1_.rest_0_ = bf16[2,224,768]{2,1,0:T(8,128)(2,1)S(1)} collective-permute-done((bf16[2,224,768]{2,1,0:T(8,128)(2,1)S(1)}, bf16[2,224,768]{2,1,0:T(8,128)(2,1)S(1)}, u32[]{:S(2)}, u32[]{:S(2)}) %collective-permute-start) | collective-permute-done | bytes 688160 | tf_op jit(solution)/shard_map/ppermute | solution.py:47
  19.5 0.0 collective-permute-done.5.rest_2_.other.rest_6_
  19.5 0.0 collective-permute-done.3.rest_0_.own_ref.pair
  19.5 3.8 %collective-permute-done.4.rest_1_.other.own_ref = bf16[2,224,768]{2,1,0:T(8,128)(2,1)S(1)} collective-permute-done((bf16[2,224,768]{2,1,0:T(8,128)(2,1)S(1)}, bf16[2,224,768]{2,1,0:T(8,128)(2,1)S(1)}, u32[]{:S(2)}, u32[]{:S(2)}) %collective-permute-start.4) | collective-permute-done | bytes 688160 | tf_op jit(solution)/shard_map/ppermute | solution.py:63
  23.4 0.0 copy-start.4
  23.4 0.1 collective-permute-start.6
  23.5 3.4 %collective-permute-start.7 = (bf16[2,224,768]{2,1,0:T(8,128)(2,1)S(1)}, bf16[2,224,768]{2,1,0:T(8,128)(2,1)S(1)}, u32[]{:S(2)}, u32[]{:S(2)}) collective-permute-start(bf16[2,224,768]{2,1,0:T(8,128)(2,1)S(1)} %later.2), channel_id=1, source_target_pairs={{0,0},{8,16},{16,8},{24,24},{1,1},{9,17},{17,9},{25,25},{2,2},{10,... | collective-permute-start | bytes 2064392 | tf_op jit(solution)/shard_map/ppermute | solution.py:63
  26.9 3.2 %collective-permute-start.1 = (bf16[2,224,768]{2,1,0:T(8,128)(2,1)S(1)}, bf16[2,224,768]{2,1,0:T(8,128)(2,1)S(1)}, u32[]{:S(2)}, u32[]{:S(2)}) collective-permute-start(bf16[2,224,768]{2,1,0:T(8,128)(2,1)S(1)} %collective-permute-done.x_ref.own.near.rest_1_.rest_0_), channel_id=1, source_target_pairs={{0,2},{2,4},{3,1},{4,6},{5,3},{7,5},{8,10},{10,12},{11,9},{12,14},... | collective-permute-start | bytes 2064392 | tf_op jit(solution)/shard_map/ppermute | solution.py:51
  30.2 0.1 collective-permute-start.10
  30.2 0.0 copy-done.1
  30.2 0.0 copy-done.5
  30.3 0.0 copy-done.6
  30.3 2.6 %scores_0.1 = (bf16[6,224,672]{2,1,0:T(8,128)(2,1)S(1)}, f32[224,768]{1,0:T(8,128)S(1)}, f32[224,768]{1,0:T(8,128)S(1)}, f32[224,768]{1,0:T(8,128)S(1)}) custom-call(s32[4,8,9]{2,1,0:T(8,128)S(1)} %copy-done.5, s32[8]{0:T(128)S(1)} %copy-done.6, bf16[224,768]{1,0:T(8,128)(2,1)S(1)} %bitcast.10, bf16[2,224,768]{2,1,0:T(8,128)(2,1)S(1)} %pad_maximum_fusion.own.rest_0_, ...), custom_call_target="tpu_custom_call" | custom-call | flops 462422016 | bytes 2752512 | tf_op jit(solution)/shard_map/scores_0/pallas_call | solution.py:389
  32.9 0.0 collective-permute-done.6.pair.near_pair.rest_4_
  32.9 3.2 %collective-permute-done.7.other.near_other.rest_7_ = bf16[2,224,768]{2,1,0:T(8,128)(2,1)S(1)} collective-permute-done((bf16[2,224,768]{2,1,0:T(8,128)(2,1)S(1)}, bf16[2,224,768]{2,1,0:T(8,128)(2,1)S(1)}, u32[]{:S(2)}, u32[]{:S(2)}) %collective-permute-start.7) | collective-permute-done | bytes 688160 | tf_op jit(solution)/shard_map/ppermute | solution.py:63
  36.1 0.0 copy-done.4
  36.1 1.8 %convolution.2.rest_2_.rest_7_.rest_17_ = f32[224,768]{1,0:T(8,128)S(1)} custom-call(bf16[2,224,768]{2,1,0:T(8,128)(2,1)S(1)} %pad_maximum_fusion.own.rest_0_, bf16[2,224,768]{2,1,0:T(8,128)(2,1)S(1)} %collective-permute-done.x_ref.own.near.rest_1_.rest_0_, bf16[2,224,768]{2,1,0:T(8,128)(2,1)S(1)} %collective-permute-done.2.rest_0_.pair.rest_3_, ...), custom_call_target="tpu_custom_call" | custom-call | flops 231211008 | bytes 2752512 | tf_op jit(solution)/shard_map/convolution/pallas_call | solution.py:389
  37.8 2.6 %scores_1.1 = (bf16[6,224,672]{2,1,0:T(8,128)(2,1)S(1)}, f32[224,768]{1,0:T(8,128)S(1)}, f32[224,768]{1,0:T(8,128)S(1)}, f32[224,768]{1,0:T(8,128)S(1)}) custom-call(s32[4,8,9]{2,1,0:T(8,128)S(1)} %copy-done.5, s32[8]{0:T(128)S(1)} %copy-done.6, bf16[224,768]{1,0:T(8,128)(2,1)S(1)} %bitcast.11, ...), custom_call_target="tpu_custom_call" | custom-call | flops 462422016 | bytes 2752512 | tf_op jit(solution)/shard_map/scores_1/pallas_call | solution.py:389
  40.5 4.1 %collective-permute-done.1.x_ref = bf16[2,224,768]{2,1,0:T(8,128)(2,1)S(1)} collective-permute-done((bf16[2,224,768]{2,1,0:T(8,128)(2,1)S(1)}, bf16[2,224,768]{2,1,0:T(8,128)(2,1)S(1)}, u32[]{:S(2)}, u32[]{:S(2)}) %collective-permute-start.1) | collective-permute-done | bytes 688160 | tf_op jit(solution)/shard_map/ppermute | solution.py:51
  44.5 0.0 copy-start.3
  44.6 0.1 collective-permute-start.8
  44.6 2.8 %collective-permute-start.9 = (bf16[2,224,768]{2,1,0:T(8,128)(2,1)S(1)}, bf16[2,224,768]{2,1,0:T(8,128)(2,1)S(1)}, u32[]{:S(2)}, u32[]{:S(2)}) collective-permute-start(bf16[2,224,768]{2,1,0:T(8,128)(2,1)S(1)} %later.3.own.rest_2_), channel_id=1, source_target_pairs={{0,0},{8,16},{16,8},{24,24},{1,1},{9,17},{17,9},{25,25},{2,2},{10,... | collective-permute-start | bytes 2064392 | tf_op jit(solution)/shard_map/ppermute | solution.py:63
  47.5 0.0 collective-permute-done.10.refs_0_
  47.5 2.8 %collective-permute-start.11 = (bf16[2,224,768]{2,1,0:T(8,128)(2,1)S(1)}, bf16[2,224,768]{2,1,0:T(8,128)(2,1)S(1)}, u32[]{:S(2)}, u32[]{:S(2)}) collective-permute-start(bf16[2,224,768]{2,1,0:T(8,128)(2,1)S(1)} %gate.1.near_ref.near), channel_id=1, source_target_pairs={{0,0},{8,16},{16,8},{24,24},{1,1},{9,17},{17,9},{25,25},{2,2},{10,... | collective-permute-start | bytes 2064392 | tf_op jit(solution)/shard_map/ppermute | solution.py:63
  50.2 3.2 %collective-permute-start.12 = (bf16[2,224,768]{2,1,0:T(8,128)(2,1)S(1)}, bf16[2,224,768]{2,1,0:T(8,128)(2,1)S(1)}, u32[]{:S(2)}, u32[]{:S(2)}) collective-permute-start(bf16[2,224,768]{2,1,0:T(8,128)(2,1)S(1)} %gate.1.near_ref.near), channel_id=1, source_target_pairs={{0,2},{2,4},{3,1},{4,6},{5,3},{7,5},{8,10},{10,12},{11,9},{12,14},... | collective-permute-start | bytes 2064392 | tf_op jit(solution)/shard_map/ppermute | solution.py:51
  53.5 0.1 collective-permute-start.15
  53.5 0.0 collective-permute-done.8.pair.rest_5_
  53.5 3.6 %collective-permute-done.9.other.rest_8_ = bf16[2,224,768]{2,1,0:T(8,128)(2,1)S(1)} collective-permute-done((bf16[2,224,768]{2,1,0:T(8,128)(2,1)S(1)}, bf16[2,224,768]{2,1,0:T(8,128)(2,1)S(1)}, u32[]{:S(2)}, u32[]{:S(2)}) %collective-permute-start.9) | collective-permute-done | bytes 688160 | tf_op jit(solution)/shard_map/ppermute | solution.py:63
  57.2 0.0 copy-done.3
  57.2 3.2 %scores_2.1 = (bf16[6,224,672]{2,1,0:T(8,128)(2,1)S(1)}, f32[224,768]{1,0:T(8,128)S(1)}, f32[224,768]{1,0:T(8,128)S(1)}, f32[224,768]{1,0:T(8,128)S(1)}, f32[224...) custom-call(s32[4,8,9]{2,1,0:T(8,128)S(1)} %copy-done.5, s32[8]{0:T(128)S(1)} %copy-done.6, ...), custom_call_target="tpu_custom_call" | custom-call | flops 462422016 | bytes 2752512 | tf_op jit(solution)/shard_map/scores_2/pallas_call | solution.py:389
  60.4 0.0 collective-permute-start.13
  60.4 2.0 %collective-permute-start.14 = (f32[16,224]{1,0:T(8,128)S(1)}, f32[16,224]{1,0:T(8,128)S(1)}, u32[]{:S(2)}, u32[]{:S(2)}) collective-permute-start(f32[16,224]{1,0:T(8,128)S(1)} %get-tuple-element.44.own_ref.rest_0_), channel_id=1, source_target_pairs={{0,0},{1,2},{2,1},{3,4},{4,3},{5,6},{6,5},{7,7},{8,8},{9,10},{10,9... | collective-permute-start | bytes 43016 | tf_op jit(solution)/shard_map/ppermute | solution.py:55
  62.4 5.7 %query_side.1 = (bf16[224,768]{1,0:T(8,128)(2,1)}, bf16[224,768]{1,0:T(8,128)(2,1)}, f32[8,128]{1,0:T(8,128)S(1)}) custom-call(bf16[224,768]{1,0:T(8,128)(2,1)S(1)} %bitcast.16, bf16[27,768]{1,0:T(8,128)(2,1)S(1)} %copy-done.4, bf16[2,224,768]{2,1,0:T(8,128)(2,1)S(1)} %pad_maximum_fusion.own.rest_0_, ...), custom_call_target="tpu_custom_call" | custom-call | flops 1387266048 | bytes 8257536 | tf_op jit(solution)/shard_map/query_side/pallas_call | solution.py:389
  68.1 0.0 collective-permute-done.11.rest_2_.near_other.near_ref
  68.1 0.0 collective-permute-done.12.qg_ref.far_ref.rest_4_
  68.1 0.0 collective-permute-done.15.rest_1_.near_ref.near_pair
  68.1 0.0 collective-permute-done.13.near_ref.rest_1_
  68.1 0.0 collective-permute-done.14.far_ref.rest_2_
  68.1 0.1 pack.1
  68.2 0.1 collective-permute-start.17
  68.3 3.5 %collective-permute-start.16 = (bf16[496,768]{1,0:T(8,128)(2,1)S(1)}, bf16[496,768]{1,0:T(8,128)(2,1)S(1)}, u32[]{:S(2)}, u32[]{:S(2)}) collective-permute-start(bf16[496,768]{1,0:T(8,128)(2,1)S(1)} %pack.1), channel_id=1, source_target_pairs={{0,0},{8,16},{16,8},{24,24},{1,1},{9,17},{17,9},{25,25},{2,2},{10,... | collective-permute-start | bytes 2285576 | tf_op jit(solution)/shard_map/ppermute | solution.py:63
  71.8 1.8 %convolution.3.rest_3_ = f32[224,768]{1,0:T(8,128)S(1)} custom-call(bf16[2,224,768]{2,1,0:T(8,128)(2,1)S(1)} %pair_up.2.own_ref.own, bf16[2,224,768]{2,1,0:T(8,128)(2,1)S(1)} %gate.1.near_ref.near, bf16[2,224,768]{2,1,0:T(8,128)(2,1)S(1)} %collective-permute-done.3.rest_0_.own_ref.pair, ...), custom_call_target="tpu_custom_call" | custom-call | flops 231211008 | bytes 2752512 | tf_op jit(solution)/shard_map/convolution/pallas_call | solution.py:389
  73.6 3.5 %key_side_0.1 = (f32[224,768]{1,0:T(8,128)S(1)}, f32[224,768]{1,0:T(8,128)S(1)}) custom-call(s32[4,8,9]{2,1,0:T(8,128)S(1)} %copy-done.5, s32[8]{0:T(128)S(1)} %copy-done.6, bf16[2,224,768]{2,1,0:T(8,128)(2,1)S(1)} %pad_maximum_fusion.own.rest_0_, bf16[2,224,768]{2,1,0:T(8,128)(2,1)S(1)} %pair_up.2.own_ref.own, bf16[2,224,768]{2,1,0:T(8,128)(2,1)S(1)} %gate.1.near_ref.near, ...), custom_call_target="tpu_custom_call" | custom-call | flops 924844032 | bytes 2752512 | tf_op jit(solution)/shard_map/key_side_0/pallas_call | solution.py:389
  77.1 0.0 collective-permute-done.17.far_ref.rest_5_
  77.1 3.7 %key_side_1.1 = (f32[224,768]{1,0:T(8,128)S(1)}, f32[224,768]{1,0:T(8,128)S(1)}) custom-call(s32[4,8,9]{2,1,0:T(8,128)S(1)} %copy-done.5, s32[8]{0:T(128)S(1)} %copy-done.6, bf16[2,224,768]{2,1,0:T(8,128)(2,1)S(1)} %pad_maximum_fusion.own.rest_0_, bf16[2,224,768]{2,1,0:T(8,128)(2,1)S(1)} %collective-permute-done.3.rest_0_.own_ref.pair, ...), custom_call_target="tpu_custom_call" | custom-call | flops 924844032 | bytes 2752512 | tf_op jit(solution)/shard_map/key_side_1/pallas_call | solution.py:389
  80.8 0.6 collective-permute-done.16.far_ref
  81.3 4.6 %key_side_2.1 = (bf16[224,768]{1,0:T(8,128)(2,1)}, bf16[224,768]{1,0:T(8,128)(2,1)}) custom-call(s32[4,8,9]{2,1,0:T(8,128)S(1)} %copy-done.5, s32[8]{0:T(128)S(1)} %copy-done.6, bf16[2,224,768]{2,1,0:T(8,128)(2,1)S(1)} %pad_maximum_fusion.own.rest_0_, bf16[2,224,768]{2,1,0:T(8,128)(2,1)S(1)} %collective-permute-done.4.rest_1_.other.own_ref, ...), custom_call_target="tpu_custom_call" | custom-call | flops 924844032 | bytes 2752512 | tf_op jit(solution)/shard_map/key_side_2/pallas_call | solution.py:389
  (5 shorter events, 0.2 us)
Async XLA Ops:
  1.8 5.3 %collective-permute-start.2 = (bf16[2,224,768]{2,1,0:T(8,128)(2,1)S(1)}, bf16[2,224,768]{2,1,0:T(8,128)(2,1)S(1)}, u32[]{:S(2)}, u32[]{:S(2)}) collective-permute-start(bf16[2,224,768]{2,1,0:T(8,128)(2,1)S(1)} %pad_maximum_fusion.own.rest_0_), channel_id=1, source_target_pairs={{0,8},{8,0},{16,24},{24,16},{1,9},{9,1},{17,25},{25,17},{2,10},{10... | collective-permute-start | bytes 2064392 | tf_op jit(solution)/shard_map/ppermute | solution.py:59
  2.5 17.0 %collective-permute-start = (bf16[2,224,768]{2,1,0:T(8,128)(2,1)S(1)}, bf16[2,224,768]{2,1,0:T(8,128)(2,1)S(1)}, u32[]{:S(2)}, u32[]{:S(2)}) collective-permute-start(bf16[2,224,768]{2,1,0:T(8,128)(2,1)S(1)} %pad_maximum_fusion.own.rest_0_), channel_id=1, source_target_pairs={{0,1},{1,0},{2,3},{3,2},{4,5},{5,4},{6,7},{7,6},{8,9},{9,8},{10,11... | collective-permute-start | bytes 2064392 | tf_op jit(solution)/shard_map/ppermute | solution.py:47
  3.7 15.8 %collective-permute-start.5 = (bf16[2,224,768]{2,1,0:T(8,128)(2,1)S(1)}, bf16[2,224,768]{2,1,0:T(8,128)(2,1)S(1)}, u32[]{:S(2)}, u32[]{:S(2)}) collective-permute-start(bf16[2,224,768]{2,1,0:T(8,128)(2,1)S(1)} %pad_maximum_fusion.own.rest_0_), channel_id=1, source_target_pairs={{0,0},{8,16},{16,8},{24,24},{1,1},{9,17},{17,9},{25,25},{2,2},{10,... | collective-permute-start | bytes 2064392 | tf_op jit(solution)/shard_map/ppermute | solution.py:63
  7.1 1.0 %copy-start = (bf16[2,2,56,768]{3,2,1,0:T(8,128)(2,1)S(1)}, bf16[2,2,56,768]{3,2,1,0:T(8,128)(2,1)}, u32[]{:S(2)}) copy-start(bf16[2,2,56,768]{3,2,1,0:T(8,128)(2,1)} %param.7) | copy-start | bytes 1032196
  8.1 1.0 %copy-start.2 = (bf16[2,2,56,768]{3,2,1,0:T(8,128)(2,1)S(1)}, bf16[2,2,56,768]{3,2,1,0:T(8,128)(2,1)}, u32[]{:S(2)}) copy-start(bf16[2,2,56,768]{3,2,1,0:T(8,128)(2,1)} %param.11) | copy-start | bytes 1032196
  9.1 21.1 %copy-start.1 = (bf16[2,2,56,768]{3,2,1,0:T(8,128)(2,1)S(1)}, bf16[2,2,56,768]{3,2,1,0:T(8,128)(2,1)}, u32[]{:S(2)}) copy-start(bf16[2,2,56,768]{3,2,1,0:T(8,128)(2,1)} %param.7) | copy-start | bytes 1032196
  9.2 21.1 %copy-start.5 = (s32[4,8,9]{2,1,0:T(8,128)S(1)}, s32[4,8,9]{2,1,0:T(8,128)}, u32[]{:S(2)}) copy-start(s32[4,8,9]{2,1,0:T(8,128)} %mask_ref.11) | copy-start | bytes 3460
  9.2 21.1 %copy-start.6 = (s32[8]{0:T(128)S(1)}, s32[8]{0:T(128)}, u32[]{:S(2)}) copy-start(s32[8]{0:T(128)} %clip_ref.11) | copy-start | bytes 100
  9.2 10.4 %collective-permute-start.3 = (bf16[2,224,768]{2,1,0:T(8,128)(2,1)S(1)}, bf16[2,224,768]{2,1,0:T(8,128)(2,1)S(1)}, u32[]{:S(2)}, u32[]{:S(2)}) collective-permute-start(bf16[2,224,768]{2,1,0:T(8,128)(2,1)S(1)} %pair_up.2.own_ref.own), channel_id=1, source_target_pairs={{0,8},{8,0},{16,24},{24,16},{1,9},{9,1},{17,25},{25,17},{2,10},{10... | collective-permute-start | bytes 2064392 | tf_op jit(solution)/shard_map/ppermute | solution.py:59
  9.3 14.1 %collective-permute-start.4 = (bf16[2,224,768]{2,1,0:T(8,128)(2,1)S(1)}, bf16[2,224,768]{2,1,0:T(8,128)(2,1)S(1)}, u32[]{:S(2)}, u32[]{:S(2)}) collective-permute-start(bf16[2,224,768]{2,1,0:T(8,128)(2,1)S(1)} %pair_up.2.own_ref.own), channel_id=1, source_target_pairs={{0,0},{8,16},{16,8},{24,24},{1,1},{9,17},{17,9},{25,25},{2,2},{10,... | collective-permute-start | bytes 2064392 | tf_op jit(solution)/shard_map/ppermute | solution.py:63
  23.4 12.6 %copy-start.4 = (bf16[27,768]{1,0:T(8,128)(2,1)S(1)}, bf16[27,768]{1,0:T(8,128)(2,1)}, u32[]{:S(2)}) copy-start(bf16[27,768]{1,0:T(8,128)(2,1)} %rest_2_.1) | copy-start | bytes 124420
  23.4 9.5 %collective-permute-start.6 = (bf16[2,224,768]{2,1,0:T(8,128)(2,1)S(1)}, bf16[2,224,768]{2,1,0:T(8,128)(2,1)S(1)}, u32[]{:S(2)}, u32[]{:S(2)}) collective-permute-start(bf16[2,224,768]{2,1,0:T(8,128)(2,1)S(1)} %later.2), channel_id=1, source_target_pairs={{0,8},{8,0},{16,24},{24,16},{1,9},{9,1},{17,25},{25,17},{2,10},{10... | collective-permute-start | bytes 2064392 | tf_op jit(solution)/shard_map/ppermute | solution.py:59
  23.5 12.6 %collective-permute-start.7 = (bf16[2,224,768]{2,1,0:T(8,128)(2,1)S(1)}, bf16[2,224,768]{2,1,0:T(8,128)(2,1)S(1)}, u32[]{:S(2)}, u32[]{:S(2)}) collective-permute-start(bf16[2,224,768]{2,1,0:T(8,128)(2,1)S(1)} %later.2), channel_id=1, source_target_pairs={{0,0},{8,16},{16,8},{24,24},{1,1},{9,17},{17,9},{25,25},{2,2},{10,... | collective-permute-start | bytes 2064392 | tf_op jit(solution)/shard_map/ppermute | solution.py:63
  26.9 17.6 %collective-permute-start.1 = (bf16[2,224,768]{2,1,0:T(8,128)(2,1)S(1)}, bf16[2,224,768]{2,1,0:T(8,128)(2,1)S(1)}, u32[]{:S(2)}, u32[]{:S(2)}) collective-permute-start(bf16[2,224,768]{2,1,0:T(8,128)(2,1)S(1)} %collective-permute-done.x_ref.own.near.rest_1_.rest_0_), channel_id=1, source_target_pairs={{0,2},{2,4},{3,1},{4,6},{5,3},{7,5},{8,10},{10,12},{11,9},{12,14},... | collective-permute-start | bytes 2064392 | tf_op jit(solution)/shard_map/ppermute | solution.py:51
  30.2 17.3 %collective-permute-start.10 = (bf16[2,224,768]{2,1,0:T(8,128)(2,1)S(1)}, bf16[2,224,768]{2,1,0:T(8,128)(2,1)S(1)}, u32[]{:S(2)}, u32[]{:S(2)}) collective-permute-start(bf16[2,224,768]{2,1,0:T(8,128)(2,1)S(1)} %pair_up.3), channel_id=1, source_target_pairs={{0,1},{1,0},{2,3},{3,2},{4,5},{5,4},{6,7},{7,6},{8,9},{9,8},{10,11... | collective-permute-start | bytes 2064392 | tf_op jit(solution)/shard_map/ppermute | solution.py:47
  44.5 12.7 %copy-start.3 = (bf16[2,2,56,768]{3,2,1,0:T(8,128)(2,1)S(1)}, bf16[2,2,56,768]{3,2,1,0:T(8,128)(2,1)}, u32[]{:S(2)}) copy-start(bf16[2,2,56,768]{3,2,1,0:T(8,128)(2,1)} %param.11) | copy-start | bytes 1032196
  44.6 9.0 %collective-permute-start.8 = (bf16[2,224,768]{2,1,0:T(8,128)(2,1)S(1)}, bf16[2,224,768]{2,1,0:T(8,128)(2,1)S(1)}, u32[]{:S(2)}, u32[]{:S(2)}) collective-permute-start(bf16[2,224,768]{2,1,0:T(8,128)(2,1)S(1)} %later.3.own.rest_2_), channel_id=1, source_target_pairs={{0,8},{8,0},{16,24},{24,16},{1,9},{9,1},{17,25},{25,17},{2,10},{10... | collective-permute-start | bytes 2064392 | tf_op jit(solution)/shard_map/ppermute | solution.py:59
  44.6 12.6 %collective-permute-start.9 = (bf16[2,224,768]{2,1,0:T(8,128)(2,1)S(1)}, bf16[2,224,768]{2,1,0:T(8,128)(2,1)S(1)}, u32[]{:S(2)}, u32[]{:S(2)}) collective-permute-start(bf16[2,224,768]{2,1,0:T(8,128)(2,1)S(1)} %later.3.own.rest_2_), channel_id=1, source_target_pairs={{0,0},{8,16},{16,8},{24,24},{1,1},{9,17},{17,9},{25,25},{2,2},{10,... | collective-permute-start | bytes 2064392 | tf_op jit(solution)/shard_map/ppermute | solution.py:63
  47.5 20.6 %collective-permute-start.11 = (bf16[2,224,768]{2,1,0:T(8,128)(2,1)S(1)}, bf16[2,224,768]{2,1,0:T(8,128)(2,1)S(1)}, u32[]{:S(2)}, u32[]{:S(2)}) collective-permute-start(bf16[2,224,768]{2,1,0:T(8,128)(2,1)S(1)} %gate.1.near_ref.near), channel_id=1, source_target_pairs={{0,0},{8,16},{16,8},{24,24},{1,1},{9,17},{17,9},{25,25},{2,2},{10,... | collective-permute-start | bytes 2064392 | tf_op jit(solution)/shard_map/ppermute | solution.py:63
  50.2 17.9 %collective-permute-start.12 = (bf16[2,224,768]{2,1,0:T(8,128)(2,1)S(1)}, bf16[2,224,768]{2,1,0:T(8,128)(2,1)S(1)}, u32[]{:S(2)}, u32[]{:S(2)}) collective-permute-start(bf16[2,224,768]{2,1,0:T(8,128)(2,1)S(1)} %gate.1.near_ref.near), channel_id=1, source_target_pairs={{0,2},{2,4},{3,1},{4,6},{5,3},{7,5},{8,10},{10,12},{11,9},{12,14},... | collective-permute-start | bytes 2064392 | tf_op jit(solution)/shard_map/ppermute | solution.py:51
  53.5 14.7 %collective-permute-start.15 = (bf16[2,224,768]{2,1,0:T(8,128)(2,1)S(1)}, bf16[2,224,768]{2,1,0:T(8,128)(2,1)S(1)}, u32[]{:S(2)}, u32[]{:S(2)}) collective-permute-start(bf16[2,224,768]{2,1,0:T(8,128)(2,1)S(1)} %gate.1.near_ref.near), channel_id=1, source_target_pairs={{0,8},{8,0},{16,24},{24,16},{1,9},{9,1},{17,25},{25,17},{2,10},{10... | collective-permute-start | bytes 2064392 | tf_op jit(solution)/shard_map/ppermute | solution.py:59
  60.4 7.8 %collective-permute-start.13 = (f32[16,224]{1,0:T(8,128)S(1)}, f32[16,224]{1,0:T(8,128)S(1)}, u32[]{:S(2)}, u32[]{:S(2)}) collective-permute-start(f32[16,224]{1,0:T(8,128)S(1)} %get-tuple-element.44.own_ref.rest_0_), channel_id=1, source_target_pairs={{0,1},{1,0},{2,3},{3,2},{4,5},{5,4},{6,7},{7,6},{8,9},{9,8},{10,11... | collective-permute-start | bytes 43016 | tf_op jit(solution)/shard_map/ppermute | solution.py:47
  60.4 7.7 %collective-permute-start.14 = (f32[16,224]{1,0:T(8,128)S(1)}, f32[16,224]{1,0:T(8,128)S(1)}, u32[]{:S(2)}, u32[]{:S(2)}) collective-permute-start(f32[16,224]{1,0:T(8,128)S(1)} %get-tuple-element.44.own_ref.rest_0_), channel_id=1, source_target_pairs={{0,0},{1,2},{2,1},{3,4},{4,3},{5,6},{6,5},{7,7},{8,8},{9,10},{10,9... | collective-permute-start | bytes 43016 | tf_op jit(solution)/shard_map/ppermute | solution.py:55
  68.2 8.9 %collective-permute-start.17 = (bf16[496,768]{1,0:T(8,128)(2,1)S(1)}, bf16[496,768]{1,0:T(8,128)(2,1)S(1)}, u32[]{:S(2)}, u32[]{:S(2)}) collective-permute-start(bf16[496,768]{1,0:T(8,128)(2,1)S(1)} %pack.1), channel_id=1, source_target_pairs={{0,8},{8,0},{16,24},{24,16},{1,9},{9,1},{17,25},{25,17},{2,10},{10... | collective-permute-start | bytes 2285576 | tf_op jit(solution)/shard_map/ppermute | solution.py:59
  68.3 13.0 %collective-permute-start.16 = (bf16[496,768]{1,0:T(8,128)(2,1)S(1)}, bf16[496,768]{1,0:T(8,128)(2,1)S(1)}, u32[]{:S(2)}, u32[]{:S(2)}) collective-permute-start(bf16[496,768]{1,0:T(8,128)(2,1)S(1)} %pack.1), channel_id=1, source_target_pairs={{0,0},{8,16},{16,8},{24,24},{1,1},{9,17},{17,9},{25,25},{2,2},{10,... | collective-permute-start | bytes 2285576 | tf_op jit(solution)/shard_map/ppermute | solution.py:63

commit v10 on v8

--- a/solution.py
+++ b/solution.py
@@ -12,7 +12,7 @@
 ROW_DELTA = 8
 STAT_ROWS = 16
 STAT_LANES = 256
-UNROLL = 2
+UNROLL = 6
 FLOOR = -1e30
 SMALL = 2 * 1024 * 1024
 LARGE = 8 * 1024 * 1024

time: 84.8 us -> 83 us (0.979)
  Pallas kernels: 31.8 us -> 28.2 us
  waiting for transfers between devices: 8.84 us -> 9.99 us
    pallas_call x9, Pallas kernels: 31.5 us -> 28 us  [call(): pl.pallas_call(kernel, in_specs=[smem] * scalars + [vmem] * (len(args) -...]
    ppermute x6, waiting for transfers between devices: 5.82 us -> 6.97 us  [ta_other(): return lax.ppermute(x, 'ta', other_pairs(lax.axis_size('ta')))]
  transfers between devices with their start and end apart: 20 -> 20, of which waited for: 5 -> 5; matrix products, arithmetic and copies ran while one was open for 0% -> 0% of each run, Pallas kernels for 32% -> 29%
where the time goes in v10:
time: 83 us; the launch traced here: 82.4 us
  starting transfers between devices  39.9 us (48%)
  Pallas kernels  28.2 us (34%)
  waiting for transfers between devices  9.99 us (12%)
  local copies, waits for them, and re-layouts  1.99 us (2%)
  other arithmetic  1.19 us (1%)
  between operations  1.02 us (1%)
    pallas_call x9, Pallas kernels, call(): pl.pallas_call(kernel, in_specs=[smem] * scalars + [vmem] * (len(args) -...  28 us
    ppermute x6, starting transfers between devices, ta_other(): return lax.ppermute(x, 'ta', other_pairs(lax.axis_size('ta')))  20.3 us
    ppermute x3, starting transfers between devices, ha_relay(): return lax.ppermute(near, 'ha', relay_pairs(lax.axis_size('ha')))  9.6 us
    ppermute x6, waiting for transfers between devices, ta_other(): return lax.ppermute(x, 'ta', other_pairs(lax.axis_size('ta')))  6.97 us
    ppermute x4, starting transfers between devices, ha_near(): return lax.ppermute(x, 'ha', flip_pairs(lax.axis_size('ha')))  3.81 us
    ppermute x1, starting transfers between devices, ha_far(): return lax.ppermute(x, 'ha', other_pairs(lax.axis_size('ha')))  3.13 us
    ppermute x6, starting transfers between devices, ta_pair(): return lax.ppermute(x, 'ta', flip_pairs(lax.axis_size('ta')))  3.04 us
    ppermute x4, waiting for transfers between devices, ha_near(): return lax.ppermute(x, 'ha', flip_pairs(lax.axis_size('ha')))  2.45 us
  transfers between devices with their start and end apart: 20, of which 5 were waited for; matrix products, arithmetic and copies ran while one was open for 0% of the time, Pallas kernels for 29%

profile of v10, /device:TPU:9, one launch (start us, length us, event | category | flops | bytes accessed | tf_op | source)
XLA Modules:
  0.0 82.4 jit_solution(12863254201576981659)
XLA Ops:
  0.6 0.0 copy-start.4
  0.6 1.2 %pad_maximum_fusion.own.rest_0_ = bf16[2,224,768]{2,1,0:T(8,128)(2,1)S(1)} fusion(bf16[1,224,768]{2,1,0:T(8,128)(2,1)} %bitcast.19, bf16[1,224,768]{2,1,0:T(8,128)(2,1)} %bitcast.21), kind=kLoop, calls=%fused_computation | loop fusion | flops 344064 | bytes 1376256 | tf_op jit(solution)/shard_map/stack | solution.py:447
  1.8 0.7 collective-permute-start.2
  2.6 1.2 %collective-permute-start = (bf16[224,768]{1,0:T(8,128)(2,1)}, bf16[224,768]{1,0:T(8,128)(2,1)S(1)}, u32[]{:S(2)}, u32[]{:S(2)}) collective-permute-start(bf16[224,768]{1,0:T(8,128)(2,1)} %bitcast.22), channel_id=1, source_target_pairs={{0,1},{1,0},{2,3},{3,2},{4,5},{5,4},{6,7},{7,6},{8,9},{9,8},{10,11... | collective-permute-start | bytes 1032200 | tf_op jit(solution)/shard_map/ppermute | solution.py:46
  3.8 0.5 collective-permute-done.2.rest_0_.pair.rest_3_
  4.4 1.0 %copy-done = bf16[2,2,56,768]{3,2,1,0:T(8,128)(2,1)S(1)} copy-done((bf16[2,2,56,768]{3,2,1,0:T(8,128)(2,1)S(1)}, bf16[2,2,56,768]{3,2,1,0:T(8,128)(2,1)}, u32[]{:S(2)}) %copy-start) | copy-done | bytes 344088
  5.3 1.0 %copy-done.2 = bf16[2,2,56,768]{3,2,1,0:T(8,128)(2,1)S(1)} copy-done((bf16[2,2,56,768]{3,2,1,0:T(8,128)(2,1)S(1)}, bf16[2,2,56,768]{3,2,1,0:T(8,128)(2,1)}, u32[]{:S(2)}) %copy-start.2) | copy-done | bytes 344088
  6.4 0.0 copy-start.1
  6.4 0.0 copy-start.3
  6.4 0.4 collective-permute-start.3
  6.8 3.2 %collective-permute-start.4 = (bf16[2,224,768]{2,1,0:T(8,128)(2,1)S(1)}, bf16[2,224,768]{2,1,0:T(8,128)(2,1)S(1)}, u32[]{:S(2)}, u32[]{:S(2)}) collective-permute-start(bf16[2,224,768]{2,1,0:T(8,128)(2,1)S(1)} %pair_up.4.own_ref.own), channel_id=1, source_target_pairs={{0,0},{8,16},{16,8},{24,24},{1,1},{9,17},{17,9},{25,25},{2,2},{10,... | collective-permute-start | bytes 2064392 | tf_op jit(solution)/shard_map/ppermute | solution.py:62
  10.0 2.4 %collective-permute-done.rest_0_.x_ref = bf16[224,768]{1,0:T(8,128)(2,1)S(1)} collective-permute-done((bf16[224,768]{1,0:T(8,128)(2,1)}, bf16[224,768]{1,0:T(8,128)(2,1)S(1)}, u32[]{:S(2)}, u32[]{:S(2)}) %collective-permute-start) | collective-permute-done | bytes 344096 | tf_op jit(solution)/shard_map/ppermute | solution.py:46
  12.4 0.0 copy-done.4
  12.5 0.0 copy-start.6
  12.5 0.0 copy-start.7
  12.5 1.3 %collective-permute-start.1 = (bf16[224,768]{1,0:T(8,128)(2,1)S(1)}, bf16[224,768]{1,0:T(8,128)(2,1)S(1)}, u32[]{:S(2)}, u32[]{:S(2)}) collective-permute-start(bf16[224,768]{1,0:T(8,128)(2,1)S(1)} %later.1), channel_id=1, source_target_pairs={{0,1},{1,0},{2,3},{3,2},{4,5},{5,4},{6,7},{7,6},{8,9},{9,8},{10,11... | collective-permute-start | bytes 1032200 | tf_op jit(solution)/shard_map/ppermute | solution.py:46
  13.8 3.2 %collective-permute-start.5 = (bf16[224,768]{1,0:T(8,128)(2,1)S(1)}, bf16[224,768]{1,0:T(8,128)(2,1)S(1)}, u32[]{:S(2)}, u32[]{:S(2)}) collective-permute-start(bf16[224,768]{1,0:T(8,128)(2,1)S(1)} %collective-permute-done.rest_0_.x_ref), channel_id=1, source_target_pairs={{0,2},{2,4},{3,1},{4,6},{5,3},{7,5},{8,10},{10,12},{11,9},{12,14},... | collective-permute-start | bytes 1032200 | tf_op jit(solution)/shard_map/ppermute | solution.py:50
  17.0 4.4 %collective-permute-start.7 = (bf16[2,224,768]{2,1,0:T(8,128)(2,1)S(1)}, bf16[2,224,768]{2,1,0:T(8,128)(2,1)S(1)}, u32[]{:S(2)}, u32[]{:S(2)}) collective-permute-start(bf16[2,224,768]{2,1,0:T(8,128)(2,1)S(1)} %pad_maximum_fusion.own.rest_0_), channel_id=1, source_target_pairs={{0,0},{8,16},{16,8},{24,24},{1,1},{9,17},{17,9},{25,25},{2,2},{10,... | collective-permute-start | bytes 2064392 | tf_op jit(solution)/shard_map/ppermute | solution.py:62
  21.4 0.0 collective-permute-done.1.y_ref.rest_0_
  21.4 0.0 collective-permute-done.3.rest_0_.own_ref.pair
  21.4 0.0 collective-permute-done.4.rest_1_.other.own_ref
  21.5 1.6 %collective-permute-start.8 = (bf16[2,224,768]{2,1,0:T(8,128)(2,1)S(1)}, bf16[2,224,768]{2,1,0:T(8,128)(2,1)S(1)}, u32[]{:S(2)}, u32[]{:S(2)}) collective-permute-start(bf16[2,224,768]{2,1,0:T(8,128)(2,1)S(1)} %pair_up.5.own.near.rest_1_), channel_id=1, source_target_pairs={{0,8},{8,0},{16,24},{24,16},{1,9},{9,1},{17,25},{25,17},{2,10},{10... | collective-permute-start | bytes 2064392 | tf_op jit(solution)/shard_map/ppermute | solution.py:58
  23.1 3.0 %collective-permute-start.9 = (bf16[2,224,768]{2,1,0:T(8,128)(2,1)S(1)}, bf16[2,224,768]{2,1,0:T(8,128)(2,1)S(1)}, u32[]{:S(2)}, u32[]{:S(2)}) collective-permute-start(bf16[2,224,768]{2,1,0:T(8,128)(2,1)S(1)} %pair_up.5.own.near.rest_1_), channel_id=1, source_target_pairs={{0,0},{8,16},{16,8},{24,24},{1,1},{9,17},{17,9},{25,25},{2,2},{10,... | collective-permute-start | bytes 2064392 | tf_op jit(solution)/shard_map/ppermute | solution.py:62
  26.2 0.0 collective-permute-done.5.x_ref.rest_1_
  26.2 0.0 copy-done.1
  26.2 0.0 copy-done.3
  26.3 1.3 %collective-permute-start.12 = (bf16[2,224,768]{2,1,0:T(8,128)(2,1)S(1)}, bf16[2,224,768]{2,1,0:T(8,128)(2,1)S(1)}, u32[]{:S(2)}, u32[]{:S(2)}) collective-permute-start(bf16[2,224,768]{2,1,0:T(8,128)(2,1)S(1)} %pair_up.7), channel_id=1, source_target_pairs={{0,1},{1,0},{2,3},{3,2},{4,5},{5,4},{6,7},{7,6},{8,9},{9,8},{10,11... | collective-permute-start | bytes 2064392 | tf_op jit(solution)/shard_map/ppermute | solution.py:46
  27.6 3.2 %collective-permute-start.6 = (bf16[224,768]{1,0:T(8,128)(2,1)S(1)}, bf16[224,768]{1,0:T(8,128)(2,1)S(1)}, u32[]{:S(2)}, u32[]{:S(2)}) collective-permute-start(bf16[224,768]{1,0:T(8,128)(2,1)S(1)} %collective-permute-done.1.y_ref.rest_0_), channel_id=1, source_target_pairs={{0,2},{2,4},{3,1},{4,6},{5,3},{7,5},{8,10},{10,12},{11,9},{12,14},... | collective-permute-start | bytes 1032200 | tf_op jit(solution)/shard_map/ppermute | solution.py:50
  30.8 0.0 collective-permute-done.7.other.rest_6_
  30.8 0.0 copy-done.6
  30.8 0.0 copy-done.7
  30.8 2.6 %scores_0.1 = (bf16[6,224,672]{2,1,0:T(8,128)(2,1)S(1)}, f32[224,768]{1,0:T(8,128)S(1)}, f32[224,768]{1,0:T(8,128)S(1)}, f32[224,768]{1,0:T(8,128)S(1)}) custom-call(s32[4,8,9]{2,1,0:T(8,128)S(1)} %copy-done.6, s32[8]{0:T(128)S(1)} %copy-done.7, bf16[224,768]{1,0:T(8,128)(2,1)S(1)} %bitcast.12, bf16[2,224,768]{2,1,0:T(8,128)(2,1)S(1)} %pad_maximum_fusion.own.rest_0_, ...), custom_call_target="tpu_custom_call" | custom-call | flops 462422016 | bytes 2752512 | tf_op jit(solution)/shard_map/scores_0/pallas_call | solution.py:388
  33.4 0.0 collective-permute-done.8.pair.near_pair.rest_4_
  33.4 4.3 %collective-permute-done.9.other.near_other.rest_7_ = bf16[2,224,768]{2,1,0:T(8,128)(2,1)S(1)} collective-permute-done((bf16[2,224,768]{2,1,0:T(8,128)(2,1)S(1)}, bf16[2,224,768]{2,1,0:T(8,128)(2,1)S(1)}, u32[]{:S(2)}, u32[]{:S(2)}) %collective-permute-start.9) | collective-permute-done | bytes 688160 | tf_op jit(solution)/shard_map/ppermute | solution.py:62
  37.7 2.6 %scores_1.1 = (bf16[6,224,672]{2,1,0:T(8,128)(2,1)S(1)}, f32[224,768]{1,0:T(8,128)S(1)}, f32[224,768]{1,0:T(8,128)S(1)}, f32[224,768]{1,0:T(8,128)S(1)}) custom-call(s32[4,8,9]{2,1,0:T(8,128)S(1)} %copy-done.6, s32[8]{0:T(128)S(1)} %copy-done.7, bf16[224,768]{1,0:T(8,128)(2,1)S(1)} %bitcast.13, bf16[2,224,768]{2,1,0:T(8,128)(2,1)S(1)} %pair_up.5.own.near.rest_1_, ...), custom_call_target="tpu_custom_call" | custom-call | flops 462422016 | bytes 2752512 | tf_op jit(solution)/shard_map/scores_1/pallas_call | solution.py:388
  40.3 0.0 collective-permute-done.6.y_ref
  40.3 0.0 copy-start.5
  40.4 0.1 collective-permute-start.10
  40.5 3.4 %collective-permute-start.11 = (bf16[2,224,768]{2,1,0:T(8,128)(2,1)S(1)}, bf16[2,224,768]{2,1,0:T(8,128)(2,1)S(1)}, u32[]{:S(2)}, u32[]{:S(2)}) collective-permute-start(bf16[2,224,768]{2,1,0:T(8,128)(2,1)S(1)} %pair_up.6.own.rest_2_), channel_id=1, source_target_pairs={{0,0},{8,16},{16,8},{24,24},{1,1},{9,17},{17,9},{25,25},{2,2},{10,... | collective-permute-start | bytes 2064392 | tf_op jit(solution)/shard_map/ppermute | solution.py:62
  43.8 0.0 collective-permute-done.12.refs_0_
  43.8 2.2 %collective-permute-start.13 = (bf16[2,224,768]{2,1,0:T(8,128)(2,1)S(1)}, bf16[2,224,768]{2,1,0:T(8,128)(2,1)S(1)}, u32[]{:S(2)}, u32[]{:S(2)}) collective-permute-start(bf16[2,224,768]{2,1,0:T(8,128)(2,1)S(1)} %gate.1.near_ref.near), channel_id=1, source_target_pairs={{0,0},{8,16},{16,8},{24,24},{1,1},{9,17},{17,9},{25,25},{2,2},{10,... | collective-permute-start | bytes 2064392 | tf_op jit(solution)/shard_map/ppermute | solution.py:62
  46.1 3.2 %collective-permute-start.14 = (bf16[2,224,768]{2,1,0:T(8,128)(2,1)S(1)}, bf16[2,224,768]{2,1,0:T(8,128)(2,1)S(1)}, u32[]{:S(2)}, u32[]{:S(2)}) collective-permute-start(bf16[2,224,768]{2,1,0:T(8,128)(2,1)S(1)} %gate.1.near_ref.near), channel_id=1, source_target_pairs={{0,2},{2,4},{3,1},{4,6},{5,3},{7,5},{8,10},{10,12},{11,9},{12,14},... | collective-permute-start | bytes 2064392 | tf_op jit(solution)/shard_map/ppermute | solution.py:50
  49.3 0.1 collective-permute-start.17
  49.4 1.8 %convolution.2.rest_7_.rest_17_ = f32[224,768]{1,0:T(8,128)S(1)} custom-call(bf16[2,224,768]{2,1,0:T(8,128)(2,1)S(1)} %pad_maximum_fusion.own.rest_0_, bf16[2,224,768]{2,1,0:T(8,128)(2,1)S(1)} %pair_up.5.own.near.rest_1_, bf16[2,224,768]{2,1,0:T(8,128)(2,1)S(1)} %collective-permute-done.2.rest_0_.pair.rest_3_, ...), custom_call_target="tpu_custom_call" | custom-call | flops 231211008 | bytes 2752512 | tf_op jit(solution)/shard_map/convolution/pallas_call | solution.py:388
  51.1 0.0 collective-permute-done.10.pair.rest_5_
  51.1 1.9 %collective-permute-done.11.other.rest_8_ = bf16[2,224,768]{2,1,0:T(8,128)(2,1)S(1)} collective-permute-done((bf16[2,224,768]{2,1,0:T(8,128)(2,1)S(1)}, bf16[2,224,768]{2,1,0:T(8,128)(2,1)S(1)}, u32[]{:S(2)}, u32[]{:S(2)}) %collective-permute-start.11) | collective-permute-done | bytes 688160 | tf_op jit(solution)/shard_map/ppermute | solution.py:62
  53.0 3.2 %scores_2.1 = (bf16[6,224,672]{2,1,0:T(8,128)(2,1)S(1)}, f32[224,768]{1,0:T(8,128)S(1)}, f32[224,768]{1,0:T(8,128)S(1)}, f32[224,768]{1,0:T(8,128)S(1)}, f32[224...) custom-call(s32[4,8,9]{2,1,0:T(8,128)S(1)} %copy-done.6, s32[8]{0:T(128)S(1)} %copy-done.7, ...), custom_call_target="tpu_custom_call" | custom-call | flops 462422016 | bytes 2752512 | tf_op jit(solution)/shard_map/scores_2/pallas_call | solution.py:388
  56.2 0.0 collective-permute-start.15
  56.2 3.1 %collective-permute-start.16 = (f32[16,224]{1,0:T(8,128)S(1)}, f32[16,224]{1,0:T(8,128)S(1)}, u32[]{:S(2)}, u32[]{:S(2)}) collective-permute-start(f32[16,224]{1,0:T(8,128)S(1)} %get-tuple-element.44.own_ref.rest_0_), channel_id=1, source_target_pairs={{0,0},{1,2},{2,1},{3,4},{4,3},{5,6},{6,5},{7,7},{8,8},{9,10},{10,9... | collective-permute-start | bytes 43016 | tf_op jit(solution)/shard_map/ppermute | solution.py:54
  59.4 5.3 %query_side.1 = (bf16[224,768]{1,0:T(8,128)(2,1)}, bf16[224,768]{1,0:T(8,128)(2,1)}, f32[8,128]{1,0:T(8,128)S(1)}) custom-call(bf16[224,768]{1,0:T(8,128)(2,1)S(1)} %bitcast.18, bf16[27,768]{1,0:T(8,128)(2,1)S(1)} %copy-done.5, bf16[2,224,768]{2,1,0:T(8,128)(2,1)S(1)} %pad_maximum_fusion.own.rest_0_, bf16[2,224,768]{2,1,0:T(8,128)(2,1)S(1)} %pair_up.5.own.near.rest_1_, ...), custom_call_target="tpu_custom_call" | custom-call | flops 1387266048 | bytes 8257536 | tf_op jit(solution)/shard_map/query_side/pallas_call | solution.py:388
  64.7 0.0 collective-permute-done.13.rest_2_.near_other.near_ref
  64.7 0.0 collective-permute-done.14.qg_ref.far_ref.rest_4_
  64.7 0.0 collective-permute-done.17.rest_1_.near_ref.near_pair
  64.7 0.0 collective-permute-done.15.near_ref.rest_1_
  64.7 0.0 collective-permute-done.16.far_ref.rest_2_
  64.7 0.1 pack.1
  64.8 0.1 collective-permute-start.19
  64.8 4.1 %collective-permute-start.18 = (bf16[496,768]{1,0:T(8,128)(2,1)S(1)}, bf16[496,768]{1,0:T(8,128)(2,1)S(1)}, u32[]{:S(2)}, u32[]{:S(2)}) collective-permute-start(bf16[496,768]{1,0:T(8,128)(2,1)S(1)} %pack.1), channel_id=1, source_target_pairs={{0,0},{8,16},{16,8},{24,24},{1,1},{9,17},{17,9},{25,25},{2,2},{10,... | collective-permute-start | bytes 2285576 | tf_op jit(solution)/shard_map/ppermute | solution.py:62
  69.0 1.8 %convolution.3.rest_3_ = f32[224,768]{1,0:T(8,128)S(1)} custom-call(bf16[2,224,768]{2,1,0:T(8,128)(2,1)S(1)} %pair_up.4.own_ref.own, bf16[2,224,768]{2,1,0:T(8,128)(2,1)S(1)} %gate.1.near_ref.near, bf16[2,224,768]{2,1,0:T(8,128)(2,1)S(1)} %collective-permute-done.3.rest_0_.own_ref.pair, ...), custom_call_target="tpu_custom_call" | custom-call | flops 231211008 | bytes 2752512 | tf_op jit(solution)/shard_map/convolution/pallas_call | solution.py:388
  70.7 3.2 %key_side_0.1 = (f32[224,768]{1,0:T(8,128)S(1)}, f32[224,768]{1,0:T(8,128)S(1)}) custom-call(s32[4,8,9]{2,1,0:T(8,128)S(1)} %copy-done.6, s32[8]{0:T(128)S(1)} %copy-done.7, bf16[2,224,768]{2,1,0:T(8,128)(2,1)S(1)} %pad_maximum_fusion.own.rest_0_, bf16[2,224,768]{2,1,0:T(8,128)(2,1)S(1)} %pair_up.4.own_ref.own, bf16[2,224,768]{2,1,0:T(8,128)(2,1)S(1)} %gate.1.near_ref.near, ...), custom_call_target="tpu_custom_call" | custom-call | flops 924844032 | bytes 2752512 | tf_op jit(solution)/shard_map/key_side_0/pallas_call | solution.py:388
  73.9 0.0 collective-permute-done.19.far_ref.rest_5_
  73.9 3.4 %key_side_1.1 = (f32[224,768]{1,0:T(8,128)S(1)}, f32[224,768]{1,0:T(8,128)S(1)}) custom-call(s32[4,8,9]{2,1,0:T(8,128)S(1)} %copy-done.6, s32[8]{0:T(128)S(1)} %copy-done.7, bf16[2,224,768]{2,1,0:T(8,128)(2,1)S(1)} %pad_maximum_fusion.own.rest_0_, bf16[2,224,768]{2,1,0:T(8,128)(2,1)S(1)} %collective-permute-done.3.rest_0_.own_ref.pair, ...), custom_call_target="tpu_custom_call" | custom-call | flops 924844032 | bytes 2752512 | tf_op jit(solution)/shard_map/key_side_1/pallas_call | solution.py:388
  77.3 0.8 %collective-permute-done.18.far_ref = bf16[496,768]{1,0:T(8,128)(2,1)S(1)} collective-permute-done((bf16[496,768]{1,0:T(8,128)(2,1)S(1)}, bf16[496,768]{1,0:T(8,128)(2,1)S(1)}, u32[]{:S(2)}, u32[]{:S(2)}) %collective-permute-start.18) | collective-permute-done | bytes 761888 | tf_op jit(solution)/shard_map/ppermute | solution.py:62
  78.2 4.2 %key_side_2.1 = (bf16[224,768]{1,0:T(8,128)(2,1)}, bf16[224,768]{1,0:T(8,128)(2,1)}) custom-call(s32[4,8,9]{2,1,0:T(8,128)S(1)} %copy-done.6, s32[8]{0:T(128)S(1)} %copy-done.7, bf16[2,224,768]{2,1,0:T(8,128)(2,1)S(1)} %pad_maximum_fusion.own.rest_0_, bf16[2,224,768]{2,1,0:T(8,128)(2,1)S(1)} %collective-permute-done.4.rest_1_.other.own_ref, ...), custom_call_target="tpu_custom_call" | custom-call | flops 924844032 | bytes 2752512 | tf_op jit(solution)/shard_map/key_side_2/pallas_call | solution.py:388
  (9 shorter events, 0.2 us)
Async XLA Ops:
  0.6 11.8 %copy-start.4 = (bf16[2,2,56,768]{3,2,1,0:T(8,128)(2,1)S(1)}, bf16[2,2,56,768]{3,2,1,0:T(8,128)(2,1)}, u32[]{:S(2)}) copy-start(bf16[2,2,56,768]{3,2,1,0:T(8,128)(2,1)} %param.9) | copy-start | bytes 1032196
  1.8 2.5 %collective-permute-start.2 = (bf16[2,224,768]{2,1,0:T(8,128)(2,1)S(1)}, bf16[2,224,768]{2,1,0:T(8,128)(2,1)S(1)}, u32[]{:S(2)}, u32[]{:S(2)}) collective-permute-start(bf16[2,224,768]{2,1,0:T(8,128)(2,1)S(1)} %pad_maximum_fusion.own.rest_0_), channel_id=1, source_target_pairs={{0,8},{8,0},{16,24},{24,16},{1,9},{9,1},{17,25},{25,17},{2,10},{10... | collective-permute-start | bytes 2064392 | tf_op jit(solution)/shard_map/ppermute | solution.py:58
  2.6 9.9 %collective-permute-start = (bf16[224,768]{1,0:T(8,128)(2,1)}, bf16[224,768]{1,0:T(8,128)(2,1)S(1)}, u32[]{:S(2)}, u32[]{:S(2)}) collective-permute-start(bf16[224,768]{1,0:T(8,128)(2,1)} %bitcast.22), channel_id=1, source_target_pairs={{0,1},{1,0},{2,3},{3,2},{4,5},{5,4},{6,7},{7,6},{8,9},{9,8},{10,11... | collective-permute-start | bytes 1032200 | tf_op jit(solution)/shard_map/ppermute | solution.py:46
  4.3 1.0 %copy-start = (bf16[2,2,56,768]{3,2,1,0:T(8,128)(2,1)S(1)}, bf16[2,2,56,768]{3,2,1,0:T(8,128)(2,1)}, u32[]{:S(2)}) copy-start(bf16[2,2,56,768]{3,2,1,0:T(8,128)(2,1)} %param.7) | copy-start | bytes 1032196
  5.3 1.0 %copy-start.2 = (bf16[2,2,56,768]{3,2,1,0:T(8,128)(2,1)S(1)}, bf16[2,2,56,768]{3,2,1,0:T(8,128)(2,1)}, u32[]{:S(2)}) copy-start(bf16[2,2,56,768]{3,2,1,0:T(8,128)(2,1)} %param.11) | copy-start | bytes 1032196
  6.4 19.9 %copy-start.1 = (bf16[2,2,56,768]{3,2,1,0:T(8,128)(2,1)S(1)}, bf16[2,2,56,768]{3,2,1,0:T(8,128)(2,1)}, u32[]{:S(2)}) copy-start(bf16[2,2,56,768]{3,2,1,0:T(8,128)(2,1)} %param.7) | copy-start | bytes 1032196
  6.4 19.9 %copy-start.3 = (bf16[2,2,56,768]{3,2,1,0:T(8,128)(2,1)S(1)}, bf16[2,2,56,768]{3,2,1,0:T(8,128)(2,1)}, u32[]{:S(2)}) copy-start(bf16[2,2,56,768]{3,2,1,0:T(8,128)(2,1)} %param.11) | copy-start | bytes 1032196
  6.4 15.0 %collective-permute-start.3 = (bf16[2,224,768]{2,1,0:T(8,128)(2,1)S(1)}, bf16[2,224,768]{2,1,0:T(8,128)(2,1)S(1)}, u32[]{:S(2)}, u32[]{:S(2)}) collective-permute-start(bf16[2,224,768]{2,1,0:T(8,128)(2,1)S(1)} %pair_up.4.own_ref.own), channel_id=1, source_target_pairs={{0,8},{8,0},{16,24},{24,16},{1,9},{9,1},{17,25},{25,17},{2,10},{10... | collective-permute-start | bytes 2064392 | tf_op jit(solution)/shard_map/ppermute | solution.py:58
  6.8 14.6 %collective-permute-start.4 = (bf16[2,224,768]{2,1,0:T(8,128)(2,1)S(1)}, bf16[2,224,768]{2,1,0:T(8,128)(2,1)S(1)}, u32[]{:S(2)}, u32[]{:S(2)}) collective-permute-start(bf16[2,224,768]{2,1,0:T(8,128)(2,1)S(1)} %pair_up.4.own_ref.own), channel_id=1, source_target_pairs={{0,0},{8,16},{16,8},{24,24},{1,1},{9,17},{17,9},{25,25},{2,2},{10,... | collective-permute-start | bytes 2064392 | tf_op jit(solution)/shard_map/ppermute | solution.py:62
  12.5 18.3 %copy-start.6 = (s32[4,8,9]{2,1,0:T(8,128)S(1)}, s32[4,8,9]{2,1,0:T(8,128)}, u32[]{:S(2)}) copy-start(s32[4,8,9]{2,1,0:T(8,128)} %mask_ref.11) | copy-start | bytes 3460
  12.5 18.3 %copy-start.7 = (s32[8]{0:T(128)S(1)}, s32[8]{0:T(128)}, u32[]{:S(2)}) copy-start(s32[8]{0:T(128)} %clip_ref.11) | copy-start | bytes 100
  12.5 8.9 %collective-permute-start.1 = (bf16[224,768]{1,0:T(8,128)(2,1)S(1)}, bf16[224,768]{1,0:T(8,128)(2,1)S(1)}, u32[]{:S(2)}, u32[]{:S(2)}) collective-permute-start(bf16[224,768]{1,0:T(8,128)(2,1)S(1)} %later.1), channel_id=1, source_target_pairs={{0,1},{1,0},{2,3},{3,2},{4,5},{5,4},{6,7},{7,6},{8,9},{9,8},{10,11... | collective-permute-start | bytes 1032200 | tf_op jit(solution)/shard_map/ppermute | solution.py:46
  13.8 12.4 %collective-permute-start.5 = (bf16[224,768]{1,0:T(8,128)(2,1)S(1)}, bf16[224,768]{1,0:T(8,128)(2,1)S(1)}, u32[]{:S(2)}, u32[]{:S(2)}) collective-permute-start(bf16[224,768]{1,0:T(8,128)(2,1)S(1)} %collective-permute-done.rest_0_.x_ref), channel_id=1, source_target_pairs={{0,2},{2,4},{3,1},{4,6},{5,3},{7,5},{8,10},{10,12},{11,9},{12,14},... | collective-permute-start | bytes 1032200 | tf_op jit(solution)/shard_map/ppermute | solution.py:50
  17.0 13.8 %collective-permute-start.7 = (bf16[2,224,768]{2,1,0:T(8,128)(2,1)S(1)}, bf16[2,224,768]{2,1,0:T(8,128)(2,1)S(1)}, u32[]{:S(2)}, u32[]{:S(2)}) collective-permute-start(bf16[2,224,768]{2,1,0:T(8,128)(2,1)S(1)} %pad_maximum_fusion.own.rest_0_), channel_id=1, source_target_pairs={{0,0},{8,16},{16,8},{24,24},{1,1},{9,17},{17,9},{25,25},{2,2},{10,... | collective-permute-start | bytes 2064392 | tf_op jit(solution)/shard_map/ppermute | solution.py:62
  21.5 11.9 %collective-permute-start.8 = (bf16[2,224,768]{2,1,0:T(8,128)(2,1)S(1)}, bf16[2,224,768]{2,1,0:T(8,128)(2,1)S(1)}, u32[]{:S(2)}, u32[]{:S(2)}) collective-permute-start(bf16[2,224,768]{2,1,0:T(8,128)(2,1)S(1)} %pair_up.5.own.near.rest_1_), channel_id=1, source_target_pairs={{0,8},{8,0},{16,24},{24,16},{1,9},{9,1},{17,25},{25,17},{2,10},{10... | collective-permute-start | bytes 2064392 | tf_op jit(solution)/shard_map/ppermute | solution.py:58
  23.1 14.5 %collective-permute-start.9 = (bf16[2,224,768]{2,1,0:T(8,128)(2,1)S(1)}, bf16[2,224,768]{2,1,0:T(8,128)(2,1)S(1)}, u32[]{:S(2)}, u32[]{:S(2)}) collective-permute-start(bf16[2,224,768]{2,1,0:T(8,128)(2,1)S(1)} %pair_up.5.own.near.rest_1_), channel_id=1, source_target_pairs={{0,0},{8,16},{16,8},{24,24},{1,1},{9,17},{17,9},{25,25},{2,2},{10,... | collective-permute-start | bytes 2064392 | tf_op jit(solution)/shard_map/ppermute | solution.py:62
  26.3 17.5 %collective-permute-start.12 = (bf16[2,224,768]{2,1,0:T(8,128)(2,1)S(1)}, bf16[2,224,768]{2,1,0:T(8,128)(2,1)S(1)}, u32[]{:S(2)}, u32[]{:S(2)}) collective-permute-start(bf16[2,224,768]{2,1,0:T(8,128)(2,1)S(1)} %pair_up.7), channel_id=1, source_target_pairs={{0,1},{1,0},{2,3},{3,2},{4,5},{5,4},{6,7},{7,6},{8,9},{9,8},{10,11... | collective-permute-start | bytes 2064392 | tf_op jit(solution)/shard_map/ppermute | solution.py:46
  27.6 12.7 %collective-permute-start.6 = (bf16[224,768]{1,0:T(8,128)(2,1)S(1)}, bf16[224,768]{1,0:T(8,128)(2,1)S(1)}, u32[]{:S(2)}, u32[]{:S(2)}) collective-permute-start(bf16[224,768]{1,0:T(8,128)(2,1)S(1)} %collective-permute-done.1.y_ref.rest_0_), channel_id=1, source_target_pairs={{0,2},{2,4},{3,1},{4,6},{5,3},{7,5},{8,10},{10,12},{11,9},{12,14},... | collective-permute-start | bytes 1032200 | tf_op jit(solution)/shard_map/ppermute | solution.py:50
  40.3 9.0 %copy-start.5 = (bf16[27,768]{1,0:T(8,128)(2,1)S(1)}, bf16[27,768]{1,0:T(8,128)(2,1)}, u32[]{:S(2)}) copy-start(bf16[27,768]{1,0:T(8,128)(2,1)} %rest_2_.1) | copy-start | bytes 124420
  40.4 10.8 %collective-permute-start.10 = (bf16[2,224,768]{2,1,0:T(8,128)(2,1)S(1)}, bf16[2,224,768]{2,1,0:T(8,128)(2,1)S(1)}, u32[]{:S(2)}, u32[]{:S(2)}) collective-permute-start(bf16[2,224,768]{2,1,0:T(8,128)(2,1)S(1)} %pair_up.6.own.rest_2_), channel_id=1, source_target_pairs={{0,8},{8,0},{16,24},{24,16},{1,9},{9,1},{17,25},{25,17},{2,10},{10... | collective-permute-start | bytes 2064392 | tf_op jit(solution)/shard_map/ppermute | solution.py:58
  40.5 12.6 %collective-permute-start.11 = (bf16[2,224,768]{2,1,0:T(8,128)(2,1)S(1)}, bf16[2,224,768]{2,1,0:T(8,128)(2,1)S(1)}, u32[]{:S(2)}, u32[]{:S(2)}) collective-permute-start(bf16[2,224,768]{2,1,0:T(8,128)(2,1)S(1)} %pair_up.6.own.rest_2_), channel_id=1, source_target_pairs={{0,0},{8,16},{16,8},{24,24},{1,1},{9,17},{17,9},{25,25},{2,2},{10,... | collective-permute-start | bytes 2064392 | tf_op jit(solution)/shard_map/ppermute | solution.py:62
  43.8 20.8 %collective-permute-start.13 = (bf16[2,224,768]{2,1,0:T(8,128)(2,1)S(1)}, bf16[2,224,768]{2,1,0:T(8,128)(2,1)S(1)}, u32[]{:S(2)}, u32[]{:S(2)}) collective-permute-start(bf16[2,224,768]{2,1,0:T(8,128)(2,1)S(1)} %gate.1.near_ref.near), channel_id=1, source_target_pairs={{0,0},{8,16},{16,8},{24,24},{1,1},{9,17},{17,9},{25,25},{2,2},{10,... | collective-permute-start | bytes 2064392 | tf_op jit(solution)/shard_map/ppermute | solution.py:62
  46.1 18.6 %collective-permute-start.14 = (bf16[2,224,768]{2,1,0:T(8,128)(2,1)S(1)}, bf16[2,224,768]{2,1,0:T(8,128)(2,1)S(1)}, u32[]{:S(2)}, u32[]{:S(2)}) collective-permute-start(bf16[2,224,768]{2,1,0:T(8,128)(2,1)S(1)} %gate.1.near_ref.near), channel_id=1, source_target_pairs={{0,2},{2,4},{3,1},{4,6},{5,3},{7,5},{8,10},{10,12},{11,9},{12,14},... | collective-permute-start | bytes 2064392 | tf_op jit(solution)/shard_map/ppermute | solution.py:50
  49.3 15.4 %collective-permute-start.17 = (bf16[2,224,768]{2,1,0:T(8,128)(2,1)S(1)}, bf16[2,224,768]{2,1,0:T(8,128)(2,1)S(1)}, u32[]{:S(2)}, u32[]{:S(2)}) collective-permute-start(bf16[2,224,768]{2,1,0:T(8,128)(2,1)S(1)} %gate.1.near_ref.near), channel_id=1, source_target_pairs={{0,8},{8,0},{16,24},{24,16},{1,9},{9,1},{17,25},{25,17},{2,10},{10... | collective-permute-start | bytes 2064392 | tf_op jit(solution)/shard_map/ppermute | solution.py:58
  56.2 8.5 %collective-permute-start.15 = (f32[16,224]{1,0:T(8,128)S(1)}, f32[16,224]{1,0:T(8,128)S(1)}, u32[]{:S(2)}, u32[]{:S(2)}) collective-permute-start(f32[16,224]{1,0:T(8,128)S(1)} %get-tuple-element.44.own_ref.rest_0_), channel_id=1, source_target_pairs={{0,1},{1,0},{2,3},{3,2},{4,5},{5,4},{6,7},{7,6},{8,9},{9,8},{10,11... | collective-permute-start | bytes 43016 | tf_op jit(solution)/shard_map/ppermute | solution.py:46
  56.2 8.5 %collective-permute-start.16 = (f32[16,224]{1,0:T(8,128)S(1)}, f32[16,224]{1,0:T(8,128)S(1)}, u32[]{:S(2)}, u32[]{:S(2)}) collective-permute-start(f32[16,224]{1,0:T(8,128)S(1)} %get-tuple-element.44.own_ref.rest_0_), channel_id=1, source_target_pairs={{0,0},{1,2},{2,1},{3,4},{4,3},{5,6},{6,5},{7,7},{8,8},{9,10},{10,9... | collective-permute-start | bytes 43016 | tf_op jit(solution)/shard_map/ppermute | solution.py:54
  64.8 9.2 %collective-permute-start.19 = (bf16[496,768]{1,0:T(8,128)(2,1)S(1)}, bf16[496,768]{1,0:T(8,128)(2,1)S(1)}, u32[]{:S(2)}, u32[]{:S(2)}) collective-permute-start(bf16[496,768]{1,0:T(8,128)(2,1)S(1)} %pack.1), channel_id=1, source_target_pairs={{0,8},{8,0},{16,24},{24,16},{1,9},{9,1},{17,25},{25,17},{2,10},{10... | collective-permute-start | bytes 2285576 | tf_op jit(solution)/shard_map/ppermute | solution.py:58
  64.8 13.3 %collective-permute-start.18 = (bf16[496,768]{1,0:T(8,128)(2,1)S(1)}, bf16[496,768]{1,0:T(8,128)(2,1)S(1)}, u32[]{:S(2)}, u32[]{:S(2)}) collective-permute-start(bf16[496,768]{1,0:T(8,128)(2,1)S(1)} %pack.1), channel_id=1, source_target_pairs={{0,0},{8,16},{16,8},{24,24},{1,1},{9,17},{17,9},{25,25},{2,2},{10,... | collective-permute-start | bytes 2285576 | tf_op jit(solution)/shard_map/ppermute | solution.py:62

commit v11 on v10

--- a/solution.py
+++ b/solution.py
@@ -251,14 +251,13 @@
         out_ref[:, cols] = conv_inner(tiles, weight_ref[:, cols].astype(jnp.float32), flipped, place_now, width)
         return 0
 
-    lax.fori_loop(0, channels // HEAD_DIM, body, 0)
-
-
-def query_kernel(counts, width, grad_ref, weight_ref, *rest):
+    lax.fori_loop(0, channels // HEAD_DIM, body, 0, unroll=3)
+
+
+def query_kernel(grad_ref, *rest):
     slots, exps, factors = rest[:9], rest[9:12], rest[12:15]
-    att_ref, delta_ref, conv_ref, out_ref, dq_ref, done_ref = rest[15:]
+    delta_ref, dq_ref, done_ref = rest[15:]
     done_ref[...] = jnp.zeros_like(done_ref)
-    _, _, place_now = place(counts)
     rows, channels = grad_ref.shape
     heads = channels // HEAD_DIM
     scale = HEAD_DIM**-0.5
@@ -279,12 +278,22 @@
                 part = dot(ds.astype(jnp.bfloat16), keys) * (factors[column][:, cols] * scale)
                 dq = part if dq is None else dq + part
             dq_ref[:, cols] = dq.astype(jnp.bfloat16)
-            tiles = [slots[i][1, :, cols] for i in (2, 5, 8)]
-            conv = conv_ref[:, cols] + conv_far(tiles, weight_ref[:, cols].astype(jnp.float32), False, place_now, width)
-            out_ref[:, cols] = (att_ref[:, cols] + conv).astype(jnp.bfloat16)
         return 0
 
     lax.fori_loop(0, heads // UNROLL, body, 0)
+
+
+def out_kernel(counts, width, att_ref, conv_ref, own, pair, other, weight_ref, _, out_ref):
+    _, _, place_now = place(counts)
+
+    def body(head, _):
+        cols = head_columns(head)
+        tiles = [ref[1, :, cols] for ref in (own, pair, other)]
+        conv = conv_ref[:, cols] + conv_far(tiles, weight_ref[:, cols].astype(jnp.float32), False, place_now, width)
+        out_ref[:, cols] = (att_ref[:, cols] + conv).astype(jnp.bfloat16)
+        return 0
+
+    lax.fori_loop(0, out_ref.shape[1] // HEAD_DIM, body, 0, unroll=3)
 
 
 def pack_kernel(rows, qg_ref, own_ref, near_ref, far_ref, *rest):
@@ -474,14 +483,14 @@
         tile_mask, clip_lengths, query, far_kv, far_kv_a, far_kv_b, grad, *own_parts, *near_parts, conv_value,
     )
     near_stat, far_stat = ha_near(stat), ha_far(stat)
-    layer_out, query_grad, done = call(
-        functools.partial(query_kernel, counts, width),
+    query_grad, done = call(
+        query_kernel,
         "query_side",
-        [half, half, jax.ShapeDtypeStruct((8, HEAD_DIM), jnp.float32)],
+        [half, jax.ShapeDtypeStruct((8, HEAD_DIM), jnp.float32)],
         [],
         cost(heads, rows, 2, 3),
-        grad, conv_weight, kv, near_kv, far_kv, kv_a, near_kv_a, far_kv_a, kv_b, near_kv_b, far_kv_b,
-        exp_own, exp_near, exp_far, fac_own, fac_near, fac_far, attention, delta, conv_value,
+        grad, kv, near_kv, far_kv, kv_a, near_kv_a, far_kv_a, kv_b, near_kv_b, far_kv_b,
+        exp_own, exp_near, exp_far, fac_own, fac_near, fac_far, delta,
     )
     message = pl.pallas_call(
         functools.partial(pack_kernel, rows),
@@ -492,6 +501,10 @@
         name="pack",
     )(far_qg, stat, near_stat, far_stat, done, near_qg_a, near_qg_b)
     message_a, message_b = ta_pair(message), ta_other(message)
+    layer_out = call(
+        functools.partial(out_kernel, counts, width), "layer_out", [half], [], cost(heads, rows, 1, 1),
+        attention, conv_value, far_kv, far_kv_a, far_kv_b, conv_weight, message_a,
+    )[0]
 
     conv_grad = convolution(True, qg, near_qg, qg_a, near_qg_a, qg_b, near_qg_b)
     scratch = [pltpu.VMEM((STAT_ROWS, 3 * rows), jnp.float32)]

time: 83 us -> 82.5 us (level)
  waiting for transfers between devices: 9.99 us -> 8.88 us
    ppermute x6, waiting for transfers between devices: 6.97 us -> 5.86 us  [ta_other(): return lax.ppermute(x, 'ta', other_pairs(lax.axis_size('ta')))]
    pallas_call x9 -> x10, Pallas kernels: 28 us -> 28.7 us  [call(): pl.pallas_call(kernel, in_specs=[smem] * scalars + [vmem] * (len(args) -...]
  transfers between devices with their start and end apart: 20 -> 20, of which waited for: 5 -> 4; matrix products, arithmetic and copies ran while one was open for 0% -> 0% of each run, Pallas kernels for 29% -> 30%
where the time goes in v11:
time: 82.5 us; the launch traced here: 82.1 us
  starting transfers between devices  40 us (48%)
  Pallas kernels  28.9 us (35%)
  waiting for transfers between devices  8.88 us (11%)
  local copies, waits for them, and re-layouts  1.99 us (2%)
  other arithmetic  1.19 us (1%)
  between operations  1.03 us (1%)
    pallas_call x10, Pallas kernels, call(): pl.pallas_call(kernel, in_specs=[smem] * scalars + [vmem] * (len(args) -...  28.7 us
    ppermute x6, starting transfers between devices, ta_other(): return lax.ppermute(x, 'ta', other_pairs(lax.axis_size('ta')))  19.8 us
    ppermute x3, starting transfers between devices, ha_relay(): return lax.ppermute(near, 'ha', relay_pairs(lax.axis_size('ha')))  9.59 us
    ppermute x6, waiting for transfers between devices, ta_other(): return lax.ppermute(x, 'ta', other_pairs(lax.axis_size('ta')))  5.86 us
    ppermute x4, starting transfers between devices, ha_near(): return lax.ppermute(x, 'ha', flip_pairs(lax.axis_size('ha')))  3.81 us
    ppermute x6, starting transfers between devices, ta_pair(): return lax.ppermute(x, 'ta', flip_pairs(lax.axis_size('ta')))  3.66 us
    ppermute x1, starting transfers between devices, ha_far(): return lax.ppermute(x, 'ha', other_pairs(lax.axis_size('ha')))  3.14 us
    ppermute x4, waiting for transfers between devices, ha_near(): return lax.ppermute(x, 'ha', flip_pairs(lax.axis_size('ha')))  2.45 us
  transfers between devices with their start and end apart: 20, of which 4 were waited for; matrix products, arithmetic and copies ran while one was open for 0% of the time, Pallas kernels for 30%

profile of v11, /device:TPU:9, one launch (start us, length us, event | category | flops | bytes accessed | tf_op | source)
XLA Modules:
  0.0 82.1 jit_solution(6369758964778574907)
XLA Ops:
  0.6 0.0 copy-start.4
  0.6 1.2 %pad_maximum_fusion.own.rest_0_ = bf16[2,224,768]{2,1,0:T(8,128)(2,1)S(1)} fusion(bf16[1,224,768]{2,1,0:T(8,128)(2,1)} %bitcast.19, bf16[1,224,768]{2,1,0:T(8,128)(2,1)} %bitcast.21), kind=kLoop, calls=%fused_computation | loop fusion | flops 344064 | bytes 1376256 | tf_op jit(solution)/shard_map/stack | solution.py:456
  1.8 0.7 collective-permute-start.4
  2.6 1.2 %collective-permute-start = (bf16[224,768]{1,0:T(8,128)(2,1)}, bf16[224,768]{1,0:T(8,128)(2,1)S(1)}, u32[]{:S(2)}, u32[]{:S(2)}) collective-permute-start(bf16[224,768]{1,0:T(8,128)(2,1)} %bitcast.22), channel_id=1, source_target_pairs={{0,1},{1,0},{2,3},{3,2},{4,5},{5,4},{6,7},{7,6},{8,9},{9,8},{10,11... | collective-permute-start | bytes 1032200 | tf_op jit(solution)/shard_map/ppermute | solution.py:46
  3.8 0.5 collective-permute-done.4.pair.rest_0_.rest_3_
  4.4 1.0 %copy-done = bf16[2,2,56,768]{3,2,1,0:T(8,128)(2,1)S(1)} copy-done((bf16[2,2,56,768]{3,2,1,0:T(8,128)(2,1)S(1)}, bf16[2,2,56,768]{3,2,1,0:T(8,128)(2,1)}, u32[]{:S(2)}) %copy-start) | copy-done | bytes 344088
  5.3 1.0 %copy-done.2 = bf16[2,2,56,768]{3,2,1,0:T(8,128)(2,1)S(1)} copy-done((bf16[2,2,56,768]{3,2,1,0:T(8,128)(2,1)S(1)}, bf16[2,2,56,768]{3,2,1,0:T(8,128)(2,1)}, u32[]{:S(2)}) %copy-start.2) | copy-done | bytes 344088
  6.4 0.0 copy-start.1
  6.4 0.0 copy-start.3
  6.4 0.4 collective-permute-start.6
  6.8 3.2 %collective-permute-start.7 = (bf16[2,224,768]{2,1,0:T(8,128)(2,1)S(1)}, bf16[2,224,768]{2,1,0:T(8,128)(2,1)S(1)}, u32[]{:S(2)}, u32[]{:S(2)}) collective-permute-start(bf16[2,224,768]{2,1,0:T(8,128)(2,1)S(1)} %pair_up.4.own_ref.own), channel_id=1, source_target_pairs={{0,0},{8,16},{16,8},{24,24},{1,1},{9,17},{17,9},{25,25},{2,2},{10,... | collective-permute-start | bytes 2064392 | tf_op jit(solution)/shard_map/ppermute | solution.py:62
  10.0 2.4 %collective-permute-done.rest_0_.x_ref = bf16[224,768]{1,0:T(8,128)(2,1)S(1)} collective-permute-done((bf16[224,768]{1,0:T(8,128)(2,1)}, bf16[224,768]{1,0:T(8,128)(2,1)S(1)}, u32[]{:S(2)}, u32[]{:S(2)}) %collective-permute-start) | collective-permute-done | bytes 344096 | tf_op jit(solution)/shard_map/ppermute | solution.py:46
  12.4 0.0 copy-done.4
  12.5 0.0 copy-start.6
  12.5 0.0 copy-start.7
  12.5 1.3 %collective-permute-start.2 = (bf16[224,768]{1,0:T(8,128)(2,1)S(1)}, bf16[224,768]{1,0:T(8,128)(2,1)S(1)}, u32[]{:S(2)}, u32[]{:S(2)}) collective-permute-start(bf16[224,768]{1,0:T(8,128)(2,1)S(1)} %later.1), channel_id=1, source_target_pairs={{0,1},{1,0},{2,3},{3,2},{4,5},{5,4},{6,7},{7,6},{8,9},{9,8},{10,11... | collective-permute-start | bytes 1032200 | tf_op jit(solution)/shard_map/ppermute | solution.py:46
  13.8 3.2 %collective-permute-start.1 = (bf16[224,768]{1,0:T(8,128)(2,1)S(1)}, bf16[224,768]{1,0:T(8,128)(2,1)S(1)}, u32[]{:S(2)}, u32[]{:S(2)}) collective-permute-start(bf16[224,768]{1,0:T(8,128)(2,1)S(1)} %collective-permute-done.rest_0_.x_ref), channel_id=1, source_target_pairs={{0,2},{2,4},{3,1},{4,6},{5,3},{7,5},{8,10},{10,12},{11,9},{12,14},... | collective-permute-start | bytes 1032200 | tf_op jit(solution)/shard_map/ppermute | solution.py:50
  17.0 4.4 %collective-permute-start.5 = (bf16[2,224,768]{2,1,0:T(8,128)(2,1)S(1)}, bf16[2,224,768]{2,1,0:T(8,128)(2,1)S(1)}, u32[]{:S(2)}, u32[]{:S(2)}) collective-permute-start(bf16[2,224,768]{2,1,0:T(8,128)(2,1)S(1)} %pad_maximum_fusion.own.rest_0_), channel_id=1, source_target_pairs={{0,0},{8,16},{16,8},{24,24},{1,1},{9,17},{17,9},{25,25},{2,2},{10,... | collective-permute-start | bytes 2064392 | tf_op jit(solution)/shard_map/ppermute | solution.py:62
  21.4 0.0 collective-permute-done.2.y_ref.rest_0_
  21.4 0.0 collective-permute-done.6.rest_0_.own_ref.pair
  21.4 0.0 collective-permute-done.7.rest_1_.other.own_ref
  21.5 1.6 %collective-permute-start.8 = (bf16[2,224,768]{2,1,0:T(8,128)(2,1)S(1)}, bf16[2,224,768]{2,1,0:T(8,128)(2,1)S(1)}, u32[]{:S(2)}, u32[]{:S(2)}) collective-permute-start(bf16[2,224,768]{2,1,0:T(8,128)(2,1)S(1)} %pair_up.5.own.near.rest_1_), channel_id=1, source_target_pairs={{0,8},{8,0},{16,24},{24,16},{1,9},{9,1},{17,25},{25,17},{2,10},{10... | collective-permute-start | bytes 2064392 | tf_op jit(solution)/shard_map/ppermute | solution.py:58
  23.1 3.0 %collective-permute-start.9 = (bf16[2,224,768]{2,1,0:T(8,128)(2,1)S(1)}, bf16[2,224,768]{2,1,0:T(8,128)(2,1)S(1)}, u32[]{:S(2)}, u32[]{:S(2)}) collective-permute-start(bf16[2,224,768]{2,1,0:T(8,128)(2,1)S(1)} %pair_up.5.own.near.rest_1_), channel_id=1, source_target_pairs={{0,0},{8,16},{16,8},{24,24},{1,1},{9,17},{17,9},{25,25},{2,2},{10,... | collective-permute-start | bytes 2064392 | tf_op jit(solution)/shard_map/ppermute | solution.py:62
  26.2 0.0 collective-permute-done.1.x_ref.rest_1_
  26.2 0.0 copy-done.1
  26.2 0.0 copy-done.3
  26.3 1.3 %collective-permute-start.12 = (bf16[2,224,768]{2,1,0:T(8,128)(2,1)S(1)}, bf16[2,224,768]{2,1,0:T(8,128)(2,1)S(1)}, u32[]{:S(2)}, u32[]{:S(2)}) collective-permute-start(bf16[2,224,768]{2,1,0:T(8,128)(2,1)S(1)} %pair_up.7), channel_id=1, source_target_pairs={{0,1},{1,0},{2,3},{3,2},{4,5},{5,4},{6,7},{7,6},{8,9},{9,8},{10,11... | collective-permute-start | bytes 2064392 | tf_op jit(solution)/shard_map/ppermute | solution.py:46
  27.6 3.2 %collective-permute-start.3 = (bf16[224,768]{1,0:T(8,128)(2,1)S(1)}, bf16[224,768]{1,0:T(8,128)(2,1)S(1)}, u32[]{:S(2)}, u32[]{:S(2)}) collective-permute-start(bf16[224,768]{1,0:T(8,128)(2,1)S(1)} %collective-permute-done.2.y_ref.rest_0_), channel_id=1, source_target_pairs={{0,2},{2,4},{3,1},{4,6},{5,3},{7,5},{8,10},{10,12},{11,9},{12,14},... | collective-permute-start | bytes 1032200 | tf_op jit(solution)/shard_map/ppermute | solution.py:50
  30.8 0.0 collective-permute-done.5.other.rest_6_
  30.8 0.0 copy-done.6
  30.8 2.6 %scores_0.1 = (bf16[6,224,672]{2,1,0:T(8,128)(2,1)S(1)}, f32[224,768]{1,0:T(8,128)S(1)}, f32[224,768]{1,0:T(8,128)S(1)}, f32[224,768]{1,0:T(8,128)S(1)}) custom-call(s32[4,8,9]{2,1,0:T(8,128)S(1)} %copy-done.6, s32[8]{0:T(128)S(1)} %copy-done.7, bf16[224,768]{1,0:T(8,128)(2,1)S(1)} %bitcast.12, bf16[2,224,768]{2,1,0:T(8,128)(2,1)S(1)} %pad_maximum_fusion.own.rest_0_, ...), custom_call_target="tpu_custom_call" | custom-call | flops 462422016 | bytes 2752512 | tf_op jit(solution)/shard_map/scores_0/pallas_call | solution.py:397
  33.4 0.0 collective-permute-done.8.pair.near_pair.rest_4_
  33.4 4.3 %collective-permute-done.9.other.near_other.rest_7_ = bf16[2,224,768]{2,1,0:T(8,128)(2,1)S(1)} collective-permute-done((bf16[2,224,768]{2,1,0:T(8,128)(2,1)S(1)}, bf16[2,224,768]{2,1,0:T(8,128)(2,1)S(1)}, u32[]{:S(2)}, u32[]{:S(2)}) %collective-permute-start.9) | collective-permute-done | bytes 688160 | tf_op jit(solution)/shard_map/ppermute | solution.py:62
  37.7 2.6 %scores_1.1 = (bf16[6,224,672]{2,1,0:T(8,128)(2,1)S(1)}, f32[224,768]{1,0:T(8,128)S(1)}, f32[224,768]{1,0:T(8,128)S(1)}, f32[224,768]{1,0:T(8,128)S(1)}) custom-call(s32[4,8,9]{2,1,0:T(8,128)S(1)} %copy-done.6, s32[8]{0:T(128)S(1)} %copy-done.7, bf16[224,768]{1,0:T(8,128)(2,1)S(1)} %bitcast.13, bf16[2,224,768]{2,1,0:T(8,128)(2,1)S(1)} %pair_up.5.own.near.rest_1_, ...), custom_call_target="tpu_custom_call" | custom-call | flops 462422016 | bytes 2752512 | tf_op jit(solution)/shard_map/scores_1/pallas_call | solution.py:397
  40.3 0.0 collective-permute-done.3.y_ref
  40.3 0.0 copy-start.5
  40.4 0.1 collective-permute-start.10
  40.5 3.4 %collective-permute-start.11 = (bf16[2,224,768]{2,1,0:T(8,128)(2,1)S(1)}, bf16[2,224,768]{2,1,0:T(8,128)(2,1)S(1)}, u32[]{:S(2)}, u32[]{:S(2)}) collective-permute-start(bf16[2,224,768]{2,1,0:T(8,128)(2,1)S(1)} %pair_up.6.own.rest_2_), channel_id=1, source_target_pairs={{0,0},{8,16},{16,8},{24,24},{1,1},{9,17},{17,9},{25,25},{2,2},{10,... | collective-permute-start | bytes 2064392 | tf_op jit(solution)/shard_map/ppermute | solution.py:62
  43.8 0.0 collective-permute-done.12.refs_0_
  43.8 3.2 %collective-permute-start.13 = (bf16[2,224,768]{2,1,0:T(8,128)(2,1)S(1)}, bf16[2,224,768]{2,1,0:T(8,128)(2,1)S(1)}, u32[]{:S(2)}, u32[]{:S(2)}) collective-permute-start(bf16[2,224,768]{2,1,0:T(8,128)(2,1)S(1)} %gate.1.near_ref.near), channel_id=1, source_target_pairs={{0,2},{2,4},{3,1},{4,6},{5,3},{7,5},{8,10},{10,12},{11,9},{12,14},... | collective-permute-start | bytes 2064392 | tf_op jit(solution)/shard_map/ppermute | solution.py:50
  47.1 0.7 collective-permute-start.16
  47.8 1.9 %collective-permute-start.17 = (bf16[2,224,768]{2,1,0:T(8,128)(2,1)S(1)}, bf16[2,224,768]{2,1,0:T(8,128)(2,1)S(1)}, u32[]{:S(2)}, u32[]{:S(2)}) collective-permute-start(bf16[2,224,768]{2,1,0:T(8,128)(2,1)S(1)} %gate.1.near_ref.near), channel_id=1, source_target_pairs={{0,0},{8,16},{16,8},{24,24},{1,1},{9,17},{17,9},{25,25},{2,2},{10,... | collective-permute-start | bytes 2064392 | tf_op jit(solution)/shard_map/ppermute | solution.py:62
  49.7 1.7 %convolution.2.rest_7_.conv_ref = f32[224,768]{1,0:T(8,128)S(1)} custom-call(bf16[2,224,768]{2,1,0:T(8,128)(2,1)S(1)} %pad_maximum_fusion.own.rest_0_, bf16[2,224,768]{2,1,0:T(8,128)(2,1)S(1)} %pair_up.5.own.near.rest_1_, bf16[2,224,768]{2,1,0:T(8,128)(2,1)S(1)} %collective-permute-done.4.pair.rest_0_.rest_3_, ...), custom_call_target="tpu_custom_call" | custom-call | flops 231211008 | bytes 2752512 | tf_op jit(solution)/shard_map/convolution/pallas_call | solution.py:397
  51.4 0.0 collective-permute-done.10.pair.rest_5_
  51.4 1.6 %collective-permute-done.11.other.rest_8_ = bf16[2,224,768]{2,1,0:T(8,128)(2,1)S(1)} collective-permute-done((bf16[2,224,768]{2,1,0:T(8,128)(2,1)S(1)}, bf16[2,224,768]{2,1,0:T(8,128)(2,1)S(1)}, u32[]{:S(2)}, u32[]{:S(2)}) %collective-permute-start.11) | collective-permute-done | bytes 688160 | tf_op jit(solution)/shard_map/ppermute | solution.py:62
  53.0 3.1 %scores_2.1 = (bf16[6,224,672]{2,1,0:T(8,128)(2,1)S(1)}, f32[224,768]{1,0:T(8,128)S(1)}, f32[224,768]{1,0:T(8,128)S(1)}, f32[224,768]{1,0:T(8,128)S(1)}, f32[224...) custom-call(s32[4,8,9]{2,1,0:T(8,128)S(1)} %copy-done.6, s32[8]{0:T(128)S(1)} %copy-done.7, ...), custom_call_target="tpu_custom_call" | custom-call | flops 462422016 | bytes 2752512 | tf_op jit(solution)/shard_map/scores_2/pallas_call | solution.py:397
  56.2 0.0 collective-permute-start.14
  56.2 3.1 %collective-permute-start.15 = (f32[16,224]{1,0:T(8,128)S(1)}, f32[16,224]{1,0:T(8,128)S(1)}, u32[]{:S(2)}, u32[]{:S(2)}) collective-permute-start(f32[16,224]{1,0:T(8,128)S(1)} %get-tuple-element.34.own_ref.rest_0_), channel_id=1, source_target_pairs={{0,0},{1,2},{2,1},{3,4},{4,3},{5,6},{6,5},{7,7},{8,8},{9,10},{10,9... | collective-permute-start | bytes 43016 | tf_op jit(solution)/shard_map/ppermute | solution.py:54
  59.4 4.8 %query_side.1 = (bf16[224,768]{1,0:T(8,128)(2,1)}, f32[8,128]{1,0:T(8,128)S(1)}) custom-call(bf16[224,768]{1,0:T(8,128)(2,1)S(1)} %bitcast.18, bf16[2,224,768]{2,1,0:T(8,128)(2,1)S(1)} %pad_maximum_fusion.own.rest_0_, bf16[2,224,768]{2,1,0:T(8,128)(2,1)S(1)} %pair_up.5.own.near.rest_1_, bf16[2,224,768]{2,1,0:T(8,128)(2,1)S(1)} %pair_up.6.own.rest_2_, ...), custom_call_target="tpu_custom_call" | custom-call | flops 1387266048 | bytes 8257536 | tf_op jit(solution)/shard_map/query_side/pallas_call | solution.py:397
  64.1 0.0 collective-permute-done.13.qg_ref.far_ref.rest_4_
  64.1 0.0 collective-permute-done.16.rest_1_.near_ref.near_pair
  64.1 0.0 collective-permute-done.17.rest_2_.near_other.near_ref
  64.1 0.0 collective-permute-done.14.near_ref.rest_1_
  64.1 0.0 collective-permute-done.15.far_ref.rest_2_
  64.2 0.1 pack.1
  64.2 0.1 collective-permute-start.18
  64.3 3.9 %collective-permute-start.19 = (bf16[496,768]{1,0:T(8,128)(2,1)S(1)}, bf16[496,768]{1,0:T(8,128)(2,1)S(1)}, u32[]{:S(2)}, u32[]{:S(2)}) collective-permute-start(bf16[496,768]{1,0:T(8,128)(2,1)S(1)} %pack.1), channel_id=1, source_target_pairs={{0,0},{8,16},{16,8},{24,24},{1,1},{9,17},{17,9},{25,25},{2,2},{10,... | collective-permute-start | bytes 2285576 | tf_op jit(solution)/shard_map/ppermute | solution.py:62
  68.2 1.7 %convolution.3.rest_3_ = f32[224,768]{1,0:T(8,128)S(1)} custom-call(bf16[2,224,768]{2,1,0:T(8,128)(2,1)S(1)} %pair_up.4.own_ref.own, bf16[2,224,768]{2,1,0:T(8,128)(2,1)S(1)} %gate.1.near_ref.near, bf16[2,224,768]{2,1,0:T(8,128)(2,1)S(1)} %collective-permute-done.6.rest_0_.own_ref.pair, ...), custom_call_target="tpu_custom_call" | custom-call | flops 231211008 | bytes 2752512 | tf_op jit(solution)/shard_map/convolution/pallas_call | solution.py:397
  69.9 3.2 %key_side_0.1 = (f32[224,768]{1,0:T(8,128)S(1)}, f32[224,768]{1,0:T(8,128)S(1)}) custom-call(s32[4,8,9]{2,1,0:T(8,128)S(1)} %copy-done.6, s32[8]{0:T(128)S(1)} %copy-done.7, bf16[2,224,768]{2,1,0:T(8,128)(2,1)S(1)} %pad_maximum_fusion.own.rest_0_, bf16[2,224,768]{2,1,0:T(8,128)(2,1)S(1)} %pair_up.4.own_ref.own, bf16[2,224,768]{2,1,0:T(8,128)(2,1)S(1)} %gate.1.near_ref.near, ...), custom_call_target="tpu_custom_call" | custom-call | flops 924844032 | bytes 2752512 | tf_op jit(solution)/shard_map/key_side_0/pallas_call | solution.py:397
  73.1 0.0 collective-permute-done.18._.far_ref.rest_5_
  73.2 1.3 %layer_out.1 = bf16[224,768]{1,0:T(8,128)(2,1)} custom-call(f32[224,768]{1,0:T(8,128)S(1)} %get-tuple-element.33.att_ref, f32[224,768]{1,0:T(8,128)S(1)} %convolution.2.rest_7_.conv_ref, bf16[2,224,768]{2,1,0:T(8,128)(2,1)S(1)} %pair_up.6.own.rest_2_, bf16[2,224,768]{2,1,0:T(8,128)(2,1)S(1)} %collective-permute-done.10.pair.rest_5_, ...), custom_call_target="tpu_custom_call" | custom-call | flops 231211008 | bytes 2752512 | tf_op jit(solution)/shard_map/layer_out/pallas_call | solution.py:397
  74.5 3.3 %key_side_1.1 = (f32[224,768]{1,0:T(8,128)S(1)}, f32[224,768]{1,0:T(8,128)S(1)}) custom-call(s32[4,8,9]{2,1,0:T(8,128)S(1)} %copy-done.6, s32[8]{0:T(128)S(1)} %copy-done.7, bf16[2,224,768]{2,1,0:T(8,128)(2,1)S(1)} %pad_maximum_fusion.own.rest_0_, bf16[2,224,768]{2,1,0:T(8,128)(2,1)S(1)} %collective-permute-done.6.rest_0_.own_ref.pair, ...), custom_call_target="tpu_custom_call" | custom-call | flops 924844032 | bytes 2752512 | tf_op jit(solution)/shard_map/key_side_1/pallas_call | solution.py:397
  77.8 0.0 collective-permute-done.19.far_ref
  77.8 4.2 %key_side_2.1 = (bf16[224,768]{1,0:T(8,128)(2,1)}, bf16[224,768]{1,0:T(8,128)(2,1)}) custom-call(s32[4,8,9]{2,1,0:T(8,128)S(1)} %copy-done.6, s32[8]{0:T(128)S(1)} %copy-done.7, bf16[2,224,768]{2,1,0:T(8,128)(2,1)S(1)} %pad_maximum_fusion.own.rest_0_, bf16[2,224,768]{2,1,0:T(8,128)(2,1)S(1)} %collective-permute-done.7.rest_1_.other.own_ref, ...), custom_call_target="tpu_custom_call" | custom-call | flops 924844032 | bytes 2752512 | tf_op jit(solution)/shard_map/key_side_2/pallas_call | solution.py:397
  (10 shorter events, 0.2 us)
Async XLA Ops:
  0.6 11.8 %copy-start.4 = (bf16[2,2,56,768]{3,2,1,0:T(8,128)(2,1)S(1)}, bf16[2,2,56,768]{3,2,1,0:T(8,128)(2,1)}, u32[]{:S(2)}) copy-start(bf16[2,2,56,768]{3,2,1,0:T(8,128)(2,1)} %param.9) | copy-start | bytes 1032196
  1.8 2.5 %collective-permute-start.4 = (bf16[2,224,768]{2,1,0:T(8,128)(2,1)S(1)}, bf16[2,224,768]{2,1,0:T(8,128)(2,1)S(1)}, u32[]{:S(2)}, u32[]{:S(2)}) collective-permute-start(bf16[2,224,768]{2,1,0:T(8,128)(2,1)S(1)} %pad_maximum_fusion.own.rest_0_), channel_id=1, source_target_pairs={{0,8},{8,0},{16,24},{24,16},{1,9},{9,1},{17,25},{25,17},{2,10},{10... | collective-permute-start | bytes 2064392 | tf_op jit(solution)/shard_map/ppermute | solution.py:58
  2.6 9.9 %collective-permute-start = (bf16[224,768]{1,0:T(8,128)(2,1)}, bf16[224,768]{1,0:T(8,128)(2,1)S(1)}, u32[]{:S(2)}, u32[]{:S(2)}) collective-permute-start(bf16[224,768]{1,0:T(8,128)(2,1)} %bitcast.22), channel_id=1, source_target_pairs={{0,1},{1,0},{2,3},{3,2},{4,5},{5,4},{6,7},{7,6},{8,9},{9,8},{10,11... | collective-permute-start | bytes 1032200 | tf_op jit(solution)/shard_map/ppermute | solution.py:46
  4.3 1.0 %copy-start = (bf16[2,2,56,768]{3,2,1,0:T(8,128)(2,1)S(1)}, bf16[2,2,56,768]{3,2,1,0:T(8,128)(2,1)}, u32[]{:S(2)}) copy-start(bf16[2,2,56,768]{3,2,1,0:T(8,128)(2,1)} %param.7) | copy-start | bytes 1032196
  5.3 1.0 %copy-start.2 = (bf16[2,2,56,768]{3,2,1,0:T(8,128)(2,1)S(1)}, bf16[2,2,56,768]{3,2,1,0:T(8,128)(2,1)}, u32[]{:S(2)}) copy-start(bf16[2,2,56,768]{3,2,1,0:T(8,128)(2,1)} %param.11) | copy-start | bytes 1032196
  6.4 19.9 %copy-start.1 = (bf16[2,2,56,768]{3,2,1,0:T(8,128)(2,1)S(1)}, bf16[2,2,56,768]{3,2,1,0:T(8,128)(2,1)}, u32[]{:S(2)}) copy-start(bf16[2,2,56,768]{3,2,1,0:T(8,128)(2,1)} %param.7) | copy-start | bytes 1032196
  6.4 19.9 %copy-start.3 = (bf16[2,2,56,768]{3,2,1,0:T(8,128)(2,1)S(1)}, bf16[2,2,56,768]{3,2,1,0:T(8,128)(2,1)}, u32[]{:S(2)}) copy-start(bf16[2,2,56,768]{3,2,1,0:T(8,128)(2,1)} %param.11) | copy-start | bytes 1032196
  6.4 15.0 %collective-permute-start.6 = (bf16[2,224,768]{2,1,0:T(8,128)(2,1)S(1)}, bf16[2,224,768]{2,1,0:T(8,128)(2,1)S(1)}, u32[]{:S(2)}, u32[]{:S(2)}) collective-permute-start(bf16[2,224,768]{2,1,0:T(8,128)(2,1)S(1)} %pair_up.4.own_ref.own), channel_id=1, source_target_pairs={{0,8},{8,0},{16,24},{24,16},{1,9},{9,1},{17,25},{25,17},{2,10},{10... | collective-permute-start | bytes 2064392 | tf_op jit(solution)/shard_map/ppermute | solution.py:58
  6.8 14.6 %collective-permute-start.7 = (bf16[2,224,768]{2,1,0:T(8,128)(2,1)S(1)}, bf16[2,224,768]{2,1,0:T(8,128)(2,1)S(1)}, u32[]{:S(2)}, u32[]{:S(2)}) collective-permute-start(bf16[2,224,768]{2,1,0:T(8,128)(2,1)S(1)} %pair_up.4.own_ref.own), channel_id=1, source_target_pairs={{0,0},{8,16},{16,8},{24,24},{1,1},{9,17},{17,9},{25,25},{2,2},{10,... | collective-permute-start | bytes 2064392 | tf_op jit(solution)/shard_map/ppermute | solution.py:62
  12.5 18.3 %copy-start.6 = (s32[4,8,9]{2,1,0:T(8,128)S(1)}, s32[4,8,9]{2,1,0:T(8,128)}, u32[]{:S(2)}) copy-start(s32[4,8,9]{2,1,0:T(8,128)} %mask_ref.11) | copy-start | bytes 3460
  12.5 18.3 %copy-start.7 = (s32[8]{0:T(128)S(1)}, s32[8]{0:T(128)}, u32[]{:S(2)}) copy-start(s32[8]{0:T(128)} %clip_ref.11) | copy-start | bytes 100
  12.5 8.9 %collective-permute-start.2 = (bf16[224,768]{1,0:T(8,128)(2,1)S(1)}, bf16[224,768]{1,0:T(8,128)(2,1)S(1)}, u32[]{:S(2)}, u32[]{:S(2)}) collective-permute-start(bf16[224,768]{1,0:T(8,128)(2,1)S(1)} %later.1), channel_id=1, source_target_pairs={{0,1},{1,0},{2,3},{3,2},{4,5},{5,4},{6,7},{7,6},{8,9},{9,8},{10,11... | collective-permute-start | bytes 1032200 | tf_op jit(solution)/shard_map/ppermute | solution.py:46
  13.8 12.4 %collective-permute-start.1 = (bf16[224,768]{1,0:T(8,128)(2,1)S(1)}, bf16[224,768]{1,0:T(8,128)(2,1)S(1)}, u32[]{:S(2)}, u32[]{:S(2)}) collective-permute-start(bf16[224,768]{1,0:T(8,128)(2,1)S(1)} %collective-permute-done.rest_0_.x_ref), channel_id=1, source_target_pairs={{0,2},{2,4},{3,1},{4,6},{5,3},{7,5},{8,10},{10,12},{11,9},{12,14},... | collective-permute-start | bytes 1032200 | tf_op jit(solution)/shard_map/ppermute | solution.py:50
  17.0 13.8 %collective-permute-start.5 = (bf16[2,224,768]{2,1,0:T(8,128)(2,1)S(1)}, bf16[2,224,768]{2,1,0:T(8,128)(2,1)S(1)}, u32[]{:S(2)}, u32[]{:S(2)}) collective-permute-start(bf16[2,224,768]{2,1,0:T(8,128)(2,1)S(1)} %pad_maximum_fusion.own.rest_0_), channel_id=1, source_target_pairs={{0,0},{8,16},{16,8},{24,24},{1,1},{9,17},{17,9},{25,25},{2,2},{10,... | collective-permute-start | bytes 2064392 | tf_op jit(solution)/shard_map/ppermute | solution.py:62
  21.5 11.9 %collective-permute-start.8 = (bf16[2,224,768]{2,1,0:T(8,128)(2,1)S(1)}, bf16[2,224,768]{2,1,0:T(8,128)(2,1)S(1)}, u32[]{:S(2)}, u32[]{:S(2)}) collective-permute-start(bf16[2,224,768]{2,1,0:T(8,128)(2,1)S(1)} %pair_up.5.own.near.rest_1_), channel_id=1, source_target_pairs={{0,8},{8,0},{16,24},{24,16},{1,9},{9,1},{17,25},{25,17},{2,10},{10... | collective-permute-start | bytes 2064392 | tf_op jit(solution)/shard_map/ppermute | solution.py:58
  23.1 14.5 %collective-permute-start.9 = (bf16[2,224,768]{2,1,0:T(8,128)(2,1)S(1)}, bf16[2,224,768]{2,1,0:T(8,128)(2,1)S(1)}, u32[]{:S(2)}, u32[]{:S(2)}) collective-permute-start(bf16[2,224,768]{2,1,0:T(8,128)(2,1)S(1)} %pair_up.5.own.near.rest_1_), channel_id=1, source_target_pairs={{0,0},{8,16},{16,8},{24,24},{1,1},{9,17},{17,9},{25,25},{2,2},{10,... | collective-permute-start | bytes 2064392 | tf_op jit(solution)/shard_map/ppermute | solution.py:62
  26.3 17.5 %collective-permute-start.12 = (bf16[2,224,768]{2,1,0:T(8,128)(2,1)S(1)}, bf16[2,224,768]{2,1,0:T(8,128)(2,1)S(1)}, u32[]{:S(2)}, u32[]{:S(2)}) collective-permute-start(bf16[2,224,768]{2,1,0:T(8,128)(2,1)S(1)} %pair_up.7), channel_id=1, source_target_pairs={{0,1},{1,0},{2,3},{3,2},{4,5},{5,4},{6,7},{7,6},{8,9},{9,8},{10,11... | collective-permute-start | bytes 2064392 | tf_op jit(solution)/shard_map/ppermute | solution.py:46
  27.6 12.7 %collective-permute-start.3 = (bf16[224,768]{1,0:T(8,128)(2,1)S(1)}, bf16[224,768]{1,0:T(8,128)(2,1)S(1)}, u32[]{:S(2)}, u32[]{:S(2)}) collective-permute-start(bf16[224,768]{1,0:T(8,128)(2,1)S(1)} %collective-permute-done.2.y_ref.rest_0_), channel_id=1, source_target_pairs={{0,2},{2,4},{3,1},{4,6},{5,3},{7,5},{8,10},{10,12},{11,9},{12,14},... | collective-permute-start | bytes 1032200 | tf_op jit(solution)/shard_map/ppermute | solution.py:50
  40.3 9.3 %copy-start.5 = (bf16[27,768]{1,0:T(8,128)(2,1)S(1)}, bf16[27,768]{1,0:T(8,128)(2,1)}, u32[]{:S(2)}) copy-start(bf16[27,768]{1,0:T(8,128)(2,1)} %rest_2_.1) | copy-start | bytes 124420
  40.4 11.0 %collective-permute-start.10 = (bf16[2,224,768]{2,1,0:T(8,128)(2,1)S(1)}, bf16[2,224,768]{2,1,0:T(8,128)(2,1)S(1)}, u32[]{:S(2)}, u32[]{:S(2)}) collective-permute-start(bf16[2,224,768]{2,1,0:T(8,128)(2,1)S(1)} %pair_up.6.own.rest_2_), channel_id=1, source_target_pairs={{0,8},{8,0},{16,24},{24,16},{1,9},{9,1},{17,25},{25,17},{2,10},{10... | collective-permute-start | bytes 2064392 | tf_op jit(solution)/shard_map/ppermute | solution.py:58
  40.5 12.6 %collective-permute-start.11 = (bf16[2,224,768]{2,1,0:T(8,128)(2,1)S(1)}, bf16[2,224,768]{2,1,0:T(8,128)(2,1)S(1)}, u32[]{:S(2)}, u32[]{:S(2)}) collective-permute-start(bf16[2,224,768]{2,1,0:T(8,128)(2,1)S(1)} %pair_up.6.own.rest_2_), channel_id=1, source_target_pairs={{0,0},{8,16},{16,8},{24,24},{1,1},{9,17},{17,9},{25,25},{2,2},{10,... | collective-permute-start | bytes 2064392 | tf_op jit(solution)/shard_map/ppermute | solution.py:62
  43.8 20.3 %collective-permute-start.13 = (bf16[2,224,768]{2,1,0:T(8,128)(2,1)S(1)}, bf16[2,224,768]{2,1,0:T(8,128)(2,1)S(1)}, u32[]{:S(2)}, u32[]{:S(2)}) collective-permute-start(bf16[2,224,768]{2,1,0:T(8,128)(2,1)S(1)} %gate.1.near_ref.near), channel_id=1, source_target_pairs={{0,2},{2,4},{3,1},{4,6},{5,3},{7,5},{8,10},{10,12},{11,9},{12,14},... | collective-permute-start | bytes 2064392 | tf_op jit(solution)/shard_map/ppermute | solution.py:50
  47.1 17.1 %collective-permute-start.16 = (bf16[2,224,768]{2,1,0:T(8,128)(2,1)S(1)}, bf16[2,224,768]{2,1,0:T(8,128)(2,1)S(1)}, u32[]{:S(2)}, u32[]{:S(2)}) collective-permute-start(bf16[2,224,768]{2,1,0:T(8,128)(2,1)S(1)} %gate.1.near_ref.near), channel_id=1, source_target_pairs={{0,8},{8,0},{16,24},{24,16},{1,9},{9,1},{17,25},{25,17},{2,10},{10... | collective-permute-start | bytes 2064392 | tf_op jit(solution)/shard_map/ppermute | solution.py:58
  47.8 16.4 %collective-permute-start.17 = (bf16[2,224,768]{2,1,0:T(8,128)(2,1)S(1)}, bf16[2,224,768]{2,1,0:T(8,128)(2,1)S(1)}, u32[]{:S(2)}, u32[]{:S(2)}) collective-permute-start(bf16[2,224,768]{2,1,0:T(8,128)(2,1)S(1)} %gate.1.near_ref.near), channel_id=1, source_target_pairs={{0,0},{8,16},{16,8},{24,24},{1,1},{9,17},{17,9},{25,25},{2,2},{10,... | collective-permute-start | bytes 2064392 | tf_op jit(solution)/shard_map/ppermute | solution.py:62
  56.2 8.0 %collective-permute-start.14 = (f32[16,224]{1,0:T(8,128)S(1)}, f32[16,224]{1,0:T(8,128)S(1)}, u32[]{:S(2)}, u32[]{:S(2)}) collective-permute-start(f32[16,224]{1,0:T(8,128)S(1)} %get-tuple-element.34.own_ref.rest_0_), channel_id=1, source_target_pairs={{0,1},{1,0},{2,3},{3,2},{4,5},{5,4},{6,7},{7,6},{8,9},{9,8},{10,11... | collective-permute-start | bytes 43016 | tf_op jit(solution)/shard_map/ppermute | solution.py:46
  56.2 7.9 %collective-permute-start.15 = (f32[16,224]{1,0:T(8,128)S(1)}, f32[16,224]{1,0:T(8,128)S(1)}, u32[]{:S(2)}, u32[]{:S(2)}) collective-permute-start(f32[16,224]{1,0:T(8,128)S(1)} %get-tuple-element.34.own_ref.rest_0_), channel_id=1, source_target_pairs={{0,0},{1,2},{2,1},{3,4},{4,3},{5,6},{6,5},{7,7},{8,8},{9,10},{10,9... | collective-permute-start | bytes 43016 | tf_op jit(solution)/shard_map/ppermute | solution.py:54
  64.2 8.9 %collective-permute-start.18 = (bf16[496,768]{1,0:T(8,128)(2,1)S(1)}, bf16[496,768]{1,0:T(8,128)(2,1)S(1)}, u32[]{:S(2)}, u32[]{:S(2)}) collective-permute-start(bf16[496,768]{1,0:T(8,128)(2,1)S(1)} %pack.1), channel_id=1, source_target_pairs={{0,8},{8,0},{16,24},{24,16},{1,9},{9,1},{17,25},{25,17},{2,10},{10... | collective-permute-start | bytes 2285576 | tf_op jit(solution)/shard_map/ppermute | solution.py:58
  64.3 13.5 %collective-permute-start.19 = (bf16[496,768]{1,0:T(8,128)(2,1)S(1)}, bf16[496,768]{1,0:T(8,128)(2,1)S(1)}, u32[]{:S(2)}, u32[]{:S(2)}) collective-permute-start(bf16[496,768]{1,0:T(8,128)(2,1)S(1)} %pack.1), channel_id=1, source_target_pairs={{0,0},{8,16},{16,8},{24,24},{1,1},{9,17},{17,9},{25,25},{2,2},{10,... | collective-permute-start | bytes 2285576 | tf_op jit(solution)/shard_map/ppermute | solution.py:62

commit v12 on v11

--- a/solution.py
+++ b/solution.py
@@ -105,27 +105,29 @@
             return lambda frame: jnp.where(even_h | ~in_h[0], 0.0, row_of(tiles[slot][1], frame, 1, width))
         return lambda frame: jnp.where(even_h & in_h[1], row_of(tiles[slot][1], frame, 0, width), 0.0)
 
-    slab = [along_t(cell(0, R), cell(1, R), cell(2, R), place_now) for R in range(4)]
+    lines = range(4) if len(tiles[0]) == 2 else (1, 2)
+    slab = {R: along_t(cell(0, R), cell(1, R), cell(2, R), place_now) for R in lines}
     rows = []
     for f in range(2):
         for r in range(2):
             parts = []
             for dw in range(3):
-                taps = [(dt, dh, 9 * dt + 3 * dh + dw) for dt in range(3) for dh in range(3)]
+                taps = [(dt, dh, 9 * dt + 3 * dh + dw) for dt in range(3) for dh in range(3) if r + dh in slab]
                 taps = [(dt, dh, 26 - tap if flipped else tap) for dt, dh, tap in taps]
                 parts.append(total_of([weight[tap : tap + 1] * slab[r + dh][f + dt] for dt, dh, tap in taps]))
             rows.append(shifted_sum(parts, width))
     return jnp.concatenate(rows, axis=0)
 
 
-def conv_far(tiles, weight, flipped, place_now, width):
+def conv_beside(tiles, weight, flipped, place_now, width, far):
     _, even_h, _, in_h = place_now
+    above = even_h if far else ~even_h
     tiles = [x.astype(jnp.float32) for x in tiles]
-    there = (even_h & in_h[0]) | (~even_h & in_h[1])
+    there = (above & in_h[0]) | (~above & in_h[1])
 
     def cell(slot):
         def of(frame):
-            row = jnp.where(even_h, row_of(tiles[slot], frame, 1, width), row_of(tiles[slot], frame, 0, width))
+            row = jnp.where(above, row_of(tiles[slot], frame, 1, width), row_of(tiles[slot], frame, 0, width))
             return jnp.where(there, row, 0.0)
 
         return of
@@ -140,11 +142,11 @@
                 up, down = 9 * dt + dw, 9 * dt + 6 + dw
                 if flipped:
                     up, down = 26 - up, 26 - down
-                tap = jnp.where(even_h, weight[up : up + 1], weight[down : down + 1])
+                tap = jnp.where(above, weight[up : up + 1], weight[down : down + 1])
                 terms.append(tap * line[f + dt])
             parts.append(total_of(terms))
         beside = shifted_sum(parts, width)
-        rows += [jnp.where(even_h, beside, 0.0), jnp.where(even_h, 0.0, beside)]
+        rows += [jnp.where(above, beside, 0.0), jnp.where(above, 0.0, beside)]
     return jnp.concatenate(rows, axis=0)
 
 
@@ -241,13 +243,14 @@
         stat_ref[...] = turned[:STAT_ROWS, :rows]
 
 
-def conv_kernel(counts, width, flipped, own, near, pair, near_pair, other, near_other, weight_ref, out_ref):
+def conv_kernel(counts, width, flipped, columns, *refs):
+    *tile_refs, weight_ref, out_ref = refs
     _, _, place_now = place(counts)
     rows, channels = out_ref.shape
 
     def body(head, _):
         cols = head_columns(head)
-        tiles = [(x[1, :, cols], y[1, :, cols]) for x, y in ((own, near), (pair, near_pair), (other, near_other))]
+        tiles = [[ref[1, :, cols] for ref in tile_refs[columns * i : columns * (i + 1)]] for i in range(3)]
         out_ref[:, cols] = conv_inner(tiles, weight_ref[:, cols].astype(jnp.float32), flipped, place_now, width)
         return 0
 
@@ -289,7 +292,7 @@
     def body(head, _):
         cols = head_columns(head)
         tiles = [ref[1, :, cols] for ref in (own, pair, other)]
-        conv = conv_ref[:, cols] + conv_far(tiles, weight_ref[:, cols].astype(jnp.float32), False, place_now, width)
+        conv = conv_ref[:, cols] + conv_beside(tiles, weight_ref[:, cols].astype(jnp.float32), False, place_now, width, True)
         out_ref[:, cols] = (att_ref[:, cols] + conv).astype(jnp.bfloat16)
         return 0
 
@@ -362,9 +365,11 @@
                 dk_ref[:, cols], dv_ref[:, cols] = dk, dv
                 continue
             dk_ref[:, cols] = jnp.where(live, dk * scale, 0.0).astype(jnp.bfloat16)
-            weight_ref, conv_ref, *far_refs = edges
-            tiles = [packed(ref, 1, cols) for ref in (*far_refs, far_ref)]
-            conv = conv_ref[:, cols] + conv_far(tiles, weight_ref[:, cols].astype(jnp.float32), True, place_now, width)
+            weight_ref, conv_ref, *sides = edges
+            weight = weight_ref[:, cols].astype(jnp.float32)
+            conv = conv_ref[:, cols]
+            for far, refs in ((True, (*sides[:2], far_ref)), (False, (*sides[2:], near_ref))):
+                conv = conv + conv_beside([packed(ref, 1, cols) for ref in refs], weight, True, place_now, width, far)
             dv_ref[:, cols] = (jnp.where(live, dv, 0.0) + conv).astype(jnp.bfloat16)
         return 0
 
@@ -406,7 +411,7 @@
         )(*args)
 
     def convolution(flipped, *tiles):
-        kernel = functools.partial(conv_kernel, counts, width, flipped)
+        kernel = functools.partial(conv_kernel, counts, width, flipped, len(tiles) // 3)
         return call(kernel, "convolution", [full], [], cost(heads, rows, 1, 1), *tiles, conv_weight)[0]
 
     def scores(column, tiles):
@@ -465,8 +470,9 @@
     near_kv = pair_up(near_k, near_v, qg_a, qg_b)
     near_kv_a, near_kv_b = ta_pair(near_kv), ta_other(near_kv)
     near_qg = ha_near(pair_up(query, grad, near_v, far_k))
+    conv_grad = convolution(True, qg, qg_a, qg_b)
     exp_near, *near_parts = scores(1, (near_kv, near_kv_a, near_kv_b))
-    far_kv = pair_up(far_k, far_v, own_parts[0], near_parts[0])
+    far_kv = pair_up(far_k, far_v, own_parts[0], near_parts[0], conv_grad)
     far_kv_a, far_kv_b = ta_pair(far_kv), ta_other(far_kv)
 
     conv_value = convolution(False, kv, near_kv, kv_a, near_kv_a, kv_b, near_kv_b)
@@ -506,7 +512,6 @@
         attention, conv_value, far_kv, far_kv_a, far_kv_b, conv_weight, message_a,
     )[0]
 
-    conv_grad = convolution(True, qg, near_qg, qg_a, near_qg_a, qg_b, near_qg_b)
     scratch = [pltpu.VMEM((STAT_ROWS, 3 * rows), jnp.float32)]
     work = cost(heads, rows, 4, 1)
     sums = call(
@@ -520,7 +525,7 @@
     key_grad, value_grad = call(
         functools.partial(key_kernel, counts, width, 2), "key_side_2", [half, half], scratch, work,
         tile_mask, clip_lengths, kv, qg_b, near_qg_b, message_b, *sums,
-        conv_weight, conv_grad, far_qg, message_a,
+        conv_weight, conv_grad, far_qg, message_a, near_qg, near_qg_a,
     )
     return tuple(x.reshape(query_states.shape) for x in (layer_out, query_grad, key_grad, value_grad))
 

time: 82.5 us -> 83 us (level)
  transfers between devices with their start and end apart: 20 -> 20, of which waited for: 4 -> 5; matrix products, arithmetic and copies ran while one was open for 0% -> 0% of each run, Pallas kernels for 30% -> 29%
where the time goes in v12:
time: 83 us; the launch traced here: 82.5 us
  starting transfers between devices  40 us (48%)
  Pallas kernels  28.9 us (35%)
  waiting for transfers between devices  9.35 us (11%)
  local copies, waits for them, and re-layouts  1.99 us (2%)
  other arithmetic  1.19 us (1%)
  between operations  1.02 us (1%)
    pallas_call x10, Pallas kernels, call(): pl.pallas_call(kernel, in_specs=[smem] * scalars + [vmem] * (len(args) -...  28.6 us
    ppermute x6, starting transfers between devices, ta_other(): return lax.ppermute(x, 'ta', other_pairs(lax.axis_size('ta')))  19.8 us
    ppermute x3, starting transfers between devices, ha_relay(): return lax.ppermute(near, 'ha', relay_pairs(lax.axis_size('ha')))  9.59 us
    ppermute x6, waiting for transfers between devices, ta_other(): return lax.ppermute(x, 'ta', other_pairs(lax.axis_size('ta')))  6.33 us
    ppermute x4, starting transfers between devices, ha_near(): return lax.ppermute(x, 'ha', flip_pairs(lax.axis_size('ha')))  3.81 us
    ppermute x6, starting transfers between devices, ta_pair(): return lax.ppermute(x, 'ta', flip_pairs(lax.axis_size('ta')))  3.69 us
    ppermute x1, starting transfers between devices, ha_far(): return lax.ppermute(x, 'ha', other_pairs(lax.axis_size('ha')))  3.14 us
    ppermute x4, waiting for transfers between devices, ha_near(): return lax.ppermute(x, 'ha', flip_pairs(lax.axis_size('ha')))  2.45 us
  transfers between devices with their start and end apart: 20, of which 5 were waited for; matrix products, arithmetic and copies ran while one was open for 0% of the time, Pallas kernels for 29%

profile of v12, /device:TPU:9, one launch (start us, length us, event | category | flops | bytes accessed | tf_op | source)
XLA Modules:
  0.0 82.5 jit_solution(18132615070627638171)
XLA Ops:
  0.6 0.0 copy-start.4
  0.6 1.2 %pad_maximum_fusion.own.refs_0_.rest_0_ = bf16[2,224,768]{2,1,0:T(8,128)(2,1)S(1)} fusion(bf16[1,224,768]{2,1,0:T(8,128)(2,1)} %bitcast.19, bf16[1,224,768]{2,1,0:T(8,128)(2,1)} %bitcast.21), kind=kLoop, calls=%fused_computation | loop fusion | flops 344064 | bytes 1376256 | tf_op jit(solution)/shard_map/stack | solution.py:461
  1.8 0.7 collective-permute-start.4
  2.6 1.2 %collective-permute-start = (bf16[224,768]{1,0:T(8,128)(2,1)}, bf16[224,768]{1,0:T(8,128)(2,1)S(1)}, u32[]{:S(2)}, u32[]{:S(2)}) collective-permute-start(bf16[224,768]{1,0:T(8,128)(2,1)} %bitcast.22), channel_id=1, source_target_pairs={{0,1},{1,0},{2,3},{3,2},{4,5},{5,4},{6,7},{7,6},{8,9},{9,8},{10,11... | collective-permute-start | bytes 1032200 | tf_op jit(solution)/shard_map/ppermute | solution.py:46
  3.8 0.5 collective-permute-done.4.pair.rest_0_.refs_2_.rest_3_
  4.4 1.0 %copy-done = bf16[2,2,56,768]{3,2,1,0:T(8,128)(2,1)S(1)} copy-done((bf16[2,2,56,768]{3,2,1,0:T(8,128)(2,1)S(1)}, bf16[2,2,56,768]{3,2,1,0:T(8,128)(2,1)}, u32[]{:S(2)}) %copy-start) | copy-done | bytes 344088
  5.3 1.0 %copy-done.2 = bf16[2,2,56,768]{3,2,1,0:T(8,128)(2,1)S(1)} copy-done((bf16[2,2,56,768]{3,2,1,0:T(8,128)(2,1)S(1)}, bf16[2,2,56,768]{3,2,1,0:T(8,128)(2,1)}, u32[]{:S(2)}) %copy-start.2) | copy-done | bytes 344088
  6.4 0.0 copy-start.1
  6.4 0.0 copy-start.3
  6.4 0.4 collective-permute-start.6
  6.8 3.2 %collective-permute-start.7 = (bf16[2,224,768]{2,1,0:T(8,128)(2,1)S(1)}, bf16[2,224,768]{2,1,0:T(8,128)(2,1)S(1)}, u32[]{:S(2)}, u32[]{:S(2)}) collective-permute-start(bf16[2,224,768]{2,1,0:T(8,128)(2,1)S(1)} %pair_up.4.refs_0_.own_ref), channel_id=1, source_target_pairs={{0,0},{8,16},{16,8},{24,24},{1,1},{9,17},{17,9},{25,25},{2,2},{10,... | collective-permute-start | bytes 2064392 | tf_op jit(solution)/shard_map/ppermute | solution.py:62
  10.0 2.4 %collective-permute-done.rest_0_.x_ref = bf16[224,768]{1,0:T(8,128)(2,1)S(1)} collective-permute-done((bf16[224,768]{1,0:T(8,128)(2,1)}, bf16[224,768]{1,0:T(8,128)(2,1)S(1)}, u32[]{:S(2)}, u32[]{:S(2)}) %collective-permute-start) | collective-permute-done | bytes 344096 | tf_op jit(solution)/shard_map/ppermute | solution.py:46
  12.4 0.0 copy-done.4
  12.5 0.0 copy-start.6
  12.5 0.0 copy-start.7
  12.5 1.3 %collective-permute-start.2 = (bf16[224,768]{1,0:T(8,128)(2,1)S(1)}, bf16[224,768]{1,0:T(8,128)(2,1)S(1)}, u32[]{:S(2)}, u32[]{:S(2)}) collective-permute-start(bf16[224,768]{1,0:T(8,128)(2,1)S(1)} %later.1), channel_id=1, source_target_pairs={{0,1},{1,0},{2,3},{3,2},{4,5},{5,4},{6,7},{7,6},{8,9},{9,8},{10,11... | collective-permute-start | bytes 1032200 | tf_op jit(solution)/shard_map/ppermute | solution.py:46
  13.8 3.2 %collective-permute-start.1 = (bf16[224,768]{1,0:T(8,128)(2,1)S(1)}, bf16[224,768]{1,0:T(8,128)(2,1)S(1)}, u32[]{:S(2)}, u32[]{:S(2)}) collective-permute-start(bf16[224,768]{1,0:T(8,128)(2,1)S(1)} %collective-permute-done.rest_0_.x_ref), channel_id=1, source_target_pairs={{0,2},{2,4},{3,1},{4,6},{5,3},{7,5},{8,10},{10,12},{11,9},{12,14},... | collective-permute-start | bytes 1032200 | tf_op jit(solution)/shard_map/ppermute | solution.py:50
  17.0 4.4 %collective-permute-start.5 = (bf16[2,224,768]{2,1,0:T(8,128)(2,1)S(1)}, bf16[2,224,768]{2,1,0:T(8,128)(2,1)S(1)}, u32[]{:S(2)}, u32[]{:S(2)}) collective-permute-start(bf16[2,224,768]{2,1,0:T(8,128)(2,1)S(1)} %pad_maximum_fusion.own.refs_0_.rest_0_), channel_id=1, source_target_pairs={{0,0},{8,16},{16,8},{24,24},{1,1},{9,17},{17,9},{25,25},{2,2},{10,... | collective-permute-start | bytes 2064392 | tf_op jit(solution)/shard_map/ppermute | solution.py:62
  21.4 0.0 collective-permute-done.2.y_ref.rest_0_
  21.4 0.0 collective-permute-done.6.rest_0_.refs_1_.own_ref
  21.4 0.0 collective-permute-done.7.rest_1_.refs_2_.own_ref
  21.5 0.0 copy-start.5
  21.5 1.6 %collective-permute-start.8 = (bf16[2,224,768]{2,1,0:T(8,128)(2,1)S(1)}, bf16[2,224,768]{2,1,0:T(8,128)(2,1)S(1)}, u32[]{:S(2)}, u32[]{:S(2)}) collective-permute-start(bf16[2,224,768]{2,1,0:T(8,128)(2,1)S(1)} %pair_up.5.own.refs_1_.rest_1_), channel_id=1, source_target_pairs={{0,8},{8,0},{16,24},{24,16},{1,9},{9,1},{17,25},{25,17},{2,10},{10... | collective-permute-start | bytes 2064392 | tf_op jit(solution)/shard_map/ppermute | solution.py:58
  23.2 3.0 %collective-permute-start.9 = (bf16[2,224,768]{2,1,0:T(8,128)(2,1)S(1)}, bf16[2,224,768]{2,1,0:T(8,128)(2,1)S(1)}, u32[]{:S(2)}, u32[]{:S(2)}) collective-permute-start(bf16[2,224,768]{2,1,0:T(8,128)(2,1)S(1)} %pair_up.5.own.refs_1_.rest_1_), channel_id=1, source_target_pairs={{0,0},{8,16},{16,8},{24,24},{1,1},{9,17},{17,9},{25,25},{2,2},{10,... | collective-permute-start | bytes 2064392 | tf_op jit(solution)/shard_map/ppermute | solution.py:62
  26.2 0.0 collective-permute-done.1.x_ref.rest_1_
  26.2 0.0 copy-done.1
  26.2 0.0 copy-done.3
  26.3 1.3 %collective-permute-start.12 = (bf16[2,224,768]{2,1,0:T(8,128)(2,1)S(1)}, bf16[2,224,768]{2,1,0:T(8,128)(2,1)S(1)}, u32[]{:S(2)}, u32[]{:S(2)}) collective-permute-start(bf16[2,224,768]{2,1,0:T(8,128)(2,1)S(1)} %pair_up.7), channel_id=1, source_target_pairs={{0,1},{1,0},{2,3},{3,2},{4,5},{5,4},{6,7},{7,6},{8,9},{9,8},{10,11... | collective-permute-start | bytes 2064392 | tf_op jit(solution)/shard_map/ppermute | solution.py:46
  27.6 3.2 %collective-permute-start.3 = (bf16[224,768]{1,0:T(8,128)(2,1)S(1)}, bf16[224,768]{1,0:T(8,128)(2,1)S(1)}, u32[]{:S(2)}, u32[]{:S(2)}) collective-permute-start(bf16[224,768]{1,0:T(8,128)(2,1)S(1)} %collective-permute-done.2.y_ref.rest_0_), channel_id=1, source_target_pairs={{0,2},{2,4},{3,1},{4,6},{5,3},{7,5},{8,10},{10,12},{11,9},{12,14},... | collective-permute-start | bytes 1032200 | tf_op jit(solution)/shard_map/ppermute | solution.py:50
  30.8 0.0 collective-permute-done.5.other.refs_4_.rest_6_
  30.8 0.0 copy-done.6
  30.8 2.5 %scores_0.1 = (bf16[6,224,672]{2,1,0:T(8,128)(2,1)S(1)}, f32[224,768]{1,0:T(8,128)S(1)}, f32[224,768]{1,0:T(8,128)S(1)}, f32[224,768]{1,0:T(8,128)S(1)}) custom-call(s32[4,8,9]{2,1,0:T(8,128)S(1)} %copy-done.6, s32[8]{0:T(128)S(1)} %copy-done.7, bf16[224,768]{1,0:T(8,128)(2,1)S(1)} %bitcast.12, bf16[2,224,768]{2,1,0:T(8,128)(2,1)S(1)} %pad_maximum_fusion.own.refs_0_.rest_0_, ...), custom_call_target="tpu_custom_call" | custom-call | flops 462422016 | bytes 2752512 | tf_op jit(solution)/shard_map/scores_0/pallas_call | solution.py:402
  33.4 1.1 %convolution.2.rest_2_.rest_3_ = f32[224,768]{1,0:T(8,128)S(1)} custom-call(bf16[2,224,768]{2,1,0:T(8,128)(2,1)S(1)} %pair_up.4.refs_0_.own_ref, bf16[2,224,768]{2,1,0:T(8,128)(2,1)S(1)} %collective-permute-done.6.rest_0_.refs_1_.own_ref, bf16[2,224,768]{2,1,0:T(8,128)(2,1)S(1)} %collective-permute-done.7.rest_1_.refs_2_.own_ref, bf16[27,768]{1,0:T(8,128)(2,1)S(1)} %copy-done.5), custom_call_target="tpu_custom_call" | custom-call | flops 231211008 | bytes 2752512 | tf_op jit(solution)/shard_map/convolution/pallas_call | solution.py:402
  34.5 0.0 collective-permute-done.8.pair.refs_3_.rest_4_
  34.5 3.2 %collective-permute-done.9.other.refs_5_.rest_7_ = bf16[2,224,768]{2,1,0:T(8,128)(2,1)S(1)} collective-permute-done((bf16[2,224,768]{2,1,0:T(8,128)(2,1)S(1)}, bf16[2,224,768]{2,1,0:T(8,128)(2,1)S(1)}, u32[]{:S(2)}, u32[]{:S(2)}) %collective-permute-start.9) | collective-permute-done | bytes 688160 | tf_op jit(solution)/shard_map/ppermute | solution.py:62
  37.7 2.6 %scores_1.1 = (bf16[6,224,672]{2,1,0:T(8,128)(2,1)S(1)}, f32[224,768]{1,0:T(8,128)S(1)}, f32[224,768]{1,0:T(8,128)S(1)}, f32[224,768]{1,0:T(8,128)S(1)}) custom-call(s32[4,8,9]{2,1,0:T(8,128)S(1)} %copy-done.6, s32[8]{0:T(128)S(1)} %copy-done.7, bf16[224,768]{1,0:T(8,128)(2,1)S(1)} %bitcast.13, bf16[2,224,768]{2,1,0:T(8,128)(2,1)S(1)} %pair_up.5.own.refs_1_.rest_1_, ...), custom_call_target="tpu_custom_call" | custom-call | flops 462422016 | bytes 2752512 | tf_op jit(solution)/shard_map/scores_1/pallas_call | solution.py:402
  40.3 0.0 collective-permute-done.3.y_ref
  40.4 0.1 collective-permute-start.10
  40.5 3.4 %collective-permute-start.11 = (bf16[2,224,768]{2,1,0:T(8,128)(2,1)S(1)}, bf16[2,224,768]{2,1,0:T(8,128)(2,1)S(1)}, u32[]{:S(2)}, u32[]{:S(2)}) collective-permute-start(bf16[2,224,768]{2,1,0:T(8,128)(2,1)S(1)} %pair_up.6.own.rest_2_), channel_id=1, source_target_pairs={{0,0},{8,16},{16,8},{24,24},{1,1},{9,17},{17,9},{25,25},{2,2},{10,... | collective-permute-start | bytes 2064392 | tf_op jit(solution)/shard_map/ppermute | solution.py:62
  43.8 0.0 collective-permute-done.12.refs_0_
  43.8 3.2 %collective-permute-start.13 = (bf16[2,224,768]{2,1,0:T(8,128)(2,1)S(1)}, bf16[2,224,768]{2,1,0:T(8,128)(2,1)S(1)}, u32[]{:S(2)}, u32[]{:S(2)}) collective-permute-start(bf16[2,224,768]{2,1,0:T(8,128)(2,1)S(1)} %gate.1.near_ref.rest_6_), channel_id=1, source_target_pairs={{0,2},{2,4},{3,1},{4,6},{5,3},{7,5},{8,10},{10,12},{11,9},{12,14},... | collective-permute-start | bytes 2064392 | tf_op jit(solution)/shard_map/ppermute | solution.py:50
  47.0 0.7 collective-permute-start.16
  47.8 1.9 %collective-permute-start.17 = (bf16[2,224,768]{2,1,0:T(8,128)(2,1)S(1)}, bf16[2,224,768]{2,1,0:T(8,128)(2,1)S(1)}, u32[]{:S(2)}, u32[]{:S(2)}) collective-permute-start(bf16[2,224,768]{2,1,0:T(8,128)(2,1)S(1)} %gate.1.near_ref.rest_6_), channel_id=1, source_target_pairs={{0,0},{8,16},{16,8},{24,24},{1,1},{9,17},{17,9},{25,25},{2,2},{10,... | collective-permute-start | bytes 2064392 | tf_op jit(solution)/shard_map/ppermute | solution.py:62
  49.7 1.7 %convolution.3.rest_7_.conv_ref = f32[224,768]{1,0:T(8,128)S(1)} custom-call(bf16[2,224,768]{2,1,0:T(8,128)(2,1)S(1)} %pad_maximum_fusion.own.refs_0_.rest_0_, bf16[2,224,768]{2,1,0:T(8,128)(2,1)S(1)} %pair_up.5.own.refs_1_.rest_1_, bf16[2,224,768]{2,1,0:T(8,128)(2,1)S(1)} %collective-permute-done.4.pair.rest_0_.refs_2_.rest_3_, ...), custom_call_target="tpu_custom_call" | custom-call | flops 231211008 | bytes 2752512 | tf_op jit(solution)/shard_map/convolution/pallas_call | solution.py:402
  51.4 0.0 collective-permute-done.10.pair.rest_5_
  51.4 1.6 %collective-permute-done.11.other.rest_8_ = bf16[2,224,768]{2,1,0:T(8,128)(2,1)S(1)} collective-permute-done((bf16[2,224,768]{2,1,0:T(8,128)(2,1)S(1)}, bf16[2,224,768]{2,1,0:T(8,128)(2,1)S(1)}, u32[]{:S(2)}, u32[]{:S(2)}) %collective-permute-start.11) | collective-permute-done | bytes 688160 | tf_op jit(solution)/shard_map/ppermute | solution.py:62
  53.0 3.2 %scores_2.1 = (bf16[6,224,672]{2,1,0:T(8,128)(2,1)S(1)}, f32[224,768]{1,0:T(8,128)S(1)}, f32[224,768]{1,0:T(8,128)S(1)}, f32[224,768]{1,0:T(8,128)S(1)}, f32[224...) custom-call(s32[4,8,9]{2,1,0:T(8,128)S(1)} %copy-done.6, s32[8]{0:T(128)S(1)} %copy-done.7, ...), custom_call_target="tpu_custom_call" | custom-call | flops 462422016 | bytes 2752512 | tf_op jit(solution)/shard_map/scores_2/pallas_call | solution.py:402
  56.2 0.0 collective-permute-start.14
  56.2 3.1 %collective-permute-start.15 = (f32[16,224]{1,0:T(8,128)S(1)}, f32[16,224]{1,0:T(8,128)S(1)}, u32[]{:S(2)}, u32[]{:S(2)}) collective-permute-start(f32[16,224]{1,0:T(8,128)S(1)} %get-tuple-element.34.own_ref.rest_0_), channel_id=1, source_target_pairs={{0,0},{1,2},{2,1},{3,4},{4,3},{5,6},{6,5},{7,7},{8,8},{9,10},{10,9... | collective-permute-start | bytes 43016 | tf_op jit(solution)/shard_map/ppermute | solution.py:54
  59.4 4.7 %query_side.1 = (bf16[224,768]{1,0:T(8,128)(2,1)}, f32[8,128]{1,0:T(8,128)S(1)}) custom-call(bf16[224,768]{1,0:T(8,128)(2,1)S(1)} %bitcast.18, bf16[2,224,768]{2,1,0:T(8,128)(2,1)S(1)} %pad_maximum_fusion.own.refs_0_.rest_0_, bf16[2,224,768]{2,1,0:T(8,128)(2,1)S(1)} %pair_up.5.own.refs_1_.rest_1_, bf16[2,224,768]{2,1,0:T(8,128)(2,1)S(1)} %pair_up.6.own.rest_2_, ...), custom_call_target="tpu_custom_call" | custom-call | flops 1387266048 | bytes 8257536 | tf_op jit(solution)/shard_map/query_side/pallas_call | solution.py:402
  64.1 0.0 collective-permute-done.13.qg_ref.far_ref.rest_4_
  64.1 0.0 collective-permute-done.16.rest_1_.near_ref.rest_7_
  64.1 0.0 collective-permute-done.17.rest_2_.near_ref
  64.1 0.0 collective-permute-done.14.near_ref.rest_1_
  64.1 0.0 collective-permute-done.15.far_ref.rest_2_
  64.1 0.1 pack.1
  64.2 0.1 collective-permute-start.18
  64.3 3.9 %collective-permute-start.19 = (bf16[496,768]{1,0:T(8,128)(2,1)S(1)}, bf16[496,768]{1,0:T(8,128)(2,1)S(1)}, u32[]{:S(2)}, u32[]{:S(2)}) collective-permute-start(bf16[496,768]{1,0:T(8,128)(2,1)S(1)} %pack.1), channel_id=1, source_target_pairs={{0,0},{8,16},{16,8},{24,24},{1,1},{9,17},{17,9},{25,25},{2,2},{10,... | collective-permute-start | bytes 2285576 | tf_op jit(solution)/shard_map/ppermute | solution.py:62
  68.2 3.2 %key_side_0.1 = (f32[224,768]{1,0:T(8,128)S(1)}, f32[224,768]{1,0:T(8,128)S(1)}) custom-call(s32[4,8,9]{2,1,0:T(8,128)S(1)} %copy-done.6, s32[8]{0:T(128)S(1)} %copy-done.7, bf16[2,224,768]{2,1,0:T(8,128)(2,1)S(1)} %pad_maximum_fusion.own.refs_0_.rest_0_, bf16[2,224,768]{2,1,0:T(8,128)(2,1)S(1)} %pair_up.4.refs_0_.own_ref, ...), custom_call_target="tpu_custom_call" | custom-call | flops 924844032 | bytes 2752512 | tf_op jit(solution)/shard_map/key_side_0/pallas_call | solution.py:402
  71.4 0.0 collective-permute-done.18._.far_ref.rest_5_
  71.4 1.3 %layer_out.1 = bf16[224,768]{1,0:T(8,128)(2,1)} custom-call(f32[224,768]{1,0:T(8,128)S(1)} %get-tuple-element.33.att_ref, f32[224,768]{1,0:T(8,128)S(1)} %convolution.3.rest_7_.conv_ref, bf16[2,224,768]{2,1,0:T(8,128)(2,1)S(1)} %pair_up.6.own.rest_2_, bf16[2,224,768]{2,1,0:T(8,128)(2,1)S(1)} %collective-permute-done.10.pair.rest_5_, ...), custom_call_target="tpu_custom_call" | custom-call | flops 231211008 | bytes 2752512 | tf_op jit(solution)/shard_map/layer_out/pallas_call | solution.py:402
  72.7 3.3 %key_side_1.1 = (f32[224,768]{1,0:T(8,128)S(1)}, f32[224,768]{1,0:T(8,128)S(1)}) custom-call(s32[4,8,9]{2,1,0:T(8,128)S(1)} %copy-done.6, s32[8]{0:T(128)S(1)} %copy-done.7, bf16[2,224,768]{2,1,0:T(8,128)(2,1)S(1)} %pad_maximum_fusion.own.refs_0_.rest_0_, bf16[2,224,768]{2,1,0:T(8,128)(2,1)S(1)} %collective-permute-done.6.rest_0_.refs_1_.own_ref, ...), custom_call_target="tpu_custom_call" | custom-call | flops 924844032 | bytes 2752512 | tf_op jit(solution)/shard_map/key_side_1/pallas_call | solution.py:402
  76.1 1.5 %collective-permute-done.19.far_ref = bf16[496,768]{1,0:T(8,128)(2,1)S(1)} collective-permute-done((bf16[496,768]{1,0:T(8,128)(2,1)S(1)}, bf16[496,768]{1,0:T(8,128)(2,1)S(1)}, u32[]{:S(2)}, u32[]{:S(2)}) %collective-permute-start.19) | collective-permute-done | bytes 761888 | tf_op jit(solution)/shard_map/ppermute | solution.py:62
  77.6 4.9 %key_side_2.1 = (bf16[224,768]{1,0:T(8,128)(2,1)}, bf16[224,768]{1,0:T(8,128)(2,1)}) custom-call(s32[4,8,9]{2,1,0:T(8,128)S(1)} %copy-done.6, s32[8]{0:T(128)S(1)} %copy-done.7, bf16[2,224,768]{2,1,0:T(8,128)(2,1)S(1)} %pad_maximum_fusion.own.refs_0_.rest_0_, bf16[2,224,768]{2,1,0:T(8,128)(2,1)S(1)} %collective-permute-done.7.rest_1_.refs_2_.own_ref, ...), custom_call_target="tpu_custom_call" | custom-call | flops 924844032 | bytes 2752512 | tf_op jit(solution)/shard_map/key_side_2/pallas_call | solution.py:402
  (10 shorter events, 0.2 us)
Async XLA Ops:
  0.6 11.8 %copy-start.4 = (bf16[2,2,56,768]{3,2,1,0:T(8,128)(2,1)S(1)}, bf16[2,2,56,768]{3,2,1,0:T(8,128)(2,1)}, u32[]{:S(2)}) copy-start(bf16[2,2,56,768]{3,2,1,0:T(8,128)(2,1)} %param.9) | copy-start | bytes 1032196
  1.8 2.5 %collective-permute-start.4 = (bf16[2,224,768]{2,1,0:T(8,128)(2,1)S(1)}, bf16[2,224,768]{2,1,0:T(8,128)(2,1)S(1)}, u32[]{:S(2)}, u32[]{:S(2)}) collective-permute-start(bf16[2,224,768]{2,1,0:T(8,128)(2,1)S(1)} %pad_maximum_fusion.own.refs_0_.rest_0_), channel_id=1, source_target_pairs={{0,8},{8,0},{16,24},{24,16},{1,9},{9,1},{17,25},{25,17},{2,10},{10... | collective-permute-start | bytes 2064392 | tf_op jit(solution)/shard_map/ppermute | solution.py:58
  2.6 9.9 %collective-permute-start = (bf16[224,768]{1,0:T(8,128)(2,1)}, bf16[224,768]{1,0:T(8,128)(2,1)S(1)}, u32[]{:S(2)}, u32[]{:S(2)}) collective-permute-start(bf16[224,768]{1,0:T(8,128)(2,1)} %bitcast.22), channel_id=1, source_target_pairs={{0,1},{1,0},{2,3},{3,2},{4,5},{5,4},{6,7},{7,6},{8,9},{9,8},{10,11... | collective-permute-start | bytes 1032200 | tf_op jit(solution)/shard_map/ppermute | solution.py:46
  4.3 1.0 %copy-start = (bf16[2,2,56,768]{3,2,1,0:T(8,128)(2,1)S(1)}, bf16[2,2,56,768]{3,2,1,0:T(8,128)(2,1)}, u32[]{:S(2)}) copy-start(bf16[2,2,56,768]{3,2,1,0:T(8,128)(2,1)} %param.7) | copy-start | bytes 1032196
  5.3 1.0 %copy-start.2 = (bf16[2,2,56,768]{3,2,1,0:T(8,128)(2,1)S(1)}, bf16[2,2,56,768]{3,2,1,0:T(8,128)(2,1)}, u32[]{:S(2)}) copy-start(bf16[2,2,56,768]{3,2,1,0:T(8,128)(2,1)} %param.11) | copy-start | bytes 1032196
  6.4 19.9 %copy-start.1 = (bf16[2,2,56,768]{3,2,1,0:T(8,128)(2,1)S(1)}, bf16[2,2,56,768]{3,2,1,0:T(8,128)(2,1)}, u32[]{:S(2)}) copy-start(bf16[2,2,56,768]{3,2,1,0:T(8,128)(2,1)} %param.7) | copy-start | bytes 1032196
  6.4 19.9 %copy-start.3 = (bf16[2,2,56,768]{3,2,1,0:T(8,128)(2,1)S(1)}, bf16[2,2,56,768]{3,2,1,0:T(8,128)(2,1)}, u32[]{:S(2)}) copy-start(bf16[2,2,56,768]{3,2,1,0:T(8,128)(2,1)} %param.11) | copy-start | bytes 1032196
  6.4 15.0 %collective-permute-start.6 = (bf16[2,224,768]{2,1,0:T(8,128)(2,1)S(1)}, bf16[2,224,768]{2,1,0:T(8,128)(2,1)S(1)}, u32[]{:S(2)}, u32[]{:S(2)}) collective-permute-start(bf16[2,224,768]{2,1,0:T(8,128)(2,1)S(1)} %pair_up.4.refs_0_.own_ref), channel_id=1, source_target_pairs={{0,8},{8,0},{16,24},{24,16},{1,9},{9,1},{17,25},{25,17},{2,10},{10... | collective-permute-start | bytes 2064392 | tf_op jit(solution)/shard_map/ppermute | solution.py:58
  6.8 14.6 %collective-permute-start.7 = (bf16[2,224,768]{2,1,0:T(8,128)(2,1)S(1)}, bf16[2,224,768]{2,1,0:T(8,128)(2,1)S(1)}, u32[]{:S(2)}, u32[]{:S(2)}) collective-permute-start(bf16[2,224,768]{2,1,0:T(8,128)(2,1)S(1)} %pair_up.4.refs_0_.own_ref), channel_id=1, source_target_pairs={{0,0},{8,16},{16,8},{24,24},{1,1},{9,17},{17,9},{25,25},{2,2},{10,... | collective-permute-start | bytes 2064392 | tf_op jit(solution)/shard_map/ppermute | solution.py:62
  12.5 18.3 %copy-start.6 = (s32[4,8,9]{2,1,0:T(8,128)S(1)}, s32[4,8,9]{2,1,0:T(8,128)}, u32[]{:S(2)}) copy-start(s32[4,8,9]{2,1,0:T(8,128)} %mask_ref.11) | copy-start | bytes 3460
  12.5 18.3 %copy-start.7 = (s32[8]{0:T(128)S(1)}, s32[8]{0:T(128)}, u32[]{:S(2)}) copy-start(s32[8]{0:T(128)} %clip_ref.11) | copy-start | bytes 100
  12.5 8.9 %collective-permute-start.2 = (bf16[224,768]{1,0:T(8,128)(2,1)S(1)}, bf16[224,768]{1,0:T(8,128)(2,1)S(1)}, u32[]{:S(2)}, u32[]{:S(2)}) collective-permute-start(bf16[224,768]{1,0:T(8,128)(2,1)S(1)} %later.1), channel_id=1, source_target_pairs={{0,1},{1,0},{2,3},{3,2},{4,5},{5,4},{6,7},{7,6},{8,9},{9,8},{10,11... | collective-permute-start | bytes 1032200 | tf_op jit(solution)/shard_map/ppermute | solution.py:46
  13.8 12.5 %collective-permute-start.1 = (bf16[224,768]{1,0:T(8,128)(2,1)S(1)}, bf16[224,768]{1,0:T(8,128)(2,1)S(1)}, u32[]{:S(2)}, u32[]{:S(2)}) collective-permute-start(bf16[224,768]{1,0:T(8,128)(2,1)S(1)} %collective-permute-done.rest_0_.x_ref), channel_id=1, source_target_pairs={{0,2},{2,4},{3,1},{4,6},{5,3},{7,5},{8,10},{10,12},{11,9},{12,14},... | collective-permute-start | bytes 1032200 | tf_op jit(solution)/shard_map/ppermute | solution.py:50
  17.0 13.8 %collective-permute-start.5 = (bf16[2,224,768]{2,1,0:T(8,128)(2,1)S(1)}, bf16[2,224,768]{2,1,0:T(8,128)(2,1)S(1)}, u32[]{:S(2)}, u32[]{:S(2)}) collective-permute-start(bf16[2,224,768]{2,1,0:T(8,128)(2,1)S(1)} %pad_maximum_fusion.own.refs_0_.rest_0_), channel_id=1, source_target_pairs={{0,0},{8,16},{16,8},{24,24},{1,1},{9,17},{17,9},{25,25},{2,2},{10,... | collective-permute-start | bytes 2064392 | tf_op jit(solution)/shard_map/ppermute | solution.py:62
  21.5 11.9 %copy-start.5 = (bf16[27,768]{1,0:T(8,128)(2,1)S(1)}, bf16[27,768]{1,0:T(8,128)(2,1)}, u32[]{:S(2)}) copy-start(bf16[27,768]{1,0:T(8,128)(2,1)} %rest_2_.1) | copy-start | bytes 124420
  21.5 13.0 %collective-permute-start.8 = (bf16[2,224,768]{2,1,0:T(8,128)(2,1)S(1)}, bf16[2,224,768]{2,1,0:T(8,128)(2,1)S(1)}, u32[]{:S(2)}, u32[]{:S(2)}) collective-permute-start(bf16[2,224,768]{2,1,0:T(8,128)(2,1)S(1)} %pair_up.5.own.refs_1_.rest_1_), channel_id=1, source_target_pairs={{0,8},{8,0},{16,24},{24,16},{1,9},{9,1},{17,25},{25,17},{2,10},{10... | collective-permute-start | bytes 2064392 | tf_op jit(solution)/shard_map/ppermute | solution.py:58
  23.2 14.5 %collective-permute-start.9 = (bf16[2,224,768]{2,1,0:T(8,128)(2,1)S(1)}, bf16[2,224,768]{2,1,0:T(8,128)(2,1)S(1)}, u32[]{:S(2)}, u32[]{:S(2)}) collective-permute-start(bf16[2,224,768]{2,1,0:T(8,128)(2,1)S(1)} %pair_up.5.own.refs_1_.rest_1_), channel_id=1, source_target_pairs={{0,0},{8,16},{16,8},{24,24},{1,1},{9,17},{17,9},{25,25},{2,2},{10,... | collective-permute-start | bytes 2064392 | tf_op jit(solution)/shard_map/ppermute | solution.py:62
  26.3 17.5 %collective-permute-start.12 = (bf16[2,224,768]{2,1,0:T(8,128)(2,1)S(1)}, bf16[2,224,768]{2,1,0:T(8,128)(2,1)S(1)}, u32[]{:S(2)}, u32[]{:S(2)}) collective-permute-start(bf16[2,224,768]{2,1,0:T(8,128)(2,1)S(1)} %pair_up.7), channel_id=1, source_target_pairs={{0,1},{1,0},{2,3},{3,2},{4,5},{5,4},{6,7},{7,6},{8,9},{9,8},{10,11... | collective-permute-start | bytes 2064392 | tf_op jit(solution)/shard_map/ppermute | solution.py:46
  27.6 12.7 %collective-permute-start.3 = (bf16[224,768]{1,0:T(8,128)(2,1)S(1)}, bf16[224,768]{1,0:T(8,128)(2,1)S(1)}, u32[]{:S(2)}, u32[]{:S(2)}) collective-permute-start(bf16[224,768]{1,0:T(8,128)(2,1)S(1)} %collective-permute-done.2.y_ref.rest_0_), channel_id=1, source_target_pairs={{0,2},{2,4},{3,1},{4,6},{5,3},{7,5},{8,10},{10,12},{11,9},{12,14},... | collective-permute-start | bytes 1032200 | tf_op jit(solution)/shard_map/ppermute | solution.py:50
  40.4 11.0 %collective-permute-start.10 = (bf16[2,224,768]{2,1,0:T(8,128)(2,1)S(1)}, bf16[2,224,768]{2,1,0:T(8,128)(2,1)S(1)}, u32[]{:S(2)}, u32[]{:S(2)}) collective-permute-start(bf16[2,224,768]{2,1,0:T(8,128)(2,1)S(1)} %pair_up.6.own.rest_2_), channel_id=1, source_target_pairs={{0,8},{8,0},{16,24},{24,16},{1,9},{9,1},{17,25},{25,17},{2,10},{10... | collective-permute-start | bytes 2064392 | tf_op jit(solution)/shard_map/ppermute | solution.py:58
  40.5 12.6 %collective-permute-start.11 = (bf16[2,224,768]{2,1,0:T(8,128)(2,1)S(1)}, bf16[2,224,768]{2,1,0:T(8,128)(2,1)S(1)}, u32[]{:S(2)}, u32[]{:S(2)}) collective-permute-start(bf16[2,224,768]{2,1,0:T(8,128)(2,1)S(1)} %pair_up.6.own.rest_2_), channel_id=1, source_target_pairs={{0,0},{8,16},{16,8},{24,24},{1,1},{9,17},{17,9},{25,25},{2,2},{10,... | collective-permute-start | bytes 2064392 | tf_op jit(solution)/shard_map/ppermute | solution.py:62
  43.8 20.3 %collective-permute-start.13 = (bf16[2,224,768]{2,1,0:T(8,128)(2,1)S(1)}, bf16[2,224,768]{2,1,0:T(8,128)(2,1)S(1)}, u32[]{:S(2)}, u32[]{:S(2)}) collective-permute-start(bf16[2,224,768]{2,1,0:T(8,128)(2,1)S(1)} %gate.1.near_ref.rest_6_), channel_id=1, source_target_pairs={{0,2},{2,4},{3,1},{4,6},{5,3},{7,5},{8,10},{10,12},{11,9},{12,14},... | collective-permute-start | bytes 2064392 | tf_op jit(solution)/shard_map/ppermute | solution.py:50
  47.0 17.0 %collective-permute-start.16 = (bf16[2,224,768]{2,1,0:T(8,128)(2,1)S(1)}, bf16[2,224,768]{2,1,0:T(8,128)(2,1)S(1)}, u32[]{:S(2)}, u32[]{:S(2)}) collective-permute-start(bf16[2,224,768]{2,1,0:T(8,128)(2,1)S(1)} %gate.1.near_ref.rest_6_), channel_id=1, source_target_pairs={{0,8},{8,0},{16,24},{24,16},{1,9},{9,1},{17,25},{25,17},{2,10},{10... | collective-permute-start | bytes 2064392 | tf_op jit(solution)/shard_map/ppermute | solution.py:58
  47.8 16.3 %collective-permute-start.17 = (bf16[2,224,768]{2,1,0:T(8,128)(2,1)S(1)}, bf16[2,224,768]{2,1,0:T(8,128)(2,1)S(1)}, u32[]{:S(2)}, u32[]{:S(2)}) collective-permute-start(bf16[2,224,768]{2,1,0:T(8,128)(2,1)S(1)} %gate.1.near_ref.rest_6_), channel_id=1, source_target_pairs={{0,0},{8,16},{16,8},{24,24},{1,1},{9,17},{17,9},{25,25},{2,2},{10,... | collective-permute-start | bytes 2064392 | tf_op jit(solution)/shard_map/ppermute | solution.py:62
  56.2 7.9 %collective-permute-start.14 = (f32[16,224]{1,0:T(8,128)S(1)}, f32[16,224]{1,0:T(8,128)S(1)}, u32[]{:S(2)}, u32[]{:S(2)}) collective-permute-start(f32[16,224]{1,0:T(8,128)S(1)} %get-tuple-element.34.own_ref.rest_0_), channel_id=1, source_target_pairs={{0,1},{1,0},{2,3},{3,2},{4,5},{5,4},{6,7},{7,6},{8,9},{9,8},{10,11... | collective-permute-start | bytes 43016 | tf_op jit(solution)/shard_map/ppermute | solution.py:46
  56.2 7.9 %collective-permute-start.15 = (f32[16,224]{1,0:T(8,128)S(1)}, f32[16,224]{1,0:T(8,128)S(1)}, u32[]{:S(2)}, u32[]{:S(2)}) collective-permute-start(f32[16,224]{1,0:T(8,128)S(1)} %get-tuple-element.34.own_ref.rest_0_), channel_id=1, source_target_pairs={{0,0},{1,2},{2,1},{3,4},{4,3},{5,6},{6,5},{7,7},{8,8},{9,10},{10,9... | collective-permute-start | bytes 43016 | tf_op jit(solution)/shard_map/ppermute | solution.py:54
  64.2 7.2 %collective-permute-start.18 = (bf16[496,768]{1,0:T(8,128)(2,1)S(1)}, bf16[496,768]{1,0:T(8,128)(2,1)S(1)}, u32[]{:S(2)}, u32[]{:S(2)}) collective-permute-start(bf16[496,768]{1,0:T(8,128)(2,1)S(1)} %pack.1), channel_id=1, source_target_pairs={{0,8},{8,0},{16,24},{24,16},{1,9},{9,1},{17,25},{25,17},{2,10},{10... | collective-permute-start | bytes 2285576 | tf_op jit(solution)/shard_map/ppermute | solution.py:58
  64.3 13.3 %collective-permute-start.19 = (bf16[496,768]{1,0:T(8,128)(2,1)S(1)}, bf16[496,768]{1,0:T(8,128)(2,1)S(1)}, u32[]{:S(2)}, u32[]{:S(2)}) collective-permute-start(bf16[496,768]{1,0:T(8,128)(2,1)S(1)} %pack.1), channel_id=1, source_target_pairs={{0,0},{8,16},{16,8},{24,24},{1,1},{9,17},{17,9},{25,25},{2,2},{10,... | collective-permute-start | bytes 2285576 | tf_op jit(solution)/shard_map/ppermute | solution.py:62
